TPU v7x, 32 devices: a whole 2x2x4 slice. The times are simulated.
32 devices in a mesh: phase: 2 (over x), ctx: 16 (over z, y, core).
Axes of the slice: x: 2, y: 2, z: 4, core: 2. Of those that a mesh axis runs over, the one named last changes fastest.
Arguments:
- inputs: bfloat16 [1, 2048, 2048], P(None, 'ctx'), may hold values from -6 to 6
- segment_ids: int32 [1, 2048], P(None, 'ctx'), may hold values from 0 to 7, never falling along the last dimension, each value on 1 to 768 neighbouring positions
- w_query: bfloat16 [2, 2048, 1024], P('phase'), may hold values from -1 to 1
- w_keyval: bfloat16 [2, 2048, 2048], P('phase', 'ctx'), may hold values from -16 to 16
- w_out: bfloat16 [2, 1024, 2048], P('phase'), may hold values from -0.1875 to 0.1875
Outputs:
- section_out: bfloat16 [2, 1, 2048, 2048], P('phase', None, 'ctx')
Inputs may be any that keep to these rules, and one draw needn't show every extreme that they name: `segment_ids`: ids never fall along the tokens of a micro-batch; each trajectory is a run of 1 to 768 tokens and one run has exactly 768.
All inputs are finite; a program needn't handle non-finite values.
Results may differ from a plain program's by a relative error of at most 0.015.
Values may be sent and summed in bfloat16 or wider, within the bound.
No kernel may reach another device: no remote copies, remote signals or barrier semaphores. Data moves between devices by JAX's collectives and lax.ppermute only.
A program may use at most 64 MiB of HBM per device.

v0:
```python
import math

import jax
import jax.numpy as jnp
from jax import lax
from jax.sharding import PartitionSpec as P

HEAD = 128
WINDOW = 4


far_begin = 1 << 30


def from_behind(block, axis, distance):
    devices = range(lax.axis_size(axis))
    route = [(i - distance, i) for i in devices if i - distance in devices]
    return lax.ppermute(block, axis, route)


def rms_rows(values):
    widened = values.astype(jnp.float32)
    return (
        widened * lax.rsqrt(jnp.mean(widened * widened, axis=-1, keepdims=True) + 1e-05)
    ).astype(jnp.bfloat16)


def attend(queries, key_rows, seg_begin, query_pos, key_pos):
    row_count, head_width = queries.shape
    head_count = head_width // HEAD
    query_part = queries.reshape(row_count, head_count, HEAD)
    key_part = key_rows[:, :head_width].reshape(-1, head_count, HEAD)
    value_part = key_rows[:, head_width:].reshape(-1, head_count, HEAD)
    scores = jnp.einsum(
        "qhd,khd->hqk", query_part, key_part, preferred_element_type=jnp.float32
    ) * (1.0 / math.sqrt(HEAD))
    allowed = (key_pos[None, :] <= query_pos[:, None]) & (key_pos[None, :] >= seg_begin[:, None])
    scores = jnp.where(allowed[None], scores, -jnp.inf)
    row_top = jnp.max(scores, axis=2, keepdims=True)
    weights = jnp.exp(scores - row_top)
    weights = (weights / jnp.sum(weights, axis=2, keepdims=True)).astype(jnp.bfloat16)
    blended = jnp.einsum("hqk,khd->qhd", weights, value_part, preferred_element_type=jnp.float32)
    return blended.astype(jnp.bfloat16).reshape(row_count, head_width)


def local(inputs, segment_ids, w_query, w_keyval, w_out):
    batches = inputs.shape[0]
    row_count = inputs.shape[1]
    phase_index = lax.axis_index("phase")
    phase_count = lax.axis_size("phase")
    device = lax.axis_index("ctx")
    positions = device * row_count + jnp.arange(row_count, dtype=jnp.int32)
    before = jnp.concatenate([jnp.full((batches, 1), -1, jnp.int32), segment_ids[:, :-1]], axis=1)
    boundary = jnp.where(segment_ids != before, positions[None, :], jnp.zeros_like(segment_ids))
    local_begin = lax.cummax(boundary, axis=1)
    tail_ids = segment_ids[:, -1]
    tail_begin = local_begin[:, -1]
    all_ids, all_begins = (
        lax.all_gather(tail_ids[None, :], "ctx", axis=0, tiled=True),
        lax.all_gather(tail_begin[None, :], "ctx", axis=0, tiled=True),
    )
    device_order = jnp.arange(all_ids.shape[0], dtype=jnp.int32)
    neighbour = jnp.maximum(device - 1, 0)
    prior_id = jnp.where(
        device > 0, lax.dynamic_index_in_dim(all_ids, neighbour, 0, keepdims=False), -1
    )
    matches = (device_order[:, None] < device) & (all_ids == prior_id[None, :])
    prior_begin = jnp.min(jnp.where(matches, all_begins, far_begin), axis=0)
    begins = jnp.where(segment_ids == prior_id[:, None], prior_begin[:, None], local_begin)
    keyval_full = lax.all_gather(w_keyval, "ctx", axis=1, tiled=True)[0]
    query_mat = w_query[0]
    out_mat = w_out[0]
    key_pos = (device - WINDOW + 1) * row_count + jnp.arange(WINDOW * row_count, dtype=jnp.int32)
    empty_rows = jnp.zeros((row_count, inputs.shape[2]), jnp.bfloat16)

    def tick(tick_index, carry):
        arrived, outputs = carry
        slot_raw = tick_index - phase_index
        active = (slot_raw >= 0) & (slot_raw < batches)
        slot_index = jnp.clip(slot_raw, 0, batches - 1)
        loaded = lax.dynamic_index_in_dim(inputs, slot_index, 0, keepdims=False)
        stream = jnp.where(phase_index == 0, loaded, arrived)
        normed = rms_rows(stream)
        queries = jnp.dot(normed, query_mat, preferred_element_type=jnp.float32).astype(
            jnp.bfloat16
        )
        keyvals = jnp.dot(normed, keyval_full, preferred_element_type=jnp.float32).astype(
            jnp.bfloat16
        )
        seg_begin = lax.dynamic_index_in_dim(begins, slot_index, 0, keepdims=False)
        earlier = []
        for offset in range(WINDOW - 1, 0, -1):
            earlier.append(from_behind(keyvals, "ctx", offset))
        key_rows = jnp.concatenate(earlier + [keyvals], axis=0)
        blended = attend(queries, key_rows, seg_begin, positions, key_pos)
        update = jnp.dot(blended, out_mat, preferred_element_type=jnp.float32)
        result = (stream.astype(jnp.float32) + update).astype(jnp.bfloat16)
        previous = lax.dynamic_index_in_dim(outputs, slot_index, 0, keepdims=False)
        written = jnp.where(active, result, previous)
        outputs = lax.dynamic_update_index_in_dim(outputs, written, slot_index, 0)
        arrived = from_behind(result, "phase", 1)
        return (arrived, outputs)

    tick_count = batches + phase_count - 1
    outputs = jnp.zeros((batches, row_count, inputs.shape[2]), jnp.bfloat16)
    arrived, outputs = lax.fori_loop(0, tick_count, tick, (empty_rows, outputs))
    return outputs[None]


def solution(mesh):
    placed = (
        P(None, "ctx", None),
        P(None, "ctx"),
        P("phase", None, None),
        P("phase", "ctx", None),
        P("phase", None, None),
    )
    return jax.shard_map(
        local, mesh=mesh, in_specs=placed, out_specs=P("phase", None, "ctx", None), check_vma=False
    )
```

profile of v0, /device:TPU:14, one launch (start us, length us, event | category | flops | bytes accessed | tf_op | source)
XLA Modules:
  0.0 216.2 jit_solution(4592022458420335855)
XLA Ops:
  6.5 0.0 all-gather.2.cloned.1.call-start
  6.5 0.7 all-gather.2.cloned.1.call-update
  7.3 1.2 slice.25
  8.5 0.8 compare_select_fusion
  9.3 0.3 reduce_window_max.10
  9.6 0.6 slice.27
  10.2 1.2 dynamic-slice
  11.4 1.2 bitcast_dynamic-update-slice_fusion
  12.7 1.2 bitcast_dynamic-update-slice_fusion.1
  13.9 10.5 %all-reduce.2 = (s32[16]{0:T(128)S(1)}, s32[16]{0:T(128)S(1)}) all-reduce(s32[16]{0:T(128)S(1)} %bitcast_dynamic-update-slice_fusion, s32[16]{0:T(128)S(1)} %bitcast_dynamic-update-slice_fusion.1), channel_id=1, replica_groups=mesh['phase'=2,'ctx'=16] {'ctx'}, use_global_device_ids=true, to_apply=%add.1 | all-reduce | flops 32 | bytes 256
  24.4 0.6 dynamic-slice.2
  25.7 0.6 fusion.36
  26.3 1.2 compare_select_fusion.1
  27.5 56.6 %all-gather.2.cloned.1.call-done = bf16[1,2048,2048]{2,1,0:T(8,128)(2,1)} async-done(((bf16[1,128,2048]{2,1,0:T(8,128)(2,1)}), bf16[1,2048,2048]{2,1,0:T(8,128)(2,1)}) %all-gather.2.cloned.1.call-update) | async-done | bytes 8388624 | tf_op jit(solution)/shard_map/all_gather | solution.py:70
  84.1 0.9 broadcast_in_dim.91
  85.0 123.6 %while.17 = (s32[]{:T(128)}, bf16[128,2048]{1,0:T(8,128)(2,1)}, bf16[1,128,2048]{2,1,0:T(8,128)(2,1)S(1)}, pred[]{:T(512)}, bf16[1,128,2048]{2,1,0:T(8,128)(2,1)...) while((s32[]{:T(128)}, bf16[128,2048]{1,0:T(8,128)(2,1)}, ...), condition=%wide.region_6.7_spmd.clone, body=%wide.region_2.6_spmd.clone.sunk | while | flops 2431845632 | bytes 82461064 | solution.py:106
  85.0 1.5 fusion.70
  86.5 0.0 copy-start
  86.5 4.8 %convolution_convert_fusion.5 = bf16[128,2048]{1,0:T(8,128)(2,1)S(1)} fusion(bf16[2048,2048]{1,0:T(8,128)(2,1)} %get-tuple-element.418, bf16[128,2048]{1,0:T(8,128)(2,1)S(1)} %get-tuple-element.379, f32[128]{0:T(128)S(1)} %add_rsqrt_fusion.2), kind=kOutput, calls=%fused_computation.4.clone.1 | convolution fusion | flops 1074790400 | bytes 9437696 | tf_op jit(solution)/shard_map/while/body/eval_jaxpr/dot_general | solution.py:87
  91.4 2.2 %collective-permute-start = (bf16[128,2048]{1,0:T(8,128)(2,1)S(1)}, bf16[128,2048]{1,0:T(8,128)(2,1)S(1)}, u32[]{:S(2)}, u32[]{:S(2)}) collective-permute-start(bf16[128,2048]{1,0:T(8,128)(2,1)S(1)} %convolution_convert_fusion.5), channel_id=1, source_target_pairs={{0,1},{1,2},{2,3},{3,4},{4,5},{5,6},{6,7},{7,8},{8,9},{9,10},{10,1... | collective-permute-start | bytes 1572872 | tf_op jit(solution)/shard_map/while/body/eval_jaxpr/ppermute | solution.py:18
  93.5 4.1 %collective-permute-start.1 = (bf16[128,2048]{1,0:T(8,128)(2,1)S(1)}, bf16[128,2048]{1,0:T(8,128)(2,1)S(1)}, u32[]{:S(2)}, u32[]{:S(2)}) collective-permute-start(bf16[128,2048]{1,0:T(8,128)(2,1)S(1)} %convolution_convert_fusion.5), channel_id=1, source_target_pairs={{0,2},{1,3},{2,4},{3,5},{4,6},{5,7},{6,8},{7,9},{8,10},{9,11},{10,... | collective-permute-start | bytes 1572872 | tf_op jit(solution)/shard_map/while/body/eval_jaxpr/ppermute | solution.py:18
  97.6 3.1 %collective-permute-start.2 = (bf16[128,2048]{1,0:T(8,128)(2,1)S(1)}, bf16[128,2048]{1,0:T(8,128)(2,1)S(1)}, u32[]{:S(2)}, u32[]{:S(2)}) collective-permute-start(bf16[128,2048]{1,0:T(8,128)(2,1)S(1)} %convolution_convert_fusion.5), channel_id=1, source_target_pairs={{0,3},{1,4},{2,5},{3,6},{4,7},{5,8},{6,9},{7,10},{8,11},{9,12},{10... | collective-permute-start | bytes 1572872 | tf_op jit(solution)/shard_map/while/body/eval_jaxpr/ppermute | solution.py:18
  100.7 0.1 compare_and_fusion.2
  100.9 0.0 copy-done
  100.9 0.8 fusion.71
  101.7 3.0 %collective-permute-done = bf16[128,2048]{1,0:T(8,128)(2,1)S(1)} collective-permute-done((bf16[128,2048]{1,0:T(8,128)(2,1)S(1)}, bf16[128,2048]{1,0:T(8,128)(2,1)S(1)}, u32[]{:S(2)}, u32[]{:S(2)}) %collective-permute-start) | collective-permute-done | bytes 524320 | tf_op jit(solution)/shard_map/while/body/eval_jaxpr/ppermute | solution.py:18
  104.7 5.6 %collective-permute-done.1 = bf16[128,2048]{1,0:T(8,128)(2,1)S(1)} collective-permute-done((bf16[128,2048]{1,0:T(8,128)(2,1)S(1)}, bf16[128,2048]{1,0:T(8,128)(2,1)S(1)}, u32[]{:S(2)}, u32[]{:S(2)}) %collective-permute-start.1) | collective-permute-done | bytes 524320 | tf_op jit(solution)/shard_map/while/body/eval_jaxpr/ppermute | solution.py:18
  110.3 14.9 %collective-permute-done.2 = bf16[128,2048]{1,0:T(8,128)(2,1)S(1)} collective-permute-done((bf16[128,2048]{1,0:T(8,128)(2,1)S(1)}, bf16[128,2048]{1,0:T(8,128)(2,1)S(1)}, u32[]{:S(2)}, u32[]{:S(2)}) %collective-permute-start.2) | collective-permute-done | bytes 524320 | tf_op jit(solution)/shard_map/while/body/eval_jaxpr/ppermute | solution.py:18
  125.2 0.2 pad_maximum_fusion.2
  125.4 1.2 slice_bitcast_fusion.2
  126.6 0.5 copy.41
  127.2 3.5 %fusion.72 = (f32[8,128]{1,0:T(8,128)S(1)}, f32[8,128,512]{2,1,0:T(8,128)}) fusion(pred[128,512]{1,0:T(8,128)(4,1)S(1)} %compare_and_fusion.2, bf16[64,8,8,128]{3,2,1,0:T(8,128)(2,1)} %get-tuple-element.382, bf16[16,8,8,128]{3,2,1,0:T(8,128)(2,1)S(1)} %fusion.71), kind=kOutput, calls=%fused_computation.43.clone.1 | convolution fusion | flops 136315392 | bytes 3477504 | tf_op jit(solution)/shard_map/while/body/eval_jaxpr/sub | solution.py:40
  130.7 0.0 copy-start.1
  130.7 2.3 %convolution_convert_fusion.6 = bf16[8,128,128]{2,1,0:T(8,128)(2,1)S(1)} fusion(bf16[512,8,128]{0,2,1:T(8,128)(2,1)S(1)} %bitcast.98, f32[8,128,512]{2,1,0:T(8,128)} %get-tuple-element.383, f32[8,128]{1,0:T(8,128)S(1)} %get-tuple-element.384), kind=kOutput, calls=%fused_computation.13.clone.1 | convolution fusion | flops 135397376 | bytes 3411968 | tf_op jit(solution)/shard_map/while/body/eval_jaxpr/hqk,khd->qhd/dot_general | solution.py:42
  133.0 0.5 copy-done.1
  133.5 0.7 fusion.73
  134.2 1.3 collective-permute-start.3
  135.6 0.1 fusion.74
  135.7 13.3 %collective-permute-done.3 = bf16[128,2048]{1,0:T(8,128)(2,1)} collective-permute-done((bf16[128,2048]{1,0:T(8,128)(2,1)S(1)}, bf16[128,2048]{1,0:T(8,128)(2,1)}, u32[]{:S(2)}, u32[]{:S(2)}) %collective-permute-start.3) | collective-permute-done | bytes 524320 | tf_op jit(solution)/shard_map/while/body/eval_jaxpr/ppermute | solution.py:18
  149.0 1.5 fusion.70
  150.4 0.0 copy-start
  150.5 4.8 %convolution_convert_fusion.5 = bf16[128,2048]{1,0:T(8,128)(2,1)S(1)} fusion(bf16[2048,2048]{1,0:T(8,128)(2,1)} %get-tuple-element.418, bf16[128,2048]{1,0:T(8,128)(2,1)S(1)} %get-tuple-element.379, f32[128]{0:T(128)S(1)} %add_rsqrt_fusion.2), kind=kOutput, calls=%fused_computation.4.clone.1 | convolution fusion | flops 1074790400 | bytes 9437696 | tf_op jit(solution)/shard_map/while/body/eval_jaxpr/dot_general | solution.py:87
  155.3 1.9 collective-permute-start
  157.2 1.9 collective-permute-start.1
  159.1 3.6 %collective-permute-start.2 = (bf16[128,2048]{1,0:T(8,128)(2,1)S(1)}, bf16[128,2048]{1,0:T(8,128)(2,1)S(1)}, u32[]{:S(2)}, u32[]{:S(2)}) collective-permute-start(bf16[128,2048]{1,0:T(8,128)(2,1)S(1)} %convolution_convert_fusion.5), channel_id=1, source_target_pairs={{0,3},{1,4},{2,5},{3,6},{4,7},{5,8},{6,9},{7,10},{8,11},{9,12},{10... | collective-permute-start | bytes 1572872 | tf_op jit(solution)/shard_map/while/body/eval_jaxpr/ppermute | solution.py:18
  162.8 0.1 compare_and_fusion.2
  162.9 0.0 copy-done
  162.9 0.8 fusion.71
  163.7 5.1 %collective-permute-done = bf16[128,2048]{1,0:T(8,128)(2,1)S(1)} collective-permute-done((bf16[128,2048]{1,0:T(8,128)(2,1)S(1)}, bf16[128,2048]{1,0:T(8,128)(2,1)S(1)}, u32[]{:S(2)}, u32[]{:S(2)}) %collective-permute-start) | collective-permute-done | bytes 524320 | tf_op jit(solution)/shard_map/while/body/eval_jaxpr/ppermute | solution.py:18
  168.8 5.1 %collective-permute-done.1 = bf16[128,2048]{1,0:T(8,128)(2,1)S(1)} collective-permute-done((bf16[128,2048]{1,0:T(8,128)(2,1)S(1)}, bf16[128,2048]{1,0:T(8,128)(2,1)S(1)}, u32[]{:S(2)}, u32[]{:S(2)}) %collective-permute-start.1) | collective-permute-done | bytes 524320 | tf_op jit(solution)/shard_map/while/body/eval_jaxpr/ppermute | solution.py:18
  174.0 10.8 %collective-permute-done.2 = bf16[128,2048]{1,0:T(8,128)(2,1)S(1)} collective-permute-done((bf16[128,2048]{1,0:T(8,128)(2,1)S(1)}, bf16[128,2048]{1,0:T(8,128)(2,1)S(1)}, u32[]{:S(2)}, u32[]{:S(2)}) %collective-permute-start.2) | collective-permute-done | bytes 524320 | tf_op jit(solution)/shard_map/while/body/eval_jaxpr/ppermute | solution.py:18
  184.8 0.2 pad_maximum_fusion.2
  184.9 1.2 slice_bitcast_fusion.2
  186.1 0.5 copy.41
  186.7 3.5 %fusion.72 = (f32[8,128]{1,0:T(8,128)S(1)}, f32[8,128,512]{2,1,0:T(8,128)}) fusion(pred[128,512]{1,0:T(8,128)(4,1)S(1)} %compare_and_fusion.2, bf16[64,8,8,128]{3,2,1,0:T(8,128)(2,1)} %get-tuple-element.382, bf16[16,8,8,128]{3,2,1,0:T(8,128)(2,1)S(1)} %fusion.71), kind=kOutput, calls=%fused_computation.43.clone.1 | convolution fusion | flops 136315392 | bytes 3477504 | tf_op jit(solution)/shard_map/while/body/eval_jaxpr/sub | solution.py:40
  190.2 0.0 copy-start.1
  190.2 2.3 %convolution_convert_fusion.6 = bf16[8,128,128]{2,1,0:T(8,128)(2,1)S(1)} fusion(bf16[512,8,128]{0,2,1:T(8,128)(2,1)S(1)} %bitcast.98, f32[8,128,512]{2,1,0:T(8,128)} %get-tuple-element.383, f32[8,128]{1,0:T(8,128)S(1)} %get-tuple-element.384), kind=kOutput, calls=%fused_computation.13.clone.1 | convolution fusion | flops 135397376 | bytes 3411968 | tf_op jit(solution)/shard_map/while/body/eval_jaxpr/hqk,khd->qhd/dot_general | solution.py:42
  192.5 0.5 copy-done.1
  193.0 0.7 fusion.73
  193.8 1.3 collective-permute-start.3
  195.1 0.1 fusion.74
  195.2 13.4 %collective-permute-done.3 = bf16[128,2048]{1,0:T(8,128)(2,1)} collective-permute-done((bf16[128,2048]{1,0:T(8,128)(2,1)S(1)}, bf16[128,2048]{1,0:T(8,128)(2,1)}, u32[]{:S(2)}, u32[]{:S(2)}) %collective-permute-start.3) | collective-permute-done | bytes 524320 | tf_op jit(solution)/shard_map/while/body/eval_jaxpr/ppermute | solution.py:18
  208.6 0.0 copy-start.2
  208.6 0.8 copy-done.2
  (9 shorter events, 0.1 us)
Async XLA Ops:
  6.5 77.5 %all-gather.2.cloned.1.call-start = ((), (), s32[]{:S(2)}) async-start(), calls=%async_computation | async-start | bytes 8912896 | tf_op jit(solution)/shard_map/all_gather | solution.py:70
  86.5 14.4 %copy-start = (bf16[2048,1024]{1,0:T(8,128)(2,1)S(1)}, bf16[2048,1024]{1,0:T(8,128)(2,1)}, u32[]{:S(2)}) copy-start(bf16[2048,1024]{1,0:T(8,128)(2,1)} %get-tuple-element.420) | copy-start | bytes 12582916 | tf_op jit(solution)/shard_map/while
  91.4 13.3 %collective-permute-start = (bf16[128,2048]{1,0:T(8,128)(2,1)S(1)}, bf16[128,2048]{1,0:T(8,128)(2,1)S(1)}, u32[]{:S(2)}, u32[]{:S(2)}) collective-permute-start(bf16[128,2048]{1,0:T(8,128)(2,1)S(1)} %convolution_convert_fusion.5), channel_id=1, source_target_pairs={{0,1},{1,2},{2,3},{3,4},{4,5},{5,6},{6,7},{7,8},{8,9},{9,10},{10,1... | collective-permute-start | bytes 1572872 | tf_op jit(solution)/shard_map/while/body/eval_jaxpr/ppermute | solution.py:18
  93.5 16.8 %collective-permute-start.1 = (bf16[128,2048]{1,0:T(8,128)(2,1)S(1)}, bf16[128,2048]{1,0:T(8,128)(2,1)S(1)}, u32[]{:S(2)}, u32[]{:S(2)}) collective-permute-start(bf16[128,2048]{1,0:T(8,128)(2,1)S(1)} %convolution_convert_fusion.5), channel_id=1, source_target_pairs={{0,2},{1,3},{2,4},{3,5},{4,6},{5,7},{6,8},{7,9},{8,10},{9,11},{10,... | collective-permute-start | bytes 1572872 | tf_op jit(solution)/shard_map/while/body/eval_jaxpr/ppermute | solution.py:18
  97.6 27.6 %collective-permute-start.2 = (bf16[128,2048]{1,0:T(8,128)(2,1)S(1)}, bf16[128,2048]{1,0:T(8,128)(2,1)S(1)}, u32[]{:S(2)}, u32[]{:S(2)}) collective-permute-start(bf16[128,2048]{1,0:T(8,128)(2,1)S(1)} %convolution_convert_fusion.5), channel_id=1, source_target_pairs={{0,3},{1,4},{2,5},{3,6},{4,7},{5,8},{6,9},{7,10},{8,11},{9,12},{10... | collective-permute-start | bytes 1572872 | tf_op jit(solution)/shard_map/while/body/eval_jaxpr/ppermute | solution.py:18
  130.7 2.8 %copy-start.1 = (bf16[1024,2048]{1,0:T(8,128)(2,1)S(1)}, bf16[1024,2048]{1,0:T(8,128)(2,1)}, u32[]{:S(2)}) copy-start(bf16[1024,2048]{1,0:T(8,128)(2,1)} %get-tuple-element.421) | copy-start | bytes 12582916 | tf_op jit(solution)/shard_map/while
  134.2 14.7 %collective-permute-start.3 = (bf16[128,2048]{1,0:T(8,128)(2,1)S(1)}, bf16[128,2048]{1,0:T(8,128)(2,1)}, u32[]{:S(2)}, u32[]{:S(2)}) collective-permute-start(bf16[128,2048]{1,0:T(8,128)(2,1)S(1)} %fusion.73), channel_id=1, source_target_pairs={{0,16},{1,17},{2,18},{3,19},{4,20},{5,21},{6,22},{7,23},{8,24},{9,... | collective-permute-start | bytes 1572872 | tf_op jit(solution)/shard_map/while/body/eval_jaxpr/ppermute | solution.py:18
  150.4 12.5 %copy-start = (bf16[2048,1024]{1,0:T(8,128)(2,1)S(1)}, bf16[2048,1024]{1,0:T(8,128)(2,1)}, u32[]{:S(2)}) copy-start(bf16[2048,1024]{1,0:T(8,128)(2,1)} %get-tuple-element.420) | copy-start | bytes 12582916 | tf_op jit(solution)/shard_map/while
  155.3 13.5 %collective-permute-start = (bf16[128,2048]{1,0:T(8,128)(2,1)S(1)}, bf16[128,2048]{1,0:T(8,128)(2,1)S(1)}, u32[]{:S(2)}, u32[]{:S(2)}) collective-permute-start(bf16[128,2048]{1,0:T(8,128)(2,1)S(1)} %convolution_convert_fusion.5), channel_id=1, source_target_pairs={{0,1},{1,2},{2,3},{3,4},{4,5},{5,6},{6,7},{7,8},{8,9},{9,10},{10,1... | collective-permute-start | bytes 1572872 | tf_op jit(solution)/shard_map/while/body/eval_jaxpr/ppermute | solution.py:18
  157.2 16.8 %collective-permute-start.1 = (bf16[128,2048]{1,0:T(8,128)(2,1)S(1)}, bf16[128,2048]{1,0:T(8,128)(2,1)S(1)}, u32[]{:S(2)}, u32[]{:S(2)}) collective-permute-start(bf16[128,2048]{1,0:T(8,128)(2,1)S(1)} %convolution_convert_fusion.5), channel_id=1, source_target_pairs={{0,2},{1,3},{2,4},{3,5},{4,6},{5,7},{6,8},{7,9},{8,10},{9,11},{10,... | collective-permute-start | bytes 1572872 | tf_op jit(solution)/shard_map/while/body/eval_jaxpr/ppermute | solution.py:18
  159.1 25.6 %collective-permute-start.2 = (bf16[128,2048]{1,0:T(8,128)(2,1)S(1)}, bf16[128,2048]{1,0:T(8,128)(2,1)S(1)}, u32[]{:S(2)}, u32[]{:S(2)}) collective-permute-start(bf16[128,2048]{1,0:T(8,128)(2,1)S(1)} %convolution_convert_fusion.5), channel_id=1, source_target_pairs={{0,3},{1,4},{2,5},{3,6},{4,7},{5,8},{6,9},{7,10},{8,11},{9,12},{10... | collective-permute-start | bytes 1572872 | tf_op jit(solution)/shard_map/while/body/eval_jaxpr/ppermute | solution.py:18
  190.2 2.8 %copy-start.1 = (bf16[1024,2048]{1,0:T(8,128)(2,1)S(1)}, bf16[1024,2048]{1,0:T(8,128)(2,1)}, u32[]{:S(2)}) copy-start(bf16[1024,2048]{1,0:T(8,128)(2,1)} %get-tuple-element.421) | copy-start | bytes 12582916 | tf_op jit(solution)/shard_map/while
  193.8 14.8 %collective-permute-start.3 = (bf16[128,2048]{1,0:T(8,128)(2,1)S(1)}, bf16[128,2048]{1,0:T(8,128)(2,1)}, u32[]{:S(2)}, u32[]{:S(2)}) collective-permute-start(bf16[128,2048]{1,0:T(8,128)(2,1)S(1)} %fusion.73), channel_id=1, source_target_pairs={{0,16},{1,17},{2,18},{3,19},{4,20},{5,21},{6,22},{7,23},{8,24},{9,... | collective-permute-start | bytes 1572872 | tf_op jit(solution)/shard_map/while/body/eval_jaxpr/ppermute | solution.py:18
  208.6 0.8 copy-start.2
Sparse Core Ops, SparseCore 0:
  9.5 74.5 all-gather.1
where the time goes:
time: 217 us; the launch traced here: 216 us
  waiting for transfers between devices  128 us (59%)
  matrix products  24.3 us (11%)
  starting transfers between devices  19.4 us (9%)
  between operations  14.1 us (6%)
  local copies, waits for them, and re-layouts  12.4 us (6%)
  blocking collectives  10.5 us (5%)
  other arithmetic  6.76 us (3%)
    ppermute x8, waiting for transfers between devices, from_behind(): return lax.ppermute(block, axis, route)  71.2 us
    all_gather x1, waiting for transfers between devices, local(): keyval_full = lax.all_gather(w_keyval, 'ctx', axis=1, tiled=True)[0]  56.6 us
    ppermute x8, starting transfers between devices, from_behind(): return lax.ppermute(block, axis, route)  19.4 us
    unnamed x1, blocking collectives  10.5 us
    dot_general x2, matrix products, tick(): jnp.dot(normed, keyval_full, preferred_element_type=jnp.float32)  9.66 us
    sub x2, matrix products, attend(): weights = jnp.exp(scores - row_top)  7.01 us
    dot_general x2, matrix products, attend(): jnp.einsum('hqk,khd->qhd', weights, value_part, preferred_element_type=jn...  4.54 us
    unnamed x7, local copies, waits for them, and re-layouts  4.49 us
  transfers between devices with their start and end apart: 9, of which 9 were waited for; matrix products, arithmetic and copies ran while one was open for 5% of the time, Pallas kernels for 0%

commit v1 on v0

v1 whole, which is shorter than its diff:
```python
import functools
import math

import jax
import jax.numpy as jnp
from jax import lax
from jax.experimental import pallas as pl
from jax.experimental.pallas import tpu as pltpu
from jax.sharding import PartitionSpec as P

HEAD = 128
WINDOW = 4
PLANE = 4
ORDER = (0, 2, 1, 3)
BOTH = ("phase", "ctx")
VMEM_BYTES = 48 * 1024 * 1024


def swap(block, phase_bit, ctx_bits):
    wide = lax.axis_size("ctx")
    route = [
        (f * wide + d, (f ^ phase_bit) * wide + (d ^ ctx_bits))
        for f in range(lax.axis_size("phase"))
        for d in range(wide)
    ]
    return lax.ppermute(block, BOTH, route)


def from_plane_behind(block):
    wide = lax.axis_size("ctx")
    return lax.ppermute(block, "ctx", [(i, i + PLANE) for i in range(wide - PLANE)])


def pick(blocks, index):
    return lax.dynamic_index_in_dim(blocks, index, 0, keepdims=False)


def rms_rows(values):
    widened = values.astype(jnp.float32)
    scale = lax.rsqrt(jnp.mean(widened * widened, axis=-1, keepdims=True) + 1e-05)
    return (widened * scale).astype(jnp.bfloat16)


def dot(a, b):
    return jnp.dot(a, b, preferred_element_type=jnp.float32)


def call(kernel, outs, scratch, flops, *operands):
    moved = sum(o.size * o.dtype.itemsize for o in operands)
    return pl.pallas_call(
        kernel,
        out_shape=[jax.ShapeDtypeStruct(s, d) for s, d in outs],
        in_specs=[pl.BlockSpec(memory_space=pltpu.VMEM)] * len(operands),
        out_specs=[pl.BlockSpec(memory_space=pltpu.VMEM)] * len(outs),
        scratch_shapes=[pltpu.VMEM(s, d) for s, d in scratch],
        cost_estimate=pl.CostEstimate(flops=flops, bytes_accessed=moved, transcendentals=0),
        compiler_params=pltpu.CompilerParams(vmem_limit_bytes=VMEM_BYTES),
    )(*operands)


def fill_weights(ctx, weight_refs, weights):
    rows = weight_refs[0].shape[0] // PLANE
    for m, ref in enumerate(weight_refs):
        for r, o in enumerate(ORDER):
            source = ctx ^ (PLANE * m + o)
            weights[pl.ds(pl.multiple_of(source * rows, rows), rows), :] = ref[
                r * rows : (r + 1) * rows, :
            ]


def project(normed, weights, wq_ref, q_ref, kv_ref, tail_ref):
    rows = tail_ref.shape[0]
    keyvals = dot(normed[...], weights[...]).astype(jnp.bfloat16)
    kv_ref[...] = keyvals
    tail_ref[...] = keyvals[keyvals.shape[0] - rows :]
    q_ref[...] = dot(normed[...], wq_ref[...]).astype(jnp.bfloat16)


def first_kernel(pieces, *refs):
    x_refs, weight_refs = refs[:PLANE], refs[PLANE : PLANE + pieces]
    wq_ref, q_ref, kv_ref, tail_ref, normed, weights = refs[PLANE + pieces :]
    ctx = lax.axis_index("ctx")
    rows = x_refs[0].shape[0]
    own = lax.rem(ctx, PLANE)
    for r, o in enumerate(ORDER):
        normed[pl.ds(pl.multiple_of((own ^ o) * rows, rows), rows), :] = rms_rows(x_refs[r][...])
    fill_weights(ctx, weight_refs, weights)
    project(normed, weights, wq_ref, q_ref, kv_ref, tail_ref)


def second_kernel(pieces, *refs):
    x_refs, b_refs = refs[:PLANE], refs[PLANE : 3 * PLANE]
    wo_refs, refs = refs[3 * PLANE : 4 * PLANE], refs[4 * PLANE :]
    weight_refs, refs = refs[:pieces], refs[pieces:]
    wq_ref, own_ref, q_ref, kv_ref, tail_ref, stream, blended, normed, weights = refs
    ctx = lax.axis_index("ctx")
    side = lax.rem(lax.axis_index("phase"), 2)
    rows = x_refs[0].shape[0]
    own = lax.rem(ctx, PLANE)
    part = b_refs[0].shape[1]
    deep = wo_refs[0].shape[0]
    fill_weights(ctx, weight_refs, weights)
    for r, o in enumerate(ORDER):
        stream[pl.ds(pl.multiple_of((own ^ o) * rows, rows), rows), :] = x_refs[r][...]
    for m, ref in enumerate(b_refs):
        place = (side * PLANE + own) ^ m
        blended[:, pl.ds(pl.multiple_of(place * part, part), part)] = ref[...]
    width = stream.shape[1]
    step = min(512, width)
    for n in range(0, width, step):
        total = stream[:, n : n + step].astype(jnp.float32)
        for r, o in enumerate(ORDER):
            place = pl.multiple_of((own ^ o) * deep, deep)
            total = total + dot(blended[:, pl.ds(place, deep)], wo_refs[r][:, n : n + step])
        stream[:, n : n + step] = total.astype(jnp.bfloat16)
    normed[...] = rms_rows(stream[...])
    own_ref[...] = stream[pl.ds(pl.multiple_of(own * rows, rows), rows), :]
    project(normed, weights, wq_ref, q_ref, kv_ref, tail_ref)


def mask_kernel(rows, id_ref, past_ref, bias_ref):
    ctx = lax.axis_index("ctx")
    own = lax.rem(ctx, PLANE)
    first = ctx < PLANE

    def ids(group):
        ref = id_ref if group >= WINDOW - 1 else past_ref
        natural = group - (WINDOW - 1) if group >= WINDOW - 1 else group + PLANE - (WINDOW - 1)
        row = jnp.zeros((1, rows), jnp.int32)
        for r, o in enumerate(ORDER):
            row = row + jnp.where((own ^ o) == natural, 1, 0) * ref[r : r + 1, :]
        return row

    keys = [ids(t) for t in range(PLANE + WINDOW - 1)]
    causal = lax.broadcasted_iota(jnp.int32, (rows, rows), 0) >= lax.broadcasted_iota(
        jnp.int32, (rows, rows), 1
    )
    for g in range(PLANE):
        mine = keys[g + WINDOW - 1].astype(jnp.float32)
        mine = jnp.transpose(jnp.broadcast_to(mine, (rows, rows)))
        for t in range(WINDOW):
            allowed = mine == keys[g + t].astype(jnp.float32)
            if t == WINDOW - 1:
                allowed = allowed & causal
            if g + t < WINDOW - 1:
                allowed = allowed & jnp.logical_not(first)
            bias_ref[g, :, t * rows : (t + 1) * rows] = jnp.where(allowed, 0.0, -jnp.inf)


def attend_kernel(split, q_ref, kv_ref, past_ref, bias_ref, *refs):
    out_refs, window = refs[:-1], refs[-1]
    rows = bias_ref.shape[1]
    past = past_ref.shape[0]
    part = q_ref.shape[1]
    window[:past] = past_ref[...]
    window[past:] = kv_ref[...]
    upper = lax.rem(lax.axis_index("ctx"), PLANE) // 2
    for g in range(PLANE):
        keys = window[g * rows : (g + WINDOW) * rows]
        for h in range(0, part, HEAD):
            query = q_ref[g * rows : (g + 1) * rows, h : h + HEAD]
            scores = lax.dot_general(
                query, keys[:, h : h + HEAD], (((1,), (1,)), ((), ())),
                preferred_element_type=jnp.float32,
            )
            scores = scores * (1.0 / math.sqrt(HEAD)) + bias_ref[g]
            weights = jnp.exp(scores - jnp.max(scores, axis=1, keepdims=True))
            total = jnp.sum(weights, axis=1, keepdims=True)
            values = keys[:, part + h : part + h + HEAD]
            result = (dot(weights.astype(jnp.bfloat16), values) / total).astype(jnp.bfloat16)
            if not split:
                out_refs[0][g * rows : (g + 1) * rows, h : h + HEAD] = result
                continue
            place = (g % 2) * rows

            def put(ref):
                ref[place : place + rows, h : h + HEAD] = result

            pl.when(upper == g // 2)(functools.partial(put, out_refs[0]))
            pl.when(upper != g // 2)(functools.partial(put, out_refs[1]))


def last_kernel(*refs):
    b_refs, (wo_ref, own_ref, out_ref, blended) = refs[: 2 * PLANE], refs[2 * PLANE :]
    own = lax.rem(lax.axis_index("ctx"), PLANE)
    side = lax.rem(lax.axis_index("phase"), 2)
    rows, part = own_ref.shape[0], b_refs[0].shape[1]

    @pl.when(side == 0)
    def _():
        out_ref[...] = own_ref[...]

    @pl.when(side == 1)
    def _():
        for m, ref in enumerate(b_refs):
            place = (side * PLANE + own) ^ m
            start = pl.multiple_of(lax.rem(own, 2) * rows, rows)
            blended[:, pl.ds(pl.multiple_of(place * part, part), part)] = ref[pl.ds(start, rows), :]
        total = own_ref[...].astype(jnp.float32) + dot(blended[...], wo_ref[...])
        out_ref[...] = total.astype(jnp.bfloat16)


def plane_rows(block):
    across = swap(block, 0, 2)
    return [block, across, swap(block, 0, 1), swap(across, 0, 1)]


def key_weights(blocks, own):
    upper, core = own // 2, own % 2
    pairs = blocks.reshape((2, 2) + blocks.shape[1:])
    kept = pick(pairs, upper)
    got = swap(pick(pairs, 1 - upper), 0, 2)
    near = [pick(kept, core), pick(got, core)]
    far = swap(jnp.stack([pick(kept, 1 - core), pick(got, 1 - core)]), 0, 1)
    piece = jnp.concatenate(near + [far[0], far[1]], axis=0)
    count = lax.axis_size("ctx") // PLANE
    return [piece] + [swap(piece, 0, PLANE * m) for m in range(count - 1, 0, -1)][::-1]


def local(inputs, segment_ids, w_query, w_keyval, w_out):
    batches, rows, width = inputs.shape
    phases = lax.axis_size("phase")
    phase = lax.axis_index("phase")
    side = phase % 2
    ctx = lax.axis_index("ctx")
    own = ctx % PLANE
    bf16 = jnp.bfloat16

    head_width = w_query.shape[2]
    part = head_width // (2 * PLANE)
    depth = w_keyval.shape[1]
    blocks = w_keyval[0].reshape(depth, 2, 2 * PLANE, part).transpose(2, 0, 1, 3)
    blocks = blocks.reshape(2, PLANE, depth, 2 * part)
    kept, got = pick(blocks, side), swap(pick(blocks, 1 - side), 1, 0)
    early = key_weights(jnp.where(side == 0, kept, got), own)
    late = key_weights(jnp.where(side == 0, got, kept), own)

    mat = w_query[0]
    kept = lax.dynamic_slice_in_dim(mat, (side * PLANE + own) * part, part, 1)
    sent = lax.dynamic_slice_in_dim(mat, ((1 - side) * PLANE + own) * part, part, 1)
    got = swap(sent, 1, 0)
    early_query, late_query = jnp.where(side == 0, kept, got), jnp.where(side == 0, got, kept)

    mat = w_out[0]
    quarter = head_width // PLANE
    kept = lax.dynamic_slice_in_dim(mat, own * quarter, quarter, 0)
    early_out = plane_rows(jnp.where(side == 0, kept, swap(kept, 1, 0)))

    tall, past = PLANE * rows, (WINDOW - 1) * rows
    pieces = len(early)
    qkv = [((tall, part), bf16), ((tall, 2 * part), bf16), ((past, 2 * part), bf16)]
    weights = ((width, 2 * part), bf16)
    qkv_flops = 2 * tall * width * 3 * part
    attend_flops = 4 * tall * WINDOW * rows * part
    window = [((past + tall, 2 * part), bf16)]

    def bias_of(ids):
        plane = jnp.concatenate([ids, swap(ids, 0, 2)], axis=0)
        plane = jnp.concatenate([plane, swap(plane, 0, 1)], axis=0)
        shape = ((PLANE, rows, WINDOW * rows), jnp.float32)
        return call(
            functools.partial(mask_kernel, rows), [shape], [], 0, plane, from_plane_behind(plane)
        )[0]

    biases = [bias_of(segment_ids[b : b + 1]) for b in range(batches)]

    def two_layers(x, bias):
        xs = plane_rows(x)
        q, kv, tail = call(
            functools.partial(first_kernel, pieces), qkv, [((tall, width), bf16), weights],
            qkv_flops, *xs, *early, early_query,
        )
        blended = call(
            functools.partial(attend_kernel, False), [((tall, part), bf16)], window,
            attend_flops, q, kv, from_plane_behind(tail), bias,
        )[0]
        near = [blended, swap(blended, 0, 2), swap(blended, 1, 0), swap(blended, 1, 2)]
        heads = [b for n in near for b in (n, swap(n, 0, 1))]
        stream, q, kv, tail = call(
            functools.partial(second_kernel, pieces), [((rows, width), bf16)] + qkv,
            [((tall, width), bf16), ((tall, head_width), bf16), ((tall, width), bf16), weights],
            qkv_flops + 2 * tall * head_width * width,
            *xs, *heads, *early_out, *late, late_query,
        )
        mine, other = call(
            functools.partial(attend_kernel, True), [((tall // 2, part), bf16)] * 2, window,
            attend_flops, q, kv, from_plane_behind(tail), bias,
        )
        near = [mine, swap(other, 0, 2), swap(mine, 1, 0), swap(other, 1, 2)]
        heads = [b for n in near for b in (n, swap(n, 0, 1))]
        return call(
            last_kernel, [((rows, width), bf16)], [((rows, head_width), bf16)],
            2 * rows * head_width * width, *heads, w_out[0], stream,
        )[0]

    outs = []
    for b in range(batches):
        x, out = inputs[b], None
        for tick in range(phases // 2):
            result = two_layers(x, biases[b])
            out = result if out is None else jnp.where(phase // 2 == tick, result, out)
            if tick + 1 < phases // 2:
                ahead = [
                    lax.ppermute(result, "phase", [(f, f + d) for f in range(1, phases - d, 2)])
                    for d in (1, 2)
                ]
                x = jnp.where(side == 0, ahead[0], ahead[1])
        outs.append(out)
    return jnp.stack(outs)[None]


def solution(mesh):
    placed = (
        P(None, "ctx", None),
        P(None, "ctx"),
        P("phase", None, None),
        P("phase", "ctx", None),
        P("phase", None, None),
    )
    return jax.shard_map(
        local, mesh=mesh, in_specs=placed, out_specs=P("phase", None, "ctx", None), check_vma=False
    )
```

time: 217 us -> 133 us (0.61)
  waiting for transfers between devices: 128 us -> 67.9 us
  matrix products: 24.3 us -> 0 us
  starting transfers between devices: 19.4 us -> 35.3 us
  between operations: 14.1 us -> 0.31 us
  Pallas kernels: 0 us -> 13 us
  blocking collectives: 10.5 us -> 0 us
  other arithmetic: 6.76 us -> 4.02 us
    all_gather x1 -> x0, waiting for transfers between devices: 56.6 us -> none  [local(): keyval_full = lax.all_gather(w_keyval, 'ctx', axis=1, tiled=True)[0]]
    dot_general x8 -> x0, matrix products: 17.3 us -> none  [the longest x2 9.66 us: tick(): jnp.dot(normed, keyval_full, preferred_element_type=jnp.float32)]
    ppermute x8 -> x38, starting transfers between devices: 19.4 us -> 35.3 us  [the longest x35 24.8 us: swap(): return lax.ppermute(block, BOTH, route)]
    pallas_call x0 -> x6, Pallas kernels: none -> 13 us  [call(): pl.pallas_call(kernel, out_shape=[jax.ShapeDtypeStruct(s, d) for s, d in...]
    unnamed x1 -> x0, blocking collectives: 10.5 us -> none
    sub x2 -> x0, matrix products: 7.01 us -> none  [attend(): weights = jnp.exp(scores - row_top)]
    dynamic_slice x0 -> x5, local copies, waits for them, and re-layouts: none -> 4.91 us  [the longest x1 1.87 us: local(): lax.dynamic_slice_in_dim(mat, ((1 - side) * PLANE + own) * part, part, 1)]
    while x10 -> x0, local copies, waits for them, and re-layouts: 3.53 us -> none
  transfers between devices with their start and end apart: 9 -> 38, of which waited for: 9 -> 21; matrix products, arithmetic and copies ran while one was open for 5% -> 8% of each run, Pallas kernels for 0% -> 3%
where the time goes in v1:
time: 133 us; the launch traced here: 131 us
  waiting for transfers between devices  67.9 us (51%)
  starting transfers between devices  35.3 us (27%)
  Pallas kernels  13 us (10%)
  local copies, waits for them, and re-layouts  10.3 us (8%)
  other arithmetic  4.02 us (3%)
    ppermute x35, waiting for transfers between devices, swap(): return lax.ppermute(block, BOTH, route)  58.2 us
    ppermute x35, starting transfers between devices, swap(): return lax.ppermute(block, BOTH, route)  24.8 us
    pallas_call x6, Pallas kernels, call(): pl.pallas_call(kernel, out_shape=[jax.ShapeDtypeStruct(s, d) for s, d in...  13 us
    ppermute x3, starting transfers between devices, from_plane_behind(): lax.ppermute(block, 'ctx', [(i, i + PLANE) for i in range(wide - PLANE)])  10.6 us
    ppermute x3, waiting for transfers between devices, from_plane_behind(): lax.ppermute(block, 'ctx', [(i, i + PLANE) for i in range(wide - PLANE)])  9.7 us
    unnamed x17, local copies, waits for them, and re-layouts  2.66 us
  transfers between devices with their start and end apart: 38, of which 21 were waited for; matrix products, arithmetic and copies ran while one was open for 8% of the time, Pallas kernels for 3%

profile of v1, /device:TPU:14, one launch (start us, length us, event | category | flops | bytes accessed | tf_op | source)
XLA Modules:
  0.0 130.9 jit_solution(10883032164969728963)
XLA Ops:
  0.0 1.3 copy.6
  1.4 0.8 copy.9
  2.3 0.5 collective-permute-start.3
  2.8 0.5 collective-permute-start
  3.3 1.3 dynamic-slice_bitcast_fusion
  4.6 1.6 %collective-permute-start.21 = (bf16[256,2048]{1,0:T(8,128)(2,1)S(1)}, bf16[256,2048]{1,0:T(8,128)(2,1)S(1)}, u32[]{:S(2)}, u32[]{:S(2)}) collective-permute-start(bf16[256,2048]{1,0:T(8,128)(2,1)S(1)} %dynamic-slice_bitcast_fusion), channel_id=1, source_target_pairs={{0,16},{1,17},{2,18},{3,19},{4,20},{5,21},{6,22},{7,23},{8,24},{9,... | collective-permute-start | bytes 3145736 | tf_op jit(solution)/shard_map/ppermute | solution.py:26
  6.2 0.9 copy.8
  7.0 4.8 %collective-permute-done.3 = bf16[4,128,256]{2,1,0:T(8,128)(2,1)} collective-permute-done((bf16[4,128,256]{2,1,0:T(8,128)(2,1)}, bf16[4,128,256]{2,1,0:T(8,128)(2,1)}, u32[]{:S(2)}, u32[]{:S(2)}) %collective-permute-start.3) | collective-permute-done | bytes 262176 | tf_op jit(solution)/shard_map/ppermute | solution.py:26
  11.8 1.1 bitcast_select_fusion.2
  12.9 0.7 dynamic-slice_bitcast_fusion.2
  13.6 0.5 collective-permute-start.25
  14.1 1.6 %collective-permute-start.4 = (bf16[2,128,256]{2,1,0:T(8,128)(2,1)S(1)}, bf16[2,128,256]{2,1,0:T(8,128)(2,1)}, u32[]{:S(2)}, u32[]{:S(2)}) collective-permute-start(bf16[2,128,256]{2,1,0:T(8,128)(2,1)S(1)} %dynamic-slice_bitcast_fusion.3), channel_id=1, source_target_pairs={{0,2},{1,3},{2,0},{3,1},{4,6},{5,7},{6,4},{7,5},{8,10},{9,11},{10,... | collective-permute-start | bytes 393224 | tf_op jit(solution)/shard_map/ppermute | solution.py:26
  15.7 1.9 %dynamic-slice_bitcast_fusion.1 = bf16[2048,128]{1,0:T(8,128)(2,1)} fusion(bf16[1,2048,1024]{2,1,0:T(8,128)(2,1)} %param.7, s32[]{:T(128)S(6)} %select_n.115), kind=kLoop, calls=%fused_computation.4 | loop fusion | bytes 1048580 | tf_op jit(solution)/shard_map/dynamic_slice | solution.py:240
  17.6 0.9 dynamic-slice_bitcast_fusion.9
  18.5 2.1 %collective-permute-done.25 = bf16[2,128,256]{2,1,0:T(8,128)(2,1)} collective-permute-done((bf16[2,128,256]{2,1,0:T(8,128)(2,1)}, bf16[2,128,256]{2,1,0:T(8,128)(2,1)}, u32[]{:S(2)}, u32[]{:S(2)}) %collective-permute-start.25) | collective-permute-done | bytes 131104 | tf_op jit(solution)/shard_map/ppermute | solution.py:26
  20.7 1.5 %collective-permute-start.9 = (bf16[2048,128]{1,0:T(8,128)(2,1)}, bf16[2048,128]{1,0:T(8,128)(2,1)S(1)}, u32[]{:S(2)}, u32[]{:S(2)}) collective-permute-start(bf16[2048,128]{1,0:T(8,128)(2,1)} %dynamic-slice_bitcast_fusion.1), channel_id=1, source_target_pairs={{0,16},{1,17},{2,18},{3,19},{4,20},{5,21},{6,22},{7,23},{8,24},{9,... | collective-permute-start | bytes 1572872 | tf_op jit(solution)/shard_map/ppermute | solution.py:26
  22.2 0.9 collective-permute-done.4
  23.1 1.0 dynamic-slice_bitcast_fusion.5
  24.1 10.0 %collective-permute-done.21 = bf16[256,2048]{1,0:T(8,128)(2,1)S(1)} collective-permute-done((bf16[256,2048]{1,0:T(8,128)(2,1)S(1)}, bf16[256,2048]{1,0:T(8,128)(2,1)S(1)}, u32[]{:S(2)}, u32[]{:S(2)}) %collective-permute-start.21) | collective-permute-done | bytes 1048608 | tf_op jit(solution)/shard_map/ppermute | solution.py:26
  34.2 1.6 %broadcast_select_fusion.refs_12_ = bf16[256,2048]{1,0:T(8,128)(2,1)S(1)} fusion(bf16[256,2048]{1,0:T(8,128)(2,1)S(1)} %collective-permute-done.21, pred[]{:T(512)S(6)} %eq.12, bf16[1,1024,2048]{2,1,0:T(8,128)(2,1)} %param.9, s32[]{:T(128)S(6)} %select_n.118), kind=kLoop, calls=%fused_computation.1 | loop fusion | flops 524288 | bytes 3145733 | tf_op jit(solution)/shard_map/jit(_where)/select_n | solution.py:247
  35.8 0.6 collective-permute-start.22
  36.5 7.7 %collective-permute-done.9 = bf16[2048,128]{1,0:T(8,128)(2,1)S(1)} collective-permute-done((bf16[2048,128]{1,0:T(8,128)(2,1)}, bf16[2048,128]{1,0:T(8,128)(2,1)S(1)}, u32[]{:S(2)}, u32[]{:S(2)}) %collective-permute-start.9) | collective-permute-done | bytes 524320 | tf_op jit(solution)/shard_map/ppermute | solution.py:26
  44.2 1.6 %collective-permute-start.8 = (bf16[512,256]{1,0:T(8,128)(2,1)S(1)}, bf16[512,256]{1,0:T(8,128)(2,1)S(1)}, u32[]{:S(2)}, u32[]{:S(2)}) collective-permute-start(bf16[512,256]{1,0:T(8,128)(2,1)S(1)} %pad_maximum_fusion.refs_4_), channel_id=1, source_target_pairs={{0,12},{1,13},{2,14},{3,15},{4,8},{5,9},{6,10},{7,11},{8,4},{9,5},... | collective-permute-start | bytes 786440 | tf_op jit(solution)/shard_map/ppermute | solution.py:26
  45.8 1.2 bitcast_select_fusion
  47.1 1.3 collective-permute-start.7
  48.4 1.3 %collective-permute-start.6 = (bf16[512,256]{1,0:T(8,128)(2,1)S(1)}, bf16[512,256]{1,0:T(8,128)(2,1)S(1)}, u32[]{:S(2)}, u32[]{:S(2)}) collective-permute-start(bf16[512,256]{1,0:T(8,128)(2,1)S(1)} %pad_maximum_fusion.refs_4_), channel_id=1, source_target_pairs={{0,4},{1,5},{2,6},{3,7},{4,0},{5,1},{6,2},{7,3},{8,12},{9,13},{10,... | collective-permute-start | bytes 786440 | tf_op jit(solution)/shard_map/ppermute | solution.py:26
  49.7 14.1 %collective-permute-done.8.refs_7_ = bf16[512,256]{1,0:T(8,128)(2,1)S(1)} collective-permute-done((bf16[512,256]{1,0:T(8,128)(2,1)S(1)}, bf16[512,256]{1,0:T(8,128)(2,1)S(1)}, u32[]{:S(2)}, u32[]{:S(2)}) %collective-permute-start.8) | collective-permute-done | bytes 262176 | tf_op jit(solution)/shard_map/ppermute | solution.py:26
  63.8 0.5 collective-permute-start.24
  64.4 3.0 %collective-permute-done.7.refs_6_ = bf16[512,256]{1,0:T(8,128)(2,1)S(1)} collective-permute-done((bf16[512,256]{1,0:T(8,128)(2,1)S(1)}, bf16[512,256]{1,0:T(8,128)(2,1)S(1)}, u32[]{:S(2)}, u32[]{:S(2)}) %collective-permute-start.7) | collective-permute-done | bytes 262176 | tf_op jit(solution)/shard_map/ppermute | solution.py:26
  67.4 0.5 collective-permute-start.11
  67.9 0.5 collective-permute-start.29
  68.3 2.0 %shard_map.55 = (bf16[512,128]{1,0:T(8,128)(2,1)S(1)}, bf16[512,256]{1,0:T(8,128)(2,1)S(1)}, bf16[384,256]{1,0:T(8,128)(2,1)S(1)}) custom-call(bf16[128,2048]{1,0:T(8,128)(2,1)S(1)} %bitcast.49, bf16[128,2048]{1,0:T(8,128)(2,1)S(1)} %collective-permute-done.refs_1_, bf16[128,2048]{1,0:T(8,128)(2,1)S(1)} %collective-permute-done.1.refs_2_, ...), custom_call_target="tpu_custom_call" | custom-call | flops 805306368 | bytes 3670016 | tf_op jit(solution)/shard_map/pallas_call | solution.py:50
  70.3 3.5 %collective-permute-start.10 = (bf16[384,256]{1,0:T(8,128)(2,1)S(1)}, bf16[384,256]{1,0:T(8,128)(2,1)S(1)}, u32[]{:S(2)}, u32[]{:S(2)}) collective-permute-start(bf16[384,256]{1,0:T(8,128)(2,1)S(1)} %get-tuple-element.16), channel_id=1, source_target_pairs={{0,4},{1,5},{2,6},{3,7},{4,8},{5,9},{6,10},{7,11},{8,12},{9,13},{1... | collective-permute-start | bytes 589832 | tf_op jit(solution)/shard_map/ppermute | solution.py:31
  73.9 1.1 collective-permute-done.12
  75.1 5.2 %collective-permute-start.13 = (s32[4,128]{1,0:T(4,128)S(1)}, s32[4,128]{1,0:T(4,128)S(1)}, u32[]{:S(2)}, u32[]{:S(2)}) collective-permute-start(s32[4,128]{1,0:T(4,128)S(1)} %pad_add_fusion.id_ref), channel_id=1, source_target_pairs={{0,4},{1,5},{2,6},{3,7},{4,8},{5,9},{6,10},{7,11},{8,12},{9,13},{1... | collective-permute-start | bytes 6152 | tf_op jit(solution)/shard_map/ppermute | solution.py:31
  80.3 2.6 %collective-permute-done.13.past_ref = s32[4,128]{1,0:T(4,128)S(1)} collective-permute-done((s32[4,128]{1,0:T(4,128)S(1)}, s32[4,128]{1,0:T(4,128)S(1)}, u32[]{:S(2)}, u32[]{:S(2)}) %collective-permute-start.13) | collective-permute-done | bytes 2080 | tf_op jit(solution)/shard_map/ppermute | solution.py:31
  82.9 1.3 collective-permute-start.28
  84.2 2.6 %collective-permute-start.27 = (bf16[512,256]{1,0:T(8,128)(2,1)S(1)}, bf16[512,256]{1,0:T(8,128)(2,1)S(1)}, u32[]{:S(2)}, u32[]{:S(2)}) collective-permute-start(bf16[512,256]{1,0:T(8,128)(2,1)S(1)} %pad_maximum_fusion.1.refs_16_), channel_id=1, source_target_pairs={{0,4},{1,5},{2,6},{3,7},{4,0},{5,1},{6,2},{7,3},{8,12},{9,13},{10,... | collective-permute-start | bytes 786440 | tf_op jit(solution)/shard_map/ppermute | solution.py:26
  87.0 1.2 shard_map.57.refs_4_
  88.2 1.5 %collective-permute-start.19 = (bf16[512,128]{1,0:T(8,128)(2,1)S(1)}, bf16[512,128]{1,0:T(8,128)(2,1)S(1)}, u32[]{:S(2)}, u32[]{:S(2)}) collective-permute-start(bf16[512,128]{1,0:T(8,128)(2,1)S(1)} %shard_map.57.refs_4_), channel_id=1, source_target_pairs={{0,18},{1,19},{2,16},{3,17},{4,22},{5,23},{6,20},{7,21},{8,26},{9,... | collective-permute-start | bytes 393224 | tf_op jit(solution)/shard_map/ppermute | solution.py:26
  89.7 4.7 %collective-permute-done.28.refs_18_ = bf16[512,256]{1,0:T(8,128)(2,1)S(1)} collective-permute-done((bf16[512,256]{1,0:T(8,128)(2,1)S(1)}, bf16[512,256]{1,0:T(8,128)(2,1)S(1)}, u32[]{:S(2)}, u32[]{:S(2)}) %collective-permute-start.28) | collective-permute-done | bytes 262176 | tf_op jit(solution)/shard_map/ppermute | solution.py:26
  94.4 0.6 collective-permute-start.17
  95.0 1.7 %collective-permute-done.27.refs_17_ = bf16[512,256]{1,0:T(8,128)(2,1)S(1)} collective-permute-done((bf16[512,256]{1,0:T(8,128)(2,1)S(1)}, bf16[512,256]{1,0:T(8,128)(2,1)S(1)}, u32[]{:S(2)}, u32[]{:S(2)}) %collective-permute-start.27) | collective-permute-done | bytes 262176 | tf_op jit(solution)/shard_map/ppermute | solution.py:26
  96.7 1.5 %collective-permute-start.15 = (bf16[512,128]{1,0:T(8,128)(2,1)S(1)}, bf16[512,128]{1,0:T(8,128)(2,1)S(1)}, u32[]{:S(2)}, u32[]{:S(2)}) collective-permute-start(bf16[512,128]{1,0:T(8,128)(2,1)S(1)} %shard_map.57.refs_4_), channel_id=1, source_target_pairs={{0,2},{1,3},{2,0},{3,1},{4,6},{5,7},{6,4},{7,5},{8,10},{9,11},{10,... | collective-permute-start | bytes 393224 | tf_op jit(solution)/shard_map/ppermute | solution.py:26
  98.1 1.2 collective-permute-done.17.refs_8_
  99.4 2.3 %collective-permute-done.15.refs_6_ = bf16[512,128]{1,0:T(8,128)(2,1)S(1)} collective-permute-done((bf16[512,128]{1,0:T(8,128)(2,1)S(1)}, bf16[512,128]{1,0:T(8,128)(2,1)S(1)}, u32[]{:S(2)}, u32[]{:S(2)}) %collective-permute-start.15) | collective-permute-done | bytes 131104 | tf_op jit(solution)/shard_map/ppermute | solution.py:26
  101.6 0.5 collective-permute-start.16
  102.1 0.8 collective-permute-done.18.refs_9_
  103.2 1.0 copy-done.6
  104.2 0.4 copy-done.7
  104.5 6.4 %shard_map.58 = (bf16[128,2048]{1,0:T(8,128)(2,1)S(1)}, bf16[512,128]{1,0:T(8,128)(2,1)S(1)}, bf16[512,256]{1,0:T(8,128)(2,1)S(1)}, bf16[384,256]{1,0:T(8,128)(2,1)S(1)}) custom-call(bf16[128,2048]{1,0:T(8,128)(2,1)S(1)} %bitcast.50, bf16[128,2048]{1,0:T(8,128)(2,1)S(1)} %collective-permute-done.refs_1_, ...), custom_call_target="tpu_custom_call" | custom-call | flops 2952790016 | bytes 8912896 | tf_op jit(solution)/shard_map/pallas_call | solution.py:50
  111.0 1.9 %collective-permute-start.30 = (bf16[384,256]{1,0:T(8,128)(2,1)S(1)}, bf16[384,256]{1,0:T(8,128)(2,1)S(1)}, u32[]{:S(2)}, u32[]{:S(2)}) collective-permute-start(bf16[384,256]{1,0:T(8,128)(2,1)S(1)} %get-tuple-element.19), channel_id=1, source_target_pairs={{0,4},{1,5},{2,6},{3,7},{4,8},{5,9},{6,10},{7,11},{8,12},{9,13},{1... | collective-permute-start | bytes 589832 | tf_op jit(solution)/shard_map/ppermute | solution.py:31
  112.9 7.1 %collective-permute-done.30.past_ref = bf16[384,256]{1,0:T(8,128)(2,1)S(1)} collective-permute-done((bf16[384,256]{1,0:T(8,128)(2,1)S(1)}, bf16[384,256]{1,0:T(8,128)(2,1)S(1)}, u32[]{:S(2)}, u32[]{:S(2)}) %collective-permute-start.30) | collective-permute-done | bytes 196640 | tf_op jit(solution)/shard_map/ppermute | solution.py:31
  120.0 1.7 %shard_map.59 = (bf16[256,128]{1,0:T(8,128)(2,1)S(1)}, bf16[256,128]{1,0:T(8,128)(2,1)S(1)}) custom-call(bf16[512,128]{1,0:T(8,128)(2,1)S(1)} %get-tuple-element.17.q_ref, bf16[512,256]{1,0:T(8,128)(2,1)S(1)} %get-tuple-element.18.kv_ref, bf16[384,256]{1,0:T(8,128)(2,1)S(1)} %collective-permute-done.30.past_ref, f32[4,128,512]{2,1,0:T(8,128)S(1)} %shard_map.56.bias_ref), custom_call_target="tpu_custom_call" | custom-call | flops 134217728 | bytes 1638400 | tf_op jit(solution)/shard_map/pallas_call | solution.py:50
  121.7 1.5 %collective-permute-start.36 = (bf16[256,128]{1,0:T(8,128)(2,1)S(1)}, bf16[256,128]{1,0:T(8,128)(2,1)S(1)}, u32[]{:S(2)}, u32[]{:S(2)}) collective-permute-start(bf16[256,128]{1,0:T(8,128)(2,1)S(1)} %get-tuple-element.21), channel_id=1, source_target_pairs={{0,18},{1,19},{2,16},{3,17},{4,22},{5,23},{6,20},{7,21},{8,26},{9,... | collective-permute-start | bytes 196616 | tf_op jit(solution)/shard_map/ppermute | solution.py:26
  123.2 0.6 collective-permute-start.32
  123.8 1.4 %collective-permute-start.34 = (bf16[256,128]{1,0:T(8,128)(2,1)S(1)}, bf16[256,128]{1,0:T(8,128)(2,1)S(1)}, u32[]{:S(2)}, u32[]{:S(2)}) collective-permute-start(bf16[256,128]{1,0:T(8,128)(2,1)S(1)} %get-tuple-element.20.refs_0_), channel_id=1, source_target_pairs={{0,16},{1,17},{2,18},{3,19},{4,20},{5,21},{6,22},{7,23},{8,24},{9,... | collective-permute-start | bytes 196616 | tf_op jit(solution)/shard_map/ppermute | solution.py:26
  125.2 2.3 %collective-permute-done.36.refs_6_ = bf16[256,128]{1,0:T(8,128)(2,1)S(1)} collective-permute-done((bf16[256,128]{1,0:T(8,128)(2,1)S(1)}, bf16[256,128]{1,0:T(8,128)(2,1)S(1)}, u32[]{:S(2)}, u32[]{:S(2)}) %collective-permute-start.36) | collective-permute-done | bytes 65568 | tf_op jit(solution)/shard_map/ppermute | solution.py:26
  127.6 0.3 collective-permute-done.32.refs_2_
  128.1 0.3 collective-permute-start.35
  128.4 0.5 collective-permute-done.37.refs_7_
  128.8 0.3 collective-permute-done.33.refs_3_
  129.1 0.2 collective-permute-done.35.refs_5_
  129.3 1.6 %shard_map.60 = bf16[128,2048]{1,0:T(8,128)(2,1)} custom-call(bf16[256,128]{1,0:T(8,128)(2,1)S(1)} %get-tuple-element.20.refs_0_, bf16[256,128]{1,0:T(8,128)(2,1)S(1)} %collective-permute-done.31.refs_1_, bf16[256,128]{1,0:T(8,128)(2,1)S(1)} %collective-permute-done.32.refs_2_, bf16[256,128]{1,0:T(8,128)(2,1)S(1)} %collective-permute-done.33.refs_3_, ...), custom_call_target="tpu_custom_call" | custom-call | flops 536870912 | bytes 5242880 | tf_op jit(solution)/shard_map/pallas_call | solution.py:50
  (57 shorter events, 1.1 us)
Async XLA Ops:
  2.3 9.5 %collective-permute-start.3 = (bf16[4,128,256]{2,1,0:T(8,128)(2,1)}, bf16[4,128,256]{2,1,0:T(8,128)(2,1)}, u32[]{:S(2)}, u32[]{:S(2)}) collective-permute-start(bf16[4,128,256]{2,1,0:T(8,128)(2,1)} %bitcast.5), channel_id=1, source_target_pairs={{0,16},{1,17},{2,18},{3,19},{4,20},{5,21},{6,22},{7,23},{8,24},{9,... | collective-permute-start | bytes 786440 | tf_op jit(solution)/shard_map/ppermute | solution.py:26
  2.8 45.6 %collective-permute-start.1 = (bf16[128,2048]{1,0:T(8,128)(2,1)}, bf16[128,2048]{1,0:T(8,128)(2,1)S(1)}, u32[]{:S(2)}, u32[]{:S(2)}) collective-permute-start(bf16[128,2048]{1,0:T(8,128)(2,1)} %bitcast.47), channel_id=1, source_target_pairs={{0,1},{1,0},{2,3},{3,2},{4,5},{5,4},{6,7},{7,6},{8,9},{9,8},{10,11... | collective-permute-start | bytes 1572872 | tf_op jit(solution)/shard_map/ppermute | solution.py:26
  2.8 43.0 %collective-permute-start = (bf16[128,2048]{1,0:T(8,128)(2,1)}, bf16[128,2048]{1,0:T(8,128)(2,1)S(1)}, u32[]{:S(2)}, u32[]{:S(2)}) collective-permute-start(bf16[128,2048]{1,0:T(8,128)(2,1)} %bitcast.48), channel_id=1, source_target_pairs={{0,2},{1,3},{2,0},{3,1},{4,6},{5,7},{6,4},{7,5},{8,10},{9,11},{10,... | collective-permute-start | bytes 1572872 | tf_op jit(solution)/shard_map/ppermute | solution.py:26
  4.6 29.5 %collective-permute-start.21 = (bf16[256,2048]{1,0:T(8,128)(2,1)S(1)}, bf16[256,2048]{1,0:T(8,128)(2,1)S(1)}, u32[]{:S(2)}, u32[]{:S(2)}) collective-permute-start(bf16[256,2048]{1,0:T(8,128)(2,1)S(1)} %dynamic-slice_bitcast_fusion), channel_id=1, source_target_pairs={{0,16},{1,17},{2,18},{3,19},{4,20},{5,21},{6,22},{7,23},{8,24},{9,... | collective-permute-start | bytes 3145736 | tf_op jit(solution)/shard_map/ppermute | solution.py:26
  12.9 1.3 copy-start.3
  13.6 7.1 %collective-permute-start.25 = (bf16[2,128,256]{2,1,0:T(8,128)(2,1)}, bf16[2,128,256]{2,1,0:T(8,128)(2,1)}, u32[]{:S(2)}, u32[]{:S(2)}) collective-permute-start(bf16[2,128,256]{2,1,0:T(8,128)(2,1)} %dynamic-slice_bitcast_fusion.2), channel_id=1, source_target_pairs={{0,2},{1,3},{2,0},{3,1},{4,6},{5,7},{6,4},{7,5},{8,10},{9,11},{10,... | collective-permute-start | bytes 393224 | tf_op jit(solution)/shard_map/ppermute | solution.py:26
  14.1 9.0 %collective-permute-start.4 = (bf16[2,128,256]{2,1,0:T(8,128)(2,1)S(1)}, bf16[2,128,256]{2,1,0:T(8,128)(2,1)}, u32[]{:S(2)}, u32[]{:S(2)}) collective-permute-start(bf16[2,128,256]{2,1,0:T(8,128)(2,1)S(1)} %dynamic-slice_bitcast_fusion.3), channel_id=1, source_target_pairs={{0,2},{1,3},{2,0},{3,1},{4,6},{5,7},{6,4},{7,5},{8,10},{9,11},{10,... | collective-permute-start | bytes 393224 | tf_op jit(solution)/shard_map/ppermute | solution.py:26
  17.6 49.8 %copy-start.4 = (s32[1,128]{1,0:T(1,128)S(1)}, s32[1,128]{1,0:T(1,128)}, u32[]{:S(2)}) copy-start(s32[1,128]{1,0:T(1,128)} %param.6) | copy-start | bytes 1540
  17.6 50.7 %copy-start.1 = (bf16[1,128,2048]{2,1,0:T(8,128)(2,1)S(1)}, bf16[1,128,2048]{2,1,0:T(8,128)(2,1)}, u32[]{:S(2)}) copy-start(bf16[1,128,2048]{2,1,0:T(8,128)(2,1)} %param.5) | copy-start | bytes 1572868
  20.7 23.6 %collective-permute-start.9 = (bf16[2048,128]{1,0:T(8,128)(2,1)}, bf16[2048,128]{1,0:T(8,128)(2,1)S(1)}, u32[]{:S(2)}, u32[]{:S(2)}) collective-permute-start(bf16[2048,128]{1,0:T(8,128)(2,1)} %dynamic-slice_bitcast_fusion.1), channel_id=1, source_target_pairs={{0,16},{1,17},{2,18},{3,19},{4,20},{5,21},{6,22},{7,23},{8,24},{9,... | collective-permute-start | bytes 1572872 | tf_op jit(solution)/shard_map/ppermute | solution.py:26
  24.1 12.3 %collective-permute-start.5 = (bf16[2,128,256]{2,1,0:T(8,128)(2,1)S(1)}, bf16[2,128,256]{2,1,0:T(8,128)(2,1)S(1)}, u32[]{:S(2)}, u32[]{:S(2)}) collective-permute-start(bf16[2,128,256]{2,1,0:T(8,128)(2,1)S(1)} %pad_maximum_fusion.2), channel_id=1, source_target_pairs={{0,1},{1,0},{2,3},{3,2},{4,5},{5,4},{6,7},{7,6},{8,9},{9,8},{10,11... | collective-permute-start | bytes 393224 | tf_op jit(solution)/shard_map/ppermute | solution.py:26
  35.8 51.2 %copy-start.2 = (bf16[256,2048]{1,0:T(8,128)(2,1)}, bf16[256,2048]{1,0:T(8,128)(2,1)S(1)}, u32[]{:S(2)}) copy-start(bf16[256,2048]{1,0:T(8,128)(2,1)S(1)} %broadcast_select_fusion.refs_12_) | copy-start | bytes 3145732
  35.8 28.0 %collective-permute-start.22 = (bf16[256,2048]{1,0:T(8,128)(2,1)S(1)}, bf16[256,2048]{1,0:T(8,128)(2,1)S(1)}, u32[]{:S(2)}, u32[]{:S(2)}) collective-permute-start(bf16[256,2048]{1,0:T(8,128)(2,1)S(1)} %broadcast_select_fusion.refs_12_), channel_id=1, source_target_pairs={{0,2},{1,3},{2,0},{3,1},{4,6},{5,7},{6,4},{7,5},{8,10},{9,11},{10,... | collective-permute-start | bytes 3145736 | tf_op jit(solution)/shard_map/ppermute | solution.py:26
  36.4 10.7 %collective-permute-start.26 = (bf16[2,128,256]{2,1,0:T(8,128)(2,1)S(1)}, bf16[2,128,256]{2,1,0:T(8,128)(2,1)S(1)}, u32[]{:S(2)}, u32[]{:S(2)}) collective-permute-start(bf16[2,128,256]{2,1,0:T(8,128)(2,1)S(1)} %pad_maximum_fusion.3), channel_id=1, source_target_pairs={{0,1},{1,0},{2,3},{3,2},{4,5},{5,4},{6,7},{7,6},{8,9},{9,8},{10,11... | collective-permute-start | bytes 393224 | tf_op jit(solution)/shard_map/ppermute | solution.py:26
  44.2 19.6 %collective-permute-start.8 = (bf16[512,256]{1,0:T(8,128)(2,1)S(1)}, bf16[512,256]{1,0:T(8,128)(2,1)S(1)}, u32[]{:S(2)}, u32[]{:S(2)}) collective-permute-start(bf16[512,256]{1,0:T(8,128)(2,1)S(1)} %pad_maximum_fusion.refs_4_), channel_id=1, source_target_pairs={{0,12},{1,13},{2,14},{3,15},{4,8},{5,9},{6,10},{7,11},{8,4},{9,5},... | collective-permute-start | bytes 786440 | tf_op jit(solution)/shard_map/ppermute | solution.py:26
  45.8 22.5 %collective-permute-start.2 = (bf16[128,2048]{1,0:T(8,128)(2,1)S(1)}, bf16[128,2048]{1,0:T(8,128)(2,1)S(1)}, u32[]{:S(2)}, u32[]{:S(2)}) collective-permute-start(bf16[128,2048]{1,0:T(8,128)(2,1)S(1)} %collective-permute-done.refs_1_), channel_id=1, source_target_pairs={{0,1},{1,0},{2,3},{3,2},{4,5},{5,4},{6,7},{7,6},{8,9},{9,8},{10,11... | collective-permute-start | bytes 1572872 | tf_op jit(solution)/shard_map/ppermute | solution.py:26
  47.1 20.3 %collective-permute-start.7 = (bf16[512,256]{1,0:T(8,128)(2,1)S(1)}, bf16[512,256]{1,0:T(8,128)(2,1)S(1)}, u32[]{:S(2)}, u32[]{:S(2)}) collective-permute-start(bf16[512,256]{1,0:T(8,128)(2,1)S(1)} %pad_maximum_fusion.refs_4_), channel_id=1, source_target_pairs={{0,8},{1,9},{2,10},{3,11},{4,12},{5,13},{6,14},{7,15},{8,0},{9,1},... | collective-permute-start | bytes 786440 | tf_op jit(solution)/shard_map/ppermute | solution.py:26
  48.4 19.5 %collective-permute-start.6 = (bf16[512,256]{1,0:T(8,128)(2,1)S(1)}, bf16[512,256]{1,0:T(8,128)(2,1)S(1)}, u32[]{:S(2)}, u32[]{:S(2)}) collective-permute-start(bf16[512,256]{1,0:T(8,128)(2,1)S(1)} %pad_maximum_fusion.refs_4_), channel_id=1, source_target_pairs={{0,4},{1,5},{2,6},{3,7},{4,0},{5,1},{6,2},{7,3},{8,12},{9,13},{10,... | collective-permute-start | bytes 786440 | tf_op jit(solution)/shard_map/ppermute | solution.py:26
  63.8 39.4 %collective-permute-start.23 = (bf16[256,2048]{1,0:T(8,128)(2,1)S(1)}, bf16[256,2048]{1,0:T(8,128)(2,1)S(1)}, u32[]{:S(2)}, u32[]{:S(2)}) collective-permute-start(bf16[256,2048]{1,0:T(8,128)(2,1)S(1)} %broadcast_select_fusion.refs_12_), channel_id=1, source_target_pairs={{0,1},{1,0},{2,3},{3,2},{4,5},{5,4},{6,7},{7,6},{8,9},{9,8},{10,11... | collective-permute-start | bytes 3145736 | tf_op jit(solution)/shard_map/ppermute | solution.py:26
  63.8 39.4 %copy-start.5 = (bf16[256,2048]{1,0:T(8,128)(2,1)}, bf16[256,2048]{1,0:T(8,128)(2,1)S(1)}, u32[]{:S(2)}) copy-start(bf16[256,2048]{1,0:T(8,128)(2,1)S(1)} %collective-permute-done.22.refs_13_) | copy-start | bytes 3145732
  63.8 39.4 %collective-permute-start.24 = (bf16[256,2048]{1,0:T(8,128)(2,1)S(1)}, bf16[256,2048]{1,0:T(8,128)(2,1)S(1)}, u32[]{:S(2)}, u32[]{:S(2)}) collective-permute-start(bf16[256,2048]{1,0:T(8,128)(2,1)S(1)} %collective-permute-done.22.refs_13_), channel_id=1, source_target_pairs={{0,1},{1,0},{2,3},{3,2},{4,5},{5,4},{6,7},{7,6},{8,9},{9,8},{10,11... | collective-permute-start | bytes 3145736 | tf_op jit(solution)/shard_map/ppermute | solution.py:26
  67.4 6.5 %collective-permute-start.11 = (s32[1,128]{1,0:T(1,128)S(1)}, s32[1,128]{1,0:T(1,128)S(1)}, u32[]{:S(2)}, u32[]{:S(2)}) collective-permute-start(s32[1,128]{1,0:T(1,128)S(1)} %copy-done.4), channel_id=1, source_target_pairs={{0,2},{1,3},{2,0},{3,1},{4,6},{5,7},{6,4},{7,5},{8,10},{9,11},{10,... | collective-permute-start | bytes 1544 | tf_op jit(solution)/shard_map/ppermute | solution.py:26
  67.9 20.3 %collective-permute-start.29 = (bf16[512,256]{1,0:T(8,128)(2,1)S(1)}, bf16[512,256]{1,0:T(8,128)(2,1)S(1)}, u32[]{:S(2)}, u32[]{:S(2)}) collective-permute-start(bf16[512,256]{1,0:T(8,128)(2,1)S(1)} %pad_maximum_fusion.1.refs_16_), channel_id=1, source_target_pairs={{0,12},{1,13},{2,14},{3,15},{4,8},{5,9},{6,10},{7,11},{8,4},{9,5},... | collective-permute-start | bytes 786440 | tf_op jit(solution)/shard_map/ppermute | solution.py:26
  70.3 13.8 %collective-permute-start.10 = (bf16[384,256]{1,0:T(8,128)(2,1)S(1)}, bf16[384,256]{1,0:T(8,128)(2,1)S(1)}, u32[]{:S(2)}, u32[]{:S(2)}) collective-permute-start(bf16[384,256]{1,0:T(8,128)(2,1)S(1)} %get-tuple-element.16), channel_id=1, source_target_pairs={{0,4},{1,5},{2,6},{3,7},{4,8},{5,9},{6,10},{7,11},{8,12},{9,13},{1... | collective-permute-start | bytes 589832 | tf_op jit(solution)/shard_map/ppermute | solution.py:31
  73.9 1.2 collective-permute-start.12
  75.1 7.8 %collective-permute-start.13 = (s32[4,128]{1,0:T(4,128)S(1)}, s32[4,128]{1,0:T(4,128)S(1)}, u32[]{:S(2)}, u32[]{:S(2)}) collective-permute-start(s32[4,128]{1,0:T(4,128)S(1)} %pad_add_fusion.id_ref), channel_id=1, source_target_pairs={{0,4},{1,5},{2,6},{3,7},{4,8},{5,9},{6,10},{7,11},{8,12},{9,13},{1... | collective-permute-start | bytes 6152 | tf_op jit(solution)/shard_map/ppermute | solution.py:31
  82.9 11.5 %collective-permute-start.28 = (bf16[512,256]{1,0:T(8,128)(2,1)S(1)}, bf16[512,256]{1,0:T(8,128)(2,1)S(1)}, u32[]{:S(2)}, u32[]{:S(2)}) collective-permute-start(bf16[512,256]{1,0:T(8,128)(2,1)S(1)} %pad_maximum_fusion.1.refs_16_), channel_id=1, source_target_pairs={{0,8},{1,9},{2,10},{3,11},{4,12},{5,13},{6,14},{7,15},{8,0},{9,1},... | collective-permute-start | bytes 786440 | tf_op jit(solution)/shard_map/ppermute | solution.py:26
  84.2 12.5 %collective-permute-start.27 = (bf16[512,256]{1,0:T(8,128)(2,1)S(1)}, bf16[512,256]{1,0:T(8,128)(2,1)S(1)}, u32[]{:S(2)}, u32[]{:S(2)}) collective-permute-start(bf16[512,256]{1,0:T(8,128)(2,1)S(1)} %pad_maximum_fusion.1.refs_16_), channel_id=1, source_target_pairs={{0,4},{1,5},{2,6},{3,7},{4,0},{5,1},{6,2},{7,3},{8,12},{9,13},{10,... | collective-permute-start | bytes 786440 | tf_op jit(solution)/shard_map/ppermute | solution.py:26
  88.2 9.9 %collective-permute-start.19 = (bf16[512,128]{1,0:T(8,128)(2,1)S(1)}, bf16[512,128]{1,0:T(8,128)(2,1)S(1)}, u32[]{:S(2)}, u32[]{:S(2)}) collective-permute-start(bf16[512,128]{1,0:T(8,128)(2,1)S(1)} %shard_map.57.refs_4_), channel_id=1, source_target_pairs={{0,18},{1,19},{2,16},{3,17},{4,22},{5,23},{6,20},{7,21},{8,26},{9,... | collective-permute-start | bytes 393224 | tf_op jit(solution)/shard_map/ppermute | solution.py:26
  94.4 5.0 %collective-permute-start.17 = (bf16[512,128]{1,0:T(8,128)(2,1)S(1)}, bf16[512,128]{1,0:T(8,128)(2,1)S(1)}, u32[]{:S(2)}, u32[]{:S(2)}) collective-permute-start(bf16[512,128]{1,0:T(8,128)(2,1)S(1)} %shard_map.57.refs_4_), channel_id=1, source_target_pairs={{0,16},{1,17},{2,18},{3,19},{4,20},{5,21},{6,22},{7,23},{8,24},{9,... | collective-permute-start | bytes 393224 | tf_op jit(solution)/shard_map/ppermute | solution.py:26
  96.7 5.0 %collective-permute-start.15 = (bf16[512,128]{1,0:T(8,128)(2,1)S(1)}, bf16[512,128]{1,0:T(8,128)(2,1)S(1)}, u32[]{:S(2)}, u32[]{:S(2)}) collective-permute-start(bf16[512,128]{1,0:T(8,128)(2,1)S(1)} %shard_map.57.refs_4_), channel_id=1, source_target_pairs={{0,2},{1,3},{2,0},{3,1},{4,6},{5,7},{6,4},{7,5},{8,10},{9,11},{10,... | collective-permute-start | bytes 393224 | tf_op jit(solution)/shard_map/ppermute | solution.py:26
  98.1 3.5 %collective-permute-start.14 = (bf16[512,128]{1,0:T(8,128)(2,1)S(1)}, bf16[512,128]{1,0:T(8,128)(2,1)S(1)}, u32[]{:S(2)}, u32[]{:S(2)}) collective-permute-start(bf16[512,128]{1,0:T(8,128)(2,1)S(1)} %shard_map.57.refs_4_), channel_id=1, source_target_pairs={{0,1},{1,0},{2,3},{3,2},{4,5},{5,4},{6,7},{7,6},{8,9},{9,8},{10,11... | collective-permute-start | bytes 393224 | tf_op jit(solution)/shard_map/ppermute | solution.py:26
  99.4 2.8 %collective-permute-start.20 = (bf16[512,128]{1,0:T(8,128)(2,1)S(1)}, bf16[512,128]{1,0:T(8,128)(2,1)S(1)}, u32[]{:S(2)}, u32[]{:S(2)}) collective-permute-start(bf16[512,128]{1,0:T(8,128)(2,1)S(1)} %collective-permute-done.19.refs_10_), channel_id=1, source_target_pairs={{0,1},{1,0},{2,3},{3,2},{4,5},{5,4},{6,7},{7,6},{8,9},{9,8},{10,11... | collective-permute-start | bytes 393224 | tf_op jit(solution)/shard_map/ppermute | solution.py:26
  101.6 1.3 %collective-permute-start.18 = (bf16[512,128]{1,0:T(8,128)(2,1)S(1)}, bf16[512,128]{1,0:T(8,128)(2,1)S(1)}, u32[]{:S(2)}, u32[]{:S(2)}) collective-permute-start(bf16[512,128]{1,0:T(8,128)(2,1)S(1)} %collective-permute-done.17.refs_8_), channel_id=1, source_target_pairs={{0,1},{1,0},{2,3},{3,2},{4,5},{5,4},{6,7},{7,6},{8,9},{9,8},{10,11... | collective-permute-start | bytes 393224 | tf_op jit(solution)/shard_map/ppermute | solution.py:26
  101.6 1.5 %collective-permute-start.16 = (bf16[512,128]{1,0:T(8,128)(2,1)S(1)}, bf16[512,128]{1,0:T(8,128)(2,1)S(1)}, u32[]{:S(2)}, u32[]{:S(2)}) collective-permute-start(bf16[512,128]{1,0:T(8,128)(2,1)S(1)} %collective-permute-done.15.refs_6_), channel_id=1, source_target_pairs={{0,1},{1,0},{2,3},{3,2},{4,5},{5,4},{6,7},{7,6},{8,9},{9,8},{10,11... | collective-permute-start | bytes 393224 | tf_op jit(solution)/shard_map/ppermute | solution.py:26
  103.2 1.0 copy-start.6
  103.2 1.3 %copy-start.7 = (bf16[256,2048]{1,0:T(8,128)(2,1)}, bf16[256,2048]{1,0:T(8,128)(2,1)S(1)}, u32[]{:S(2)}) copy-start(bf16[256,2048]{1,0:T(8,128)(2,1)S(1)} %collective-permute-done.24.refs_15_) | copy-start | bytes 3145732
  104.5 24.8 %copy-start = (bf16[1,1024,2048]{2,1,0:T(8,128)(2,1)S(1)}, bf16[1,1024,2048]{2,1,0:T(8,128)(2,1)}, u32[]{:S(2)}) copy-start(bf16[1,1024,2048]{2,1,0:T(8,128)(2,1)} %param.9) | copy-start | bytes 12582916
  111.0 9.0 %collective-permute-start.30 = (bf16[384,256]{1,0:T(8,128)(2,1)S(1)}, bf16[384,256]{1,0:T(8,128)(2,1)S(1)}, u32[]{:S(2)}, u32[]{:S(2)}) collective-permute-start(bf16[384,256]{1,0:T(8,128)(2,1)S(1)} %get-tuple-element.19), channel_id=1, source_target_pairs={{0,4},{1,5},{2,6},{3,7},{4,8},{5,9},{6,10},{7,11},{8,12},{9,13},{1... | collective-permute-start | bytes 589832 | tf_op jit(solution)/shard_map/ppermute | solution.py:31
  121.7 5.9 %collective-permute-start.36 = (bf16[256,128]{1,0:T(8,128)(2,1)S(1)}, bf16[256,128]{1,0:T(8,128)(2,1)S(1)}, u32[]{:S(2)}, u32[]{:S(2)}) collective-permute-start(bf16[256,128]{1,0:T(8,128)(2,1)S(1)} %get-tuple-element.21), channel_id=1, source_target_pairs={{0,18},{1,19},{2,16},{3,17},{4,22},{5,23},{6,20},{7,21},{8,26},{9,... | collective-permute-start | bytes 196616 | tf_op jit(solution)/shard_map/ppermute | solution.py:26
  123.2 4.7 %collective-permute-start.32 = (bf16[256,128]{1,0:T(8,128)(2,1)S(1)}, bf16[256,128]{1,0:T(8,128)(2,1)S(1)}, u32[]{:S(2)}, u32[]{:S(2)}) collective-permute-start(bf16[256,128]{1,0:T(8,128)(2,1)S(1)} %get-tuple-element.21), channel_id=1, source_target_pairs={{0,2},{1,3},{2,0},{3,1},{4,6},{5,7},{6,4},{7,5},{8,10},{9,11},{10,... | collective-permute-start | bytes 196616 | tf_op jit(solution)/shard_map/ppermute | solution.py:26
  123.8 4.3 %collective-permute-start.34 = (bf16[256,128]{1,0:T(8,128)(2,1)S(1)}, bf16[256,128]{1,0:T(8,128)(2,1)S(1)}, u32[]{:S(2)}, u32[]{:S(2)}) collective-permute-start(bf16[256,128]{1,0:T(8,128)(2,1)S(1)} %get-tuple-element.20.refs_0_), channel_id=1, source_target_pairs={{0,16},{1,17},{2,18},{3,19},{4,20},{5,21},{6,22},{7,23},{8,24},{9,... | collective-permute-start | bytes 196616 | tf_op jit(solution)/shard_map/ppermute | solution.py:26
  125.2 3.2 %collective-permute-start.31 = (bf16[256,128]{1,0:T(8,128)(2,1)S(1)}, bf16[256,128]{1,0:T(8,128)(2,1)S(1)}, u32[]{:S(2)}, u32[]{:S(2)}) collective-permute-start(bf16[256,128]{1,0:T(8,128)(2,1)S(1)} %get-tuple-element.20.refs_0_), channel_id=1, source_target_pairs={{0,1},{1,0},{2,3},{3,2},{4,5},{5,4},{6,7},{7,6},{8,9},{9,8},{10,11... | collective-permute-start | bytes 196616 | tf_op jit(solution)/shard_map/ppermute | solution.py:26
  127.6 1.3 collective-permute-start.37
  127.9 1.3 collective-permute-start.33
  128.1 1.3 collective-permute-start.35

commit v2 on v1

v2 whole, which is shorter than its diff:
```python
import functools
import math

import jax
import jax.numpy as jnp
from jax import lax
from jax.experimental import pallas as pl
from jax.experimental.pallas import tpu as pltpu
from jax.sharding import PartitionSpec as P

HEAD = 128
WINDOW = 4
PLANE = 4
ORDER = (0, 2, 1, 3)
BOTH = ("phase", "ctx")
VMEM_BYTES = 24 * 1024 * 1024
LONG = 10**11


def swap(block, phase_bit, ctx_bits):
    wide = lax.axis_size("ctx")
    route = [
        (f * wide + d, (f ^ phase_bit) * wide + (d ^ ctx_bits))
        for f in range(lax.axis_size("phase"))
        for d in range(wide)
    ]
    return lax.ppermute(block, BOTH, route)


def from_plane_behind(block):
    wide = lax.axis_size("ctx")
    return lax.ppermute(block, "ctx", [(i, i + PLANE) for i in range(wide - PLANE)])


def rms_rows(values):
    widened = values.astype(jnp.float32)
    scale = lax.rsqrt(jnp.mean(widened * widened, axis=-1, keepdims=True) + 1e-05)
    return (widened * scale).astype(jnp.bfloat16)


def dot(a, b):
    return jnp.dot(a, b, preferred_element_type=jnp.float32)


def call(kernel, outs, scratch, flops, *operands, far=()):
    moved = sum(o.size * o.dtype.itemsize for o in operands)
    place = lambda i: pltpu.HBM if i in far else pltpu.VMEM
    return pl.pallas_call(
        kernel,
        out_shape=[jax.ShapeDtypeStruct(s, d) for s, d in outs],
        in_specs=[pl.BlockSpec(memory_space=place(i)) for i in range(len(operands))],
        out_specs=[pl.BlockSpec(memory_space=pltpu.VMEM)] * len(outs),
        scratch_shapes=[pltpu.VMEM(*s) if isinstance(s, tuple) else s for s in scratch],
        cost_estimate=pl.CostEstimate(flops=flops, bytes_accessed=moved, transcendentals=0),
        compiler_params=pltpu.CompilerParams(vmem_limit_bytes=VMEM_BYTES),
    )(*operands)


def extend_kernel(x_ref, id_ref, out_ref):
    rows, width = x_ref.shape
    lanes = out_ref.shape[1] - width
    out_ref[:, :width] = x_ref[...]
    ids = jnp.broadcast_to(id_ref[...].astype(jnp.float32), (rows, rows))
    out_ref[:, width:] = jnp.broadcast_to(
        jnp.transpose(ids)[:, :1], (rows, lanes)
    ).astype(jnp.bfloat16)


def slice_kernel(out_ref, query_ref, sent_out, query_mat, sems):
    side = lax.rem(lax.axis_index("phase"), 2)
    own = lax.rem(lax.axis_index("ctx"), PLANE)
    half, part = sent_out.shape[0] // 3, query_mat.shape[1] // 2
    copies = []
    for i, (first, count, place) in enumerate(((0, 2, 2 * own), (2, 1, 2 * (own ^ 2)))):
        at = pl.ds(pl.multiple_of(place * half, half), count * half)
        to = sent_out.at[pl.ds(first * half, count * half)]
        copies.append(pltpu.make_async_copy(out_ref.at[at], to, sems.at[i]))
    for flip in (0, 1):
        at = pl.ds(pl.multiple_of(((side ^ flip) * PLANE + own) * part, part), part)
        to = query_mat.at[:, pl.ds(flip * part, part)]
        copies.append(pltpu.make_async_copy(query_ref.at[:, at], to, sems.at[2 + flip]))
    for copy in copies:
        copy.start()
    for copy in copies:
        copy.wait()


def cut_kernel(w_ref, *out_refs):
    side = lax.rem(lax.axis_index("phase"), 2)
    upper = lax.rem(lax.axis_index("ctx"), PLANE) // 2
    half = w_ref.shape[1] // 2
    pair = out_refs[0].shape[1] // 2
    for ref, (flip_side, flip_upper) in zip(out_refs, ((0, 0), (0, 1), (1, 0), (1, 1))):
        place = ((side ^ flip_side) * 2 + (upper ^ flip_upper)) * pair
        ref[:, :pair] = w_ref[:, pl.ds(pl.multiple_of(place, pair), pair)]
        ref[:, pair:] = w_ref[:, pl.ds(pl.multiple_of(place + half, pair), pair)]


def sort_kernel(kept, across_y, across_x, across_both, near_ref, far_ref):
    side = lax.rem(lax.axis_index("phase"), 2)
    core = lax.rem(lax.axis_index("ctx"), 2)
    rows, part = kept.shape[0], kept.shape[1] // 4
    for layer in range(2):
        for flip, out_ref in enumerate((near_ref, far_ref)):
            head = pl.multiple_of((core ^ flip) * part, part)

            def put(sources):
                for r, ref in enumerate(sources):
                    at = slice(r * rows, (r + 1) * rows)
                    out_ref[layer, at, :part] = ref[:, pl.ds(head, part)]
                    out_ref[layer, at, part:] = ref[:, pl.ds(head + 2 * part, part)]

            pl.when(side == layer)(functools.partial(put, (kept, across_y)))
            pl.when(side != layer)(functools.partial(put, (across_x, across_both)))


def merge_kernel(near_ref, far_ref, early_ref, late_ref):
    rows = near_ref.shape[1]
    for layer, ref in enumerate((early_ref, late_ref)):
        ref[:rows] = near_ref[layer]
        ref[rows:] = far_ref[layer]


def fill_weights(ctx, weight_refs, weights):
    rows = weight_refs[0].shape[0] // PLANE
    for m, ref in enumerate(weight_refs):
        for r, o in enumerate(ORDER):
            source = ctx ^ (PLANE * m + o)
            at = pl.ds(pl.multiple_of(source * rows, rows), rows)
            weights[at, :] = ref[r * rows : (r + 1) * rows, :]


def project_query(normed, wq_ref, mine_ref, other_ref):
    queries = dot(normed, wq_ref[...]).astype(jnp.bfloat16)
    part = mine_ref.shape[1]
    mine_ref[...] = queries[:, :part]
    other_ref[...] = queries[:, part:]


def norm_kernel(*refs):
    x_refs, (normed_ref,) = refs[:PLANE], refs[PLANE:]
    rows = x_refs[0].shape[0]
    own = lax.rem(lax.axis_index("ctx"), PLANE)
    for r, o in enumerate(ORDER):
        at = pl.ds(pl.multiple_of((own ^ o) * rows, rows), rows)
        normed_ref[at, :] = rms_rows(x_refs[r][:, : normed_ref.shape[1]])


def group_ids(x_refs, own, group):
    rows, width = x_refs[0].shape[0], x_refs[0].shape[1] - HEAD
    column = jnp.zeros((rows, 1), jnp.float32)
    for r, o in enumerate(ORDER):
        chosen = jnp.where((own ^ o) == group, 1.0, 0.0)
        column = column + chosen * x_refs[r][:, width : width + 1].astype(jnp.float32)
    return jnp.broadcast_to(column, (rows, rows))


def first_kernel(pieces, *refs):
    x_refs, weight_refs, refs = refs[:PLANE], refs[PLANE : PLANE + pieces], refs[PLANE + pieces :]
    wq_ref, mine_ref, other_ref, kv_ref, tail_ref, normed, weights = refs
    ctx = lax.axis_index("ctx")
    own, rows = lax.rem(ctx, PLANE), x_refs[0].shape[0]
    fill_weights(ctx, weight_refs, weights)
    norm_kernel(*x_refs, normed)
    keyvals = dot(normed[...], weights[...]).astype(jnp.bfloat16)
    kv_ref[...] = keyvals
    past = (WINDOW - 1) * rows
    tail_ref[:past] = keyvals[keyvals.shape[0] - past :]
    extra = tail_ref.shape[0] - past
    line = lax.broadcasted_iota(jnp.int32, (extra, rows), 0)
    block = jnp.zeros((extra, rows), jnp.float32)
    for t in range(WINDOW - 1):
        row = jnp.transpose(group_ids(x_refs, own, PLANE - WINDOW + 1 + t))[:extra]
        block = jnp.where(line == t, row, block)
    tail_ref[past:, :rows] = block.astype(jnp.bfloat16)
    tail_ref[past:, rows:] = jnp.zeros((extra, tail_ref.shape[1] - rows), jnp.bfloat16)
    project_query(normed[...], wq_ref, mine_ref, other_ref)


def out_copies(own, local_ref, piece_refs, whole, sems):
    half = piece_refs[1].shape[0]
    pieces = []
    for flip in (0, 1):
        three, one = piece_refs[2 * flip : 2 * flip + 2]
        pieces += [(three, 0, flip, 0), (three, 1, flip, 1)]
        pieces += [(three, 2, flip ^ 2, 0), (one, 0, flip ^ 2, 1)]
    from_own, from_pieces = [], []
    for i, (ref, part, o, second) in enumerate(pieces):
        at = pl.ds(i * half, half)
        from_own.append(pltpu.make_async_copy(local_ref.at[at], whole.at[at], sems.at[i]))
        place = pl.ds(pl.multiple_of(((own ^ o) * 2 + second) * half, half), half)
        source = ref.at[pl.ds(part * half, half)]
        from_pieces.append(pltpu.make_async_copy(source, whole.at[place], sems.at[i]))
    return from_own, from_pieces


def second_kernel(pieces, *refs):
    x_refs, b_refs = refs[:PLANE], refs[PLANE : 3 * PLANE]
    weight_refs, refs = refs[3 * PLANE : 3 * PLANE + pieces], refs[3 * PLANE + pieces :]
    wq_ref, wo_ref, piece_refs, refs = refs[0], refs[1], refs[2:6], refs[6:]
    own_ref, mine_ref, other_ref, kv_ref, tail_ref = refs[:5]
    stream, blended, normed, weights, whole, sems = refs[5:]
    ctx = lax.axis_index("ctx")
    side = lax.rem(lax.axis_index("phase"), 2)
    rows = x_refs[0].shape[0]
    own = lax.rem(ctx, PLANE)
    from_own, from_pieces = out_copies(own, wo_ref, piece_refs, whole, sems)

    @pl.when(side == 0)
    def _():
        for copy in from_own:
            copy.start()

    @pl.when(side == 1)
    def _():
        for copy in from_pieces:
            copy.start()

    fill_weights(ctx, weight_refs, weights)
    part = b_refs[0].shape[1]
    for r, o in enumerate(ORDER):
        stream[pl.ds(pl.multiple_of((own ^ o) * rows, rows), rows), :] = x_refs[r][:, : stream.shape[1]]
    for m, ref in enumerate(b_refs):
        place = (side * PLANE + own) ^ m
        blended[:, pl.ds(pl.multiple_of(place * part, part), part)] = ref[...]
    for copy in from_own:
        copy.wait()
    width = stream.shape[1]
    step = min(512, width)
    for n in range(0, width, step):
        total = dot(blended[...], whole[:, n : n + step])
        total = total + stream[:, n : n + step].astype(jnp.float32)
        stream[:, n : n + step] = total.astype(jnp.bfloat16)
    normed[...] = rms_rows(stream[...])
    own_ref[...] = stream[pl.ds(pl.multiple_of(own * rows, rows), rows), :]
    keyvals = dot(normed[...], weights[...]).astype(jnp.bfloat16)
    kv_ref[...] = keyvals
    tail_ref[...] = keyvals[keyvals.shape[0] - tail_ref.shape[0] :]
    project_query(normed[...], wq_ref, mine_ref, other_ref)


def mask_kernel(*refs):
    x_refs, (past_ref, bias_ref) = refs[:PLANE], refs[PLANE:]
    rows = bias_ref.shape[1]
    ctx = lax.axis_index("ctx")
    own = lax.rem(ctx, PLANE)
    before = WINDOW - 1
    columns = [group_ids(x_refs, own, g) for g in range(PLANE)]
    past = past_ref[before * rows :, :rows].astype(jnp.float32)
    keys = [jnp.broadcast_to(past[t : t + 1], (rows, rows)) for t in range(before)]
    keys += [jnp.transpose(column) for column in columns]
    causal = lax.broadcasted_iota(jnp.int32, (rows, rows), 0) >= lax.broadcasted_iota(
        jnp.int32, (rows, rows), 1
    )
    for g in range(PLANE):
        for t in range(WINDOW):
            allowed = columns[g] == keys[g + t]
            if t == before:
                allowed = allowed & causal
            if g + t < before:
                allowed = allowed & (ctx >= PLANE)
            bias_ref[g, :, t * rows : (t + 1) * rows] = jnp.where(allowed, 0.0, -jnp.inf)


def attend_kernel(layer, mine_ref, got_ref, bias_ref, kv_ref, past_ref, *refs):
    out_refs, window = refs[:-1], refs[-1]
    rows = bias_ref.shape[1]
    part = mine_ref.shape[1]
    tall, past = kv_ref.shape[0], (WINDOW - 1) * rows
    local_query = lax.rem(lax.axis_index("phase"), 2) == layer
    window[tall - past : tall] = past_ref[:past]
    window[tall:] = kv_ref[...]
    upper = lax.rem(lax.axis_index("ctx"), PLANE) // 2
    for g in range(PLANE):
        keys = window[(g + 1) * rows : (g + 1 + WINDOW) * rows]
        for h in range(0, part, HEAD):
            at = (slice(g * rows, (g + 1) * rows), slice(h, h + HEAD))
            query = jnp.where(local_query, mine_ref[at], got_ref[at])
            scores = lax.dot_general(
                query, keys[:, h : h + HEAD], (((1,), (1,)), ((), ())),
                preferred_element_type=jnp.float32,
            )
            scores = scores * (1.0 / math.sqrt(HEAD)) + bias_ref[g]
            weights = jnp.exp(scores - jnp.max(scores, axis=1, keepdims=True))
            total = jnp.sum(weights, axis=1, keepdims=True)
            values = keys[:, part + h : part + h + HEAD]
            result = (dot(weights.astype(jnp.bfloat16), values) / total).astype(jnp.bfloat16)
            if layer == 0:
                out_refs[0][g * rows : (g + 1) * rows, h : h + HEAD] = result
                continue
            place = (g % 2) * rows

            def put(ref):
                ref[place : place + rows, h : h + HEAD] = result

            pl.when(upper == g // 2)(functools.partial(put, out_refs[0]))
            pl.when(upper != g // 2)(functools.partial(put, out_refs[1]))


def last_kernel(*refs):
    b_refs, (wo_ref, own_ref, out_ref, blended) = refs[: 2 * PLANE], refs[2 * PLANE :]
    own = lax.rem(lax.axis_index("ctx"), PLANE)
    side = lax.rem(lax.axis_index("phase"), 2)
    rows, part = own_ref.shape[0], b_refs[0].shape[1]

    @pl.when(side == 0)
    def _():
        out_ref[...] = own_ref[...]

    @pl.when(side == 1)
    def _():
        for m, ref in enumerate(b_refs):
            place = (side * PLANE + own) ^ m
            start = pl.multiple_of(lax.rem(own, 2) * rows, rows)
            blended[:, pl.ds(pl.multiple_of(place * part, part), part)] = ref[pl.ds(start, rows), :]
        total = own_ref[...].astype(jnp.float32) + dot(blended[...], wo_ref[...])
        out_ref[...] = total.astype(jnp.bfloat16)


def after(value, *others):
    return lax.optimization_barrier((value,) + others)[0]


def along_planes(piece):
    count = lax.axis_size("ctx") // PLANE
    return [piece] + [swap(piece, 0, PLANE * m) for m in range(1, count)]


def local(inputs, segment_ids, w_query, w_keyval, w_out):
    batches, rows, width = inputs.shape
    phases = lax.axis_size("phase")
    phase = lax.axis_index("phase")
    side = phase % 2
    own = lax.axis_index("ctx") % PLANE
    bf16 = jnp.bfloat16

    head_width = w_query.shape[2]
    part = head_width // (2 * PLANE)
    depth = w_keyval.shape[1]
    tall, past = PLANE * rows, (WINDOW - 1) * rows

    half = head_width // PLANE // 2
    sent_out, query_mat = call(
        slice_kernel, [((3 * half, width), bf16), ((width, 2 * part), bf16)],
        [pltpu.SemaphoreType.DMA((4,))], LONG, w_out[0], w_query[0], far=(0, 1),
    )

    kept, for_y, for_x, for_both = call(
        cut_kernel, [((depth, 4 * part), bf16)] * 4, [], 0, w_keyval[0]
    )
    across_both, across_x, across_y = swap(for_both, 1, 2), swap(for_x, 1, 0), swap(for_y, 0, 2)
    kept, sent_out, query_mat = lax.optimization_barrier((kept, sent_out, query_mat))
    near, far = call(
        sort_kernel, [((2, 2 * depth, 2 * part), bf16)] * 2, [], 0,
        kept, across_y, across_x, across_both,
    )
    early, late_start = call(
        merge_kernel, [((4 * depth, 2 * part), bf16)] * 2, [], 0, near, swap(far, 0, 1)
    )
    got_out = swap(after(sent_out, near), 1, 0)
    early = along_planes(early)
    pieces = len(early)

    keyval_out = [((tall, 2 * part), bf16), ((past, 2 * part), bf16)]
    first_out = [((tall, 2 * part), bf16), ((past + 16, 2 * part), bf16)]
    query_out = [((tall, part), bf16)] * 2
    weights = ((width, 2 * part), bf16)
    dot_flops = 2 * tall * width * 2 * part
    attend_flops = 4 * tall * WINDOW * rows * part

    def two_layers(x, ids, bias):
        x = call(extend_kernel, [((rows, width + HEAD), bf16)], [], 0, x, ids)[0]
        across = swap(after(x, early[0]), 0, 2)
        xs = [x, across] + [swap(after(b, *early), 0, 1) for b in (x, across)]
        xs[0], got = lax.optimization_barrier((x, got_out))
        got_across = swap(got[half : 2 * half], 0, 2)
        late = {m: swap(after(late_start, early[3]), 0, PLANE * m) for m in (2, 1)}
        late[0] = late_start
        mine, other, kv, tail = call(
            functools.partial(first_kernel, pieces), query_out + first_out,
            [((tall, width), bf16), weights], LONG, *xs, *early, query_mat,
        )
        past_kv = from_plane_behind(tail)
        if bias is None:
            shape = ((PLANE, rows, WINDOW * rows), jnp.float32)
            bias = call(mask_kernel, [shape], [], 0, *xs, past_kv)[0]
        bias, late[1], late[2], got_across = lax.optimization_barrier(
            (bias, late[1], late[2], got_across)
        )
        blended = call(
            functools.partial(attend_kernel, 0), [((tall, part), bf16)],
            [((2 * tall, 2 * part), bf16)], 0, mine, swap(other, 1, 0), bias, kv, past_kv,
        )[0]
        for m in range(4, pieces):
            late[m] = swap(after(late_start, kv), 0, PLANE * m)
        near = [blended, swap(blended, 0, 2), swap(blended, 1, 0), swap(blended, 1, 2)]
        heads = [b for n in near for b in (n, swap(n, 0, 1))]
        late[3] = swap(after(late[2], blended), 0, PLANE)
        out = [got, got_across]
        out += [swap(after(b, blended), 0, 1) for b in out]
        stream, mine, other, kv, tail = call(
            functools.partial(second_kernel, pieces),
            [((rows, width), bf16)] + query_out + keyval_out,
            [((tall, width), bf16), ((tall, head_width), bf16), ((tall, width), bf16), weights,
             ((head_width, width), bf16), pltpu.SemaphoreType.DMA((2 * PLANE,))],
            2 * dot_flops + 2 * tall * head_width * width,
            *xs, *heads, *(late[m] for m in range(pieces)), query_mat, w_out[0], *out,
            far=range(3 * PLANE + pieces + 1, 3 * PLANE + pieces + 6),
        )
        mine, other = call(
            functools.partial(attend_kernel, 1), [((tall // 2, part), bf16)] * 2,
            [((2 * tall, 2 * part), bf16)],
            attend_flops, mine, swap(other, 1, 0), bias, kv, from_plane_behind(tail),
        )
        near = [mine, swap(other, 0, 2), swap(mine, 1, 0), swap(other, 1, 2)]
        heads = [b for n in near for b in (n, swap(n, 0, 1))]
        out = call(
            last_kernel, [((rows, width), bf16)], [((rows, head_width), bf16)],
            2 * rows * head_width * width, *heads, w_out[0], stream,
        )[0]
        return out, bias

    outs = []
    for b in range(batches):
        x, out, bias = inputs[b], None, None
        for tick in range(phases // 2):
            result, bias = two_layers(x, segment_ids[b : b + 1], bias)
            out = result if out is None else jnp.where(phase // 2 == tick, result, out)
            if tick + 1 < phases // 2:
                ahead = [
                    lax.ppermute(result, "phase", [(f, f + d) for f in range(1, phases - d, 2)])
                    for d in (1, 2)
                ]
                x = jnp.where(side == 0, ahead[0], ahead[1])
        outs.append(out)
    return jnp.stack(outs)[None]


def solution(mesh):
    placed = (
        P(None, "ctx", None),
        P(None, "ctx"),
        P("phase", None, None),
        P("phase", "ctx", None),
        P("phase", None, None),
    )
    return jax.shard_map(
        local, mesh=mesh, in_specs=placed, out_specs=P("phase", None, "ctx", None), check_vma=False
    )
```

time: 133 us -> 100 us (0.75)
  waiting for transfers between devices: 67.9 us -> 48.4 us
  local copies, waits for them, and re-layouts: 10.3 us -> 5.47 us
  other arithmetic: 4.02 us -> 0 us
  starting transfers between devices: 35.3 us -> 32.1 us
    ppermute x35 -> x33, waiting for transfers between devices: 58.2 us -> 44.1 us  [swap(): return lax.ppermute(block, BOTH, route)]
    ppermute x3 -> x2, waiting for transfers between devices: 9.7 us -> 4.26 us  [from_plane_behind(): lax.ppermute(block, 'ctx', [(i, i + PLANE) for i in range(wide - PLANE)])]
    dynamic_slice x5 -> x0, local copies, waits for them, and re-layouts: 4.91 us -> none  [the longest x1 1.87 us: local(): lax.dynamic_slice_in_dim(mat, ((1 - side) * PLANE + own) * part, part, 1)]
    select_n x3 -> x0, other arithmetic: 3.93 us -> none  [the longest x1 1.61 us: local(): early_out = plane_rows(jnp.where(side == 0, kept, swap(kept, 1, 0)))]
    ppermute x3 -> x2, starting transfers between devices: 10.6 us -> 6.86 us  [from_plane_behind(): lax.ppermute(block, 'ctx', [(i, i + PLANE) for i in range(wide - PLANE)])]
    unnamed x17 -> x12, local copies, waits for them, and re-layouts: 2.66 us -> 5.43 us
    squeeze x7 -> x0, local copies, waits for them, and re-layouts: 2.67 us -> none  [the longest x5 2.65 us: pick(): return lax.dynamic_index_in_dim(blocks, index, 0, keepdims=False)]
    pallas_call x6 -> x11, Pallas kernels: 13 us -> 12.1 us  [call(): pl.pallas_call(kernel, out_shape=[jax.ShapeDtypeStruct(s, d) for s, d in...]
  transfers between devices with their start and end apart: 38 -> 35, of which waited for: 21 -> 19; matrix products, arithmetic and copies ran while one was open for 8% -> 0% of each run, Pallas kernels for 3% -> 3%
where the time goes in v2:
time: 100 us; the launch traced here: 98.2 us
  waiting for transfers between devices  48.4 us (48%)
  starting transfers between devices  32.1 us (32%)
  Pallas kernels  12.1 us (12%)
  local copies, waits for them, and re-layouts  5.47 us (5%)
    ppermute x33, waiting for transfers between devices, swap(): return lax.ppermute(block, BOTH, route)  44.1 us
    ppermute x33, starting transfers between devices, swap(): return lax.ppermute(block, BOTH, route)  25.3 us
    pallas_call x11, Pallas kernels, call(): pl.pallas_call(kernel, out_shape=[jax.ShapeDtypeStruct(s, d) for s, d in...  12.1 us
    ppermute x2, starting transfers between devices, from_plane_behind(): lax.ppermute(block, 'ctx', [(i, i + PLANE) for i in range(wide - PLANE)])  6.86 us
    unnamed x12, local copies, waits for them, and re-layouts  5.43 us
    ppermute x2, waiting for transfers between devices, from_plane_behind(): lax.ppermute(block, 'ctx', [(i, i + PLANE) for i in range(wide - PLANE)])  4.26 us
  transfers between devices with their start and end apart: 35, of which 19 were waited for; matrix products, arithmetic and copies ran while one was open for 0% of the time, Pallas kernels for 3%

profile of v2, /device:TPU:14, one launch (start us, length us, event | category | flops | bytes accessed | tf_op | source)
XLA Modules:
  0.0 98.2 jit_solution(9803516051646026628)
XLA Ops:
  0.0 1.0 %copy-done.2 = bf16[1,128,2048]{2,1,0:T(8,128)(2,1)S(1)} copy-done((bf16[1,128,2048]{2,1,0:T(8,128)(2,1)S(1)}, bf16[1,128,2048]{2,1,0:T(8,128)(2,1)}, u32[]{:S(2)}) %copy-start.2) | copy-done | bytes 524312
  1.0 0.1 shard_map.56
  1.1 0.6 collective-permute-start
  1.7 0.5 collective-permute-start.1
  2.2 2.4 %collective-permute-start.2 = (bf16[128,512]{1,0:T(8,128)(2,1)S(1)}, bf16[128,512]{1,0:T(8,128)(2,1)S(1)}, u32[]{:S(2)}, u32[]{:S(2)}) collective-permute-start(bf16[128,512]{1,0:T(8,128)(2,1)S(1)} %get-tuple-element.50), channel_id=1, source_target_pairs={{0,18},{1,19},{2,16},{3,17},{4,22},{5,23},{6,20},{7,21},{8,26},{9,... | collective-permute-start | bytes 393224 | tf_op jit(solution)/shard_map/ppermute | solution.py:27
  4.7 2.2 %copy-done = bf16[1,1024,2048]{2,1,0:T(8,128)(2,1)S(1)} copy-done((bf16[1,1024,2048]{2,1,0:T(8,128)(2,1)S(1)}, bf16[1,1024,2048]{2,1,0:T(8,128)(2,1)}, u32[]{:S(2)}) %copy-start) | copy-done | bytes 4194328
  6.9 2.2 %copy-done.5 = bf16[1,2048,1024]{2,1,0:T(8,128)(2,1)S(1)} copy-done((bf16[1,2048,1024]{2,1,0:T(8,128)(2,1)S(1)}, bf16[1,2048,1024]{2,1,0:T(8,128)(2,1)}, u32[]{:S(2)}) %copy-start.5) | copy-done | bytes 4194328
  9.1 0.4 shard_map.57
  9.5 0.0 collective-permute-done.across_y
  9.5 0.0 collective-permute-done.1.across_x
  9.5 0.9 collective-permute-done.2.across_both
  10.4 0.1 shard_map.58
  10.5 0.6 collective-permute-start.3
  11.1 0.0 collective-permute-start.4
  11.1 0.2 shard_map.55.refs_0_
  11.3 1.4 %collective-permute-done.4.far_ref = bf16[2,256,256]{2,1,0:T(8,128)(2,1)S(1)} collective-permute-done((bf16[2,256,256]{2,1,0:T(8,128)(2,1)S(1)}, bf16[2,256,256]{2,1,0:T(8,128)(2,1)S(1)}, u32[]{:S(2)}, u32[]{:S(2)}) %collective-permute-start.4) | collective-permute-done | bytes 262176 | tf_op jit(solution)/shard_map/ppermute | solution.py:27
  12.7 0.6 collective-permute-start.5
  13.3 1.6 %collective-permute-start.8 = (bf16[512,256]{1,0:T(8,128)(2,1)S(1)}, bf16[512,256]{1,0:T(8,128)(2,1)S(1)}, u32[]{:S(2)}, u32[]{:S(2)}) collective-permute-start(bf16[512,256]{1,0:T(8,128)(2,1)S(1)} %get-tuple-element.55.refs_4_), channel_id=1, source_target_pairs={{0,12},{1,13},{2,14},{3,15},{4,8},{5,9},{6,10},{7,11},{8,4},{9,5},... | collective-permute-start | bytes 786440 | tf_op jit(solution)/shard_map/ppermute | solution.py:27
  14.9 1.1 %collective-permute-start.7 = (bf16[512,256]{1,0:T(8,128)(2,1)S(1)}, bf16[512,256]{1,0:T(8,128)(2,1)S(1)}, u32[]{:S(2)}, u32[]{:S(2)}) collective-permute-start(bf16[512,256]{1,0:T(8,128)(2,1)S(1)} %get-tuple-element.55.refs_4_), channel_id=1, source_target_pairs={{0,8},{1,9},{2,10},{3,11},{4,12},{5,13},{6,14},{7,15},{8,0},{9,1},... | collective-permute-start | bytes 786440 | tf_op jit(solution)/shard_map/ppermute | solution.py:27
  15.9 1.4 %collective-permute-start.6 = (bf16[512,256]{1,0:T(8,128)(2,1)S(1)}, bf16[512,256]{1,0:T(8,128)(2,1)S(1)}, u32[]{:S(2)}, u32[]{:S(2)}) collective-permute-start(bf16[512,256]{1,0:T(8,128)(2,1)S(1)} %get-tuple-element.55.refs_4_), channel_id=1, source_target_pairs={{0,4},{1,5},{2,6},{3,7},{4,0},{5,1},{6,2},{7,3},{8,12},{9,13},{10,... | collective-permute-start | bytes 786440 | tf_op jit(solution)/shard_map/ppermute | solution.py:27
  17.3 16.2 %collective-permute-done.8.refs_7_ = bf16[512,256]{1,0:T(8,128)(2,1)S(1)} collective-permute-done((bf16[512,256]{1,0:T(8,128)(2,1)S(1)}, bf16[512,256]{1,0:T(8,128)(2,1)S(1)}, u32[]{:S(2)}, u32[]{:S(2)}) %collective-permute-start.8) | collective-permute-done | bytes 262176 | tf_op jit(solution)/shard_map/ppermute | solution.py:27
  33.5 3.8 %collective-permute-done.7.refs_6_ = bf16[512,256]{1,0:T(8,128)(2,1)S(1)} collective-permute-done((bf16[512,256]{1,0:T(8,128)(2,1)S(1)}, bf16[512,256]{1,0:T(8,128)(2,1)S(1)}, u32[]{:S(2)}, u32[]{:S(2)}) %collective-permute-start.7) | collective-permute-done | bytes 262176 | tf_op jit(solution)/shard_map/ppermute | solution.py:27
  37.3 0.0 collective-permute-done.6.refs_5_
  37.3 0.5 collective-permute-start.10
  37.8 3.4 %collective-permute-start.14 = (bf16[512,256]{1,0:T(8,128)(2,1)S(1)}, bf16[512,256]{1,0:T(8,128)(2,1)S(1)}, u32[]{:S(2)}, u32[]{:S(2)}) collective-permute-start(bf16[512,256]{1,0:T(8,128)(2,1)S(1)} %get-tuple-element.64.refs_12_), channel_id=1, source_target_pairs={{0,8},{1,9},{2,10},{3,11},{4,12},{5,13},{6,14},{7,15},{8,0},{9,1},... | collective-permute-start | bytes 786440 | tf_op jit(solution)/shard_map/ppermute | solution.py:27
  41.2 4.0 %collective-permute-done.3.refs_18_ = bf16[384,2048]{1,0:T(8,128)(2,1)S(1)} collective-permute-done((bf16[384,2048]{1,0:T(8,128)(2,1)S(1)}, bf16[384,2048]{1,0:T(8,128)(2,1)S(1)}, u32[]{:S(2)}, u32[]{:S(2)}) %collective-permute-start.3) | collective-permute-done | bytes 1572896 | tf_op jit(solution)/shard_map/ppermute | solution.py:27
  45.3 0.6 collective-permute-start.15
  45.9 0.0 collective-permute-done.9.refs_2_
  45.9 0.0 collective-permute-done.10.refs_3_
  45.9 2.0 %shard_map.60 = (bf16[512,128]{1,0:T(8,128)(2,1)S(1)}, bf16[512,128]{1,0:T(8,128)(2,1)S(1)}, bf16[512,256]{1,0:T(8,128)(2,1)S(1)}, bf16[400,256]{1,0:T(8,128)(2,1)S(1)}) custom-call(bf16[128,2176]{1,0:T(8,128)(2,1)S(1)} %shard_map.55.refs_0_, bf16[128,2176]{1,0:T(8,128)(2,1)S(1)} %collective-permute-done.5.refs_1_, ...), custom_call_target="tpu_custom_call" | custom-call | flops 99999997952 | bytes 4325376 | tf_op jit(solution)/shard_map/pallas_call | solution.py:48
  47.9 3.5 %collective-permute-start.12 = (bf16[400,256]{1,0:T(8,128)(2,1)S(1)}, bf16[400,256]{1,0:T(8,128)(2,1)S(1)}, u32[]{:S(2)}, u32[]{:S(2)}) collective-permute-start(bf16[400,256]{1,0:T(8,128)(2,1)S(1)} %get-tuple-element.62), channel_id=1, source_target_pairs={{0,4},{1,5},{2,6},{3,7},{4,8},{5,9},{6,10},{7,11},{8,12},{9,13},{1... | collective-permute-start | bytes 614408 | tf_op jit(solution)/shard_map/ppermute | solution.py:32
  51.4 1.3 %collective-permute-start.11 = (bf16[512,128]{1,0:T(8,128)(2,1)S(1)}, bf16[512,128]{1,0:T(8,128)(2,1)S(1)}, u32[]{:S(2)}, u32[]{:S(2)}) collective-permute-start(bf16[512,128]{1,0:T(8,128)(2,1)S(1)} %get-tuple-element.61), channel_id=1, source_target_pairs={{0,16},{1,17},{2,18},{3,19},{4,20},{5,21},{6,22},{7,23},{8,24},{9,... | collective-permute-start | bytes 393224 | tf_op jit(solution)/shard_map/ppermute | solution.py:27
  52.6 4.1 %collective-permute-done.12.refs_4_.past_ref = bf16[400,256]{1,0:T(8,128)(2,1)S(1)} collective-permute-done((bf16[400,256]{1,0:T(8,128)(2,1)S(1)}, bf16[400,256]{1,0:T(8,128)(2,1)S(1)}, u32[]{:S(2)}, u32[]{:S(2)}) %collective-permute-start.12) | collective-permute-done | bytes 204832 | tf_op jit(solution)/shard_map/ppermute | solution.py:32
  56.8 0.2 shard_map.61.bias_ref
  57.0 0.0 collective-permute-done.14.refs_14_
  57.1 1.2 %shard_map.62.refs_4_ = bf16[512,128]{1,0:T(8,128)(2,1)S(1)} custom-call(bf16[512,128]{1,0:T(8,128)(2,1)S(1)} %get-tuple-element.60.mine_ref, bf16[512,128]{1,0:T(8,128)(2,1)S(1)} %collective-permute-done.11.got_ref, f32[4,128,512]{2,1,0:T(8,128)S(1)} %shard_map.61.bias_ref, bf16[512,256]{1,0:T(8,128)(2,1)S(1)} %get-tuple-element.67.kv_ref, ...), custom_call_target="tpu_custom_call" | custom-call | bytes 1777664 | tf_op jit(solution)/shard_map/pallas_call | solution.py:48
  58.3 0.1 collective-permute-start.24
  58.4 0.5 collective-permute-start.25
  58.9 2.4 %collective-permute-start.21 = (bf16[512,128]{1,0:T(8,128)(2,1)S(1)}, bf16[512,128]{1,0:T(8,128)(2,1)S(1)}, u32[]{:S(2)}, u32[]{:S(2)}) collective-permute-start(bf16[512,128]{1,0:T(8,128)(2,1)S(1)} %shard_map.62.refs_4_), channel_id=1, source_target_pairs={{0,18},{1,19},{2,16},{3,17},{4,22},{5,23},{6,20},{7,21},{8,26},{9,... | collective-permute-start | bytes 393224 | tf_op jit(solution)/shard_map/ppermute | solution.py:27
  61.3 0.5 collective-permute-start.19
  61.8 4.3 %collective-permute-done.21.refs_10_ = bf16[512,128]{1,0:T(8,128)(2,1)S(1)} collective-permute-done((bf16[512,128]{1,0:T(8,128)(2,1)S(1)}, bf16[512,128]{1,0:T(8,128)(2,1)S(1)}, u32[]{:S(2)}, u32[]{:S(2)}) %collective-permute-start.21) | collective-permute-done | bytes 131104 | tf_op jit(solution)/shard_map/ppermute | solution.py:27
  66.1 1.5 %collective-permute-start.17 = (bf16[512,128]{1,0:T(8,128)(2,1)S(1)}, bf16[512,128]{1,0:T(8,128)(2,1)S(1)}, u32[]{:S(2)}, u32[]{:S(2)}) collective-permute-start(bf16[512,128]{1,0:T(8,128)(2,1)S(1)} %shard_map.62.refs_4_), channel_id=1, source_target_pairs={{0,2},{1,3},{2,0},{3,1},{4,6},{5,7},{6,4},{7,5},{8,10},{9,11},{10,... | collective-permute-start | bytes 393224 | tf_op jit(solution)/shard_map/ppermute | solution.py:27
  67.6 0.5 collective-permute-done.19.refs_8_
  68.1 3.0 %collective-permute-done.17.refs_6_ = bf16[512,128]{1,0:T(8,128)(2,1)S(1)} collective-permute-done((bf16[512,128]{1,0:T(8,128)(2,1)S(1)}, bf16[512,128]{1,0:T(8,128)(2,1)S(1)}, u32[]{:S(2)}, u32[]{:S(2)}) %collective-permute-start.17) | collective-permute-done | bytes 131104 | tf_op jit(solution)/shard_map/ppermute | solution.py:27
  71.1 0.5 collective-permute-start.20
  71.6 0.1 collective-permute-start.18
  71.7 0.8 collective-permute-done.22.refs_11_
  72.4 0.2 collective-permute-done.20.refs_9_
  72.6 0.3 collective-permute-done.18.refs_7_
  73.0 4.6 %shard_map.63 = (bf16[128,2048]{1,0:T(8,128)(2,1)S(1)}, bf16[512,128]{1,0:T(8,128)(2,1)S(1)}, bf16[512,128]{1,0:T(8,128)(2,1)S(1)}, bf16[512,256]{1,0:T(8,128)(2,1)S(1)}, bf16[384,256]{1,0:T(8,128)(2,1)S(1)}) custom-call(bf16[128,2176]{1,0:T(8,128)(2,1)S(1)} %shard_map.55.refs_0_, bf16[128,2176]{1,0:T(8,128)(2,1)S(1)} %collective-permute-done.5.refs_1_, ...), custom_call_target="tpu_custom_call" | custom-call | flops 3221225472 | bytes 13762560 | tf_op jit(solution)/shard_map/pallas_call | solution.py:48
  77.5 3.4 %collective-permute-start.27 = (bf16[384,256]{1,0:T(8,128)(2,1)S(1)}, bf16[384,256]{1,0:T(8,128)(2,1)S(1)}, u32[]{:S(2)}, u32[]{:S(2)}) collective-permute-start(bf16[384,256]{1,0:T(8,128)(2,1)S(1)} %get-tuple-element.77), channel_id=1, source_target_pairs={{0,4},{1,5},{2,6},{3,7},{4,8},{5,9},{6,10},{7,11},{8,12},{9,13},{1... | collective-permute-start | bytes 589832 | tf_op jit(solution)/shard_map/ppermute | solution.py:32
  80.9 1.5 %collective-permute-start.26 = (bf16[512,128]{1,0:T(8,128)(2,1)S(1)}, bf16[512,128]{1,0:T(8,128)(2,1)S(1)}, u32[]{:S(2)}, u32[]{:S(2)}) collective-permute-start(bf16[512,128]{1,0:T(8,128)(2,1)S(1)} %get-tuple-element.75), channel_id=1, source_target_pairs={{0,16},{1,17},{2,18},{3,19},{4,20},{5,21},{6,22},{7,23},{8,24},{9,... | collective-permute-start | bytes 393224 | tf_op jit(solution)/shard_map/ppermute | solution.py:27
  82.5 3.9 %collective-permute-done.26.got_ref = bf16[512,128]{1,0:T(8,128)(2,1)S(1)} collective-permute-done((bf16[512,128]{1,0:T(8,128)(2,1)S(1)}, bf16[512,128]{1,0:T(8,128)(2,1)S(1)}, u32[]{:S(2)}, u32[]{:S(2)}) %collective-permute-start.26) | collective-permute-done | bytes 131104 | tf_op jit(solution)/shard_map/ppermute | solution.py:27
  86.3 0.1 collective-permute-done.27.past_ref
  86.5 1.7 %shard_map.64 = (bf16[256,128]{1,0:T(8,128)(2,1)S(1)}, bf16[256,128]{1,0:T(8,128)(2,1)S(1)}) custom-call(bf16[512,128]{1,0:T(8,128)(2,1)S(1)} %get-tuple-element.74.mine_ref, bf16[512,128]{1,0:T(8,128)(2,1)S(1)} %collective-permute-done.26.got_ref, f32[4,128,512]{2,1,0:T(8,128)S(1)} %shard_map.61.bias_ref, bf16[512,256]{1,0:T(8,128)(2,1)S(1)} %get-tuple-element.76.kv_ref, ...), custom_call_target="tpu_custom_call" | custom-call | flops 134217728 | bytes 1769472 | tf_op jit(solution)/shard_map/pallas_call | solution.py:48
  88.1 2.5 %collective-permute-start.33 = (bf16[256,128]{1,0:T(8,128)(2,1)S(1)}, bf16[256,128]{1,0:T(8,128)(2,1)S(1)}, u32[]{:S(2)}, u32[]{:S(2)}) collective-permute-start(bf16[256,128]{1,0:T(8,128)(2,1)S(1)} %get-tuple-element.79), channel_id=1, source_target_pairs={{0,18},{1,19},{2,16},{3,17},{4,22},{5,23},{6,20},{7,21},{8,26},{9,... | collective-permute-start | bytes 196616 | tf_op jit(solution)/shard_map/ppermute | solution.py:27
  90.6 0.5 collective-permute-start.29
  91.1 0.6 collective-permute-start.31
  91.7 1.8 %collective-permute-done.33.refs_6_ = bf16[256,128]{1,0:T(8,128)(2,1)S(1)} collective-permute-done((bf16[256,128]{1,0:T(8,128)(2,1)S(1)}, bf16[256,128]{1,0:T(8,128)(2,1)S(1)}, u32[]{:S(2)}, u32[]{:S(2)}) %collective-permute-start.33) | collective-permute-done | bytes 65568 | tf_op jit(solution)/shard_map/ppermute | solution.py:27
  93.5 1.4 %collective-permute-done.29.refs_2_ = bf16[256,128]{1,0:T(8,128)(2,1)S(1)} collective-permute-done((bf16[256,128]{1,0:T(8,128)(2,1)S(1)}, bf16[256,128]{1,0:T(8,128)(2,1)S(1)}, u32[]{:S(2)}, u32[]{:S(2)}) %collective-permute-start.29) | collective-permute-done | bytes 65568 | tf_op jit(solution)/shard_map/ppermute | solution.py:27
  94.9 0.5 collective-permute-done.31.refs_4_
  95.4 0.7 collective-permute-done.30.refs_3_
  96.1 0.5 collective-permute-done.32.refs_5_
  96.7 1.6 %shard_map.65 = bf16[128,2048]{1,0:T(8,128)(2,1)} custom-call(bf16[256,128]{1,0:T(8,128)(2,1)S(1)} %get-tuple-element.78.refs_0_, bf16[256,128]{1,0:T(8,128)(2,1)S(1)} %collective-permute-done.28.refs_1_, bf16[256,128]{1,0:T(8,128)(2,1)S(1)} %collective-permute-done.29.refs_2_, bf16[256,128]{1,0:T(8,128)(2,1)S(1)} %collective-permute-done.30.refs_3_, ...), custom_call_target="tpu_custom_call" | custom-call | flops 536870912 | bytes 5242880 | tf_op jit(solution)/shard_map/pallas_call | solution.py:48
  (30 shorter events, 0.1 us)
Async XLA Ops:
  0.0 1.0 %copy-start.2 = (bf16[1,128,2048]{2,1,0:T(8,128)(2,1)S(1)}, bf16[1,128,2048]{2,1,0:T(8,128)(2,1)}, u32[]{:S(2)}) copy-start(bf16[1,128,2048]{2,1,0:T(8,128)(2,1)} %param.8) | copy-start | bytes 1572868
  1.1 8.4 %collective-permute-start = (bf16[128,512]{1,0:T(8,128)(2,1)S(1)}, bf16[128,512]{1,0:T(8,128)(2,1)S(1)}, u32[]{:S(2)}, u32[]{:S(2)}) collective-permute-start(bf16[128,512]{1,0:T(8,128)(2,1)S(1)} %get-tuple-element.48), channel_id=1, source_target_pairs={{0,2},{1,3},{2,0},{3,1},{4,6},{5,7},{6,4},{7,5},{8,10},{9,11},{10,... | collective-permute-start | bytes 393224 | tf_op jit(solution)/shard_map/ppermute | solution.py:27
  1.7 7.8 %collective-permute-start.1 = (bf16[128,512]{1,0:T(8,128)(2,1)S(1)}, bf16[128,512]{1,0:T(8,128)(2,1)S(1)}, u32[]{:S(2)}, u32[]{:S(2)}) collective-permute-start(bf16[128,512]{1,0:T(8,128)(2,1)S(1)} %get-tuple-element.49), channel_id=1, source_target_pairs={{0,16},{1,17},{2,18},{3,19},{4,20},{5,21},{6,22},{7,23},{8,24},{9,... | collective-permute-start | bytes 393224 | tf_op jit(solution)/shard_map/ppermute | solution.py:27
  2.2 8.2 %collective-permute-start.2 = (bf16[128,512]{1,0:T(8,128)(2,1)S(1)}, bf16[128,512]{1,0:T(8,128)(2,1)S(1)}, u32[]{:S(2)}, u32[]{:S(2)}) collective-permute-start(bf16[128,512]{1,0:T(8,128)(2,1)S(1)} %get-tuple-element.50), channel_id=1, source_target_pairs={{0,18},{1,19},{2,16},{3,17},{4,22},{5,23},{6,20},{7,21},{8,26},{9,... | collective-permute-start | bytes 393224 | tf_op jit(solution)/shard_map/ppermute | solution.py:27
  4.7 2.2 %copy-start = (bf16[1,1024,2048]{2,1,0:T(8,128)(2,1)S(1)}, bf16[1,1024,2048]{2,1,0:T(8,128)(2,1)}, u32[]{:S(2)}) copy-start(bf16[1,1024,2048]{2,1,0:T(8,128)(2,1)} %param.9) | copy-start | bytes 12582916
  6.9 2.2 %copy-start.5 = (bf16[1,2048,1024]{2,1,0:T(8,128)(2,1)S(1)}, bf16[1,2048,1024]{2,1,0:T(8,128)(2,1)}, u32[]{:S(2)}) copy-start(bf16[1,2048,1024]{2,1,0:T(8,128)(2,1)} %param.7) | copy-start | bytes 12582916
  9.0 2.1 %copy-start.3 = (bf16[1,128,2048]{2,1,0:T(8,128)(2,1)S(1)}, bf16[1,128,2048]{2,1,0:T(8,128)(2,1)}, u32[]{:S(2)}) copy-start(bf16[1,128,2048]{2,1,0:T(8,128)(2,1)} %param.5) | copy-start | bytes 1572868
  9.0 2.1 %copy-start.4 = (s32[1,128]{1,0:T(1,128)S(1)}, s32[1,128]{1,0:T(1,128)}, u32[]{:S(2)}) copy-start(s32[1,128]{1,0:T(1,128)} %id_ref.1) | copy-start | bytes 1540
  10.5 34.7 %collective-permute-start.3 = (bf16[384,2048]{1,0:T(8,128)(2,1)S(1)}, bf16[384,2048]{1,0:T(8,128)(2,1)S(1)}, u32[]{:S(2)}, u32[]{:S(2)}) collective-permute-start(bf16[384,2048]{1,0:T(8,128)(2,1)S(1)} %get-tuple-element.52), channel_id=1, source_target_pairs={{0,16},{1,17},{2,18},{3,19},{4,20},{5,21},{6,22},{7,23},{8,24},{9,... | collective-permute-start | bytes 4718600 | tf_op jit(solution)/shard_map/ppermute | solution.py:27
  11.1 1.5 %collective-permute-start.4 = (bf16[2,256,256]{2,1,0:T(8,128)(2,1)S(1)}, bf16[2,256,256]{2,1,0:T(8,128)(2,1)S(1)}, u32[]{:S(2)}, u32[]{:S(2)}) collective-permute-start(bf16[2,256,256]{2,1,0:T(8,128)(2,1)S(1)} %get-tuple-element.54), channel_id=1, source_target_pairs={{0,1},{1,0},{2,3},{3,2},{4,5},{5,4},{6,7},{7,6},{8,9},{9,8},{10,11... | collective-permute-start | bytes 786440 | tf_op jit(solution)/shard_map/ppermute | solution.py:27
  12.7 24.6 %collective-permute-start.5 = (bf16[128,2176]{1,0:T(8,128)(2,1)S(1)}, bf16[128,2176]{1,0:T(8,128)(2,1)S(1)}, u32[]{:S(2)}, u32[]{:S(2)}) collective-permute-start(bf16[128,2176]{1,0:T(8,128)(2,1)S(1)} %shard_map.55.refs_0_), channel_id=1, source_target_pairs={{0,2},{1,3},{2,0},{3,1},{4,6},{5,7},{6,4},{7,5},{8,10},{9,11},{10,... | collective-permute-start | bytes 1671176 | tf_op jit(solution)/shard_map/ppermute | solution.py:27
  13.3 20.3 %collective-permute-start.8 = (bf16[512,256]{1,0:T(8,128)(2,1)S(1)}, bf16[512,256]{1,0:T(8,128)(2,1)S(1)}, u32[]{:S(2)}, u32[]{:S(2)}) collective-permute-start(bf16[512,256]{1,0:T(8,128)(2,1)S(1)} %get-tuple-element.55.refs_4_), channel_id=1, source_target_pairs={{0,12},{1,13},{2,14},{3,15},{4,8},{5,9},{6,10},{7,11},{8,4},{9,5},... | collective-permute-start | bytes 786440 | tf_op jit(solution)/shard_map/ppermute | solution.py:27
  14.9 22.4 %collective-permute-start.7 = (bf16[512,256]{1,0:T(8,128)(2,1)S(1)}, bf16[512,256]{1,0:T(8,128)(2,1)S(1)}, u32[]{:S(2)}, u32[]{:S(2)}) collective-permute-start(bf16[512,256]{1,0:T(8,128)(2,1)S(1)} %get-tuple-element.55.refs_4_), channel_id=1, source_target_pairs={{0,8},{1,9},{2,10},{3,11},{4,12},{5,13},{6,14},{7,15},{8,0},{9,1},... | collective-permute-start | bytes 786440 | tf_op jit(solution)/shard_map/ppermute | solution.py:27
  15.9 21.4 %collective-permute-start.6 = (bf16[512,256]{1,0:T(8,128)(2,1)S(1)}, bf16[512,256]{1,0:T(8,128)(2,1)S(1)}, u32[]{:S(2)}, u32[]{:S(2)}) collective-permute-start(bf16[512,256]{1,0:T(8,128)(2,1)S(1)} %get-tuple-element.55.refs_4_), channel_id=1, source_target_pairs={{0,4},{1,5},{2,6},{3,7},{4,0},{5,1},{6,2},{7,3},{8,12},{9,13},{10,... | collective-permute-start | bytes 786440 | tf_op jit(solution)/shard_map/ppermute | solution.py:27
  37.3 8.6 %collective-permute-start.9 = (bf16[128,2176]{1,0:T(8,128)(2,1)S(1)}, bf16[128,2176]{1,0:T(8,128)(2,1)S(1)}, u32[]{:S(2)}, u32[]{:S(2)}) collective-permute-start(bf16[128,2176]{1,0:T(8,128)(2,1)S(1)} %shard_map.55.refs_0_), channel_id=1, source_target_pairs={{0,1},{1,0},{2,3},{3,2},{4,5},{5,4},{6,7},{7,6},{8,9},{9,8},{10,11... | collective-permute-start | bytes 1671176 | tf_op jit(solution)/shard_map/ppermute | solution.py:27
  37.3 8.5 %collective-permute-start.10 = (bf16[128,2176]{1,0:T(8,128)(2,1)S(1)}, bf16[128,2176]{1,0:T(8,128)(2,1)S(1)}, u32[]{:S(2)}, u32[]{:S(2)}) collective-permute-start(bf16[128,2176]{1,0:T(8,128)(2,1)S(1)} %collective-permute-done.5.refs_1_), channel_id=1, source_target_pairs={{0,1},{1,0},{2,3},{3,2},{4,5},{5,4},{6,7},{7,6},{8,9},{9,8},{10,11... | collective-permute-start | bytes 1671176 | tf_op jit(solution)/shard_map/ppermute | solution.py:27
  37.8 19.2 %collective-permute-start.14 = (bf16[512,256]{1,0:T(8,128)(2,1)S(1)}, bf16[512,256]{1,0:T(8,128)(2,1)S(1)}, u32[]{:S(2)}, u32[]{:S(2)}) collective-permute-start(bf16[512,256]{1,0:T(8,128)(2,1)S(1)} %get-tuple-element.64.refs_12_), channel_id=1, source_target_pairs={{0,8},{1,9},{2,10},{3,11},{4,12},{5,13},{6,14},{7,15},{8,0},{9,1},... | collective-permute-start | bytes 786440 | tf_op jit(solution)/shard_map/ppermute | solution.py:27
  41.2 15.8 %collective-permute-start.13 = (bf16[512,256]{1,0:T(8,128)(2,1)S(1)}, bf16[512,256]{1,0:T(8,128)(2,1)S(1)}, u32[]{:S(2)}, u32[]{:S(2)}) collective-permute-start(bf16[512,256]{1,0:T(8,128)(2,1)S(1)} %get-tuple-element.64.refs_12_), channel_id=1, source_target_pairs={{0,4},{1,5},{2,6},{3,7},{4,0},{5,1},{6,2},{7,3},{8,12},{9,13},{10,... | collective-permute-start | bytes 786440 | tf_op jit(solution)/shard_map/ppermute | solution.py:27
  45.3 11.8 %collective-permute-start.15 = (bf16[128,2048]{1,0:T(8,128)(2,1)S(1)}, bf16[128,2048]{1,0:T(8,128)(2,1)S(1)}, u32[]{:S(2)}, u32[]{:S(2)}) collective-permute-start(bf16[128,2048]{1,0:T(8,128)(2,1)S(1)} %slice.3), channel_id=1, source_target_pairs={{0,2},{1,3},{2,0},{3,1},{4,6},{5,7},{6,4},{7,5},{8,10},{9,11},{10,... | collective-permute-start | bytes 1572872 | tf_op jit(solution)/shard_map/ppermute | solution.py:27
  47.9 8.9 %collective-permute-start.12 = (bf16[400,256]{1,0:T(8,128)(2,1)S(1)}, bf16[400,256]{1,0:T(8,128)(2,1)S(1)}, u32[]{:S(2)}, u32[]{:S(2)}) collective-permute-start(bf16[400,256]{1,0:T(8,128)(2,1)S(1)} %get-tuple-element.62), channel_id=1, source_target_pairs={{0,4},{1,5},{2,6},{3,7},{4,8},{5,9},{6,10},{7,11},{8,12},{9,13},{1... | collective-permute-start | bytes 614408 | tf_op jit(solution)/shard_map/ppermute | solution.py:32
  51.4 5.7 %collective-permute-start.11 = (bf16[512,128]{1,0:T(8,128)(2,1)S(1)}, bf16[512,128]{1,0:T(8,128)(2,1)S(1)}, u32[]{:S(2)}, u32[]{:S(2)}) collective-permute-start(bf16[512,128]{1,0:T(8,128)(2,1)S(1)} %get-tuple-element.61), channel_id=1, source_target_pairs={{0,16},{1,17},{2,18},{3,19},{4,20},{5,21},{6,22},{7,23},{8,24},{9,... | collective-permute-start | bytes 393224 | tf_op jit(solution)/shard_map/ppermute | solution.py:27
  56.8 16.2 %copy-start.1 = (bf16[1,1024,2048]{2,1,0:T(8,128)(2,1)S(1)}, bf16[1,1024,2048]{2,1,0:T(8,128)(2,1)}, u32[]{:S(2)}) copy-start(bf16[1,1024,2048]{2,1,0:T(8,128)(2,1)} %param.9) | copy-start | bytes 12582916
  58.3 14.7 %collective-permute-start.24 = (bf16[384,2048]{1,0:T(8,128)(2,1)S(1)}, bf16[384,2048]{1,0:T(8,128)(2,1)S(1)}, u32[]{:S(2)}, u32[]{:S(2)}) collective-permute-start(bf16[384,2048]{1,0:T(8,128)(2,1)S(1)} %collective-permute-done.3.refs_18_), channel_id=1, source_target_pairs={{0,1},{1,0},{2,3},{3,2},{4,5},{5,4},{6,7},{7,6},{8,9},{9,8},{10,11... | collective-permute-start | bytes 4718600 | tf_op jit(solution)/shard_map/ppermute | solution.py:27
  58.4 14.6 %collective-permute-start.25 = (bf16[128,2048]{1,0:T(8,128)(2,1)S(1)}, bf16[128,2048]{1,0:T(8,128)(2,1)S(1)}, u32[]{:S(2)}, u32[]{:S(2)}) collective-permute-start(bf16[128,2048]{1,0:T(8,128)(2,1)S(1)} %collective-permute-done.15.refs_19_), channel_id=1, source_target_pairs={{0,1},{1,0},{2,3},{3,2},{4,5},{5,4},{6,7},{7,6},{8,9},{9,8},{10,11... | collective-permute-start | bytes 1572872 | tf_op jit(solution)/shard_map/ppermute | solution.py:27
  58.9 7.3 %collective-permute-start.21 = (bf16[512,128]{1,0:T(8,128)(2,1)S(1)}, bf16[512,128]{1,0:T(8,128)(2,1)S(1)}, u32[]{:S(2)}, u32[]{:S(2)}) collective-permute-start(bf16[512,128]{1,0:T(8,128)(2,1)S(1)} %shard_map.62.refs_4_), channel_id=1, source_target_pairs={{0,18},{1,19},{2,16},{3,17},{4,22},{5,23},{6,20},{7,21},{8,26},{9,... | collective-permute-start | bytes 393224 | tf_op jit(solution)/shard_map/ppermute | solution.py:27
  61.3 6.8 %collective-permute-start.19 = (bf16[512,128]{1,0:T(8,128)(2,1)S(1)}, bf16[512,128]{1,0:T(8,128)(2,1)S(1)}, u32[]{:S(2)}, u32[]{:S(2)}) collective-permute-start(bf16[512,128]{1,0:T(8,128)(2,1)S(1)} %shard_map.62.refs_4_), channel_id=1, source_target_pairs={{0,16},{1,17},{2,18},{3,19},{4,20},{5,21},{6,22},{7,23},{8,24},{9,... | collective-permute-start | bytes 393224 | tf_op jit(solution)/shard_map/ppermute | solution.py:27
  61.8 9.8 %collective-permute-start.23 = (bf16[512,256]{1,0:T(8,128)(2,1)S(1)}, bf16[512,256]{1,0:T(8,128)(2,1)S(1)}, u32[]{:S(2)}, u32[]{:S(2)}) collective-permute-start(bf16[512,256]{1,0:T(8,128)(2,1)S(1)} %collective-permute-done.14.refs_14_), channel_id=1, source_target_pairs={{0,4},{1,5},{2,6},{3,7},{4,0},{5,1},{6,2},{7,3},{8,12},{9,13},{10,... | collective-permute-start | bytes 786440 | tf_op jit(solution)/shard_map/ppermute | solution.py:27
  66.1 5.0 %collective-permute-start.17 = (bf16[512,128]{1,0:T(8,128)(2,1)S(1)}, bf16[512,128]{1,0:T(8,128)(2,1)S(1)}, u32[]{:S(2)}, u32[]{:S(2)}) collective-permute-start(bf16[512,128]{1,0:T(8,128)(2,1)S(1)} %shard_map.62.refs_4_), channel_id=1, source_target_pairs={{0,2},{1,3},{2,0},{3,1},{4,6},{5,7},{6,4},{7,5},{8,10},{9,11},{10,... | collective-permute-start | bytes 393224 | tf_op jit(solution)/shard_map/ppermute | solution.py:27
  68.1 3.0 %collective-permute-start.16 = (bf16[512,128]{1,0:T(8,128)(2,1)S(1)}, bf16[512,128]{1,0:T(8,128)(2,1)S(1)}, u32[]{:S(2)}, u32[]{:S(2)}) collective-permute-start(bf16[512,128]{1,0:T(8,128)(2,1)S(1)} %shard_map.62.refs_4_), channel_id=1, source_target_pairs={{0,1},{1,0},{2,3},{3,2},{4,5},{5,4},{6,7},{7,6},{8,9},{9,8},{10,11... | collective-permute-start | bytes 393224 | tf_op jit(solution)/shard_map/ppermute | solution.py:27
  71.1 1.3 %collective-permute-start.22 = (bf16[512,128]{1,0:T(8,128)(2,1)S(1)}, bf16[512,128]{1,0:T(8,128)(2,1)S(1)}, u32[]{:S(2)}, u32[]{:S(2)}) collective-permute-start(bf16[512,128]{1,0:T(8,128)(2,1)S(1)} %collective-permute-done.21.refs_10_), channel_id=1, source_target_pairs={{0,1},{1,0},{2,3},{3,2},{4,5},{5,4},{6,7},{7,6},{8,9},{9,8},{10,11... | collective-permute-start | bytes 393224 | tf_op jit(solution)/shard_map/ppermute | solution.py:27
  71.1 1.5 %collective-permute-start.20 = (bf16[512,128]{1,0:T(8,128)(2,1)S(1)}, bf16[512,128]{1,0:T(8,128)(2,1)S(1)}, u32[]{:S(2)}, u32[]{:S(2)}) collective-permute-start(bf16[512,128]{1,0:T(8,128)(2,1)S(1)} %collective-permute-done.19.refs_8_), channel_id=1, source_target_pairs={{0,1},{1,0},{2,3},{3,2},{4,5},{5,4},{6,7},{7,6},{8,9},{9,8},{10,11... | collective-permute-start | bytes 393224 | tf_op jit(solution)/shard_map/ppermute | solution.py:27
  71.6 1.3 %collective-permute-start.18 = (bf16[512,128]{1,0:T(8,128)(2,1)S(1)}, bf16[512,128]{1,0:T(8,128)(2,1)S(1)}, u32[]{:S(2)}, u32[]{:S(2)}) collective-permute-start(bf16[512,128]{1,0:T(8,128)(2,1)S(1)} %collective-permute-done.17.refs_6_), channel_id=1, source_target_pairs={{0,1},{1,0},{2,3},{3,2},{4,5},{5,4},{6,7},{7,6},{8,9},{9,8},{10,11... | collective-permute-start | bytes 393224 | tf_op jit(solution)/shard_map/ppermute | solution.py:27
  77.5 8.9 %collective-permute-start.27 = (bf16[384,256]{1,0:T(8,128)(2,1)S(1)}, bf16[384,256]{1,0:T(8,128)(2,1)S(1)}, u32[]{:S(2)}, u32[]{:S(2)}) collective-permute-start(bf16[384,256]{1,0:T(8,128)(2,1)S(1)} %get-tuple-element.77), channel_id=1, source_target_pairs={{0,4},{1,5},{2,6},{3,7},{4,8},{5,9},{6,10},{7,11},{8,12},{9,13},{1... | collective-permute-start | bytes 589832 | tf_op jit(solution)/shard_map/ppermute | solution.py:32
  80.9 5.4 %collective-permute-start.26 = (bf16[512,128]{1,0:T(8,128)(2,1)S(1)}, bf16[512,128]{1,0:T(8,128)(2,1)S(1)}, u32[]{:S(2)}, u32[]{:S(2)}) collective-permute-start(bf16[512,128]{1,0:T(8,128)(2,1)S(1)} %get-tuple-element.75), channel_id=1, source_target_pairs={{0,16},{1,17},{2,18},{3,19},{4,20},{5,21},{6,22},{7,23},{8,24},{9,... | collective-permute-start | bytes 393224 | tf_op jit(solution)/shard_map/ppermute | solution.py:27
  88.1 5.3 %collective-permute-start.33 = (bf16[256,128]{1,0:T(8,128)(2,1)S(1)}, bf16[256,128]{1,0:T(8,128)(2,1)S(1)}, u32[]{:S(2)}, u32[]{:S(2)}) collective-permute-start(bf16[256,128]{1,0:T(8,128)(2,1)S(1)} %get-tuple-element.79), channel_id=1, source_target_pairs={{0,18},{1,19},{2,16},{3,17},{4,22},{5,23},{6,20},{7,21},{8,26},{9,... | collective-permute-start | bytes 196616 | tf_op jit(solution)/shard_map/ppermute | solution.py:27
  90.6 4.3 %collective-permute-start.29 = (bf16[256,128]{1,0:T(8,128)(2,1)S(1)}, bf16[256,128]{1,0:T(8,128)(2,1)S(1)}, u32[]{:S(2)}, u32[]{:S(2)}) collective-permute-start(bf16[256,128]{1,0:T(8,128)(2,1)S(1)} %get-tuple-element.79), channel_id=1, source_target_pairs={{0,2},{1,3},{2,0},{3,1},{4,6},{5,7},{6,4},{7,5},{8,10},{9,11},{10,... | collective-permute-start | bytes 196616 | tf_op jit(solution)/shard_map/ppermute | solution.py:27
  91.1 4.3 %collective-permute-start.31 = (bf16[256,128]{1,0:T(8,128)(2,1)S(1)}, bf16[256,128]{1,0:T(8,128)(2,1)S(1)}, u32[]{:S(2)}, u32[]{:S(2)}) collective-permute-start(bf16[256,128]{1,0:T(8,128)(2,1)S(1)} %get-tuple-element.78.refs_0_), channel_id=1, source_target_pairs={{0,16},{1,17},{2,18},{3,19},{4,20},{5,21},{6,22},{7,23},{8,24},{9,... | collective-permute-start | bytes 196616 | tf_op jit(solution)/shard_map/ppermute | solution.py:27
  91.7 3.7 %collective-permute-start.28 = (bf16[256,128]{1,0:T(8,128)(2,1)S(1)}, bf16[256,128]{1,0:T(8,128)(2,1)S(1)}, u32[]{:S(2)}, u32[]{:S(2)}) collective-permute-start(bf16[256,128]{1,0:T(8,128)(2,1)S(1)} %get-tuple-element.78.refs_0_), channel_id=1, source_target_pairs={{0,1},{1,0},{2,3},{3,2},{4,5},{5,4},{6,7},{7,6},{8,9},{9,8},{10,11... | collective-permute-start | bytes 196616 | tf_op jit(solution)/shard_map/ppermute | solution.py:27
  93.5 1.9 %collective-permute-start.34 = (bf16[256,128]{1,0:T(8,128)(2,1)S(1)}, bf16[256,128]{1,0:T(8,128)(2,1)S(1)}, u32[]{:S(2)}, u32[]{:S(2)}) collective-permute-start(bf16[256,128]{1,0:T(8,128)(2,1)S(1)} %collective-permute-done.33.refs_6_), channel_id=1, source_target_pairs={{0,1},{1,0},{2,3},{3,2},{4,5},{5,4},{6,7},{7,6},{8,9},{9,8},{10,11... | collective-permute-start | bytes 196616 | tf_op jit(solution)/shard_map/ppermute | solution.py:27
  94.9 1.3 %collective-permute-start.30 = (bf16[256,128]{1,0:T(8,128)(2,1)S(1)}, bf16[256,128]{1,0:T(8,128)(2,1)S(1)}, u32[]{:S(2)}, u32[]{:S(2)}) collective-permute-start(bf16[256,128]{1,0:T(8,128)(2,1)S(1)} %collective-permute-done.29.refs_2_), channel_id=1, source_target_pairs={{0,1},{1,0},{2,3},{3,2},{4,5},{5,4},{6,7},{7,6},{8,9},{9,8},{10,11... | collective-permute-start | bytes 196616 | tf_op jit(solution)/shard_map/ppermute | solution.py:27
  95.4 1.3 %collective-permute-start.32 = (bf16[256,128]{1,0:T(8,128)(2,1)S(1)}, bf16[256,128]{1,0:T(8,128)(2,1)S(1)}, u32[]{:S(2)}, u32[]{:S(2)}) collective-permute-start(bf16[256,128]{1,0:T(8,128)(2,1)S(1)} %collective-permute-done.31.refs_4_), channel_id=1, source_target_pairs={{0,1},{1,0},{2,3},{3,2},{4,5},{5,4},{6,7},{7,6},{8,9},{9,8},{10,11... | collective-permute-start | bytes 196616 | tf_op jit(solution)/shard_map/ppermute | solution.py:27

commit v3 on v2

--- a/solution.py
+++ b/solution.py
@@ -42,9 +42,9 @@
     return jnp.dot(a, b, preferred_element_type=jnp.float32)
 
 
-def call(kernel, outs, scratch, flops, *operands, far=()):
+def call(kernel, outs, scratch, flops, *operands, far={}):
     moved = sum(o.size * o.dtype.itemsize for o in operands)
-    place = lambda i: pltpu.HBM if i in far else pltpu.VMEM
+    place = lambda i: far.get(i, pltpu.VMEM)
     return pl.pallas_call(
         kernel,
         out_shape=[jax.ShapeDtypeStruct(s, d) for s, d in outs],
@@ -66,19 +66,24 @@
     ).astype(jnp.bfloat16)
 
 
-def slice_kernel(out_ref, query_ref, sent_out, query_mat, sems):
+def slice_kernel(out_ref, query_ref, sent_first, sent_second, query_mat, sems):
     side = lax.rem(lax.axis_index("phase"), 2)
     own = lax.rem(lax.axis_index("ctx"), PLANE)
-    half, part = sent_out.shape[0] // 3, query_mat.shape[1] // 2
+    unit, wide = sent_first.shape[0] // 6, sent_first.shape[1]
+    part = query_mat.shape[1] // 2
+    columns = pl.ds(pl.multiple_of(lax.rem(own, 2) * wide, wide), wide)
     copies = []
-    for i, (first, count, place) in enumerate(((0, 2, 2 * own), (2, 1, 2 * (own ^ 2)))):
-        at = pl.ds(pl.multiple_of(place * half, half), count * half)
-        to = sent_out.at[pl.ds(first * half, count * half)]
-        copies.append(pltpu.make_async_copy(out_ref.at[at], to, sems.at[i]))
+    for i, (ref, first, count, upper, skip) in enumerate((
+        (sent_first, 0, 6, own // 2, 2), (sent_second, 0, 2, own // 2, 0),
+        (sent_second, 2, 2, 1 - own // 2, 0),
+    )):
+        at = pl.ds(pl.multiple_of((upper * 8 + skip) * unit, unit), count * unit)
+        to = ref.at[pl.ds(first * unit, count * unit)]
+        copies.append(pltpu.make_async_copy(out_ref.at[at, columns], to, sems.at[i]))
     for flip in (0, 1):
         at = pl.ds(pl.multiple_of(((side ^ flip) * PLANE + own) * part, part), part)
         to = query_mat.at[:, pl.ds(flip * part, part)]
-        copies.append(pltpu.make_async_copy(query_ref.at[:, at], to, sems.at[2 + flip]))
+        copies.append(pltpu.make_async_copy(query_ref.at[:, at], to, sems.at[3 + flip]))
     for copy in copies:
         copy.start()
     for copy in copies:
@@ -121,6 +126,14 @@
         ref[rows:] = far_ref[layer]
 
 
+def token_kernel(*refs):
+    refs[-1][...] = jnp.zeros(refs[-1].shape, refs[-1].dtype)
+
+
+def copy_kernel(block_ref, out_ref):
+    out_ref[...] = block_ref[...]
+
+
 def fill_weights(ctx, weight_refs, weights):
     rows = weight_refs[0].shape[0] // PLANE
     for m, ref in enumerate(weight_refs):
@@ -155,55 +168,56 @@
     return jnp.broadcast_to(column, (rows, rows))
 
 
-def first_kernel(pieces, *refs):
-    x_refs, weight_refs, refs = refs[:PLANE], refs[PLANE : PLANE + pieces], refs[PLANE + pieces :]
-    wq_ref, mine_ref, other_ref, kv_ref, tail_ref, normed, weights = refs
-    ctx = lax.axis_index("ctx")
-    own, rows = lax.rem(ctx, PLANE), x_refs[0].shape[0]
-    fill_weights(ctx, weight_refs, weights)
-    norm_kernel(*x_refs, normed)
-    keyvals = dot(normed[...], weights[...]).astype(jnp.bfloat16)
-    kv_ref[...] = keyvals
-    past = (WINDOW - 1) * rows
-    tail_ref[:past] = keyvals[keyvals.shape[0] - past :]
-    extra = tail_ref.shape[0] - past
+def query_kernel(*refs):
+    x_refs, (wq_ref, normed_ref, mine_ref, other_ref, ids_ref) = refs[:PLANE], refs[PLANE:]
+    own, rows = lax.rem(lax.axis_index("ctx"), PLANE), x_refs[0].shape[0]
+    norm_kernel(*x_refs, normed_ref)
+    project_query(normed_ref[...], wq_ref, mine_ref, other_ref)
+    extra, wide = ids_ref.shape
     line = lax.broadcasted_iota(jnp.int32, (extra, rows), 0)
     block = jnp.zeros((extra, rows), jnp.float32)
     for t in range(WINDOW - 1):
         row = jnp.transpose(group_ids(x_refs, own, PLANE - WINDOW + 1 + t))[:extra]
         block = jnp.where(line == t, row, block)
-    tail_ref[past:, :rows] = block.astype(jnp.bfloat16)
-    tail_ref[past:, rows:] = jnp.zeros((extra, tail_ref.shape[1] - rows), jnp.bfloat16)
-    project_query(normed[...], wq_ref, mine_ref, other_ref)
+    ids_ref[:, :rows] = block.astype(jnp.bfloat16)
+    ids_ref[:, rows:] = jnp.zeros((extra, wide - rows), jnp.bfloat16)
+
+
+def keyval_kernel(pieces, *refs):
+    weight_refs, (normed_ref, ids_ref, kv_ref, tail_ref, weights) = refs[:pieces], refs[pieces:]
+    fill_weights(lax.axis_index("ctx"), weight_refs, weights)
+    keyvals = dot(normed_ref[...], weights[...]).astype(jnp.bfloat16)
+    kv_ref[...] = keyvals
+    past = tail_ref.shape[0] - ids_ref.shape[0]
+    tail_ref[:past] = keyvals[keyvals.shape[0] - past :]
+    tail_ref[past:] = ids_ref[...]
 
 
 def out_copies(own, local_ref, piece_refs, whole, sems):
-    half = piece_refs[1].shape[0]
-    pieces = []
-    for flip in (0, 1):
-        three, one = piece_refs[2 * flip : 2 * flip + 2]
-        pieces += [(three, 0, flip, 0), (three, 1, flip, 1)]
-        pieces += [(three, 2, flip ^ 2, 0), (one, 0, flip ^ 2, 1)]
+    first_ref, second_ref, across_ref = piece_refs
+    rows, wide = first_ref.shape[0] // 6, first_ref.shape[1]
+    columns = pl.ds(pl.multiple_of(lax.rem(own, 2) * wide, wide), wide)
+    upper = own // 2
     from_own, from_pieces = [], []
-    for i, (ref, part, o, second) in enumerate(pieces):
-        at = pl.ds(i * half, half)
-        from_own.append(pltpu.make_async_copy(local_ref.at[at], whole.at[at], sems.at[i]))
-        place = pl.ds(pl.multiple_of(((own ^ o) * 2 + second) * half, half), half)
-        source = ref.at[pl.ds(part * half, half)]
-        from_pieces.append(pltpu.make_async_copy(source, whole.at[place], sems.at[i]))
+    for i, (ref, first, place, count) in enumerate((
+        (first_ref, 0, upper * 8 + 2, 6), (second_ref, 0, upper * 8, 2),
+        (second_ref, 2, (1 - upper) * 8, 2), (across_ref, 0, (1 - upper) * 8 + 2, 6),
+    )):
+        at = pl.ds(pl.multiple_of(place * rows, rows), count * rows)
+        source = ref.at[pl.ds(first * rows, count * rows)]
+        from_own.append(
+            pltpu.make_async_copy(local_ref.at[at, columns], whole.at[at], sems.at[i])
+        )
+        from_pieces.append(pltpu.make_async_copy(source, whole.at[at], sems.at[i]))
     return from_own, from_pieces
 
 
-def second_kernel(pieces, *refs):
+def stream_kernel(*refs):
     x_refs, b_refs = refs[:PLANE], refs[PLANE : 3 * PLANE]
-    weight_refs, refs = refs[3 * PLANE : 3 * PLANE + pieces], refs[3 * PLANE + pieces :]
-    wq_ref, wo_ref, piece_refs, refs = refs[0], refs[1], refs[2:6], refs[6:]
-    own_ref, mine_ref, other_ref, kv_ref, tail_ref = refs[:5]
-    stream, blended, normed, weights, whole, sems = refs[5:]
-    ctx = lax.axis_index("ctx")
+    wo_ref, piece_refs = refs[3 * PLANE], refs[3 * PLANE + 1 : 3 * PLANE + 4]
+    half_ref, blended, whole, sems = refs[3 * PLANE + 4 :]
     side = lax.rem(lax.axis_index("phase"), 2)
-    rows = x_refs[0].shape[0]
-    own = lax.rem(ctx, PLANE)
+    own = lax.rem(lax.axis_index("ctx"), PLANE)
     from_own, from_pieces = out_copies(own, wo_ref, piece_refs, whole, sems)
 
     @pl.when(side == 0)
@@ -216,21 +230,33 @@
         for copy in from_pieces:
             copy.start()
 
-    fill_weights(ctx, weight_refs, weights)
-    part = b_refs[0].shape[1]
+    rows, part, wide = x_refs[0].shape[0], b_refs[0].shape[1], half_ref.shape[1]
+    columns = pl.ds(pl.multiple_of(lax.rem(own, 2) * wide, wide), wide)
     for r, o in enumerate(ORDER):
-        stream[pl.ds(pl.multiple_of((own ^ o) * rows, rows), rows), :] = x_refs[r][:, : stream.shape[1]]
+        at = pl.ds(pl.multiple_of((own ^ o) * rows, rows), rows)
+        half_ref[at, :] = x_refs[r][:, columns]
     for m, ref in enumerate(b_refs):
         place = (side * PLANE + own) ^ m
         blended[:, pl.ds(pl.multiple_of(place * part, part), part)] = ref[...]
     for copy in from_own:
         copy.wait()
-    width = stream.shape[1]
-    step = min(512, width)
-    for n in range(0, width, step):
+    step = min(512, wide)
+    for n in range(0, wide, step):
         total = dot(blended[...], whole[:, n : n + step])
-        total = total + stream[:, n : n + step].astype(jnp.float32)
-        stream[:, n : n + step] = total.astype(jnp.bfloat16)
+        total = total + half_ref[:, n : n + step].astype(jnp.float32)
+        half_ref[:, n : n + step] = total.astype(jnp.bfloat16)
+
+
+def second_kernel(pieces, *refs):
+    mine_half, other_half, refs = refs[0], refs[1], refs[2:]
+    weight_refs, refs = refs[:pieces], refs[pieces:]
+    wq_ref, own_ref, mine_ref, other_ref, kv_ref, tail_ref, stream, normed, weights = refs
+    ctx = lax.axis_index("ctx")
+    own, core = lax.rem(ctx, PLANE), lax.rem(ctx, 2)
+    rows, wide = own_ref.shape[0], mine_half.shape[1]
+    fill_weights(ctx, weight_refs, weights)
+    for flip, ref in enumerate((mine_half, other_half)):
+        stream[:, pl.ds(pl.multiple_of((core ^ flip) * wide, wide), wide)] = ref[...]
     normed[...] = rms_rows(stream[...])
     own_ref[...] = stream[pl.ds(pl.multiple_of(own * rows, rows), rows), :]
     keyvals = dot(normed[...], weights[...]).astype(jnp.bfloat16)
@@ -321,9 +347,16 @@
     return lax.optimization_barrier((value,) + others)[0]
 
 
-def along_planes(piece):
-    count = lax.axis_size("ctx") // PLANE
-    return [piece] + [swap(piece, 0, PLANE * m) for m in range(1, count)]
+def token_of(*blocks, cost):
+    places = {i: pl.ANY for i in range(len(blocks))}
+    return call(token_kernel, [((8, HEAD), jnp.float32)], [], cost, *blocks, far=places)[0]
+
+
+def along_planes(piece, gate=()):
+    held = {0: piece, 2: swap(after(piece, *gate), 0, PLANE * 2)}
+    for m in range(4, lax.axis_size("ctx") // PLANE):
+        held[m] = swap(after(piece, *gate), 0, PLANE * m)
+    return held
 
 
 def local(inputs, segment_ids, w_query, w_keyval, w_out):
@@ -339,26 +372,35 @@
     depth = w_keyval.shape[1]
     tall, past = PLANE * rows, (WINDOW - 1) * rows
 
-    half = head_width // PLANE // 2
-    sent_out, query_mat = call(
-        slice_kernel, [((3 * half, width), bf16), ((width, 2 * part), bf16)],
-        [pltpu.SemaphoreType.DMA((4,))], LONG, w_out[0], w_query[0], far=(0, 1),
+    unit, half = head_width // 16, width // 2
+    sent_first, sent_second, query_mat = call(
+        slice_kernel,
+        [((6 * unit, half), bf16), ((4 * unit, half), bf16), ((width, 2 * part), bf16)],
+        [pltpu.SemaphoreType.DMA((5,))], LONG, w_out[0], w_query[0], far={0: pltpu.HBM, 1: pltpu.HBM},
     )
 
     kept, for_y, for_x, for_both = call(
         cut_kernel, [((depth, 4 * part), bf16)] * 4, [], 0, w_keyval[0]
     )
     across_both, across_x, across_y = swap(for_both, 1, 2), swap(for_x, 1, 0), swap(for_y, 0, 2)
-    kept, sent_out, query_mat = lax.optimization_barrier((kept, sent_out, query_mat))
+    kept, sent_first, sent_second, query_mat = lax.optimization_barrier(
+        (kept, sent_first, sent_second, query_mat)
+    )
     near, far = call(
         sort_kernel, [((2, 2 * depth, 2 * part), bf16)] * 2, [], 0,
         kept, across_y, across_x, across_both,
     )
+    piece = (4 * depth, 2 * part)
     early, late_start = call(
-        merge_kernel, [((4 * depth, 2 * part), bf16)] * 2, [], 0, near, swap(far, 0, 1)
-    )
-    got_out = swap(after(sent_out, near), 1, 0)
+        merge_kernel, [(piece, bf16)] * 2, [], 0, near, swap(far, 0, 1)
+    )
+    out_first, out_second = (swap(after(b, across_y), 1, 0) for b in (sent_first, sent_second))
+    sent_on = call(copy_kernel, [((6 * unit, half), bf16)], [], 4 * 10**9, out_first)[0]
+    out_across = swap(sent_on, 0, 2)
     early = along_planes(early)
+    early[1] = swap(early[0], 0, PLANE)
+    ready = token_of(token_of(early[2], cost=7 * 10**8), early[1], cost=24 * 10**8)
+    early[3] = swap(after(early[2], ready), 0, PLANE)
     pieces = len(early)
 
     keyval_out = [((tall, 2 * part), bf16), ((past, 2 * part), bf16)]
@@ -371,41 +413,42 @@
     def two_layers(x, ids, bias):
         x = call(extend_kernel, [((rows, width + HEAD), bf16)], [], 0, x, ids)[0]
         across = swap(after(x, early[0]), 0, 2)
-        xs = [x, across] + [swap(after(b, *early), 0, 1) for b in (x, across)]
-        xs[0], got = lax.optimization_barrier((x, got_out))
-        got_across = swap(got[half : 2 * half], 0, 2)
-        late = {m: swap(after(late_start, early[3]), 0, PLANE * m) for m in (2, 1)}
-        late[0] = late_start
-        mine, other, kv, tail = call(
-            functools.partial(first_kernel, pieces), query_out + first_out,
-            [((tall, width), bf16), weights], LONG, *xs, *early, query_mat,
+        xs = [x, across] + [swap(after(b, ready), 0, 1) for b in (x, across)]
+        normed, mine, other, ids = call(
+            query_kernel, [((tall, width), bf16)] + query_out + [((16, 2 * part), bf16)], [], 0,
+            *xs, query_mat,
         )
+        kv, tail = call(
+            functools.partial(keyval_kernel, pieces), first_out, [weights], LONG,
+            *(early[m] for m in range(pieces)), normed, ids,
+        )
+        query = swap(other, 1, 0)
+        late = along_planes(late_start, (kv,))
+        late[1] = swap(after(late_start, kv), 0, PLANE)
         past_kv = from_plane_behind(tail)
         if bias is None:
             shape = ((PLANE, rows, WINDOW * rows), jnp.float32)
-            bias = call(mask_kernel, [shape], [], 0, *xs, past_kv)[0]
-        bias, late[1], late[2], got_across = lax.optimization_barrier(
-            (bias, late[1], late[2], got_across)
-        )
+            bias = call(mask_kernel, [shape], [], 6 * 10**8, *xs, after(past_kv, query))[0]
+        bias, *out = lax.optimization_barrier((bias, out_first, out_second, out_across))
         blended = call(
             functools.partial(attend_kernel, 0), [((tall, part), bf16)],
-            [((2 * tall, 2 * part), bf16)], 0, mine, swap(other, 1, 0), bias, kv, past_kv,
+            [((2 * tall, 2 * part), bf16)], 0, mine, query, bias, kv, past_kv,
         )[0]
-        for m in range(4, pieces):
-            late[m] = swap(after(late_start, kv), 0, PLANE * m)
         near = [blended, swap(blended, 0, 2), swap(blended, 1, 0), swap(blended, 1, 2)]
         heads = [b for n in near for b in (n, swap(n, 0, 1))]
-        late[3] = swap(after(late[2], blended), 0, PLANE)
-        out = [got, got_across]
-        out += [swap(after(b, blended), 0, 1) for b in out]
+        late[3] = swap(after(late[2], late[1], near[2], near[3]), 0, PLANE)
+        half = call(
+            stream_kernel, [((tall, width // 2), bf16)],
+            [((tall, head_width), bf16), ((head_width, width // 2), bf16),
+             pltpu.SemaphoreType.DMA((4,))],
+            0, *xs, *heads, w_out[0], *out,
+            far={3 * PLANE + i: pltpu.HBM for i in range(4)},
+        )[0]
         stream, mine, other, kv, tail = call(
             functools.partial(second_kernel, pieces),
             [((rows, width), bf16)] + query_out + keyval_out,
-            [((tall, width), bf16), ((tall, head_width), bf16), ((tall, width), bf16), weights,
-             ((head_width, width), bf16), pltpu.SemaphoreType.DMA((2 * PLANE,))],
-            2 * dot_flops + 2 * tall * head_width * width,
-            *xs, *heads, *(late[m] for m in range(pieces)), query_mat, w_out[0], *out,
-            far=range(3 * PLANE + pieces + 1, 3 * PLANE + pieces + 6),
+            [((tall, width), bf16), ((tall, width), bf16), weights], 0,
+            half, swap(after(half, late[3]), 0, 1), *(late[m] for m in range(pieces)), query_mat,
         )
         mine, other = call(
             functools.partial(attend_kernel, 1), [((tall // 2, part), bf16)] * 2,

time: 100 us -> 94.5 us (0.945)
  starting transfers between devices: 32.1 us -> 29.9 us
  waiting for transfers between devices: 48.4 us -> 46.3 us
    ppermute x33, waiting for transfers between devices: 44.1 us -> 40.2 us  [swap(): return lax.ppermute(block, BOTH, route)]
    ppermute x33, starting transfers between devices: 25.3 us -> 21.6 us  [swap(): return lax.ppermute(block, BOTH, route)]
    ppermute x2, waiting for transfers between devices: 4.26 us -> 6.1 us  [from_plane_behind(): lax.ppermute(block, 'ctx', [(i, i + PLANE) for i in range(wide - PLANE)])]
    ppermute x2, starting transfers between devices: 6.86 us -> 8.26 us  [from_plane_behind(): lax.ppermute(block, 'ctx', [(i, i + PLANE) for i in range(wide - PLANE)])]
    pallas_call x11 -> x14, Pallas kernels: 12.1 us -> 11.4 us  [call(): pl.pallas_call(kernel, out_shape=[jax.ShapeDtypeStruct(s, d) for s, d in...]
  transfers between devices with their start and end apart: 35 -> 35, of which waited for: 19 -> 22; matrix products, arithmetic and copies ran while one was open for 0% -> 0% of each run, Pallas kernels for 3% -> 7%
where the time goes in v3:
time: 94.5 us; the launch traced here: 93.2 us
  waiting for transfers between devices  46.3 us (49%)
  starting transfers between devices  29.9 us (32%)
  Pallas kernels  11.4 us (12%)
  local copies, waits for them, and re-layouts  5.43 us (6%)
    ppermute x33, waiting for transfers between devices, swap(): return lax.ppermute(block, BOTH, route)  40.2 us
    ppermute x33, starting transfers between devices, swap(): return lax.ppermute(block, BOTH, route)  21.6 us
    pallas_call x14, Pallas kernels, call(): pl.pallas_call(kernel, out_shape=[jax.ShapeDtypeStruct(s, d) for s, d in...  11.4 us
    ppermute x2, starting transfers between devices, from_plane_behind(): lax.ppermute(block, 'ctx', [(i, i + PLANE) for i in range(wide - PLANE)])  8.26 us
    ppermute x2, waiting for transfers between devices, from_plane_behind(): lax.ppermute(block, 'ctx', [(i, i + PLANE) for i in range(wide - PLANE)])  6.1 us
    unnamed x12, local copies, waits for them, and re-layouts  5.43 us
  transfers between devices with their start and end apart: 35, of which 22 were waited for; matrix products, arithmetic and copies ran while one was open for 0% of the time, Pallas kernels for 7%

profile of v3, /device:TPU:14, one launch (start us, length us, event | category | flops | bytes accessed | tf_op | source)
XLA Modules:
  0.0 93.2 jit_solution(14562619044537105784)
XLA Ops:
  0.0 1.0 %copy-done.2 = bf16[1,128,2048]{2,1,0:T(8,128)(2,1)S(1)} copy-done((bf16[1,128,2048]{2,1,0:T(8,128)(2,1)S(1)}, bf16[1,128,2048]{2,1,0:T(8,128)(2,1)}, u32[]{:S(2)}) %copy-start.2) | copy-done | bytes 524312
  1.0 0.1 shard_map.56
  1.1 0.6 collective-permute-start
  1.7 0.5 collective-permute-start.1
  2.2 2.4 %collective-permute-start.2 = (bf16[128,512]{1,0:T(8,128)(2,1)S(1)}, bf16[128,512]{1,0:T(8,128)(2,1)S(1)}, u32[]{:S(2)}, u32[]{:S(2)}) collective-permute-start(bf16[128,512]{1,0:T(8,128)(2,1)S(1)} %get-tuple-element.54), channel_id=1, source_target_pairs={{0,18},{1,19},{2,16},{3,17},{4,22},{5,23},{6,20},{7,21},{8,26},{9,... | collective-permute-start | bytes 393224 | tf_op jit(solution)/shard_map/ppermute | solution.py:27
  4.7 2.2 %copy-done = bf16[1,1024,2048]{2,1,0:T(8,128)(2,1)S(1)} copy-done((bf16[1,1024,2048]{2,1,0:T(8,128)(2,1)S(1)}, bf16[1,1024,2048]{2,1,0:T(8,128)(2,1)}, u32[]{:S(2)}) %copy-start) | copy-done | bytes 4194328
  6.9 2.2 %copy-done.5 = bf16[1,2048,1024]{2,1,0:T(8,128)(2,1)S(1)} copy-done((bf16[1,2048,1024]{2,1,0:T(8,128)(2,1)S(1)}, bf16[1,2048,1024]{2,1,0:T(8,128)(2,1)}, u32[]{:S(2)}) %copy-start.5) | copy-done | bytes 4194328
  9.1 0.4 shard_map.57
  9.5 0.9 collective-permute-done.2.across_both
  10.4 0.1 shard_map.58
  10.5 0.1 collective-permute-start.3
  10.6 0.6 collective-permute-start.12
  11.2 0.2 shard_map.55.refs_0_
  11.4 0.7 collective-permute-done.3.far_ref
  12.2 0.6 collective-permute-start.4
  12.7 2.6 %collective-permute-start.5 = (bf16[512,256]{1,0:T(8,128)(2,1)S(1)}, bf16[512,256]{1,0:T(8,128)(2,1)S(1)}, u32[]{:S(2)}, u32[]{:S(2)}) collective-permute-start(bf16[512,256]{1,0:T(8,128)(2,1)S(1)} %get-tuple-element.57.refs_0_), channel_id=1, source_target_pairs={{0,8},{1,9},{2,10},{3,11},{4,12},{5,13},{6,14},{7,15},{8,0},{9,1},... | collective-permute-start | bytes 786440 | tf_op jit(solution)/shard_map/ppermute | solution.py:27
  15.3 0.4 collective-permute-start.6
  15.8 10.6 %collective-permute-done.5.refs_2_ = bf16[512,256]{1,0:T(8,128)(2,1)S(1)} collective-permute-done((bf16[512,256]{1,0:T(8,128)(2,1)S(1)}, bf16[512,256]{1,0:T(8,128)(2,1)S(1)}, u32[]{:S(2)}, u32[]{:S(2)}) %collective-permute-start.5) | collective-permute-done | bytes 262176 | tf_op jit(solution)/shard_map/ppermute | solution.py:27
  26.4 1.1 %collective-permute-done.6.refs_1_ = bf16[512,256]{1,0:T(8,128)(2,1)S(1)} collective-permute-done((bf16[512,256]{1,0:T(8,128)(2,1)S(1)}, bf16[512,256]{1,0:T(8,128)(2,1)S(1)}, u32[]{:S(2)}, u32[]{:S(2)}) %collective-permute-start.6) | collective-permute-done | bytes 262176 | tf_op jit(solution)/shard_map/ppermute | solution.py:27
  27.5 0.5 collective-permute-start.8
  28.0 0.8 collective-permute-start.13
  28.8 0.6 collective-permute-start.10
  29.4 1.2 %collective-permute-done.12.block_ref.refs_13_ = bf16[384,1024]{1,0:T(8,128)(2,1)S(1)} collective-permute-done((bf16[384,1024]{1,0:T(8,128)(2,1)S(1)}, bf16[384,1024]{1,0:T(8,128)(2,1)S(1)}, u32[]{:S(2)}, u32[]{:S(2)}) %collective-permute-start.12) | collective-permute-done | bytes 786464 | tf_op jit(solution)/shard_map/ppermute | solution.py:27
  30.6 0.1 shard_map.63
  30.6 0.6 collective-permute-start.14
  31.2 1.4 %shard_map.60 = (bf16[512,2048]{1,0:T(8,128)(2,1)S(1)}, bf16[512,128]{1,0:T(8,128)(2,1)S(1)}, bf16[512,128]{1,0:T(8,128)(2,1)S(1)}, bf16[16,256]{1,0:T(8,128)(2,1)S(1)}) custom-call(bf16[128,2176]{1,0:T(8,128)(2,1)S(1)} %shard_map.55.refs_0_, bf16[128,2176]{1,0:T(8,128)(2,1)S(1)} %collective-permute-done.4.refs_1_, ...), custom_call_target="tpu_custom_call" | custom-call | bytes 3276800 | tf_op jit(solution)/shard_map/pallas_call | solution.py:48
  32.6 1.1 %collective-permute-start.9 = (bf16[512,128]{1,0:T(8,128)(2,1)S(1)}, bf16[512,128]{1,0:T(8,128)(2,1)S(1)}, u32[]{:S(2)}, u32[]{:S(2)}) collective-permute-start(bf16[512,128]{1,0:T(8,128)(2,1)S(1)} %get-tuple-element.63), channel_id=1, source_target_pairs={{0,16},{1,17},{2,18},{3,19},{4,20},{5,21},{6,22},{7,23},{8,24},{9,... | collective-permute-start | bytes 393224 | tf_op jit(solution)/shard_map/ppermute | solution.py:27
  33.8 3.0 %collective-permute-done.10.refs_3_ = bf16[512,256]{1,0:T(8,128)(2,1)S(1)} collective-permute-done((bf16[512,256]{1,0:T(8,128)(2,1)S(1)}, bf16[512,256]{1,0:T(8,128)(2,1)S(1)}, u32[]{:S(2)}, u32[]{:S(2)}) %collective-permute-start.10) | collective-permute-done | bytes 262176 | tf_op jit(solution)/shard_map/ppermute | solution.py:27
  36.7 0.8 shard_map.61
  37.5 0.0 copy-start.1
  37.5 3.4 %collective-permute-start.11 = (bf16[400,256]{1,0:T(8,128)(2,1)S(1)}, bf16[400,256]{1,0:T(8,128)(2,1)S(1)}, u32[]{:S(2)}, u32[]{:S(2)}) collective-permute-start(bf16[400,256]{1,0:T(8,128)(2,1)S(1)} %get-tuple-element.67), channel_id=1, source_target_pairs={{0,4},{1,5},{2,6},{3,7},{4,8},{5,9},{6,10},{7,11},{8,12},{9,13},{1... | collective-permute-start | bytes 614408 | tf_op jit(solution)/shard_map/ppermute | solution.py:32
  40.9 0.6 collective-permute-start.22
  41.5 3.1 %collective-permute-done.9.got_ref = bf16[512,128]{1,0:T(8,128)(2,1)S(1)} collective-permute-done((bf16[512,128]{1,0:T(8,128)(2,1)S(1)}, bf16[512,128]{1,0:T(8,128)(2,1)S(1)}, u32[]{:S(2)}, u32[]{:S(2)}) %collective-permute-start.9) | collective-permute-done | bytes 131104 | tf_op jit(solution)/shard_map/ppermute | solution.py:27
  44.6 0.6 collective-permute-start.23
  45.2 6.1 %collective-permute-done.11.refs_4_.past_ref = bf16[400,256]{1,0:T(8,128)(2,1)S(1)} collective-permute-done((bf16[400,256]{1,0:T(8,128)(2,1)S(1)}, bf16[400,256]{1,0:T(8,128)(2,1)S(1)}, u32[]{:S(2)}, u32[]{:S(2)}) %collective-permute-start.11) | collective-permute-done | bytes 204832 | tf_op jit(solution)/shard_map/ppermute | solution.py:32
  51.3 0.2 shard_map.62.bias_ref
  51.6 1.2 %shard_map.64.refs_4_ = bf16[512,128]{1,0:T(8,128)(2,1)S(1)} custom-call(bf16[512,128]{1,0:T(8,128)(2,1)S(1)} %get-tuple-element.62.mine_ref, bf16[512,128]{1,0:T(8,128)(2,1)S(1)} %collective-permute-done.9.got_ref, f32[4,128,512]{2,1,0:T(8,128)S(1)} %shard_map.62.bias_ref, bf16[512,256]{1,0:T(8,128)(2,1)S(1)} %get-tuple-element.74.kv_ref, ...), custom_call_target="tpu_custom_call" | custom-call | bytes 1777664 | tf_op jit(solution)/shard_map/pallas_call | solution.py:48
  52.8 1.3 %collective-permute-start.18 = (bf16[512,128]{1,0:T(8,128)(2,1)S(1)}, bf16[512,128]{1,0:T(8,128)(2,1)S(1)}, u32[]{:S(2)}, u32[]{:S(2)}) collective-permute-start(bf16[512,128]{1,0:T(8,128)(2,1)S(1)} %shard_map.64.refs_4_), channel_id=1, source_target_pairs={{0,16},{1,17},{2,18},{3,19},{4,20},{5,21},{6,22},{7,23},{8,24},{9,... | collective-permute-start | bytes 393224 | tf_op jit(solution)/shard_map/ppermute | solution.py:27
  54.1 1.7 %collective-permute-start.20 = (bf16[512,128]{1,0:T(8,128)(2,1)S(1)}, bf16[512,128]{1,0:T(8,128)(2,1)S(1)}, u32[]{:S(2)}, u32[]{:S(2)}) collective-permute-start(bf16[512,128]{1,0:T(8,128)(2,1)S(1)} %shard_map.64.refs_4_), channel_id=1, source_target_pairs={{0,18},{1,19},{2,16},{3,17},{4,22},{5,23},{6,20},{7,21},{8,26},{9,... | collective-permute-start | bytes 393224 | tf_op jit(solution)/shard_map/ppermute | solution.py:27
  55.9 0.5 collective-permute-start.16
  56.4 0.4 collective-permute-done.23.refs_3_
  56.8 1.1 %collective-permute-done.18.refs_8_ = bf16[512,128]{1,0:T(8,128)(2,1)S(1)} collective-permute-done((bf16[512,128]{1,0:T(8,128)(2,1)S(1)}, bf16[512,128]{1,0:T(8,128)(2,1)S(1)}, u32[]{:S(2)}, u32[]{:S(2)}) %collective-permute-start.18) | collective-permute-done | bytes 131104 | tf_op jit(solution)/shard_map/ppermute | solution.py:27
  57.9 2.4 %collective-permute-done.20.refs_10_ = bf16[512,128]{1,0:T(8,128)(2,1)S(1)} collective-permute-done((bf16[512,128]{1,0:T(8,128)(2,1)S(1)}, bf16[512,128]{1,0:T(8,128)(2,1)S(1)}, u32[]{:S(2)}, u32[]{:S(2)}) %collective-permute-start.20) | collective-permute-done | bytes 131104 | tf_op jit(solution)/shard_map/ppermute | solution.py:27
  60.3 1.3 %collective-permute-done.16.refs_6_ = bf16[512,128]{1,0:T(8,128)(2,1)S(1)} collective-permute-done((bf16[512,128]{1,0:T(8,128)(2,1)S(1)}, bf16[512,128]{1,0:T(8,128)(2,1)S(1)}, u32[]{:S(2)}, u32[]{:S(2)}) %collective-permute-start.16) | collective-permute-done | bytes 131104 | tf_op jit(solution)/shard_map/ppermute | solution.py:27
  61.6 0.5 collective-permute-start.19
  62.1 0.8 collective-permute-done.17.refs_7_
  63.0 0.2 collective-permute-done.19.refs_9_
  63.1 0.3 collective-permute-done.21.refs_11_
  63.5 1.8 %shard_map.65.refs_0_ = bf16[512,1024]{1,0:T(8,128)(2,1)S(1)} custom-call(bf16[128,2176]{1,0:T(8,128)(2,1)S(1)} %shard_map.55.refs_0_, bf16[128,2176]{1,0:T(8,128)(2,1)S(1)} %collective-permute-done.4.refs_1_, bf16[128,2176]{1,0:T(8,128)(2,1)S(1)} %collective-permute-done.7.refs_2_, bf16[128,2176]{1,0:T(8,128)(2,1)S(1)} %collective-permute-done.8.refs_3_, ...), custom_call_target="tpu_custom_call" | custom-call | bytes 9568256 | tf_op jit(solution)/shard_map/pallas_call | solution.py:48
  65.3 1.4 %collective-permute-done.24.refs_5_ = bf16[512,256]{1,0:T(8,128)(2,1)S(1)} collective-permute-done((bf16[512,256]{1,0:T(8,128)(2,1)S(1)}, bf16[512,256]{1,0:T(8,128)(2,1)S(1)}, u32[]{:S(2)}, u32[]{:S(2)}) %collective-permute-start.24) | collective-permute-done | bytes 262176 | tf_op jit(solution)/shard_map/ppermute | solution.py:27
  66.7 2.7 %collective-permute-done.25.refs_1_ = bf16[512,1024]{1,0:T(8,128)(2,1)S(1)} collective-permute-done((bf16[512,1024]{1,0:T(8,128)(2,1)S(1)}, bf16[512,1024]{1,0:T(8,128)(2,1)S(1)}, u32[]{:S(2)}, u32[]{:S(2)}) %collective-permute-start.25) | collective-permute-done | bytes 1048608 | tf_op jit(solution)/shard_map/ppermute | solution.py:27
  69.3 1.9 %shard_map.66 = (bf16[128,2048]{1,0:T(8,128)(2,1)S(1)}, bf16[512,128]{1,0:T(8,128)(2,1)S(1)}, bf16[512,128]{1,0:T(8,128)(2,1)S(1)}, bf16[512,256]{1,0:T(8,128)(2,1)S(1)}, bf16[384,256]{1,0:T(8,128)(2,1)S(1)}) custom-call(bf16[512,1024]{1,0:T(8,128)(2,1)S(1)} %shard_map.65.refs_0_, bf16[512,1024]{1,0:T(8,128)(2,1)S(1)} %collective-permute-done.25.refs_1_, ...), custom_call_target="tpu_custom_call" | custom-call | bytes 4194304 | tf_op jit(solution)/shard_map/pallas_call | solution.py:48
  71.2 4.9 %collective-permute-start.27 = (bf16[384,256]{1,0:T(8,128)(2,1)S(1)}, bf16[384,256]{1,0:T(8,128)(2,1)S(1)}, u32[]{:S(2)}, u32[]{:S(2)}) collective-permute-start(bf16[384,256]{1,0:T(8,128)(2,1)S(1)} %get-tuple-element.85), channel_id=1, source_target_pairs={{0,4},{1,5},{2,6},{3,7},{4,8},{5,9},{6,10},{7,11},{8,12},{9,13},{1... | collective-permute-start | bytes 589832 | tf_op jit(solution)/shard_map/ppermute | solution.py:32
  76.1 1.3 %collective-permute-start.26 = (bf16[512,128]{1,0:T(8,128)(2,1)S(1)}, bf16[512,128]{1,0:T(8,128)(2,1)S(1)}, u32[]{:S(2)}, u32[]{:S(2)}) collective-permute-start(bf16[512,128]{1,0:T(8,128)(2,1)S(1)} %get-tuple-element.83), channel_id=1, source_target_pairs={{0,16},{1,17},{2,18},{3,19},{4,20},{5,21},{6,22},{7,23},{8,24},{9,... | collective-permute-start | bytes 393224 | tf_op jit(solution)/shard_map/ppermute | solution.py:27
  77.4 4.0 %collective-permute-done.26.got_ref = bf16[512,128]{1,0:T(8,128)(2,1)S(1)} collective-permute-done((bf16[512,128]{1,0:T(8,128)(2,1)S(1)}, bf16[512,128]{1,0:T(8,128)(2,1)S(1)}, u32[]{:S(2)}, u32[]{:S(2)}) %collective-permute-start.26) | collective-permute-done | bytes 131104 | tf_op jit(solution)/shard_map/ppermute | solution.py:27
  81.4 1.7 %shard_map.67 = (bf16[256,128]{1,0:T(8,128)(2,1)S(1)}, bf16[256,128]{1,0:T(8,128)(2,1)S(1)}) custom-call(bf16[512,128]{1,0:T(8,128)(2,1)S(1)} %get-tuple-element.82.mine_ref, bf16[512,128]{1,0:T(8,128)(2,1)S(1)} %collective-permute-done.26.got_ref, f32[4,128,512]{2,1,0:T(8,128)S(1)} %shard_map.62.bias_ref, bf16[512,256]{1,0:T(8,128)(2,1)S(1)} %get-tuple-element.84.kv_ref, ...), custom_call_target="tpu_custom_call" | custom-call | flops 134217728 | bytes 1769472 | tf_op jit(solution)/shard_map/pallas_call | solution.py:48
  83.1 1.4 %collective-permute-start.29 = (bf16[256,128]{1,0:T(8,128)(2,1)S(1)}, bf16[256,128]{1,0:T(8,128)(2,1)S(1)}, u32[]{:S(2)}, u32[]{:S(2)}) collective-permute-start(bf16[256,128]{1,0:T(8,128)(2,1)S(1)} %get-tuple-element.87), channel_id=1, source_target_pairs={{0,2},{1,3},{2,0},{3,1},{4,6},{5,7},{6,4},{7,5},{8,10},{9,11},{10,... | collective-permute-start | bytes 196616 | tf_op jit(solution)/shard_map/ppermute | solution.py:27
  84.5 0.8 collective-permute-start.31
  85.3 1.4 %collective-permute-start.33 = (bf16[256,128]{1,0:T(8,128)(2,1)S(1)}, bf16[256,128]{1,0:T(8,128)(2,1)S(1)}, u32[]{:S(2)}, u32[]{:S(2)}) collective-permute-start(bf16[256,128]{1,0:T(8,128)(2,1)S(1)} %get-tuple-element.87), channel_id=1, source_target_pairs={{0,18},{1,19},{2,16},{3,17},{4,22},{5,23},{6,20},{7,21},{8,26},{9,... | collective-permute-start | bytes 196616 | tf_op jit(solution)/shard_map/ppermute | solution.py:27
  86.6 1.5 %collective-permute-done.29.refs_2_ = bf16[256,128]{1,0:T(8,128)(2,1)S(1)} collective-permute-done((bf16[256,128]{1,0:T(8,128)(2,1)S(1)}, bf16[256,128]{1,0:T(8,128)(2,1)S(1)}, u32[]{:S(2)}, u32[]{:S(2)}) %collective-permute-start.29) | collective-permute-done | bytes 65568 | tf_op jit(solution)/shard_map/ppermute | solution.py:27
  88.1 0.6 collective-permute-done.31.refs_4_
  88.7 1.7 %collective-permute-done.33.refs_6_ = bf16[256,128]{1,0:T(8,128)(2,1)S(1)} collective-permute-done((bf16[256,128]{1,0:T(8,128)(2,1)S(1)}, bf16[256,128]{1,0:T(8,128)(2,1)S(1)}, u32[]{:S(2)}, u32[]{:S(2)}) %collective-permute-start.33) | collective-permute-done | bytes 65568 | tf_op jit(solution)/shard_map/ppermute | solution.py:27
  90.4 1.2 %collective-permute-done.34.refs_7_ = bf16[256,128]{1,0:T(8,128)(2,1)S(1)} collective-permute-done((bf16[256,128]{1,0:T(8,128)(2,1)S(1)}, bf16[256,128]{1,0:T(8,128)(2,1)S(1)}, u32[]{:S(2)}, u32[]{:S(2)}) %collective-permute-start.34) | collective-permute-done | bytes 65568 | tf_op jit(solution)/shard_map/ppermute | solution.py:27
  91.7 1.6 %shard_map.68 = bf16[128,2048]{1,0:T(8,128)(2,1)} custom-call(bf16[256,128]{1,0:T(8,128)(2,1)S(1)} %get-tuple-element.86.refs_0_, bf16[256,128]{1,0:T(8,128)(2,1)S(1)} %collective-permute-done.28.refs_1_, bf16[256,128]{1,0:T(8,128)(2,1)S(1)} %collective-permute-done.29.refs_2_, bf16[256,128]{1,0:T(8,128)(2,1)S(1)} %collective-permute-done.30.refs_3_, ...), custom_call_target="tpu_custom_call" | custom-call | flops 536870912 | bytes 5242880 | tf_op jit(solution)/shard_map/pallas_call | solution.py:48
  (32 shorter events, 0.1 us)
Async XLA Ops:
  0.0 1.0 %copy-start.2 = (bf16[1,128,2048]{2,1,0:T(8,128)(2,1)S(1)}, bf16[1,128,2048]{2,1,0:T(8,128)(2,1)}, u32[]{:S(2)}) copy-start(bf16[1,128,2048]{2,1,0:T(8,128)(2,1)} %param.8) | copy-start | bytes 1572868
  1.1 8.4 %collective-permute-start = (bf16[128,512]{1,0:T(8,128)(2,1)S(1)}, bf16[128,512]{1,0:T(8,128)(2,1)S(1)}, u32[]{:S(2)}, u32[]{:S(2)}) collective-permute-start(bf16[128,512]{1,0:T(8,128)(2,1)S(1)} %get-tuple-element.52), channel_id=1, source_target_pairs={{0,2},{1,3},{2,0},{3,1},{4,6},{5,7},{6,4},{7,5},{8,10},{9,11},{10,... | collective-permute-start | bytes 393224 | tf_op jit(solution)/shard_map/ppermute | solution.py:27
  1.7 7.8 %collective-permute-start.1 = (bf16[128,512]{1,0:T(8,128)(2,1)S(1)}, bf16[128,512]{1,0:T(8,128)(2,1)S(1)}, u32[]{:S(2)}, u32[]{:S(2)}) collective-permute-start(bf16[128,512]{1,0:T(8,128)(2,1)S(1)} %get-tuple-element.53), channel_id=1, source_target_pairs={{0,16},{1,17},{2,18},{3,19},{4,20},{5,21},{6,22},{7,23},{8,24},{9,... | collective-permute-start | bytes 393224 | tf_op jit(solution)/shard_map/ppermute | solution.py:27
  2.2 8.2 %collective-permute-start.2 = (bf16[128,512]{1,0:T(8,128)(2,1)S(1)}, bf16[128,512]{1,0:T(8,128)(2,1)S(1)}, u32[]{:S(2)}, u32[]{:S(2)}) collective-permute-start(bf16[128,512]{1,0:T(8,128)(2,1)S(1)} %get-tuple-element.54), channel_id=1, source_target_pairs={{0,18},{1,19},{2,16},{3,17},{4,22},{5,23},{6,20},{7,21},{8,26},{9,... | collective-permute-start | bytes 393224 | tf_op jit(solution)/shard_map/ppermute | solution.py:27
  4.7 2.2 %copy-start = (bf16[1,1024,2048]{2,1,0:T(8,128)(2,1)S(1)}, bf16[1,1024,2048]{2,1,0:T(8,128)(2,1)}, u32[]{:S(2)}) copy-start(bf16[1,1024,2048]{2,1,0:T(8,128)(2,1)} %param.9) | copy-start | bytes 12582916
  6.9 2.2 %copy-start.5 = (bf16[1,2048,1024]{2,1,0:T(8,128)(2,1)S(1)}, bf16[1,2048,1024]{2,1,0:T(8,128)(2,1)}, u32[]{:S(2)}) copy-start(bf16[1,2048,1024]{2,1,0:T(8,128)(2,1)} %param.7) | copy-start | bytes 12582916
  9.0 2.2 %copy-start.3 = (bf16[1,128,2048]{2,1,0:T(8,128)(2,1)S(1)}, bf16[1,128,2048]{2,1,0:T(8,128)(2,1)}, u32[]{:S(2)}) copy-start(bf16[1,128,2048]{2,1,0:T(8,128)(2,1)} %param.5) | copy-start | bytes 1572868
  9.0 2.2 %copy-start.4 = (s32[1,128]{1,0:T(1,128)S(1)}, s32[1,128]{1,0:T(1,128)}, u32[]{:S(2)}) copy-start(s32[1,128]{1,0:T(1,128)} %id_ref.1) | copy-start | bytes 1540
  10.5 1.6 %collective-permute-start.3 = (bf16[2,256,256]{2,1,0:T(8,128)(2,1)S(1)}, bf16[2,256,256]{2,1,0:T(8,128)(2,1)S(1)}, u32[]{:S(2)}, u32[]{:S(2)}) collective-permute-start(bf16[2,256,256]{2,1,0:T(8,128)(2,1)S(1)} %get-tuple-element.56), channel_id=1, source_target_pairs={{0,1},{1,0},{2,3},{3,2},{4,5},{5,4},{6,7},{7,6},{8,9},{9,8},{10,11... | collective-permute-start | bytes 786440 | tf_op jit(solution)/shard_map/ppermute | solution.py:27
  10.6 20.0 %collective-permute-start.12 = (bf16[384,1024]{1,0:T(8,128)(2,1)S(1)}, bf16[384,1024]{1,0:T(8,128)(2,1)S(1)}, u32[]{:S(2)}, u32[]{:S(2)}) collective-permute-start(bf16[384,1024]{1,0:T(8,128)(2,1)S(1)} %get-tuple-element.70), channel_id=1, source_target_pairs={{0,16},{1,17},{2,18},{3,19},{4,20},{5,21},{6,22},{7,23},{8,24},{9,... | collective-permute-start | bytes 2359304 | tf_op jit(solution)/shard_map/ppermute | solution.py:27
  12.2 15.3 %collective-permute-start.4 = (bf16[128,2176]{1,0:T(8,128)(2,1)S(1)}, bf16[128,2176]{1,0:T(8,128)(2,1)S(1)}, u32[]{:S(2)}, u32[]{:S(2)}) collective-permute-start(bf16[128,2176]{1,0:T(8,128)(2,1)S(1)} %shard_map.55.refs_0_), channel_id=1, source_target_pairs={{0,2},{1,3},{2,0},{3,1},{4,6},{5,7},{6,4},{7,5},{8,10},{9,11},{10,... | collective-permute-start | bytes 1671176 | tf_op jit(solution)/shard_map/ppermute | solution.py:27
  12.7 13.7 %collective-permute-start.5 = (bf16[512,256]{1,0:T(8,128)(2,1)S(1)}, bf16[512,256]{1,0:T(8,128)(2,1)S(1)}, u32[]{:S(2)}, u32[]{:S(2)}) collective-permute-start(bf16[512,256]{1,0:T(8,128)(2,1)S(1)} %get-tuple-element.57.refs_0_), channel_id=1, source_target_pairs={{0,8},{1,9},{2,10},{3,11},{4,12},{5,13},{6,14},{7,15},{8,0},{9,1},... | collective-permute-start | bytes 786440 | tf_op jit(solution)/shard_map/ppermute | solution.py:27
  15.3 12.2 %collective-permute-start.6 = (bf16[512,256]{1,0:T(8,128)(2,1)S(1)}, bf16[512,256]{1,0:T(8,128)(2,1)S(1)}, u32[]{:S(2)}, u32[]{:S(2)}) collective-permute-start(bf16[512,256]{1,0:T(8,128)(2,1)S(1)} %get-tuple-element.57.refs_0_), channel_id=1, source_target_pairs={{0,4},{1,5},{2,6},{3,7},{4,0},{5,1},{6,2},{7,3},{8,12},{9,13},{10,... | collective-permute-start | bytes 786440 | tf_op jit(solution)/shard_map/ppermute | solution.py:27
  27.5 3.7 %collective-permute-start.7 = (bf16[128,2176]{1,0:T(8,128)(2,1)S(1)}, bf16[128,2176]{1,0:T(8,128)(2,1)S(1)}, u32[]{:S(2)}, u32[]{:S(2)}) collective-permute-start(bf16[128,2176]{1,0:T(8,128)(2,1)S(1)} %shard_map.55.refs_0_), channel_id=1, source_target_pairs={{0,1},{1,0},{2,3},{3,2},{4,5},{5,4},{6,7},{7,6},{8,9},{9,8},{10,11... | collective-permute-start | bytes 1671176 | tf_op jit(solution)/shard_map/ppermute | solution.py:27
  27.5 3.7 %collective-permute-start.8 = (bf16[128,2176]{1,0:T(8,128)(2,1)S(1)}, bf16[128,2176]{1,0:T(8,128)(2,1)S(1)}, u32[]{:S(2)}, u32[]{:S(2)}) collective-permute-start(bf16[128,2176]{1,0:T(8,128)(2,1)S(1)} %collective-permute-done.4.refs_1_), channel_id=1, source_target_pairs={{0,1},{1,0},{2,3},{3,2},{4,5},{5,4},{6,7},{7,6},{8,9},{9,8},{10,11... | collective-permute-start | bytes 1671176 | tf_op jit(solution)/shard_map/ppermute | solution.py:27
  28.0 23.6 %collective-permute-start.13 = (bf16[256,1024]{1,0:T(8,128)(2,1)S(1)}, bf16[256,1024]{1,0:T(8,128)(2,1)S(1)}, u32[]{:S(2)}, u32[]{:S(2)}) collective-permute-start(bf16[256,1024]{1,0:T(8,128)(2,1)S(1)} %get-tuple-element.72), channel_id=1, source_target_pairs={{0,16},{1,17},{2,18},{3,19},{4,20},{5,21},{6,22},{7,23},{8,24},{9,... | collective-permute-start | bytes 1572872 | tf_op jit(solution)/shard_map/ppermute | solution.py:27
  28.8 7.9 %collective-permute-start.10 = (bf16[512,256]{1,0:T(8,128)(2,1)S(1)}, bf16[512,256]{1,0:T(8,128)(2,1)S(1)}, u32[]{:S(2)}, u32[]{:S(2)}) collective-permute-start(bf16[512,256]{1,0:T(8,128)(2,1)S(1)} %collective-permute-done.5.refs_2_), channel_id=1, source_target_pairs={{0,4},{1,5},{2,6},{3,7},{4,0},{5,1},{6,2},{7,3},{8,12},{9,13},{10,... | collective-permute-start | bytes 786440 | tf_op jit(solution)/shard_map/ppermute | solution.py:27
  30.6 21.0 %collective-permute-start.14 = (bf16[384,1024]{1,0:T(8,128)(2,1)S(1)}, bf16[384,1024]{1,0:T(8,128)(2,1)S(1)}, u32[]{:S(2)}, u32[]{:S(2)}) collective-permute-start(bf16[384,1024]{1,0:T(8,128)(2,1)S(1)} %shard_map.63), channel_id=1, source_target_pairs={{0,2},{1,3},{2,0},{3,1},{4,6},{5,7},{6,4},{7,5},{8,10},{9,11},{10,... | collective-permute-start | bytes 2359304 | tf_op jit(solution)/shard_map/ppermute | solution.py:27
  32.6 12.0 %collective-permute-start.9 = (bf16[512,128]{1,0:T(8,128)(2,1)S(1)}, bf16[512,128]{1,0:T(8,128)(2,1)S(1)}, u32[]{:S(2)}, u32[]{:S(2)}) collective-permute-start(bf16[512,128]{1,0:T(8,128)(2,1)S(1)} %get-tuple-element.63), channel_id=1, source_target_pairs={{0,16},{1,17},{2,18},{3,19},{4,20},{5,21},{6,22},{7,23},{8,24},{9,... | collective-permute-start | bytes 393224 | tf_op jit(solution)/shard_map/ppermute | solution.py:27
  37.5 26.0 %copy-start.1 = (bf16[1,1024,2048]{2,1,0:T(8,128)(2,1)S(1)}, bf16[1,1024,2048]{2,1,0:T(8,128)(2,1)}, u32[]{:S(2)}) copy-start(bf16[1,1024,2048]{2,1,0:T(8,128)(2,1)} %param.9) | copy-start | bytes 12582916
  37.5 13.8 %collective-permute-start.11 = (bf16[400,256]{1,0:T(8,128)(2,1)S(1)}, bf16[400,256]{1,0:T(8,128)(2,1)S(1)}, u32[]{:S(2)}, u32[]{:S(2)}) collective-permute-start(bf16[400,256]{1,0:T(8,128)(2,1)S(1)} %get-tuple-element.67), channel_id=1, source_target_pairs={{0,4},{1,5},{2,6},{3,7},{4,8},{5,9},{6,10},{7,11},{8,12},{9,13},{1... | collective-permute-start | bytes 614408 | tf_op jit(solution)/shard_map/ppermute | solution.py:32
  40.9 15.5 %collective-permute-start.22 = (bf16[512,256]{1,0:T(8,128)(2,1)S(1)}, bf16[512,256]{1,0:T(8,128)(2,1)S(1)}, u32[]{:S(2)}, u32[]{:S(2)}) collective-permute-start(bf16[512,256]{1,0:T(8,128)(2,1)S(1)} %get-tuple-element.79.refs_2_), channel_id=1, source_target_pairs={{0,8},{1,9},{2,10},{3,11},{4,12},{5,13},{6,14},{7,15},{8,0},{9,1},... | collective-permute-start | bytes 786440 | tf_op jit(solution)/shard_map/ppermute | solution.py:27
  44.6 12.1 %collective-permute-start.23 = (bf16[512,256]{1,0:T(8,128)(2,1)S(1)}, bf16[512,256]{1,0:T(8,128)(2,1)S(1)}, u32[]{:S(2)}, u32[]{:S(2)}) collective-permute-start(bf16[512,256]{1,0:T(8,128)(2,1)S(1)} %get-tuple-element.79.refs_2_), channel_id=1, source_target_pairs={{0,4},{1,5},{2,6},{3,7},{4,0},{5,1},{6,2},{7,3},{8,12},{9,13},{10,... | collective-permute-start | bytes 786440 | tf_op jit(solution)/shard_map/ppermute | solution.py:27
  52.8 5.0 %collective-permute-start.18 = (bf16[512,128]{1,0:T(8,128)(2,1)S(1)}, bf16[512,128]{1,0:T(8,128)(2,1)S(1)}, u32[]{:S(2)}, u32[]{:S(2)}) collective-permute-start(bf16[512,128]{1,0:T(8,128)(2,1)S(1)} %shard_map.64.refs_4_), channel_id=1, source_target_pairs={{0,16},{1,17},{2,18},{3,19},{4,20},{5,21},{6,22},{7,23},{8,24},{9,... | collective-permute-start | bytes 393224 | tf_op jit(solution)/shard_map/ppermute | solution.py:27
  54.1 6.2 %collective-permute-start.20 = (bf16[512,128]{1,0:T(8,128)(2,1)S(1)}, bf16[512,128]{1,0:T(8,128)(2,1)S(1)}, u32[]{:S(2)}, u32[]{:S(2)}) collective-permute-start(bf16[512,128]{1,0:T(8,128)(2,1)S(1)} %shard_map.64.refs_4_), channel_id=1, source_target_pairs={{0,18},{1,19},{2,16},{3,17},{4,22},{5,23},{6,20},{7,21},{8,26},{9,... | collective-permute-start | bytes 393224 | tf_op jit(solution)/shard_map/ppermute | solution.py:27
  55.9 5.8 %collective-permute-start.16 = (bf16[512,128]{1,0:T(8,128)(2,1)S(1)}, bf16[512,128]{1,0:T(8,128)(2,1)S(1)}, u32[]{:S(2)}, u32[]{:S(2)}) collective-permute-start(bf16[512,128]{1,0:T(8,128)(2,1)S(1)} %shard_map.64.refs_4_), channel_id=1, source_target_pairs={{0,2},{1,3},{2,0},{3,1},{4,6},{5,7},{6,4},{7,5},{8,10},{9,11},{10,... | collective-permute-start | bytes 393224 | tf_op jit(solution)/shard_map/ppermute | solution.py:27
  60.3 6.4 %collective-permute-start.24 = (bf16[512,256]{1,0:T(8,128)(2,1)S(1)}, bf16[512,256]{1,0:T(8,128)(2,1)S(1)}, u32[]{:S(2)}, u32[]{:S(2)}) collective-permute-start(bf16[512,256]{1,0:T(8,128)(2,1)S(1)} %collective-permute-done.22.refs_4_), channel_id=1, source_target_pairs={{0,4},{1,5},{2,6},{3,7},{4,0},{5,1},{6,2},{7,3},{8,12},{9,13},{10,... | collective-permute-start | bytes 786440 | tf_op jit(solution)/shard_map/ppermute | solution.py:27
  60.3 1.8 %collective-permute-start.15 = (bf16[512,128]{1,0:T(8,128)(2,1)S(1)}, bf16[512,128]{1,0:T(8,128)(2,1)S(1)}, u32[]{:S(2)}, u32[]{:S(2)}) collective-permute-start(bf16[512,128]{1,0:T(8,128)(2,1)S(1)} %shard_map.64.refs_4_), channel_id=1, source_target_pairs={{0,1},{1,0},{2,3},{3,2},{4,5},{5,4},{6,7},{7,6},{8,9},{9,8},{10,11... | collective-permute-start | bytes 393224 | tf_op jit(solution)/shard_map/ppermute | solution.py:27
  61.6 1.3 %collective-permute-start.17 = (bf16[512,128]{1,0:T(8,128)(2,1)S(1)}, bf16[512,128]{1,0:T(8,128)(2,1)S(1)}, u32[]{:S(2)}, u32[]{:S(2)}) collective-permute-start(bf16[512,128]{1,0:T(8,128)(2,1)S(1)} %collective-permute-done.16.refs_6_), channel_id=1, source_target_pairs={{0,1},{1,0},{2,3},{3,2},{4,5},{5,4},{6,7},{7,6},{8,9},{9,8},{10,11... | collective-permute-start | bytes 393224 | tf_op jit(solution)/shard_map/ppermute | solution.py:27
  61.6 1.5 %collective-permute-start.19 = (bf16[512,128]{1,0:T(8,128)(2,1)S(1)}, bf16[512,128]{1,0:T(8,128)(2,1)S(1)}, u32[]{:S(2)}, u32[]{:S(2)}) collective-permute-start(bf16[512,128]{1,0:T(8,128)(2,1)S(1)} %collective-permute-done.18.refs_8_), channel_id=1, source_target_pairs={{0,1},{1,0},{2,3},{3,2},{4,5},{5,4},{6,7},{7,6},{8,9},{9,8},{10,11... | collective-permute-start | bytes 393224 | tf_op jit(solution)/shard_map/ppermute | solution.py:27
  62.1 1.3 %collective-permute-start.21 = (bf16[512,128]{1,0:T(8,128)(2,1)S(1)}, bf16[512,128]{1,0:T(8,128)(2,1)S(1)}, u32[]{:S(2)}, u32[]{:S(2)}) collective-permute-start(bf16[512,128]{1,0:T(8,128)(2,1)S(1)} %collective-permute-done.20.refs_10_), channel_id=1, source_target_pairs={{0,1},{1,0},{2,3},{3,2},{4,5},{5,4},{6,7},{7,6},{8,9},{9,8},{10,11... | collective-permute-start | bytes 393224 | tf_op jit(solution)/shard_map/ppermute | solution.py:27
  66.7 2.7 %collective-permute-start.25 = (bf16[512,1024]{1,0:T(8,128)(2,1)S(1)}, bf16[512,1024]{1,0:T(8,128)(2,1)S(1)}, u32[]{:S(2)}, u32[]{:S(2)}) collective-permute-start(bf16[512,1024]{1,0:T(8,128)(2,1)S(1)} %shard_map.65.refs_0_), channel_id=1, source_target_pairs={{0,1},{1,0},{2,3},{3,2},{4,5},{5,4},{6,7},{7,6},{8,9},{9,8},{10,11... | collective-permute-start | bytes 3145736 | tf_op jit(solution)/shard_map/ppermute | solution.py:27
  71.2 10.2 %collective-permute-start.27 = (bf16[384,256]{1,0:T(8,128)(2,1)S(1)}, bf16[384,256]{1,0:T(8,128)(2,1)S(1)}, u32[]{:S(2)}, u32[]{:S(2)}) collective-permute-start(bf16[384,256]{1,0:T(8,128)(2,1)S(1)} %get-tuple-element.85), channel_id=1, source_target_pairs={{0,4},{1,5},{2,6},{3,7},{4,8},{5,9},{6,10},{7,11},{8,12},{9,13},{1... | collective-permute-start | bytes 589832 | tf_op jit(solution)/shard_map/ppermute | solution.py:32
  76.1 5.3 %collective-permute-start.26 = (bf16[512,128]{1,0:T(8,128)(2,1)S(1)}, bf16[512,128]{1,0:T(8,128)(2,1)S(1)}, u32[]{:S(2)}, u32[]{:S(2)}) collective-permute-start(bf16[512,128]{1,0:T(8,128)(2,1)S(1)} %get-tuple-element.83), channel_id=1, source_target_pairs={{0,16},{1,17},{2,18},{3,19},{4,20},{5,21},{6,22},{7,23},{8,24},{9,... | collective-permute-start | bytes 393224 | tf_op jit(solution)/shard_map/ppermute | solution.py:27
  83.1 5.0 %collective-permute-start.29 = (bf16[256,128]{1,0:T(8,128)(2,1)S(1)}, bf16[256,128]{1,0:T(8,128)(2,1)S(1)}, u32[]{:S(2)}, u32[]{:S(2)}) collective-permute-start(bf16[256,128]{1,0:T(8,128)(2,1)S(1)} %get-tuple-element.87), channel_id=1, source_target_pairs={{0,2},{1,3},{2,0},{3,1},{4,6},{5,7},{6,4},{7,5},{8,10},{9,11},{10,... | collective-permute-start | bytes 196616 | tf_op jit(solution)/shard_map/ppermute | solution.py:27
  84.5 4.3 %collective-permute-start.31 = (bf16[256,128]{1,0:T(8,128)(2,1)S(1)}, bf16[256,128]{1,0:T(8,128)(2,1)S(1)}, u32[]{:S(2)}, u32[]{:S(2)}) collective-permute-start(bf16[256,128]{1,0:T(8,128)(2,1)S(1)} %get-tuple-element.86.refs_0_), channel_id=1, source_target_pairs={{0,16},{1,17},{2,18},{3,19},{4,20},{5,21},{6,22},{7,23},{8,24},{9,... | collective-permute-start | bytes 196616 | tf_op jit(solution)/shard_map/ppermute | solution.py:27
  85.3 5.2 %collective-permute-start.33 = (bf16[256,128]{1,0:T(8,128)(2,1)S(1)}, bf16[256,128]{1,0:T(8,128)(2,1)S(1)}, u32[]{:S(2)}, u32[]{:S(2)}) collective-permute-start(bf16[256,128]{1,0:T(8,128)(2,1)S(1)} %get-tuple-element.87), channel_id=1, source_target_pairs={{0,18},{1,19},{2,16},{3,17},{4,22},{5,23},{6,20},{7,21},{8,26},{9,... | collective-permute-start | bytes 196616 | tf_op jit(solution)/shard_map/ppermute | solution.py:27
  86.6 3.8 %collective-permute-start.28 = (bf16[256,128]{1,0:T(8,128)(2,1)S(1)}, bf16[256,128]{1,0:T(8,128)(2,1)S(1)}, u32[]{:S(2)}, u32[]{:S(2)}) collective-permute-start(bf16[256,128]{1,0:T(8,128)(2,1)S(1)} %get-tuple-element.86.refs_0_), channel_id=1, source_target_pairs={{0,1},{1,0},{2,3},{3,2},{4,5},{5,4},{6,7},{7,6},{8,9},{9,8},{10,11... | collective-permute-start | bytes 196616 | tf_op jit(solution)/shard_map/ppermute | solution.py:27
  88.1 2.3 %collective-permute-start.30 = (bf16[256,128]{1,0:T(8,128)(2,1)S(1)}, bf16[256,128]{1,0:T(8,128)(2,1)S(1)}, u32[]{:S(2)}, u32[]{:S(2)}) collective-permute-start(bf16[256,128]{1,0:T(8,128)(2,1)S(1)} %collective-permute-done.29.refs_2_), channel_id=1, source_target_pairs={{0,1},{1,0},{2,3},{3,2},{4,5},{5,4},{6,7},{7,6},{8,9},{9,8},{10,11... | collective-permute-start | bytes 196616 | tf_op jit(solution)/shard_map/ppermute | solution.py:27
  88.7 1.7 %collective-permute-start.32 = (bf16[256,128]{1,0:T(8,128)(2,1)S(1)}, bf16[256,128]{1,0:T(8,128)(2,1)S(1)}, u32[]{:S(2)}, u32[]{:S(2)}) collective-permute-start(bf16[256,128]{1,0:T(8,128)(2,1)S(1)} %collective-permute-done.31.refs_4_), channel_id=1, source_target_pairs={{0,1},{1,0},{2,3},{3,2},{4,5},{5,4},{6,7},{7,6},{8,9},{9,8},{10,11... | collective-permute-start | bytes 196616 | tf_op jit(solution)/shard_map/ppermute | solution.py:27
  90.4 1.3 %collective-permute-start.34 = (bf16[256,128]{1,0:T(8,128)(2,1)S(1)}, bf16[256,128]{1,0:T(8,128)(2,1)S(1)}, u32[]{:S(2)}, u32[]{:S(2)}) collective-permute-start(bf16[256,128]{1,0:T(8,128)(2,1)S(1)} %collective-permute-done.33.refs_6_), channel_id=1, source_target_pairs={{0,1},{1,0},{2,3},{3,2},{4,5},{5,4},{6,7},{7,6},{8,9},{9,8},{10,11... | collective-permute-start | bytes 196616 | tf_op jit(solution)/shard_map/ppermute | solution.py:27

commit v4 on v3

--- a/solution.py
+++ b/solution.py
@@ -193,10 +193,13 @@
     tail_ref[past:] = ids_ref[...]
 
 
-def out_copies(own, local_ref, piece_refs, whole, sems):
+def out_copies(own, first_column, local_ref, piece_refs, whole, sems):
     first_ref, second_ref, across_ref = piece_refs
     rows, wide = first_ref.shape[0] // 6, first_ref.shape[1]
-    columns = pl.ds(pl.multiple_of(lax.rem(own, 2) * wide, wide), wide)
+    count_columns = whole.shape[1]
+    start = lax.rem(own, 2) * wide + first_column
+    columns = pl.ds(pl.multiple_of(start, count_columns), count_columns)
+    piece_columns = pl.ds(first_column, count_columns)
     upper = own // 2
     from_own, from_pieces = [], []
     for i, (ref, first, place, count) in enumerate((
@@ -204,7 +207,7 @@
         (second_ref, 2, (1 - upper) * 8, 2), (across_ref, 0, (1 - upper) * 8 + 2, 6),
     )):
         at = pl.ds(pl.multiple_of(place * rows, rows), count * rows)
-        source = ref.at[pl.ds(first * rows, count * rows)]
+        source = ref.at[pl.ds(first * rows, count * rows), piece_columns]
         from_own.append(
             pltpu.make_async_copy(local_ref.at[at, columns], whole.at[at], sems.at[i])
         )
@@ -212,13 +215,14 @@
     return from_own, from_pieces
 
 
-def stream_kernel(*refs):
+def stream_kernel(part_index, *refs):
     x_refs, b_refs = refs[:PLANE], refs[PLANE : 3 * PLANE]
     wo_ref, piece_refs = refs[3 * PLANE], refs[3 * PLANE + 1 : 3 * PLANE + 4]
     half_ref, blended, whole, sems = refs[3 * PLANE + 4 :]
     side = lax.rem(lax.axis_index("phase"), 2)
     own = lax.rem(lax.axis_index("ctx"), PLANE)
-    from_own, from_pieces = out_copies(own, wo_ref, piece_refs, whole, sems)
+    wide = half_ref.shape[1]
+    from_own, from_pieces = out_copies(own, part_index * wide, wo_ref, piece_refs, whole, sems)
 
     @pl.when(side == 0)
     def _():
@@ -230,8 +234,9 @@
         for copy in from_pieces:
             copy.start()
 
-    rows, part, wide = x_refs[0].shape[0], b_refs[0].shape[1], half_ref.shape[1]
-    columns = pl.ds(pl.multiple_of(lax.rem(own, 2) * wide, wide), wide)
+    rows, part = x_refs[0].shape[0], b_refs[0].shape[1]
+    start = (lax.rem(own, 2) * 2 + part_index) * wide
+    columns = pl.ds(pl.multiple_of(start, wide), wide)
     for r, o in enumerate(ORDER):
         at = pl.ds(pl.multiple_of((own ^ o) * rows, rows), rows)
         half_ref[at, :] = x_refs[r][:, columns]
@@ -248,15 +253,16 @@
 
 
 def second_kernel(pieces, *refs):
-    mine_half, other_half, refs = refs[0], refs[1], refs[2:]
+    quarters, refs = refs[:4], refs[4:]
     weight_refs, refs = refs[:pieces], refs[pieces:]
     wq_ref, own_ref, mine_ref, other_ref, kv_ref, tail_ref, stream, normed, weights = refs
     ctx = lax.axis_index("ctx")
     own, core = lax.rem(ctx, PLANE), lax.rem(ctx, 2)
-    rows, wide = own_ref.shape[0], mine_half.shape[1]
+    rows, wide = own_ref.shape[0], quarters[0].shape[1]
     fill_weights(ctx, weight_refs, weights)
-    for flip, ref in enumerate((mine_half, other_half)):
-        stream[:, pl.ds(pl.multiple_of((core ^ flip) * wide, wide), wide)] = ref[...]
+    for i, ref in enumerate(quarters):
+        start = ((core ^ (i // 2)) * 2 + i % 2) * wide
+        stream[:, pl.ds(pl.multiple_of(start, wide), wide)] = ref[...]
     normed[...] = rms_rows(stream[...])
     own_ref[...] = stream[pl.ds(pl.multiple_of(own * rows, rows), rows), :]
     keyvals = dot(normed[...], weights[...]).astype(jnp.bfloat16)
@@ -296,7 +302,7 @@
     local_query = lax.rem(lax.axis_index("phase"), 2) == layer
     window[tall - past : tall] = past_ref[:past]
     window[tall:] = kv_ref[...]
-    upper = lax.rem(lax.axis_index("ctx"), PLANE) // 2
+    own = lax.rem(lax.axis_index("ctx"), PLANE)
     for g in range(PLANE):
         keys = window[(g + 1) * rows : (g + 1 + WINDOW) * rows]
         for h in range(0, part, HEAD):
@@ -314,17 +320,24 @@
             if layer == 0:
                 out_refs[0][g * rows : (g + 1) * rows, h : h + HEAD] = result
                 continue
-            place = (g % 2) * rows
+            place = pl.multiple_of(jnp.where(own // 2 == g // 2, 0, rows), rows)
 
             def put(ref):
-                ref[place : place + rows, h : h + HEAD] = result
-
-            pl.when(upper == g // 2)(functools.partial(put, out_refs[0]))
-            pl.when(upper != g // 2)(functools.partial(put, out_refs[1]))
+                ref[pl.ds(place, rows), h : h + HEAD] = result
+
+            pl.when(lax.rem(own, 2) == g % 2)(functools.partial(put, out_refs[0]))
+            pl.when(lax.rem(own, 2) != g % 2)(functools.partial(put, out_refs[1]))
+
+
+def pair_kernel(kept_ref, got_ref, mine_ref, other_ref):
+    rows = kept_ref.shape[0] // 2
+    for i, ref in enumerate((mine_ref, other_ref)):
+        ref[:rows] = kept_ref[i * rows : (i + 1) * rows]
+        ref[rows:] = got_ref[i * rows : (i + 1) * rows]
 
 
 def last_kernel(*refs):
-    b_refs, (wo_ref, own_ref, out_ref, blended) = refs[: 2 * PLANE], refs[2 * PLANE :]
+    b_refs, (wo_ref, own_ref, out_ref, blended) = refs[:PLANE], refs[PLANE:]
     own = lax.rem(lax.axis_index("ctx"), PLANE)
     side = lax.rem(lax.axis_index("phase"), 2)
     rows, part = own_ref.shape[0], b_refs[0].shape[1]
@@ -335,10 +348,10 @@
 
     @pl.when(side == 1)
     def _():
-        for m, ref in enumerate(b_refs):
-            place = (side * PLANE + own) ^ m
-            start = pl.multiple_of(lax.rem(own, 2) * rows, rows)
-            blended[:, pl.ds(pl.multiple_of(place * part, part), part)] = ref[pl.ds(start, rows), :]
+        for m in range(2 * PLANE):
+            place = pl.multiple_of(((side * PLANE + own) ^ m) * part, part)
+            at = slice(m % 2 * rows, (m % 2 + 1) * rows)
+            blended[:, pl.ds(place, part)] = b_refs[m // 2][at, :]
         total = own_ref[...].astype(jnp.float32) + dot(blended[...], wo_ref[...])
         out_ref[...] = total.astype(jnp.bfloat16)
 
@@ -350,6 +363,10 @@
 def token_of(*blocks, cost):
     places = {i: pl.ANY for i in range(len(blocks))}
     return call(token_kernel, [((8, HEAD), jnp.float32)], [], cost, *blocks, far=places)[0]
+
+
+def sooner(block):
+    return after(block, token_of(block, cost=4 * 10**8))
 
 
 def along_planes(piece, gate=()):
@@ -394,7 +411,8 @@
     early, late_start = call(
         merge_kernel, [(piece, bf16)] * 2, [], 0, near, swap(far, 0, 1)
     )
-    out_first, out_second = (swap(after(b, across_y), 1, 0) for b in (sent_first, sent_second))
+    out_first = swap(after(sent_first, across_y), 1, 0)
+    shared = {}
     sent_on = call(copy_kernel, [((6 * unit, half), bf16)], [], 4 * 10**9, out_first)[0]
     out_across = swap(sent_on, 0, 2)
     early = along_planes(early)
@@ -418,6 +436,8 @@
             query_kernel, [((tall, width), bf16)] + query_out + [((16, 2 * part), bf16)], [], 0,
             *xs, query_mat,
         )
+        if not shared:
+            shared["out"] = swap(after(sent_second, mine), 1, 0)
         kv, tail = call(
             functools.partial(keyval_kernel, pieces), first_out, [weights], LONG,
             *(early[m] for m in range(pieces)), normed, ids,
@@ -429,34 +449,40 @@
         if bias is None:
             shape = ((PLANE, rows, WINDOW * rows), jnp.float32)
             bias = call(mask_kernel, [shape], [], 6 * 10**8, *xs, after(past_kv, query))[0]
-        bias, *out = lax.optimization_barrier((bias, out_first, out_second, out_across))
+        bias, *out = lax.optimization_barrier((bias, out_first, shared["out"], out_across))
         blended = call(
             functools.partial(attend_kernel, 0), [((tall, part), bf16)],
             [((2 * tall, 2 * part), bf16)], 0, mine, query, bias, kv, past_kv,
         )[0]
-        near = [blended, swap(blended, 0, 2), swap(blended, 1, 0), swap(blended, 1, 2)]
+        near = [blended, swap(blended, 0, 2), swap(blended, 1, 0), sooner(swap(blended, 1, 2))]
         heads = [b for n in near for b in (n, swap(n, 0, 1))]
         late[3] = swap(after(late[2], late[1], near[2], near[3]), 0, PLANE)
-        half = call(
-            stream_kernel, [((tall, width // 2), bf16)],
-            [((tall, head_width), bf16), ((head_width, width // 2), bf16),
-             pltpu.SemaphoreType.DMA((4,))],
-            0, *xs, *heads, w_out[0], *out,
-            far={3 * PLANE + i: pltpu.HBM for i in range(4)},
-        )[0]
+        quarters = [
+            call(
+                functools.partial(stream_kernel, i), [((tall, width // 4), bf16)],
+                [((tall, head_width), bf16), ((head_width, width // 4), bf16),
+                 pltpu.SemaphoreType.DMA((4,))],
+                0, *xs, *heads, w_out[0], *out,
+                far={3 * PLANE + i: pltpu.HBM for i in range(4)},
+            )[0]
+            for i in range(2)
+        ]
+        quarters += [swap(quarters[0], 0, 1), swap(after(quarters[1], late[3]), 0, 1)]
         stream, mine, other, kv, tail = call(
             functools.partial(second_kernel, pieces),
             [((rows, width), bf16)] + query_out + keyval_out,
             [((tall, width), bf16), ((tall, width), bf16), weights], 0,
-            half, swap(after(half, late[3]), 0, 1), *(late[m] for m in range(pieces)), query_mat,
+            *quarters, *(late[m] for m in range(pieces)), query_mat,
         )
-        mine, other = call(
+        kept, given = call(
             functools.partial(attend_kernel, 1), [((tall // 2, part), bf16)] * 2,
             [((2 * tall, 2 * part), bf16)],
             attend_flops, mine, swap(other, 1, 0), bias, kv, from_plane_behind(tail),
         )
-        near = [mine, swap(other, 0, 2), swap(mine, 1, 0), swap(other, 1, 2)]
-        heads = [b for n in near for b in (n, swap(n, 0, 1))]
+        mine, other = call(
+            pair_kernel, [((tall // 2, part), bf16)] * 2, [], 0, kept, swap(given, 0, 1)
+        )
+        heads = [mine, swap(other, 0, 2), swap(mine, 1, 0), sooner(swap(other, 1, 2))]
         out = call(
             last_kernel, [((rows, width), bf16)], [((rows, head_width), bf16)],
             2 * rows * head_width * width, *heads, w_out[0], stream,

time: 94.5 us -> 91.4 us (0.967); the launches traced: 93.2 us -> 91.1 us
  waiting for transfers between devices: 46.3 us -> 41.6 us
  starting transfers between devices: 29.9 us -> 32 us
    ppermute x33 -> x31, waiting for transfers between devices: 40.2 us -> 34.5 us  [swap(): return lax.ppermute(block, BOTH, route)]
    ppermute x33 -> x31, starting transfers between devices: 21.6 us -> 23.7 us  [swap(): return lax.ppermute(block, BOTH, route)]
    pallas_call x14 -> x16, Pallas kernels: 11.4 us -> 12 us  [call(): pl.pallas_call(kernel, out_shape=[jax.ShapeDtypeStruct(s, d) for s, d in...]
  transfers between devices with their start and end apart: 35 -> 33, of which waited for: 22 -> 21; matrix products, arithmetic and copies ran while one was open for 0% -> 0% of each run, Pallas kernels for 7% -> 7%
where the time goes in v4:
time: 91.4 us; the launch traced here: 91.1 us
  waiting for transfers between devices  41.6 us (46%)
  starting transfers between devices  32 us (35%)
  Pallas kernels  12 us (13%)
  local copies, waits for them, and re-layouts  5.43 us (6%)
    ppermute x31, waiting for transfers between devices, swap(): return lax.ppermute(block, BOTH, route)  34.5 us
    ppermute x31, starting transfers between devices, swap(): return lax.ppermute(block, BOTH, route)  23.7 us
    pallas_call x16, Pallas kernels, call(): pl.pallas_call(kernel, out_shape=[jax.ShapeDtypeStruct(s, d) for s, d in...  12 us
    ppermute x2, starting transfers between devices, from_plane_behind(): lax.ppermute(block, 'ctx', [(i, i + PLANE) for i in range(wide - PLANE)])  8.26 us
    ppermute x2, waiting for transfers between devices, from_plane_behind(): lax.ppermute(block, 'ctx', [(i, i + PLANE) for i in range(wide - PLANE)])  7.03 us
    unnamed x12, local copies, waits for them, and re-layouts  5.43 us
  transfers between devices with their start and end apart: 33, of which 21 were waited for; matrix products, arithmetic and copies ran while one was open for 0% of the time, Pallas kernels for 7%

profile of v4, /device:TPU:14, one launch (start us, length us, event | category | flops | bytes accessed | tf_op | source)
XLA Modules:
  0.0 91.1 jit_solution(15843283062173095197)
XLA Ops:
  0.0 1.0 %copy-done.2 = bf16[1,128,2048]{2,1,0:T(8,128)(2,1)S(1)} copy-done((bf16[1,128,2048]{2,1,0:T(8,128)(2,1)S(1)}, bf16[1,128,2048]{2,1,0:T(8,128)(2,1)}, u32[]{:S(2)}) %copy-start.2) | copy-done | bytes 524312
  1.0 0.1 shard_map.56
  1.1 0.6 collective-permute-start
  1.7 0.5 collective-permute-start.1
  2.2 2.4 %collective-permute-start.2 = (bf16[128,512]{1,0:T(8,128)(2,1)S(1)}, bf16[128,512]{1,0:T(8,128)(2,1)S(1)}, u32[]{:S(2)}, u32[]{:S(2)}) collective-permute-start(bf16[128,512]{1,0:T(8,128)(2,1)S(1)} %get-tuple-element.56), channel_id=1, source_target_pairs={{0,18},{1,19},{2,16},{3,17},{4,22},{5,23},{6,20},{7,21},{8,26},{9,... | collective-permute-start | bytes 393224 | tf_op jit(solution)/shard_map/ppermute | solution.py:27
  4.7 2.2 %copy-done = bf16[1,1024,2048]{2,1,0:T(8,128)(2,1)S(1)} copy-done((bf16[1,1024,2048]{2,1,0:T(8,128)(2,1)S(1)}, bf16[1,1024,2048]{2,1,0:T(8,128)(2,1)}, u32[]{:S(2)}) %copy-start) | copy-done | bytes 4194328
  6.9 2.2 %copy-done.5 = bf16[1,2048,1024]{2,1,0:T(8,128)(2,1)S(1)} copy-done((bf16[1,2048,1024]{2,1,0:T(8,128)(2,1)S(1)}, bf16[1,2048,1024]{2,1,0:T(8,128)(2,1)}, u32[]{:S(2)}) %copy-start.5) | copy-done | bytes 4194328
  9.1 0.4 shard_map.57
  9.5 0.9 collective-permute-done.2.across_both
  10.4 0.1 shard_map.58
  10.5 0.1 collective-permute-start.3
  10.6 0.6 collective-permute-start.12
  11.2 0.2 shard_map.55.refs_0_
  11.4 0.7 collective-permute-done.3.far_ref
  12.2 0.6 collective-permute-start.4
  12.7 2.6 %collective-permute-start.5 = (bf16[512,256]{1,0:T(8,128)(2,1)S(1)}, bf16[512,256]{1,0:T(8,128)(2,1)S(1)}, u32[]{:S(2)}, u32[]{:S(2)}) collective-permute-start(bf16[512,256]{1,0:T(8,128)(2,1)S(1)} %get-tuple-element.59.refs_0_), channel_id=1, source_target_pairs={{0,8},{1,9},{2,10},{3,11},{4,12},{5,13},{6,14},{7,15},{8,0},{9,1},... | collective-permute-start | bytes 786440 | tf_op jit(solution)/shard_map/ppermute | solution.py:27
  15.3 0.4 collective-permute-start.6
  15.8 10.6 %collective-permute-done.5.refs_2_ = bf16[512,256]{1,0:T(8,128)(2,1)S(1)} collective-permute-done((bf16[512,256]{1,0:T(8,128)(2,1)S(1)}, bf16[512,256]{1,0:T(8,128)(2,1)S(1)}, u32[]{:S(2)}, u32[]{:S(2)}) %collective-permute-start.5) | collective-permute-done | bytes 262176 | tf_op jit(solution)/shard_map/ppermute | solution.py:27
  26.4 1.1 %collective-permute-done.6.refs_1_ = bf16[512,256]{1,0:T(8,128)(2,1)S(1)} collective-permute-done((bf16[512,256]{1,0:T(8,128)(2,1)S(1)}, bf16[512,256]{1,0:T(8,128)(2,1)S(1)}, u32[]{:S(2)}, u32[]{:S(2)}) %collective-permute-start.6) | collective-permute-done | bytes 262176 | tf_op jit(solution)/shard_map/ppermute | solution.py:27
  27.5 0.5 collective-permute-start.8
  28.0 0.6 collective-permute-start.10
  28.6 2.0 %collective-permute-done.12.block_ref.refs_13_ = bf16[384,1024]{1,0:T(8,128)(2,1)S(1)} collective-permute-done((bf16[384,1024]{1,0:T(8,128)(2,1)S(1)}, bf16[384,1024]{1,0:T(8,128)(2,1)S(1)}, u32[]{:S(2)}, u32[]{:S(2)}) %collective-permute-start.12) | collective-permute-done | bytes 786464 | tf_op jit(solution)/shard_map/ppermute | solution.py:27
  30.6 0.6 collective-permute-start.14
  31.2 1.4 %shard_map.60 = (bf16[512,2048]{1,0:T(8,128)(2,1)S(1)}, bf16[512,128]{1,0:T(8,128)(2,1)S(1)}, bf16[512,128]{1,0:T(8,128)(2,1)S(1)}, bf16[16,256]{1,0:T(8,128)(2,1)S(1)}) custom-call(bf16[128,2176]{1,0:T(8,128)(2,1)S(1)} %shard_map.55.refs_0_, bf16[128,2176]{1,0:T(8,128)(2,1)S(1)} %collective-permute-done.4.refs_1_, ...), custom_call_target="tpu_custom_call" | custom-call | bytes 3276800 | tf_op jit(solution)/shard_map/pallas_call | solution.py:48
  32.6 0.6 collective-permute-start.9
  33.2 1.5 %collective-permute-start.13 = (bf16[256,1024]{1,0:T(8,128)(2,1)S(1)}, bf16[256,1024]{1,0:T(8,128)(2,1)S(1)}, u32[]{:S(2)}, u32[]{:S(2)}) collective-permute-start(bf16[256,1024]{1,0:T(8,128)(2,1)S(1)} %get-tuple-element.74), channel_id=1, source_target_pairs={{0,16},{1,17},{2,18},{3,19},{4,20},{5,21},{6,22},{7,23},{8,24},{9,... | collective-permute-start | bytes 1572872 | tf_op jit(solution)/shard_map/ppermute | solution.py:27
  34.7 1.5 %collective-permute-done.10.refs_3_ = bf16[512,256]{1,0:T(8,128)(2,1)S(1)} collective-permute-done((bf16[512,256]{1,0:T(8,128)(2,1)S(1)}, bf16[512,256]{1,0:T(8,128)(2,1)S(1)}, u32[]{:S(2)}, u32[]{:S(2)}) %collective-permute-start.10) | collective-permute-done | bytes 262176 | tf_op jit(solution)/shard_map/ppermute | solution.py:27
  36.2 0.8 shard_map.61
  37.0 3.4 %collective-permute-start.11 = (bf16[400,256]{1,0:T(8,128)(2,1)S(1)}, bf16[400,256]{1,0:T(8,128)(2,1)S(1)}, u32[]{:S(2)}, u32[]{:S(2)}) collective-permute-start(bf16[400,256]{1,0:T(8,128)(2,1)S(1)} %get-tuple-element.69), channel_id=1, source_target_pairs={{0,4},{1,5},{2,6},{3,7},{4,8},{5,9},{6,10},{7,11},{8,12},{9,13},{1... | collective-permute-start | bytes 614408 | tf_op jit(solution)/shard_map/ppermute | solution.py:32
  40.4 0.6 collective-permute-start.23
  41.0 2.6 %collective-permute-start.24 = (bf16[512,256]{1,0:T(8,128)(2,1)S(1)}, bf16[512,256]{1,0:T(8,128)(2,1)S(1)}, u32[]{:S(2)}, u32[]{:S(2)}) collective-permute-start(bf16[512,256]{1,0:T(8,128)(2,1)S(1)} %get-tuple-element.81.refs_4_), channel_id=1, source_target_pairs={{0,4},{1,5},{2,6},{3,7},{4,0},{5,1},{6,2},{7,3},{8,12},{9,13},{10,... | collective-permute-start | bytes 786440 | tf_op jit(solution)/shard_map/ppermute | solution.py:27
  43.7 7.0 %collective-permute-done.11.refs_4_.past_ref = bf16[400,256]{1,0:T(8,128)(2,1)S(1)} collective-permute-done((bf16[400,256]{1,0:T(8,128)(2,1)S(1)}, bf16[400,256]{1,0:T(8,128)(2,1)S(1)}, u32[]{:S(2)}, u32[]{:S(2)}) %collective-permute-start.11) | collective-permute-done | bytes 204832 | tf_op jit(solution)/shard_map/ppermute | solution.py:32
  50.7 0.2 shard_map.62.bias_ref
  51.0 1.2 %shard_map.64.refs_4_ = bf16[512,128]{1,0:T(8,128)(2,1)S(1)} custom-call(bf16[512,128]{1,0:T(8,128)(2,1)S(1)} %get-tuple-element.64.mine_ref, bf16[512,128]{1,0:T(8,128)(2,1)S(1)} %collective-permute-done.9.got_ref, f32[4,128,512]{2,1,0:T(8,128)S(1)} %shard_map.62.bias_ref, bf16[512,256]{1,0:T(8,128)(2,1)S(1)} %get-tuple-element.76.kv_ref, ...), custom_call_target="tpu_custom_call" | custom-call | bytes 1777664 | tf_op jit(solution)/shard_map/pallas_call | solution.py:48
  52.2 1.8 %collective-permute-start.20 = (bf16[512,128]{1,0:T(8,128)(2,1)S(1)}, bf16[512,128]{1,0:T(8,128)(2,1)S(1)}, u32[]{:S(2)}, u32[]{:S(2)}) collective-permute-start(bf16[512,128]{1,0:T(8,128)(2,1)S(1)} %shard_map.64.refs_4_), channel_id=1, source_target_pairs={{0,18},{1,19},{2,16},{3,17},{4,22},{5,23},{6,20},{7,21},{8,26},{9,... | collective-permute-start | bytes 393224 | tf_op jit(solution)/shard_map/ppermute | solution.py:27
  54.0 1.2 %collective-permute-start.18 = (bf16[512,128]{1,0:T(8,128)(2,1)S(1)}, bf16[512,128]{1,0:T(8,128)(2,1)S(1)}, u32[]{:S(2)}, u32[]{:S(2)}) collective-permute-start(bf16[512,128]{1,0:T(8,128)(2,1)S(1)} %shard_map.64.refs_4_), channel_id=1, source_target_pairs={{0,16},{1,17},{2,18},{3,19},{4,20},{5,21},{6,22},{7,23},{8,24},{9,... | collective-permute-start | bytes 393224 | tf_op jit(solution)/shard_map/ppermute | solution.py:27
  55.2 0.5 collective-permute-start.16
  55.7 2.4 %collective-permute-done.20.refs_10_ = bf16[512,128]{1,0:T(8,128)(2,1)S(1)} collective-permute-done((bf16[512,128]{1,0:T(8,128)(2,1)S(1)}, bf16[512,128]{1,0:T(8,128)(2,1)S(1)}, u32[]{:S(2)}, u32[]{:S(2)}) %collective-permute-start.20) | collective-permute-done | bytes 131104 | tf_op jit(solution)/shard_map/ppermute | solution.py:27
  58.1 1.5 %collective-permute-done.18.refs_8_ = bf16[512,128]{1,0:T(8,128)(2,1)S(1)} collective-permute-done((bf16[512,128]{1,0:T(8,128)(2,1)S(1)}, bf16[512,128]{1,0:T(8,128)(2,1)S(1)}, u32[]{:S(2)}, u32[]{:S(2)}) %collective-permute-start.18) | collective-permute-done | bytes 131104 | tf_op jit(solution)/shard_map/ppermute | solution.py:27
  59.6 0.6 collective-permute-done.16.refs_6_
  60.2 0.5 collective-permute-start.19
  60.7 0.2 collective-permute-done.15.refs_5_
  60.9 0.6 collective-permute-done.17.refs_7_
  61.6 0.2 collective-permute-done.19.refs_9_
  61.7 0.3 collective-permute-done.21.refs_11_
  62.1 1.2 %shard_map.65.refs_0_ = bf16[512,512]{1,0:T(8,128)(2,1)S(1)} custom-call(bf16[128,2176]{1,0:T(8,128)(2,1)S(1)} %shard_map.55.refs_0_, bf16[128,2176]{1,0:T(8,128)(2,1)S(1)} %collective-permute-done.4.refs_1_, bf16[128,2176]{1,0:T(8,128)(2,1)S(1)} %collective-permute-done.7.refs_2_, bf16[128,2176]{1,0:T(8,128)(2,1)S(1)} %collective-permute-done.8.refs_3_, ...), custom_call_target="tpu_custom_call" | custom-call | bytes 9568256 | tf_op jit(solution)/shard_map/pallas_call | solution.py:48
  63.3 0.3 collective-permute-start.22
  63.5 1.2 %shard_map.66.refs_1_ = bf16[512,512]{1,0:T(8,128)(2,1)S(1)} custom-call(bf16[128,2176]{1,0:T(8,128)(2,1)S(1)} %shard_map.55.refs_0_, bf16[128,2176]{1,0:T(8,128)(2,1)S(1)} %collective-permute-done.4.refs_1_, bf16[128,2176]{1,0:T(8,128)(2,1)S(1)} %collective-permute-done.7.refs_2_, bf16[128,2176]{1,0:T(8,128)(2,1)S(1)} %collective-permute-done.8.refs_3_, ...), custom_call_target="tpu_custom_call" | custom-call | bytes 9568256 | tf_op jit(solution)/shard_map/pallas_call | solution.py:48
  64.7 1.3 %collective-permute-done.25.refs_7_ = bf16[512,256]{1,0:T(8,128)(2,1)S(1)} collective-permute-done((bf16[512,256]{1,0:T(8,128)(2,1)S(1)}, bf16[512,256]{1,0:T(8,128)(2,1)S(1)}, u32[]{:S(2)}, u32[]{:S(2)}) %collective-permute-start.25) | collective-permute-done | bytes 262176 | tf_op jit(solution)/shard_map/ppermute | solution.py:27
  66.0 1.9 %collective-permute-done.26.refs_3_ = bf16[512,512]{1,0:T(8,128)(2,1)S(1)} collective-permute-done((bf16[512,512]{1,0:T(8,128)(2,1)S(1)}, bf16[512,512]{1,0:T(8,128)(2,1)S(1)}, u32[]{:S(2)}, u32[]{:S(2)}) %collective-permute-start.26) | collective-permute-done | bytes 524320 | tf_op jit(solution)/shard_map/ppermute | solution.py:27
  67.9 1.9 %shard_map.67 = (bf16[128,2048]{1,0:T(8,128)(2,1)S(1)}, bf16[512,128]{1,0:T(8,128)(2,1)S(1)}, bf16[512,128]{1,0:T(8,128)(2,1)S(1)}, bf16[512,256]{1,0:T(8,128)(2,1)S(1)}, bf16[384,256]{1,0:T(8,128)(2,1)S(1)}) custom-call(bf16[512,512]{1,0:T(8,128)(2,1)S(1)} %shard_map.65.refs_0_, bf16[512,512]{1,0:T(8,128)(2,1)S(1)} %shard_map.66.refs_1_, ...), custom_call_target="tpu_custom_call" | custom-call | bytes 4194304 | tf_op jit(solution)/shard_map/pallas_call | solution.py:48
  69.7 4.9 %collective-permute-start.28 = (bf16[384,256]{1,0:T(8,128)(2,1)S(1)}, bf16[384,256]{1,0:T(8,128)(2,1)S(1)}, u32[]{:S(2)}, u32[]{:S(2)}) collective-permute-start(bf16[384,256]{1,0:T(8,128)(2,1)S(1)} %get-tuple-element.87), channel_id=1, source_target_pairs={{0,4},{1,5},{2,6},{3,7},{4,8},{5,9},{6,10},{7,11},{8,12},{9,13},{1... | collective-permute-start | bytes 589832 | tf_op jit(solution)/shard_map/ppermute | solution.py:32
  74.6 0.9 collective-permute-start.27
  75.5 4.5 %collective-permute-done.27.got_ref = bf16[512,128]{1,0:T(8,128)(2,1)S(1)} collective-permute-done((bf16[512,128]{1,0:T(8,128)(2,1)S(1)}, bf16[512,128]{1,0:T(8,128)(2,1)S(1)}, u32[]{:S(2)}, u32[]{:S(2)}) %collective-permute-start.27) | collective-permute-done | bytes 131104 | tf_op jit(solution)/shard_map/ppermute | solution.py:27
  80.0 1.7 %shard_map.68 = (bf16[256,128]{1,0:T(8,128)(2,1)S(1)}, bf16[256,128]{1,0:T(8,128)(2,1)S(1)}) custom-call(bf16[512,128]{1,0:T(8,128)(2,1)S(1)} %get-tuple-element.84.mine_ref, bf16[512,128]{1,0:T(8,128)(2,1)S(1)} %collective-permute-done.27.got_ref, f32[4,128,512]{2,1,0:T(8,128)S(1)} %shard_map.62.bias_ref, bf16[512,256]{1,0:T(8,128)(2,1)S(1)} %get-tuple-element.86.kv_ref, ...), custom_call_target="tpu_custom_call" | custom-call | flops 134217728 | bytes 1769472 | tf_op jit(solution)/shard_map/pallas_call | solution.py:48
  81.6 0.1 collective-permute-start.29
  81.7 1.2 %collective-permute-done.29.got_ref = bf16[256,128]{1,0:T(8,128)(2,1)S(1)} collective-permute-done((bf16[256,128]{1,0:T(8,128)(2,1)S(1)}, bf16[256,128]{1,0:T(8,128)(2,1)S(1)}, u32[]{:S(2)}, u32[]{:S(2)}) %collective-permute-start.29) | collective-permute-done | bytes 65568 | tf_op jit(solution)/shard_map/ppermute | solution.py:27
  83.0 0.8 collective-permute-start.32
  83.8 1.5 %collective-permute-start.30 = (bf16[256,128]{1,0:T(8,128)(2,1)S(1)}, bf16[256,128]{1,0:T(8,128)(2,1)S(1)}, u32[]{:S(2)}, u32[]{:S(2)}) collective-permute-start(bf16[256,128]{1,0:T(8,128)(2,1)S(1)} %get-tuple-element.91), channel_id=1, source_target_pairs={{0,2},{1,3},{2,0},{3,1},{4,6},{5,7},{6,4},{7,5},{8,10},{9,11},{10,... | collective-permute-start | bytes 196616 | tf_op jit(solution)/shard_map/ppermute | solution.py:27
  85.3 1.2 %collective-permute-start.31 = (bf16[256,128]{1,0:T(8,128)(2,1)S(1)}, bf16[256,128]{1,0:T(8,128)(2,1)S(1)}, u32[]{:S(2)}, u32[]{:S(2)}) collective-permute-start(bf16[256,128]{1,0:T(8,128)(2,1)S(1)} %get-tuple-element.90.refs_0_), channel_id=1, source_target_pairs={{0,16},{1,17},{2,18},{3,19},{4,20},{5,21},{6,22},{7,23},{8,24},{9,... | collective-permute-start | bytes 196616 | tf_op jit(solution)/shard_map/ppermute | solution.py:27
  86.5 2.3 %collective-permute-done.32.refs_3_ = bf16[256,128]{1,0:T(8,128)(2,1)S(1)} collective-permute-done((bf16[256,128]{1,0:T(8,128)(2,1)S(1)}, bf16[256,128]{1,0:T(8,128)(2,1)S(1)}, u32[]{:S(2)}, u32[]{:S(2)}) %collective-permute-start.32) | collective-permute-done | bytes 65568 | tf_op jit(solution)/shard_map/ppermute | solution.py:27
  88.8 0.2 collective-permute-done.30.refs_1_
  89.0 0.5 collective-permute-done.31.refs_2_
  89.6 1.6 %shard_map.70 = bf16[128,2048]{1,0:T(8,128)(2,1)} custom-call(bf16[256,128]{1,0:T(8,128)(2,1)S(1)} %get-tuple-element.90.refs_0_, bf16[256,128]{1,0:T(8,128)(2,1)S(1)} %collective-permute-done.30.refs_1_, bf16[256,128]{1,0:T(8,128)(2,1)S(1)} %collective-permute-done.31.refs_2_, bf16[256,128]{1,0:T(8,128)(2,1)S(1)} %collective-permute-done.32.refs_3_, ...), custom_call_target="tpu_custom_call" | custom-call | flops 536870912 | bytes 4980736 | tf_op jit(solution)/shard_map/pallas_call | solution.py:48
  (30 shorter events, 0.2 us)
Async XLA Ops:
  0.0 1.0 %copy-start.2 = (bf16[1,128,2048]{2,1,0:T(8,128)(2,1)S(1)}, bf16[1,128,2048]{2,1,0:T(8,128)(2,1)}, u32[]{:S(2)}) copy-start(bf16[1,128,2048]{2,1,0:T(8,128)(2,1)} %param.8) | copy-start | bytes 1572868
  1.1 8.4 %collective-permute-start = (bf16[128,512]{1,0:T(8,128)(2,1)S(1)}, bf16[128,512]{1,0:T(8,128)(2,1)S(1)}, u32[]{:S(2)}, u32[]{:S(2)}) collective-permute-start(bf16[128,512]{1,0:T(8,128)(2,1)S(1)} %get-tuple-element.54), channel_id=1, source_target_pairs={{0,2},{1,3},{2,0},{3,1},{4,6},{5,7},{6,4},{7,5},{8,10},{9,11},{10,... | collective-permute-start | bytes 393224 | tf_op jit(solution)/shard_map/ppermute | solution.py:27
  1.7 7.8 %collective-permute-start.1 = (bf16[128,512]{1,0:T(8,128)(2,1)S(1)}, bf16[128,512]{1,0:T(8,128)(2,1)S(1)}, u32[]{:S(2)}, u32[]{:S(2)}) collective-permute-start(bf16[128,512]{1,0:T(8,128)(2,1)S(1)} %get-tuple-element.55), channel_id=1, source_target_pairs={{0,16},{1,17},{2,18},{3,19},{4,20},{5,21},{6,22},{7,23},{8,24},{9,... | collective-permute-start | bytes 393224 | tf_op jit(solution)/shard_map/ppermute | solution.py:27
  2.2 8.2 %collective-permute-start.2 = (bf16[128,512]{1,0:T(8,128)(2,1)S(1)}, bf16[128,512]{1,0:T(8,128)(2,1)S(1)}, u32[]{:S(2)}, u32[]{:S(2)}) collective-permute-start(bf16[128,512]{1,0:T(8,128)(2,1)S(1)} %get-tuple-element.56), channel_id=1, source_target_pairs={{0,18},{1,19},{2,16},{3,17},{4,22},{5,23},{6,20},{7,21},{8,26},{9,... | collective-permute-start | bytes 393224 | tf_op jit(solution)/shard_map/ppermute | solution.py:27
  4.7 2.2 %copy-start = (bf16[1,1024,2048]{2,1,0:T(8,128)(2,1)S(1)}, bf16[1,1024,2048]{2,1,0:T(8,128)(2,1)}, u32[]{:S(2)}) copy-start(bf16[1,1024,2048]{2,1,0:T(8,128)(2,1)} %param.9) | copy-start | bytes 12582916
  6.9 2.2 %copy-start.5 = (bf16[1,2048,1024]{2,1,0:T(8,128)(2,1)S(1)}, bf16[1,2048,1024]{2,1,0:T(8,128)(2,1)}, u32[]{:S(2)}) copy-start(bf16[1,2048,1024]{2,1,0:T(8,128)(2,1)} %param.7) | copy-start | bytes 12582916
  9.0 2.2 %copy-start.3 = (bf16[1,128,2048]{2,1,0:T(8,128)(2,1)S(1)}, bf16[1,128,2048]{2,1,0:T(8,128)(2,1)}, u32[]{:S(2)}) copy-start(bf16[1,128,2048]{2,1,0:T(8,128)(2,1)} %param.5) | copy-start | bytes 1572868
  9.0 2.2 %copy-start.4 = (s32[1,128]{1,0:T(1,128)S(1)}, s32[1,128]{1,0:T(1,128)}, u32[]{:S(2)}) copy-start(s32[1,128]{1,0:T(1,128)} %id_ref.1) | copy-start | bytes 1540
  10.5 1.6 %collective-permute-start.3 = (bf16[2,256,256]{2,1,0:T(8,128)(2,1)S(1)}, bf16[2,256,256]{2,1,0:T(8,128)(2,1)S(1)}, u32[]{:S(2)}, u32[]{:S(2)}) collective-permute-start(bf16[2,256,256]{2,1,0:T(8,128)(2,1)S(1)} %get-tuple-element.58), channel_id=1, source_target_pairs={{0,1},{1,0},{2,3},{3,2},{4,5},{5,4},{6,7},{7,6},{8,9},{9,8},{10,11... | collective-permute-start | bytes 786440 | tf_op jit(solution)/shard_map/ppermute | solution.py:27
  10.6 20.0 %collective-permute-start.12 = (bf16[384,1024]{1,0:T(8,128)(2,1)S(1)}, bf16[384,1024]{1,0:T(8,128)(2,1)S(1)}, u32[]{:S(2)}, u32[]{:S(2)}) collective-permute-start(bf16[384,1024]{1,0:T(8,128)(2,1)S(1)} %get-tuple-element.72), channel_id=1, source_target_pairs={{0,16},{1,17},{2,18},{3,19},{4,20},{5,21},{6,22},{7,23},{8,24},{9,... | collective-permute-start | bytes 2359304 | tf_op jit(solution)/shard_map/ppermute | solution.py:27
  12.2 15.3 %collective-permute-start.4 = (bf16[128,2176]{1,0:T(8,128)(2,1)S(1)}, bf16[128,2176]{1,0:T(8,128)(2,1)S(1)}, u32[]{:S(2)}, u32[]{:S(2)}) collective-permute-start(bf16[128,2176]{1,0:T(8,128)(2,1)S(1)} %shard_map.55.refs_0_), channel_id=1, source_target_pairs={{0,2},{1,3},{2,0},{3,1},{4,6},{5,7},{6,4},{7,5},{8,10},{9,11},{10,... | collective-permute-start | bytes 1671176 | tf_op jit(solution)/shard_map/ppermute | solution.py:27
  12.7 13.7 %collective-permute-start.5 = (bf16[512,256]{1,0:T(8,128)(2,1)S(1)}, bf16[512,256]{1,0:T(8,128)(2,1)S(1)}, u32[]{:S(2)}, u32[]{:S(2)}) collective-permute-start(bf16[512,256]{1,0:T(8,128)(2,1)S(1)} %get-tuple-element.59.refs_0_), channel_id=1, source_target_pairs={{0,8},{1,9},{2,10},{3,11},{4,12},{5,13},{6,14},{7,15},{8,0},{9,1},... | collective-permute-start | bytes 786440 | tf_op jit(solution)/shard_map/ppermute | solution.py:27
  15.3 12.2 %collective-permute-start.6 = (bf16[512,256]{1,0:T(8,128)(2,1)S(1)}, bf16[512,256]{1,0:T(8,128)(2,1)S(1)}, u32[]{:S(2)}, u32[]{:S(2)}) collective-permute-start(bf16[512,256]{1,0:T(8,128)(2,1)S(1)} %get-tuple-element.59.refs_0_), channel_id=1, source_target_pairs={{0,4},{1,5},{2,6},{3,7},{4,0},{5,1},{6,2},{7,3},{8,12},{9,13},{10,... | collective-permute-start | bytes 786440 | tf_op jit(solution)/shard_map/ppermute | solution.py:27
  27.5 3.7 %collective-permute-start.7 = (bf16[128,2176]{1,0:T(8,128)(2,1)S(1)}, bf16[128,2176]{1,0:T(8,128)(2,1)S(1)}, u32[]{:S(2)}, u32[]{:S(2)}) collective-permute-start(bf16[128,2176]{1,0:T(8,128)(2,1)S(1)} %shard_map.55.refs_0_), channel_id=1, source_target_pairs={{0,1},{1,0},{2,3},{3,2},{4,5},{5,4},{6,7},{7,6},{8,9},{9,8},{10,11... | collective-permute-start | bytes 1671176 | tf_op jit(solution)/shard_map/ppermute | solution.py:27
  27.5 3.7 %collective-permute-start.8 = (bf16[128,2176]{1,0:T(8,128)(2,1)S(1)}, bf16[128,2176]{1,0:T(8,128)(2,1)S(1)}, u32[]{:S(2)}, u32[]{:S(2)}) collective-permute-start(bf16[128,2176]{1,0:T(8,128)(2,1)S(1)} %collective-permute-done.4.refs_1_), channel_id=1, source_target_pairs={{0,1},{1,0},{2,3},{3,2},{4,5},{5,4},{6,7},{7,6},{8,9},{9,8},{10,11... | collective-permute-start | bytes 1671176 | tf_op jit(solution)/shard_map/ppermute | solution.py:27
  28.0 8.2 %collective-permute-start.10 = (bf16[512,256]{1,0:T(8,128)(2,1)S(1)}, bf16[512,256]{1,0:T(8,128)(2,1)S(1)}, u32[]{:S(2)}, u32[]{:S(2)}) collective-permute-start(bf16[512,256]{1,0:T(8,128)(2,1)S(1)} %collective-permute-done.5.refs_2_), channel_id=1, source_target_pairs={{0,4},{1,5},{2,6},{3,7},{4,0},{5,1},{6,2},{7,3},{8,12},{9,13},{10,... | collective-permute-start | bytes 786440 | tf_op jit(solution)/shard_map/ppermute | solution.py:27
  30.6 20.3 %collective-permute-start.14 = (bf16[384,1024]{1,0:T(8,128)(2,1)S(1)}, bf16[384,1024]{1,0:T(8,128)(2,1)S(1)}, u32[]{:S(2)}, u32[]{:S(2)}) collective-permute-start(bf16[384,1024]{1,0:T(8,128)(2,1)S(1)} %shard_map.63), channel_id=1, source_target_pairs={{0,2},{1,3},{2,0},{3,1},{4,6},{5,7},{6,4},{7,5},{8,10},{9,11},{10,... | collective-permute-start | bytes 2359304 | tf_op jit(solution)/shard_map/ppermute | solution.py:27
  32.6 8.4 %collective-permute-start.9 = (bf16[512,128]{1,0:T(8,128)(2,1)S(1)}, bf16[512,128]{1,0:T(8,128)(2,1)S(1)}, u32[]{:S(2)}, u32[]{:S(2)}) collective-permute-start(bf16[512,128]{1,0:T(8,128)(2,1)S(1)} %get-tuple-element.65), channel_id=1, source_target_pairs={{0,16},{1,17},{2,18},{3,19},{4,20},{5,21},{6,22},{7,23},{8,24},{9,... | collective-permute-start | bytes 393224 | tf_op jit(solution)/shard_map/ppermute | solution.py:27
  33.2 17.7 %collective-permute-start.13 = (bf16[256,1024]{1,0:T(8,128)(2,1)S(1)}, bf16[256,1024]{1,0:T(8,128)(2,1)S(1)}, u32[]{:S(2)}, u32[]{:S(2)}) collective-permute-start(bf16[256,1024]{1,0:T(8,128)(2,1)S(1)} %get-tuple-element.74), channel_id=1, source_target_pairs={{0,16},{1,17},{2,18},{3,19},{4,20},{5,21},{6,22},{7,23},{8,24},{9,... | collective-permute-start | bytes 1572872 | tf_op jit(solution)/shard_map/ppermute | solution.py:27
  37.0 25.1 %copy-start.1 = (bf16[1,1024,2048]{2,1,0:T(8,128)(2,1)S(1)}, bf16[1,1024,2048]{2,1,0:T(8,128)(2,1)}, u32[]{:S(2)}) copy-start(bf16[1,1024,2048]{2,1,0:T(8,128)(2,1)} %param.9) | copy-start | bytes 12582916
  37.0 13.7 %collective-permute-start.11 = (bf16[400,256]{1,0:T(8,128)(2,1)S(1)}, bf16[400,256]{1,0:T(8,128)(2,1)S(1)}, u32[]{:S(2)}, u32[]{:S(2)}) collective-permute-start(bf16[400,256]{1,0:T(8,128)(2,1)S(1)} %get-tuple-element.69), channel_id=1, source_target_pairs={{0,4},{1,5},{2,6},{3,7},{4,8},{5,9},{6,10},{7,11},{8,12},{9,13},{1... | collective-permute-start | bytes 614408 | tf_op jit(solution)/shard_map/ppermute | solution.py:32
  40.4 17.7 %collective-permute-start.23 = (bf16[512,256]{1,0:T(8,128)(2,1)S(1)}, bf16[512,256]{1,0:T(8,128)(2,1)S(1)}, u32[]{:S(2)}, u32[]{:S(2)}) collective-permute-start(bf16[512,256]{1,0:T(8,128)(2,1)S(1)} %get-tuple-element.81.refs_4_), channel_id=1, source_target_pairs={{0,8},{1,9},{2,10},{3,11},{4,12},{5,13},{6,14},{7,15},{8,0},{9,1},... | collective-permute-start | bytes 786440 | tf_op jit(solution)/shard_map/ppermute | solution.py:27
  41.0 17.1 %collective-permute-start.24 = (bf16[512,256]{1,0:T(8,128)(2,1)S(1)}, bf16[512,256]{1,0:T(8,128)(2,1)S(1)}, u32[]{:S(2)}, u32[]{:S(2)}) collective-permute-start(bf16[512,256]{1,0:T(8,128)(2,1)S(1)} %get-tuple-element.81.refs_4_), channel_id=1, source_target_pairs={{0,4},{1,5},{2,6},{3,7},{4,0},{5,1},{6,2},{7,3},{8,12},{9,13},{10,... | collective-permute-start | bytes 786440 | tf_op jit(solution)/shard_map/ppermute | solution.py:27
  52.2 5.9 %collective-permute-start.20 = (bf16[512,128]{1,0:T(8,128)(2,1)S(1)}, bf16[512,128]{1,0:T(8,128)(2,1)S(1)}, u32[]{:S(2)}, u32[]{:S(2)}) collective-permute-start(bf16[512,128]{1,0:T(8,128)(2,1)S(1)} %shard_map.64.refs_4_), channel_id=1, source_target_pairs={{0,18},{1,19},{2,16},{3,17},{4,22},{5,23},{6,20},{7,21},{8,26},{9,... | collective-permute-start | bytes 393224 | tf_op jit(solution)/shard_map/ppermute | solution.py:27
  54.0 5.6 %collective-permute-start.18 = (bf16[512,128]{1,0:T(8,128)(2,1)S(1)}, bf16[512,128]{1,0:T(8,128)(2,1)S(1)}, u32[]{:S(2)}, u32[]{:S(2)}) collective-permute-start(bf16[512,128]{1,0:T(8,128)(2,1)S(1)} %shard_map.64.refs_4_), channel_id=1, source_target_pairs={{0,16},{1,17},{2,18},{3,19},{4,20},{5,21},{6,22},{7,23},{8,24},{9,... | collective-permute-start | bytes 393224 | tf_op jit(solution)/shard_map/ppermute | solution.py:27
  55.2 5.0 %collective-permute-start.16 = (bf16[512,128]{1,0:T(8,128)(2,1)S(1)}, bf16[512,128]{1,0:T(8,128)(2,1)S(1)}, u32[]{:S(2)}, u32[]{:S(2)}) collective-permute-start(bf16[512,128]{1,0:T(8,128)(2,1)S(1)} %shard_map.64.refs_4_), channel_id=1, source_target_pairs={{0,2},{1,3},{2,0},{3,1},{4,6},{5,7},{6,4},{7,5},{8,10},{9,11},{10,... | collective-permute-start | bytes 393224 | tf_op jit(solution)/shard_map/ppermute | solution.py:27
  59.6 6.4 %collective-permute-start.25 = (bf16[512,256]{1,0:T(8,128)(2,1)S(1)}, bf16[512,256]{1,0:T(8,128)(2,1)S(1)}, u32[]{:S(2)}, u32[]{:S(2)}) collective-permute-start(bf16[512,256]{1,0:T(8,128)(2,1)S(1)} %collective-permute-done.23.refs_6_), channel_id=1, source_target_pairs={{0,4},{1,5},{2,6},{3,7},{4,0},{5,1},{6,2},{7,3},{8,12},{9,13},{10,... | collective-permute-start | bytes 786440 | tf_op jit(solution)/shard_map/ppermute | solution.py:27
  59.6 1.3 %collective-permute-start.15 = (bf16[512,128]{1,0:T(8,128)(2,1)S(1)}, bf16[512,128]{1,0:T(8,128)(2,1)S(1)}, u32[]{:S(2)}, u32[]{:S(2)}) collective-permute-start(bf16[512,128]{1,0:T(8,128)(2,1)S(1)} %shard_map.64.refs_4_), channel_id=1, source_target_pairs={{0,1},{1,0},{2,3},{3,2},{4,5},{5,4},{6,7},{7,6},{8,9},{9,8},{10,11... | collective-permute-start | bytes 393224 | tf_op jit(solution)/shard_map/ppermute | solution.py:27
  60.2 1.3 %collective-permute-start.17 = (bf16[512,128]{1,0:T(8,128)(2,1)S(1)}, bf16[512,128]{1,0:T(8,128)(2,1)S(1)}, u32[]{:S(2)}, u32[]{:S(2)}) collective-permute-start(bf16[512,128]{1,0:T(8,128)(2,1)S(1)} %collective-permute-done.16.refs_6_), channel_id=1, source_target_pairs={{0,1},{1,0},{2,3},{3,2},{4,5},{5,4},{6,7},{7,6},{8,9},{9,8},{10,11... | collective-permute-start | bytes 393224 | tf_op jit(solution)/shard_map/ppermute | solution.py:27
  60.2 1.5 %collective-permute-start.19 = (bf16[512,128]{1,0:T(8,128)(2,1)S(1)}, bf16[512,128]{1,0:T(8,128)(2,1)S(1)}, u32[]{:S(2)}, u32[]{:S(2)}) collective-permute-start(bf16[512,128]{1,0:T(8,128)(2,1)S(1)} %collective-permute-done.18.refs_8_), channel_id=1, source_target_pairs={{0,1},{1,0},{2,3},{3,2},{4,5},{5,4},{6,7},{7,6},{8,9},{9,8},{10,11... | collective-permute-start | bytes 393224 | tf_op jit(solution)/shard_map/ppermute | solution.py:27
  60.7 1.3 %collective-permute-start.21 = (bf16[512,128]{1,0:T(8,128)(2,1)S(1)}, bf16[512,128]{1,0:T(8,128)(2,1)S(1)}, u32[]{:S(2)}, u32[]{:S(2)}) collective-permute-start(bf16[512,128]{1,0:T(8,128)(2,1)S(1)} %collective-permute-done.20.refs_10_), channel_id=1, source_target_pairs={{0,1},{1,0},{2,3},{3,2},{4,5},{5,4},{6,7},{7,6},{8,9},{9,8},{10,11... | collective-permute-start | bytes 393224 | tf_op jit(solution)/shard_map/ppermute | solution.py:27
  63.3 2.7 %collective-permute-start.22 = (bf16[512,512]{1,0:T(8,128)(2,1)S(1)}, bf16[512,512]{1,0:T(8,128)(2,1)S(1)}, u32[]{:S(2)}, u32[]{:S(2)}) collective-permute-start(bf16[512,512]{1,0:T(8,128)(2,1)S(1)} %shard_map.65.refs_0_), channel_id=1, source_target_pairs={{0,1},{1,0},{2,3},{3,2},{4,5},{5,4},{6,7},{7,6},{8,9},{9,8},{10,11... | collective-permute-start | bytes 1572872 | tf_op jit(solution)/shard_map/ppermute | solution.py:27
  66.0 1.9 %collective-permute-start.26 = (bf16[512,512]{1,0:T(8,128)(2,1)S(1)}, bf16[512,512]{1,0:T(8,128)(2,1)S(1)}, u32[]{:S(2)}, u32[]{:S(2)}) collective-permute-start(bf16[512,512]{1,0:T(8,128)(2,1)S(1)} %shard_map.66.refs_1_), channel_id=1, source_target_pairs={{0,1},{1,0},{2,3},{3,2},{4,5},{5,4},{6,7},{7,6},{8,9},{9,8},{10,11... | collective-permute-start | bytes 1572872 | tf_op jit(solution)/shard_map/ppermute | solution.py:27
  69.7 10.2 %collective-permute-start.28 = (bf16[384,256]{1,0:T(8,128)(2,1)S(1)}, bf16[384,256]{1,0:T(8,128)(2,1)S(1)}, u32[]{:S(2)}, u32[]{:S(2)}) collective-permute-start(bf16[384,256]{1,0:T(8,128)(2,1)S(1)} %get-tuple-element.87), channel_id=1, source_target_pairs={{0,4},{1,5},{2,6},{3,7},{4,8},{5,9},{6,10},{7,11},{8,12},{9,13},{1... | collective-permute-start | bytes 589832 | tf_op jit(solution)/shard_map/ppermute | solution.py:32
  74.6 5.3 %collective-permute-start.27 = (bf16[512,128]{1,0:T(8,128)(2,1)S(1)}, bf16[512,128]{1,0:T(8,128)(2,1)S(1)}, u32[]{:S(2)}, u32[]{:S(2)}) collective-permute-start(bf16[512,128]{1,0:T(8,128)(2,1)S(1)} %get-tuple-element.85), channel_id=1, source_target_pairs={{0,16},{1,17},{2,18},{3,19},{4,20},{5,21},{6,22},{7,23},{8,24},{9,... | collective-permute-start | bytes 393224 | tf_op jit(solution)/shard_map/ppermute | solution.py:27
  81.6 1.3 %collective-permute-start.29 = (bf16[256,128]{1,0:T(8,128)(2,1)S(1)}, bf16[256,128]{1,0:T(8,128)(2,1)S(1)}, u32[]{:S(2)}, u32[]{:S(2)}) collective-permute-start(bf16[256,128]{1,0:T(8,128)(2,1)S(1)} %get-tuple-element.89), channel_id=1, source_target_pairs={{0,1},{1,0},{2,3},{3,2},{4,5},{5,4},{6,7},{7,6},{8,9},{9,8},{10,11... | collective-permute-start | bytes 196616 | tf_op jit(solution)/shard_map/ppermute | solution.py:27
  83.0 5.9 %collective-permute-start.32 = (bf16[256,128]{1,0:T(8,128)(2,1)S(1)}, bf16[256,128]{1,0:T(8,128)(2,1)S(1)}, u32[]{:S(2)}, u32[]{:S(2)}) collective-permute-start(bf16[256,128]{1,0:T(8,128)(2,1)S(1)} %get-tuple-element.91), channel_id=1, source_target_pairs={{0,18},{1,19},{2,16},{3,17},{4,22},{5,23},{6,20},{7,21},{8,26},{9,... | collective-permute-start | bytes 196616 | tf_op jit(solution)/shard_map/ppermute | solution.py:27
  83.8 5.3 %collective-permute-start.30 = (bf16[256,128]{1,0:T(8,128)(2,1)S(1)}, bf16[256,128]{1,0:T(8,128)(2,1)S(1)}, u32[]{:S(2)}, u32[]{:S(2)}) collective-permute-start(bf16[256,128]{1,0:T(8,128)(2,1)S(1)} %get-tuple-element.91), channel_id=1, source_target_pairs={{0,2},{1,3},{2,0},{3,1},{4,6},{5,7},{6,4},{7,5},{8,10},{9,11},{10,... | collective-permute-start | bytes 196616 | tf_op jit(solution)/shard_map/ppermute | solution.py:27
  85.3 4.3 %collective-permute-start.31 = (bf16[256,128]{1,0:T(8,128)(2,1)S(1)}, bf16[256,128]{1,0:T(8,128)(2,1)S(1)}, u32[]{:S(2)}, u32[]{:S(2)}) collective-permute-start(bf16[256,128]{1,0:T(8,128)(2,1)S(1)} %get-tuple-element.90.refs_0_), channel_id=1, source_target_pairs={{0,16},{1,17},{2,18},{3,19},{4,20},{5,21},{6,22},{7,23},{8,24},{9,... | collective-permute-start | bytes 196616 | tf_op jit(solution)/shard_map/ppermute | solution.py:27

commit v5 on v4

--- a/solution.py
+++ b/solution.py
@@ -11,6 +11,7 @@
 HEAD = 128
 WINDOW = 4
 PLANE = 4
+FIRST, REST = 11, 5
 ORDER = (0, 2, 1, 3)
 BOTH = ("phase", "ctx")
 VMEM_BYTES = 24 * 1024 * 1024
@@ -69,15 +70,15 @@
 def slice_kernel(out_ref, query_ref, sent_first, sent_second, query_mat, sems):
     side = lax.rem(lax.axis_index("phase"), 2)
     own = lax.rem(lax.axis_index("ctx"), PLANE)
-    unit, wide = sent_first.shape[0] // 6, sent_first.shape[1]
+    unit, wide = sent_first.shape[0] // FIRST, sent_first.shape[1]
     part = query_mat.shape[1] // 2
     columns = pl.ds(pl.multiple_of(lax.rem(own, 2) * wide, wide), wide)
     copies = []
     for i, (ref, first, count, upper, skip) in enumerate((
-        (sent_first, 0, 6, own // 2, 2), (sent_second, 0, 2, own // 2, 0),
-        (sent_second, 2, 2, 1 - own // 2, 0),
+        (sent_first, 0, FIRST, own // 2, REST), (sent_second, 0, REST, own // 2, 0),
+        (sent_second, REST, REST, 1 - own // 2, 0),
     )):
-        at = pl.ds(pl.multiple_of((upper * 8 + skip) * unit, unit), count * unit)
+        at = pl.ds(pl.multiple_of((upper * (FIRST + REST) + skip) * unit, unit), count * unit)
         to = ref.at[pl.ds(first * unit, count * unit)]
         copies.append(pltpu.make_async_copy(out_ref.at[at, columns], to, sems.at[i]))
     for flip in (0, 1):
@@ -195,16 +196,17 @@
 
 def out_copies(own, first_column, local_ref, piece_refs, whole, sems):
     first_ref, second_ref, across_ref = piece_refs
-    rows, wide = first_ref.shape[0] // 6, first_ref.shape[1]
+    rows, wide = first_ref.shape[0] // FIRST, first_ref.shape[1]
     count_columns = whole.shape[1]
     start = lax.rem(own, 2) * wide + first_column
     columns = pl.ds(pl.multiple_of(start, count_columns), count_columns)
     piece_columns = pl.ds(first_column, count_columns)
-    upper = own // 2
+    upper, half = own // 2, FIRST + REST
     from_own, from_pieces = [], []
     for i, (ref, first, place, count) in enumerate((
-        (first_ref, 0, upper * 8 + 2, 6), (second_ref, 0, upper * 8, 2),
-        (second_ref, 2, (1 - upper) * 8, 2), (across_ref, 0, (1 - upper) * 8 + 2, 6),
+        (first_ref, 0, upper * half + REST, FIRST), (second_ref, 0, upper * half, REST),
+        (second_ref, REST, (1 - upper) * half, REST),
+        (across_ref, 0, (1 - upper) * half + REST, FIRST),
     )):
         at = pl.ds(pl.multiple_of(place * rows, rows), count * rows)
         source = ref.at[pl.ds(first * rows, count * rows), piece_columns]
@@ -295,7 +297,10 @@
 
 
 def attend_kernel(layer, mine_ref, got_ref, bias_ref, kv_ref, past_ref, *refs):
-    out_refs, window = refs[:-1], refs[-1]
+    if layer == 0:
+        whole, window = refs
+    else:
+        out_refs, whole, window = refs[:2], refs[2], refs[3]
     rows = bias_ref.shape[1]
     part = mine_ref.shape[1]
     tall, past = kv_ref.shape[0], (WINDOW - 1) * rows
@@ -317,16 +322,14 @@
             total = jnp.sum(weights, axis=1, keepdims=True)
             values = keys[:, part + h : part + h + HEAD]
             result = (dot(weights.astype(jnp.bfloat16), values) / total).astype(jnp.bfloat16)
-            if layer == 0:
-                out_refs[0][g * rows : (g + 1) * rows, h : h + HEAD] = result
-                continue
-            place = pl.multiple_of(jnp.where(own // 2 == g // 2, 0, rows), rows)
-
-            def put(ref):
-                ref[pl.ds(place, rows), h : h + HEAD] = result
-
-            pl.when(lax.rem(own, 2) == g % 2)(functools.partial(put, out_refs[0]))
-            pl.when(lax.rem(own, 2) != g % 2)(functools.partial(put, out_refs[1]))
+            whole[g * rows : (g + 1) * rows, h : h + HEAD] = result
+    if layer == 0:
+        return
+    for core, ref in enumerate(out_refs):
+        for i in range(2):
+            group = 2 * (own // 2 ^ i) + (own % 2 ^ core)
+            place = pl.multiple_of(group * rows, rows)
+            ref[i * rows : (i + 1) * rows, :] = whole[pl.ds(place, rows), :]
 
 
 def pair_kernel(kept_ref, got_ref, mine_ref, other_ref):
@@ -365,8 +368,8 @@
     return call(token_kernel, [((8, HEAD), jnp.float32)], [], cost, *blocks, far=places)[0]
 
 
-def sooner(block):
-    return after(block, token_of(block, cost=4 * 10**8))
+def sooner(block, cost=4 * 10**8):
+    return after(block, token_of(block, cost=cost))
 
 
 def along_planes(piece, gate=()):
@@ -389,10 +392,10 @@
     depth = w_keyval.shape[1]
     tall, past = PLANE * rows, (WINDOW - 1) * rows
 
-    unit, half = head_width // 16, width // 2
+    unit, half = head_width // (2 * (FIRST + REST)), width // 2
     sent_first, sent_second, query_mat = call(
         slice_kernel,
-        [((6 * unit, half), bf16), ((4 * unit, half), bf16), ((width, 2 * part), bf16)],
+        [((FIRST * unit, half), bf16), ((2 * REST * unit, half), bf16), ((width, 2 * part), bf16)],
         [pltpu.SemaphoreType.DMA((5,))], LONG, w_out[0], w_query[0], far={0: pltpu.HBM, 1: pltpu.HBM},
     )
 
@@ -413,7 +416,7 @@
     )
     out_first = swap(after(sent_first, across_y), 1, 0)
     shared = {}
-    sent_on = call(copy_kernel, [((6 * unit, half), bf16)], [], 4 * 10**9, out_first)[0]
+    sent_on = call(copy_kernel, [((FIRST * unit, half), bf16)], [], 6 * 10**9, out_first)[0]
     out_across = swap(sent_on, 0, 2)
     early = along_planes(early)
     early[1] = swap(early[0], 0, PLANE)
@@ -449,14 +452,16 @@
         if bias is None:
             shape = ((PLANE, rows, WINDOW * rows), jnp.float32)
             bias = call(mask_kernel, [shape], [], 6 * 10**8, *xs, after(past_kv, query))[0]
-        bias, *out = lax.optimization_barrier((bias, out_first, shared["out"], out_across))
+        bias, first, across_out = lax.optimization_barrier((bias, out_first, out_across))
         blended = call(
             functools.partial(attend_kernel, 0), [((tall, part), bf16)],
             [((2 * tall, 2 * part), bf16)], 0, mine, query, bias, kv, past_kv,
         )[0]
-        near = [blended, swap(blended, 0, 2), swap(blended, 1, 0), sooner(swap(blended, 1, 2))]
+        y_block, second = lax.optimization_barrier((blended, shared["out"]))
+        out = [first, second, across_out]
+        near = [blended, swap(y_block, 0, 2), swap(blended, 1, 0), sooner(swap(blended, 1, 2))]
         heads = [b for n in near for b in (n, swap(n, 0, 1))]
-        late[3] = swap(after(late[2], late[1], near[2], near[3]), 0, PLANE)
+        late[3] = swap(after(late[2], late[1], near[3]), 0, PLANE)
         quarters = [
             call(
                 functools.partial(stream_kernel, i), [((tall, width // 4), bf16)],
@@ -476,7 +481,7 @@
         )
         kept, given = call(
             functools.partial(attend_kernel, 1), [((tall // 2, part), bf16)] * 2,
-            [((2 * tall, 2 * part), bf16)],
+            [((tall, part), bf16), ((2 * tall, 2 * part), bf16)],
             attend_flops, mine, swap(other, 1, 0), bias, kv, from_plane_behind(tail),
         )
         mine, other = call(

time: 91.4 us -> 90.3 us (0.988); the launches traced: 91.1 us -> 89 us
  waiting for transfers between devices: 41.6 us -> 40 us
    ppermute x31, waiting for transfers between devices: 34.5 us -> 33.1 us  [swap(): return lax.ppermute(block, BOTH, route)]
  transfers between devices with their start and end apart: 33 -> 33, of which waited for: 21 -> 21; matrix products, arithmetic and copies ran while one was open for 0% -> 0% of each run, Pallas kernels for 7% -> 8%
where the time goes in v5:
time: 90.3 us; the launch traced here: 89 us
  waiting for transfers between devices  40 us (44%)
  starting transfers between devices  31.9 us (35%)
  Pallas kernels  11.5 us (13%)
  local copies, waits for them, and re-layouts  5.43 us (6%)
    ppermute x31, waiting for transfers between devices, swap(): return lax.ppermute(block, BOTH, route)  33.1 us
    ppermute x31, starting transfers between devices, swap(): return lax.ppermute(block, BOTH, route)  23.7 us
    pallas_call x16, Pallas kernels, call(): pl.pallas_call(kernel, out_shape=[jax.ShapeDtypeStruct(s, d) for s, d in...  11.5 us
    ppermute x2, starting transfers between devices, from_plane_behind(): lax.ppermute(block, 'ctx', [(i, i + PLANE) for i in range(wide - PLANE)])  8.2 us
    ppermute x2, waiting for transfers between devices, from_plane_behind(): lax.ppermute(block, 'ctx', [(i, i + PLANE) for i in range(wide - PLANE)])  6.91 us
    unnamed x12, local copies, waits for them, and re-layouts  5.43 us
  transfers between devices with their start and end apart: 33, of which 21 were waited for; matrix products, arithmetic and copies ran while one was open for 0% of the time, Pallas kernels for 8%

profile of v5, /device:TPU:14, one launch (start us, length us, event | category | flops | bytes accessed | tf_op | source)
XLA Modules:
  0.0 89.0 jit_solution(13291184700952185531)
XLA Ops:
  0.0 1.0 %copy-done.2 = bf16[1,128,2048]{2,1,0:T(8,128)(2,1)S(1)} copy-done((bf16[1,128,2048]{2,1,0:T(8,128)(2,1)S(1)}, bf16[1,128,2048]{2,1,0:T(8,128)(2,1)}, u32[]{:S(2)}) %copy-start.2) | copy-done | bytes 524312
  1.1 0.6 collective-permute-start
  1.7 0.5 collective-permute-start.1
  2.2 2.4 %collective-permute-start.2 = (bf16[128,512]{1,0:T(8,128)(2,1)S(1)}, bf16[128,512]{1,0:T(8,128)(2,1)S(1)}, u32[]{:S(2)}, u32[]{:S(2)}) collective-permute-start(bf16[128,512]{1,0:T(8,128)(2,1)S(1)} %get-tuple-element.57), channel_id=1, source_target_pairs={{0,18},{1,19},{2,16},{3,17},{4,22},{5,23},{6,20},{7,21},{8,26},{9,... | collective-permute-start | bytes 393224 | tf_op jit(solution)/shard_map/ppermute | solution.py:28
  4.7 2.2 %copy-done = bf16[1,1024,2048]{2,1,0:T(8,128)(2,1)S(1)} copy-done((bf16[1,1024,2048]{2,1,0:T(8,128)(2,1)S(1)}, bf16[1,1024,2048]{2,1,0:T(8,128)(2,1)}, u32[]{:S(2)}) %copy-start) | copy-done | bytes 4194328
  6.9 2.2 %copy-done.5 = bf16[1,2048,1024]{2,1,0:T(8,128)(2,1)S(1)} copy-done((bf16[1,2048,1024]{2,1,0:T(8,128)(2,1)S(1)}, bf16[1,2048,1024]{2,1,0:T(8,128)(2,1)}, u32[]{:S(2)}) %copy-start.5) | copy-done | bytes 4194328
  9.1 0.4 shard_map.57
  9.5 0.9 %collective-permute-done.2.across_both = bf16[128,512]{1,0:T(8,128)(2,1)S(1)} collective-permute-done((bf16[128,512]{1,0:T(8,128)(2,1)S(1)}, bf16[128,512]{1,0:T(8,128)(2,1)S(1)}, u32[]{:S(2)}, u32[]{:S(2)}) %collective-permute-start.2) | collective-permute-done | bytes 131104 | tf_op jit(solution)/shard_map/ppermute | solution.py:28
  10.4 0.1 shard_map.58
  10.5 0.1 collective-permute-start.3
  10.6 0.6 collective-permute-start.12
  11.2 0.2 shard_map.55.refs_0_
  11.4 0.7 collective-permute-done.3.far_ref
  12.2 0.6 collective-permute-start.4
  12.7 2.6 %collective-permute-start.5 = (bf16[512,256]{1,0:T(8,128)(2,1)S(1)}, bf16[512,256]{1,0:T(8,128)(2,1)S(1)}, u32[]{:S(2)}, u32[]{:S(2)}) collective-permute-start(bf16[512,256]{1,0:T(8,128)(2,1)S(1)} %get-tuple-element.60.refs_0_), channel_id=1, source_target_pairs={{0,8},{1,9},{2,10},{3,11},{4,12},{5,13},{6,14},{7,15},{8,0},{9,1},... | collective-permute-start | bytes 786440 | tf_op jit(solution)/shard_map/ppermute | solution.py:28
  15.3 0.4 collective-permute-start.6
  15.8 10.6 %collective-permute-done.5.refs_2_ = bf16[512,256]{1,0:T(8,128)(2,1)S(1)} collective-permute-done((bf16[512,256]{1,0:T(8,128)(2,1)S(1)}, bf16[512,256]{1,0:T(8,128)(2,1)S(1)}, u32[]{:S(2)}, u32[]{:S(2)}) %collective-permute-start.5) | collective-permute-done | bytes 262176 | tf_op jit(solution)/shard_map/ppermute | solution.py:28
  26.4 1.1 %collective-permute-done.6.refs_1_ = bf16[512,256]{1,0:T(8,128)(2,1)S(1)} collective-permute-done((bf16[512,256]{1,0:T(8,128)(2,1)S(1)}, bf16[512,256]{1,0:T(8,128)(2,1)S(1)}, u32[]{:S(2)}, u32[]{:S(2)}) %collective-permute-start.6) | collective-permute-done | bytes 262176 | tf_op jit(solution)/shard_map/ppermute | solution.py:28
  27.5 0.6 collective-permute-start.10
  28.1 0.2 collective-permute-start.8
  28.3 0.9 collective-permute-done.12.block_ref.refs_13_
  29.2 0.7 collective-permute-start.13
  29.9 0.3 collective-permute-done.8.refs_3_
  30.2 1.4 %shard_map.60 = (bf16[512,2048]{1,0:T(8,128)(2,1)S(1)}, bf16[512,128]{1,0:T(8,128)(2,1)S(1)}, bf16[512,128]{1,0:T(8,128)(2,1)S(1)}, bf16[16,256]{1,0:T(8,128)(2,1)S(1)}) custom-call(bf16[128,2176]{1,0:T(8,128)(2,1)S(1)} %shard_map.55.refs_0_, bf16[128,2176]{1,0:T(8,128)(2,1)S(1)} %collective-permute-done.4.refs_1_, ...), custom_call_target="tpu_custom_call" | custom-call | bytes 3276800 | tf_op jit(solution)/shard_map/pallas_call | solution.py:49
  31.7 0.9 collective-permute-start.9
  32.5 1.2 %collective-permute-start.15 = (bf16[320,1024]{1,0:T(8,128)(2,1)S(1)}, bf16[320,1024]{1,0:T(8,128)(2,1)S(1)}, u32[]{:S(2)}, u32[]{:S(2)}) collective-permute-start(bf16[320,1024]{1,0:T(8,128)(2,1)S(1)} %get-tuple-element.77), channel_id=1, source_target_pairs={{0,16},{1,17},{2,18},{3,19},{4,20},{5,21},{6,22},{7,23},{8,24},{9,... | collective-permute-start | bytes 1966088 | tf_op jit(solution)/shard_map/ppermute | solution.py:28
  33.8 2.4 %collective-permute-done.10.refs_3_ = bf16[512,256]{1,0:T(8,128)(2,1)S(1)} collective-permute-done((bf16[512,256]{1,0:T(8,128)(2,1)S(1)}, bf16[512,256]{1,0:T(8,128)(2,1)S(1)}, u32[]{:S(2)}, u32[]{:S(2)}) %collective-permute-start.10) | collective-permute-done | bytes 262176 | tf_op jit(solution)/shard_map/ppermute | solution.py:28
  36.2 0.8 shard_map.61
  37.0 3.3 %collective-permute-start.11 = (bf16[400,256]{1,0:T(8,128)(2,1)S(1)}, bf16[400,256]{1,0:T(8,128)(2,1)S(1)}, u32[]{:S(2)}, u32[]{:S(2)}) collective-permute-start(bf16[400,256]{1,0:T(8,128)(2,1)S(1)} %get-tuple-element.70), channel_id=1, source_target_pairs={{0,4},{1,5},{2,6},{3,7},{4,8},{5,9},{6,10},{7,11},{8,12},{9,13},{1... | collective-permute-start | bytes 614408 | tf_op jit(solution)/shard_map/ppermute | solution.py:33
  40.3 0.6 collective-permute-start.23
  41.0 2.6 %collective-permute-start.24 = (bf16[512,256]{1,0:T(8,128)(2,1)S(1)}, bf16[512,256]{1,0:T(8,128)(2,1)S(1)}, u32[]{:S(2)}, u32[]{:S(2)}) collective-permute-start(bf16[512,256]{1,0:T(8,128)(2,1)S(1)} %get-tuple-element.83.refs_4_), channel_id=1, source_target_pairs={{0,4},{1,5},{2,6},{3,7},{4,0},{5,1},{6,2},{7,3},{8,12},{9,13},{10,... | collective-permute-start | bytes 786440 | tf_op jit(solution)/shard_map/ppermute | solution.py:28
  43.6 6.9 %collective-permute-done.11.refs_4_.past_ref = bf16[400,256]{1,0:T(8,128)(2,1)S(1)} collective-permute-done((bf16[400,256]{1,0:T(8,128)(2,1)S(1)}, bf16[400,256]{1,0:T(8,128)(2,1)S(1)}, u32[]{:S(2)}, u32[]{:S(2)}) %collective-permute-start.11) | collective-permute-done | bytes 204832 | tf_op jit(solution)/shard_map/ppermute | solution.py:33
  50.5 0.2 shard_map.62.bias_ref
  50.8 1.2 %shard_map.64.refs_4_ = bf16[512,128]{1,0:T(8,128)(2,1)S(1)} custom-call(bf16[512,128]{1,0:T(8,128)(2,1)S(1)} %get-tuple-element.65.mine_ref, bf16[512,128]{1,0:T(8,128)(2,1)S(1)} %collective-permute-done.9.got_ref, f32[4,128,512]{2,1,0:T(8,128)S(1)} %shard_map.62.bias_ref, bf16[512,256]{1,0:T(8,128)(2,1)S(1)} %get-tuple-element.75.kv_ref, ...), custom_call_target="tpu_custom_call" | custom-call | bytes 1777664 | tf_op jit(solution)/shard_map/pallas_call | solution.py:49
  52.0 1.8 %collective-permute-start.20 = (bf16[512,128]{1,0:T(8,128)(2,1)S(1)}, bf16[512,128]{1,0:T(8,128)(2,1)S(1)}, u32[]{:S(2)}, u32[]{:S(2)}) collective-permute-start(bf16[512,128]{1,0:T(8,128)(2,1)S(1)} %shard_map.64.refs_4_), channel_id=1, source_target_pairs={{0,18},{1,19},{2,16},{3,17},{4,22},{5,23},{6,20},{7,21},{8,26},{9,... | collective-permute-start | bytes 393224 | tf_op jit(solution)/shard_map/ppermute | solution.py:28
  53.8 1.3 %collective-permute-start.18 = (bf16[512,128]{1,0:T(8,128)(2,1)S(1)}, bf16[512,128]{1,0:T(8,128)(2,1)S(1)}, u32[]{:S(2)}, u32[]{:S(2)}) collective-permute-start(bf16[512,128]{1,0:T(8,128)(2,1)S(1)} %shard_map.64.refs_4_), channel_id=1, source_target_pairs={{0,16},{1,17},{2,18},{3,19},{4,20},{5,21},{6,22},{7,23},{8,24},{9,... | collective-permute-start | bytes 393224 | tf_op jit(solution)/shard_map/ppermute | solution.py:28
  55.0 0.5 collective-permute-start.16
  55.6 2.4 %collective-permute-done.20.refs_10_ = bf16[512,128]{1,0:T(8,128)(2,1)S(1)} collective-permute-done((bf16[512,128]{1,0:T(8,128)(2,1)S(1)}, bf16[512,128]{1,0:T(8,128)(2,1)S(1)}, u32[]{:S(2)}, u32[]{:S(2)}) %collective-permute-start.20) | collective-permute-done | bytes 131104 | tf_op jit(solution)/shard_map/ppermute | solution.py:28
  57.9 0.1 collective-permute-start.14
  58.0 0.5 collective-permute-start.21
  58.5 0.9 collective-permute-done.18.refs_8_
  59.4 0.6 collective-permute-done.16.refs_6_
  60.0 0.7 collective-permute-done.19.refs_9_
  60.7 0.6 collective-permute-done.17.refs_7_
  61.4 1.2 %shard_map.65.refs_0_ = bf16[512,512]{1,0:T(8,128)(2,1)S(1)} custom-call(bf16[128,2176]{1,0:T(8,128)(2,1)S(1)} %shard_map.55.refs_0_, bf16[128,2176]{1,0:T(8,128)(2,1)S(1)} %collective-permute-done.4.refs_1_, bf16[128,2176]{1,0:T(8,128)(2,1)S(1)} %collective-permute-done.7.refs_2_, bf16[128,2176]{1,0:T(8,128)(2,1)S(1)} %collective-permute-done.8.refs_3_, ...), custom_call_target="tpu_custom_call" | custom-call | bytes 9568256 | tf_op jit(solution)/shard_map/pallas_call | solution.py:49
  62.6 0.2 collective-permute-start.22
  62.8 1.2 %shard_map.66.refs_1_ = bf16[512,512]{1,0:T(8,128)(2,1)S(1)} custom-call(bf16[128,2176]{1,0:T(8,128)(2,1)S(1)} %shard_map.55.refs_0_, bf16[128,2176]{1,0:T(8,128)(2,1)S(1)} %collective-permute-done.4.refs_1_, bf16[128,2176]{1,0:T(8,128)(2,1)S(1)} %collective-permute-done.7.refs_2_, bf16[128,2176]{1,0:T(8,128)(2,1)S(1)} %collective-permute-done.8.refs_3_, ...), custom_call_target="tpu_custom_call" | custom-call | bytes 9568256 | tf_op jit(solution)/shard_map/pallas_call | solution.py:49
  64.0 0.3 collective-permute-done.25.refs_7_
  64.3 0.1 collective-permute-start.26
  64.4 0.1 collective-permute-done.22.refs_2_
  64.5 1.7 %collective-permute-done.26.refs_3_ = bf16[512,512]{1,0:T(8,128)(2,1)S(1)} collective-permute-done((bf16[512,512]{1,0:T(8,128)(2,1)S(1)}, bf16[512,512]{1,0:T(8,128)(2,1)S(1)}, u32[]{:S(2)}, u32[]{:S(2)}) %collective-permute-start.26) | collective-permute-done | bytes 524320 | tf_op jit(solution)/shard_map/ppermute | solution.py:28
  66.2 1.9 %shard_map.67 = (bf16[128,2048]{1,0:T(8,128)(2,1)S(1)}, bf16[512,128]{1,0:T(8,128)(2,1)S(1)}, bf16[512,128]{1,0:T(8,128)(2,1)S(1)}, bf16[512,256]{1,0:T(8,128)(2,1)S(1)}, bf16[384,256]{1,0:T(8,128)(2,1)S(1)}) custom-call(bf16[512,512]{1,0:T(8,128)(2,1)S(1)} %shard_map.65.refs_0_, bf16[512,512]{1,0:T(8,128)(2,1)S(1)} %shard_map.66.refs_1_, ...), custom_call_target="tpu_custom_call" | custom-call | bytes 4194304 | tf_op jit(solution)/shard_map/pallas_call | solution.py:49
  68.1 4.9 %collective-permute-start.28 = (bf16[384,256]{1,0:T(8,128)(2,1)S(1)}, bf16[384,256]{1,0:T(8,128)(2,1)S(1)}, u32[]{:S(2)}, u32[]{:S(2)}) collective-permute-start(bf16[384,256]{1,0:T(8,128)(2,1)S(1)} %get-tuple-element.89), channel_id=1, source_target_pairs={{0,4},{1,5},{2,6},{3,7},{4,8},{5,9},{6,10},{7,11},{8,12},{9,13},{1... | collective-permute-start | bytes 589832 | tf_op jit(solution)/shard_map/ppermute | solution.py:33
  73.0 0.8 collective-permute-start.27
  73.8 4.5 %collective-permute-done.27.got_ref = bf16[512,128]{1,0:T(8,128)(2,1)S(1)} collective-permute-done((bf16[512,128]{1,0:T(8,128)(2,1)S(1)}, bf16[512,128]{1,0:T(8,128)(2,1)S(1)}, u32[]{:S(2)}, u32[]{:S(2)}) %collective-permute-start.27) | collective-permute-done | bytes 131104 | tf_op jit(solution)/shard_map/ppermute | solution.py:28
  78.3 1.2 %shard_map.68 = (bf16[256,128]{1,0:T(8,128)(2,1)S(1)}, bf16[256,128]{1,0:T(8,128)(2,1)S(1)}) custom-call(bf16[512,128]{1,0:T(8,128)(2,1)S(1)} %get-tuple-element.86.mine_ref, bf16[512,128]{1,0:T(8,128)(2,1)S(1)} %collective-permute-done.27.got_ref, f32[4,128,512]{2,1,0:T(8,128)S(1)} %shard_map.62.bias_ref, bf16[512,256]{1,0:T(8,128)(2,1)S(1)} %get-tuple-element.88.kv_ref, ...), custom_call_target="tpu_custom_call" | custom-call | flops 134217728 | bytes 1769472 | tf_op jit(solution)/shard_map/pallas_call | solution.py:49
  79.6 1.2 %collective-permute-done.29.got_ref = bf16[256,128]{1,0:T(8,128)(2,1)S(1)} collective-permute-done((bf16[256,128]{1,0:T(8,128)(2,1)S(1)}, bf16[256,128]{1,0:T(8,128)(2,1)S(1)}, u32[]{:S(2)}, u32[]{:S(2)}) %collective-permute-start.29) | collective-permute-done | bytes 65568 | tf_op jit(solution)/shard_map/ppermute | solution.py:28
  80.8 1.8 %collective-permute-start.32 = (bf16[256,128]{1,0:T(8,128)(2,1)S(1)}, bf16[256,128]{1,0:T(8,128)(2,1)S(1)}, u32[]{:S(2)}, u32[]{:S(2)}) collective-permute-start(bf16[256,128]{1,0:T(8,128)(2,1)S(1)} %get-tuple-element.93), channel_id=1, source_target_pairs={{0,18},{1,19},{2,16},{3,17},{4,22},{5,23},{6,20},{7,21},{8,26},{9,... | collective-permute-start | bytes 196616 | tf_op jit(solution)/shard_map/ppermute | solution.py:28
  82.7 0.5 collective-permute-start.30
  83.2 1.2 %collective-permute-start.31 = (bf16[256,128]{1,0:T(8,128)(2,1)S(1)}, bf16[256,128]{1,0:T(8,128)(2,1)S(1)}, u32[]{:S(2)}, u32[]{:S(2)}) collective-permute-start(bf16[256,128]{1,0:T(8,128)(2,1)S(1)} %get-tuple-element.92.refs_0_), channel_id=1, source_target_pairs={{0,16},{1,17},{2,18},{3,19},{4,20},{5,21},{6,22},{7,23},{8,24},{9,... | collective-permute-start | bytes 196616 | tf_op jit(solution)/shard_map/ppermute | solution.py:28
  84.4 1.7 %collective-permute-done.32.refs_3_ = bf16[256,128]{1,0:T(8,128)(2,1)S(1)} collective-permute-done((bf16[256,128]{1,0:T(8,128)(2,1)S(1)}, bf16[256,128]{1,0:T(8,128)(2,1)S(1)}, u32[]{:S(2)}, u32[]{:S(2)}) %collective-permute-start.32) | collective-permute-done | bytes 65568 | tf_op jit(solution)/shard_map/ppermute | solution.py:28
  86.1 1.2 %collective-permute-done.30.refs_1_ = bf16[256,128]{1,0:T(8,128)(2,1)S(1)} collective-permute-done((bf16[256,128]{1,0:T(8,128)(2,1)S(1)}, bf16[256,128]{1,0:T(8,128)(2,1)S(1)}, u32[]{:S(2)}, u32[]{:S(2)}) %collective-permute-start.30) | collective-permute-done | bytes 65568 | tf_op jit(solution)/shard_map/ppermute | solution.py:28
  87.4 0.1 collective-permute-done.31.refs_2_
  87.5 1.6 %shard_map.70 = bf16[128,2048]{1,0:T(8,128)(2,1)} custom-call(bf16[256,128]{1,0:T(8,128)(2,1)S(1)} %get-tuple-element.92.refs_0_, bf16[256,128]{1,0:T(8,128)(2,1)S(1)} %collective-permute-done.30.refs_1_, bf16[256,128]{1,0:T(8,128)(2,1)S(1)} %collective-permute-done.31.refs_2_, bf16[256,128]{1,0:T(8,128)(2,1)S(1)} %collective-permute-done.32.refs_3_, ...), custom_call_target="tpu_custom_call" | custom-call | flops 536870912 | bytes 4980736 | tf_op jit(solution)/shard_map/pallas_call | solution.py:49
  (30 shorter events, 0.3 us)
Async XLA Ops:
  0.0 1.0 %copy-start.2 = (bf16[1,128,2048]{2,1,0:T(8,128)(2,1)S(1)}, bf16[1,128,2048]{2,1,0:T(8,128)(2,1)}, u32[]{:S(2)}) copy-start(bf16[1,128,2048]{2,1,0:T(8,128)(2,1)} %param.8) | copy-start | bytes 1572868
  1.1 8.4 %collective-permute-start = (bf16[128,512]{1,0:T(8,128)(2,1)S(1)}, bf16[128,512]{1,0:T(8,128)(2,1)S(1)}, u32[]{:S(2)}, u32[]{:S(2)}) collective-permute-start(bf16[128,512]{1,0:T(8,128)(2,1)S(1)} %get-tuple-element.55), channel_id=1, source_target_pairs={{0,2},{1,3},{2,0},{3,1},{4,6},{5,7},{6,4},{7,5},{8,10},{9,11},{10,... | collective-permute-start | bytes 393224 | tf_op jit(solution)/shard_map/ppermute | solution.py:28
  1.7 7.8 %collective-permute-start.1 = (bf16[128,512]{1,0:T(8,128)(2,1)S(1)}, bf16[128,512]{1,0:T(8,128)(2,1)S(1)}, u32[]{:S(2)}, u32[]{:S(2)}) collective-permute-start(bf16[128,512]{1,0:T(8,128)(2,1)S(1)} %get-tuple-element.56), channel_id=1, source_target_pairs={{0,16},{1,17},{2,18},{3,19},{4,20},{5,21},{6,22},{7,23},{8,24},{9,... | collective-permute-start | bytes 393224 | tf_op jit(solution)/shard_map/ppermute | solution.py:28
  2.2 8.2 %collective-permute-start.2 = (bf16[128,512]{1,0:T(8,128)(2,1)S(1)}, bf16[128,512]{1,0:T(8,128)(2,1)S(1)}, u32[]{:S(2)}, u32[]{:S(2)}) collective-permute-start(bf16[128,512]{1,0:T(8,128)(2,1)S(1)} %get-tuple-element.57), channel_id=1, source_target_pairs={{0,18},{1,19},{2,16},{3,17},{4,22},{5,23},{6,20},{7,21},{8,26},{9,... | collective-permute-start | bytes 393224 | tf_op jit(solution)/shard_map/ppermute | solution.py:28
  4.7 2.2 %copy-start = (bf16[1,1024,2048]{2,1,0:T(8,128)(2,1)S(1)}, bf16[1,1024,2048]{2,1,0:T(8,128)(2,1)}, u32[]{:S(2)}) copy-start(bf16[1,1024,2048]{2,1,0:T(8,128)(2,1)} %param.9) | copy-start | bytes 12582916
  6.9 2.2 %copy-start.5 = (bf16[1,2048,1024]{2,1,0:T(8,128)(2,1)S(1)}, bf16[1,2048,1024]{2,1,0:T(8,128)(2,1)}, u32[]{:S(2)}) copy-start(bf16[1,2048,1024]{2,1,0:T(8,128)(2,1)} %param.7) | copy-start | bytes 12582916
  9.0 2.2 %copy-start.3 = (bf16[1,128,2048]{2,1,0:T(8,128)(2,1)S(1)}, bf16[1,128,2048]{2,1,0:T(8,128)(2,1)}, u32[]{:S(2)}) copy-start(bf16[1,128,2048]{2,1,0:T(8,128)(2,1)} %param.5) | copy-start | bytes 1572868
  9.0 2.2 %copy-start.4 = (s32[1,128]{1,0:T(1,128)S(1)}, s32[1,128]{1,0:T(1,128)}, u32[]{:S(2)}) copy-start(s32[1,128]{1,0:T(1,128)} %id_ref.1) | copy-start | bytes 1540
  10.5 1.6 %collective-permute-start.3 = (bf16[2,256,256]{2,1,0:T(8,128)(2,1)S(1)}, bf16[2,256,256]{2,1,0:T(8,128)(2,1)S(1)}, u32[]{:S(2)}, u32[]{:S(2)}) collective-permute-start(bf16[2,256,256]{2,1,0:T(8,128)(2,1)S(1)} %get-tuple-element.59), channel_id=1, source_target_pairs={{0,1},{1,0},{2,3},{3,2},{4,5},{5,4},{6,7},{7,6},{8,9},{9,8},{10,11... | collective-permute-start | bytes 786440 | tf_op jit(solution)/shard_map/ppermute | solution.py:28
  10.6 18.6 %collective-permute-start.12 = (bf16[352,1024]{1,0:T(8,128)(2,1)S(1)}, bf16[352,1024]{1,0:T(8,128)(2,1)S(1)}, u32[]{:S(2)}, u32[]{:S(2)}) collective-permute-start(bf16[352,1024]{1,0:T(8,128)(2,1)S(1)} %get-tuple-element.73), channel_id=1, source_target_pairs={{0,16},{1,17},{2,18},{3,19},{4,20},{5,21},{6,22},{7,23},{8,24},{9,... | collective-permute-start | bytes 2162696 | tf_op jit(solution)/shard_map/ppermute | solution.py:28
  12.2 15.9 %collective-permute-start.4 = (bf16[128,2176]{1,0:T(8,128)(2,1)S(1)}, bf16[128,2176]{1,0:T(8,128)(2,1)S(1)}, u32[]{:S(2)}, u32[]{:S(2)}) collective-permute-start(bf16[128,2176]{1,0:T(8,128)(2,1)S(1)} %shard_map.55.refs_0_), channel_id=1, source_target_pairs={{0,2},{1,3},{2,0},{3,1},{4,6},{5,7},{6,4},{7,5},{8,10},{9,11},{10,... | collective-permute-start | bytes 1671176 | tf_op jit(solution)/shard_map/ppermute | solution.py:28
  12.7 13.7 %collective-permute-start.5 = (bf16[512,256]{1,0:T(8,128)(2,1)S(1)}, bf16[512,256]{1,0:T(8,128)(2,1)S(1)}, u32[]{:S(2)}, u32[]{:S(2)}) collective-permute-start(bf16[512,256]{1,0:T(8,128)(2,1)S(1)} %get-tuple-element.60.refs_0_), channel_id=1, source_target_pairs={{0,8},{1,9},{2,10},{3,11},{4,12},{5,13},{6,14},{7,15},{8,0},{9,1},... | collective-permute-start | bytes 786440 | tf_op jit(solution)/shard_map/ppermute | solution.py:28
  15.3 12.2 %collective-permute-start.6 = (bf16[512,256]{1,0:T(8,128)(2,1)S(1)}, bf16[512,256]{1,0:T(8,128)(2,1)S(1)}, u32[]{:S(2)}, u32[]{:S(2)}) collective-permute-start(bf16[512,256]{1,0:T(8,128)(2,1)S(1)} %get-tuple-element.60.refs_0_), channel_id=1, source_target_pairs={{0,4},{1,5},{2,6},{3,7},{4,0},{5,1},{6,2},{7,3},{8,12},{9,13},{10,... | collective-permute-start | bytes 786440 | tf_op jit(solution)/shard_map/ppermute | solution.py:28
  27.5 2.5 %collective-permute-start.7 = (bf16[128,2176]{1,0:T(8,128)(2,1)S(1)}, bf16[128,2176]{1,0:T(8,128)(2,1)S(1)}, u32[]{:S(2)}, u32[]{:S(2)}) collective-permute-start(bf16[128,2176]{1,0:T(8,128)(2,1)S(1)} %shard_map.55.refs_0_), channel_id=1, source_target_pairs={{0,1},{1,0},{2,3},{3,2},{4,5},{5,4},{6,7},{7,6},{8,9},{9,8},{10,11... | collective-permute-start | bytes 1671176 | tf_op jit(solution)/shard_map/ppermute | solution.py:28
  27.5 8.7 %collective-permute-start.10 = (bf16[512,256]{1,0:T(8,128)(2,1)S(1)}, bf16[512,256]{1,0:T(8,128)(2,1)S(1)}, u32[]{:S(2)}, u32[]{:S(2)}) collective-permute-start(bf16[512,256]{1,0:T(8,128)(2,1)S(1)} %collective-permute-done.5.refs_2_), channel_id=1, source_target_pairs={{0,4},{1,5},{2,6},{3,7},{4,0},{5,1},{6,2},{7,3},{8,12},{9,13},{10,... | collective-permute-start | bytes 786440 | tf_op jit(solution)/shard_map/ppermute | solution.py:28
  28.1 2.2 %collective-permute-start.8 = (bf16[128,2176]{1,0:T(8,128)(2,1)S(1)}, bf16[128,2176]{1,0:T(8,128)(2,1)S(1)}, u32[]{:S(2)}, u32[]{:S(2)}) collective-permute-start(bf16[128,2176]{1,0:T(8,128)(2,1)S(1)} %collective-permute-done.4.refs_1_), channel_id=1, source_target_pairs={{0,1},{1,0},{2,3},{3,2},{4,5},{5,4},{6,7},{7,6},{8,9},{9,8},{10,11... | collective-permute-start | bytes 1671176 | tf_op jit(solution)/shard_map/ppermute | solution.py:28
  29.2 21.6 %collective-permute-start.13 = (bf16[352,1024]{1,0:T(8,128)(2,1)S(1)}, bf16[352,1024]{1,0:T(8,128)(2,1)S(1)}, u32[]{:S(2)}, u32[]{:S(2)}) collective-permute-start(bf16[352,1024]{1,0:T(8,128)(2,1)S(1)} %shard_map.63), channel_id=1, source_target_pairs={{0,2},{1,3},{2,0},{3,1},{4,6},{5,7},{6,4},{7,5},{8,10},{9,11},{10,... | collective-permute-start | bytes 2162696 | tf_op jit(solution)/shard_map/ppermute | solution.py:28
  31.7 9.3 %collective-permute-start.9 = (bf16[512,128]{1,0:T(8,128)(2,1)S(1)}, bf16[512,128]{1,0:T(8,128)(2,1)S(1)}, u32[]{:S(2)}, u32[]{:S(2)}) collective-permute-start(bf16[512,128]{1,0:T(8,128)(2,1)S(1)} %get-tuple-element.66), channel_id=1, source_target_pairs={{0,16},{1,17},{2,18},{3,19},{4,20},{5,21},{6,22},{7,23},{8,24},{9,... | collective-permute-start | bytes 393224 | tf_op jit(solution)/shard_map/ppermute | solution.py:28
  32.5 22.5 %collective-permute-start.15 = (bf16[320,1024]{1,0:T(8,128)(2,1)S(1)}, bf16[320,1024]{1,0:T(8,128)(2,1)S(1)}, u32[]{:S(2)}, u32[]{:S(2)}) collective-permute-start(bf16[320,1024]{1,0:T(8,128)(2,1)S(1)} %get-tuple-element.77), channel_id=1, source_target_pairs={{0,16},{1,17},{2,18},{3,19},{4,20},{5,21},{6,22},{7,23},{8,24},{9,... | collective-permute-start | bytes 1966088 | tf_op jit(solution)/shard_map/ppermute | solution.py:28
  37.0 24.4 %copy-start.1 = (bf16[1,1024,2048]{2,1,0:T(8,128)(2,1)S(1)}, bf16[1,1024,2048]{2,1,0:T(8,128)(2,1)}, u32[]{:S(2)}) copy-start(bf16[1,1024,2048]{2,1,0:T(8,128)(2,1)} %param.9) | copy-start | bytes 12582916
  37.0 13.5 %collective-permute-start.11 = (bf16[400,256]{1,0:T(8,128)(2,1)S(1)}, bf16[400,256]{1,0:T(8,128)(2,1)S(1)}, u32[]{:S(2)}, u32[]{:S(2)}) collective-permute-start(bf16[400,256]{1,0:T(8,128)(2,1)S(1)} %get-tuple-element.70), channel_id=1, source_target_pairs={{0,4},{1,5},{2,6},{3,7},{4,8},{5,9},{6,10},{7,11},{8,12},{9,13},{1... | collective-permute-start | bytes 614408 | tf_op jit(solution)/shard_map/ppermute | solution.py:33
  40.3 17.6 %collective-permute-start.23 = (bf16[512,256]{1,0:T(8,128)(2,1)S(1)}, bf16[512,256]{1,0:T(8,128)(2,1)S(1)}, u32[]{:S(2)}, u32[]{:S(2)}) collective-permute-start(bf16[512,256]{1,0:T(8,128)(2,1)S(1)} %get-tuple-element.83.refs_4_), channel_id=1, source_target_pairs={{0,8},{1,9},{2,10},{3,11},{4,12},{5,13},{6,14},{7,15},{8,0},{9,1},... | collective-permute-start | bytes 786440 | tf_op jit(solution)/shard_map/ppermute | solution.py:28
  41.0 17.0 %collective-permute-start.24 = (bf16[512,256]{1,0:T(8,128)(2,1)S(1)}, bf16[512,256]{1,0:T(8,128)(2,1)S(1)}, u32[]{:S(2)}, u32[]{:S(2)}) collective-permute-start(bf16[512,256]{1,0:T(8,128)(2,1)S(1)} %get-tuple-element.83.refs_4_), channel_id=1, source_target_pairs={{0,4},{1,5},{2,6},{3,7},{4,0},{5,1},{6,2},{7,3},{8,12},{9,13},{10,... | collective-permute-start | bytes 786440 | tf_op jit(solution)/shard_map/ppermute | solution.py:28
  52.0 5.9 %collective-permute-start.20 = (bf16[512,128]{1,0:T(8,128)(2,1)S(1)}, bf16[512,128]{1,0:T(8,128)(2,1)S(1)}, u32[]{:S(2)}, u32[]{:S(2)}) collective-permute-start(bf16[512,128]{1,0:T(8,128)(2,1)S(1)} %shard_map.64.refs_4_), channel_id=1, source_target_pairs={{0,18},{1,19},{2,16},{3,17},{4,22},{5,23},{6,20},{7,21},{8,26},{9,... | collective-permute-start | bytes 393224 | tf_op jit(solution)/shard_map/ppermute | solution.py:28
  53.8 5.6 %collective-permute-start.18 = (bf16[512,128]{1,0:T(8,128)(2,1)S(1)}, bf16[512,128]{1,0:T(8,128)(2,1)S(1)}, u32[]{:S(2)}, u32[]{:S(2)}) collective-permute-start(bf16[512,128]{1,0:T(8,128)(2,1)S(1)} %shard_map.64.refs_4_), channel_id=1, source_target_pairs={{0,16},{1,17},{2,18},{3,19},{4,20},{5,21},{6,22},{7,23},{8,24},{9,... | collective-permute-start | bytes 393224 | tf_op jit(solution)/shard_map/ppermute | solution.py:28
  55.0 5.0 %collective-permute-start.16 = (bf16[512,128]{1,0:T(8,128)(2,1)S(1)}, bf16[512,128]{1,0:T(8,128)(2,1)S(1)}, u32[]{:S(2)}, u32[]{:S(2)}) collective-permute-start(bf16[512,128]{1,0:T(8,128)(2,1)S(1)} %shard_map.64.refs_4_), channel_id=1, source_target_pairs={{0,2},{1,3},{2,0},{3,1},{4,6},{5,7},{6,4},{7,5},{8,10},{9,11},{10,... | collective-permute-start | bytes 393224 | tf_op jit(solution)/shard_map/ppermute | solution.py:28
  57.9 6.4 %collective-permute-start.25 = (bf16[512,256]{1,0:T(8,128)(2,1)S(1)}, bf16[512,256]{1,0:T(8,128)(2,1)S(1)}, u32[]{:S(2)}, u32[]{:S(2)}) collective-permute-start(bf16[512,256]{1,0:T(8,128)(2,1)S(1)} %collective-permute-done.23.refs_6_), channel_id=1, source_target_pairs={{0,4},{1,5},{2,6},{3,7},{4,0},{5,1},{6,2},{7,3},{8,12},{9,13},{10,... | collective-permute-start | bytes 786440 | tf_op jit(solution)/shard_map/ppermute | solution.py:28
  57.9 2.1 %collective-permute-start.14 = (bf16[512,128]{1,0:T(8,128)(2,1)S(1)}, bf16[512,128]{1,0:T(8,128)(2,1)S(1)}, u32[]{:S(2)}, u32[]{:S(2)}) collective-permute-start(bf16[512,128]{1,0:T(8,128)(2,1)S(1)} %shard_map.64.refs_4_), channel_id=1, source_target_pairs={{0,1},{1,0},{2,3},{3,2},{4,5},{5,4},{6,7},{7,6},{8,9},{9,8},{10,11... | collective-permute-start | bytes 393224 | tf_op jit(solution)/shard_map/ppermute | solution.py:28
  58.0 2.7 %collective-permute-start.21 = (bf16[512,128]{1,0:T(8,128)(2,1)S(1)}, bf16[512,128]{1,0:T(8,128)(2,1)S(1)}, u32[]{:S(2)}, u32[]{:S(2)}) collective-permute-start(bf16[512,128]{1,0:T(8,128)(2,1)S(1)} %collective-permute-done.20.refs_10_), channel_id=1, source_target_pairs={{0,1},{1,0},{2,3},{3,2},{4,5},{5,4},{6,7},{7,6},{8,9},{9,8},{10,11... | collective-permute-start | bytes 393224 | tf_op jit(solution)/shard_map/ppermute | solution.py:28
  59.4 1.3 %collective-permute-start.19 = (bf16[512,128]{1,0:T(8,128)(2,1)S(1)}, bf16[512,128]{1,0:T(8,128)(2,1)S(1)}, u32[]{:S(2)}, u32[]{:S(2)}) collective-permute-start(bf16[512,128]{1,0:T(8,128)(2,1)S(1)} %collective-permute-done.18.refs_8_), channel_id=1, source_target_pairs={{0,1},{1,0},{2,3},{3,2},{4,5},{5,4},{6,7},{7,6},{8,9},{9,8},{10,11... | collective-permute-start | bytes 393224 | tf_op jit(solution)/shard_map/ppermute | solution.py:28
  60.0 1.3 %collective-permute-start.17 = (bf16[512,128]{1,0:T(8,128)(2,1)S(1)}, bf16[512,128]{1,0:T(8,128)(2,1)S(1)}, u32[]{:S(2)}, u32[]{:S(2)}) collective-permute-start(bf16[512,128]{1,0:T(8,128)(2,1)S(1)} %collective-permute-done.16.refs_6_), channel_id=1, source_target_pairs={{0,1},{1,0},{2,3},{3,2},{4,5},{5,4},{6,7},{7,6},{8,9},{9,8},{10,11... | collective-permute-start | bytes 393224 | tf_op jit(solution)/shard_map/ppermute | solution.py:28
  62.6 2.0 %collective-permute-start.22 = (bf16[512,512]{1,0:T(8,128)(2,1)S(1)}, bf16[512,512]{1,0:T(8,128)(2,1)S(1)}, u32[]{:S(2)}, u32[]{:S(2)}) collective-permute-start(bf16[512,512]{1,0:T(8,128)(2,1)S(1)} %shard_map.65.refs_0_), channel_id=1, source_target_pairs={{0,1},{1,0},{2,3},{3,2},{4,5},{5,4},{6,7},{7,6},{8,9},{9,8},{10,11... | collective-permute-start | bytes 1572872 | tf_op jit(solution)/shard_map/ppermute | solution.py:28
  64.3 1.9 %collective-permute-start.26 = (bf16[512,512]{1,0:T(8,128)(2,1)S(1)}, bf16[512,512]{1,0:T(8,128)(2,1)S(1)}, u32[]{:S(2)}, u32[]{:S(2)}) collective-permute-start(bf16[512,512]{1,0:T(8,128)(2,1)S(1)} %shard_map.66.refs_1_), channel_id=1, source_target_pairs={{0,1},{1,0},{2,3},{3,2},{4,5},{5,4},{6,7},{7,6},{8,9},{9,8},{10,11... | collective-permute-start | bytes 1572872 | tf_op jit(solution)/shard_map/ppermute | solution.py:28
  68.1 10.2 %collective-permute-start.28 = (bf16[384,256]{1,0:T(8,128)(2,1)S(1)}, bf16[384,256]{1,0:T(8,128)(2,1)S(1)}, u32[]{:S(2)}, u32[]{:S(2)}) collective-permute-start(bf16[384,256]{1,0:T(8,128)(2,1)S(1)} %get-tuple-element.89), channel_id=1, source_target_pairs={{0,4},{1,5},{2,6},{3,7},{4,8},{5,9},{6,10},{7,11},{8,12},{9,13},{1... | collective-permute-start | bytes 589832 | tf_op jit(solution)/shard_map/ppermute | solution.py:33
  73.0 5.3 %collective-permute-start.27 = (bf16[512,128]{1,0:T(8,128)(2,1)S(1)}, bf16[512,128]{1,0:T(8,128)(2,1)S(1)}, u32[]{:S(2)}, u32[]{:S(2)}) collective-permute-start(bf16[512,128]{1,0:T(8,128)(2,1)S(1)} %get-tuple-element.87), channel_id=1, source_target_pairs={{0,16},{1,17},{2,18},{3,19},{4,20},{5,21},{6,22},{7,23},{8,24},{9,... | collective-permute-start | bytes 393224 | tf_op jit(solution)/shard_map/ppermute | solution.py:28
  79.5 1.3 %collective-permute-start.29 = (bf16[256,128]{1,0:T(8,128)(2,1)S(1)}, bf16[256,128]{1,0:T(8,128)(2,1)S(1)}, u32[]{:S(2)}, u32[]{:S(2)}) collective-permute-start(bf16[256,128]{1,0:T(8,128)(2,1)S(1)} %get-tuple-element.91), channel_id=1, source_target_pairs={{0,1},{1,0},{2,3},{3,2},{4,5},{5,4},{6,7},{7,6},{8,9},{9,8},{10,11... | collective-permute-start | bytes 196616 | tf_op jit(solution)/shard_map/ppermute | solution.py:28
  80.8 5.3 %collective-permute-start.32 = (bf16[256,128]{1,0:T(8,128)(2,1)S(1)}, bf16[256,128]{1,0:T(8,128)(2,1)S(1)}, u32[]{:S(2)}, u32[]{:S(2)}) collective-permute-start(bf16[256,128]{1,0:T(8,128)(2,1)S(1)} %get-tuple-element.93), channel_id=1, source_target_pairs={{0,18},{1,19},{2,16},{3,17},{4,22},{5,23},{6,20},{7,21},{8,26},{9,... | collective-permute-start | bytes 196616 | tf_op jit(solution)/shard_map/ppermute | solution.py:28
  82.7 4.7 %collective-permute-start.30 = (bf16[256,128]{1,0:T(8,128)(2,1)S(1)}, bf16[256,128]{1,0:T(8,128)(2,1)S(1)}, u32[]{:S(2)}, u32[]{:S(2)}) collective-permute-start(bf16[256,128]{1,0:T(8,128)(2,1)S(1)} %get-tuple-element.93), channel_id=1, source_target_pairs={{0,2},{1,3},{2,0},{3,1},{4,6},{5,7},{6,4},{7,5},{8,10},{9,11},{10,... | collective-permute-start | bytes 196616 | tf_op jit(solution)/shard_map/ppermute | solution.py:28
  83.2 4.3 %collective-permute-start.31 = (bf16[256,128]{1,0:T(8,128)(2,1)S(1)}, bf16[256,128]{1,0:T(8,128)(2,1)S(1)}, u32[]{:S(2)}, u32[]{:S(2)}) collective-permute-start(bf16[256,128]{1,0:T(8,128)(2,1)S(1)} %get-tuple-element.92.refs_0_), channel_id=1, source_target_pairs={{0,16},{1,17},{2,18},{3,19},{4,20},{5,21},{6,22},{7,23},{8,24},{9,... | collective-permute-start | bytes 196616 | tf_op jit(solution)/shard_map/ppermute | solution.py:28

commit v6 on v5

--- a/solution.py
+++ b/solution.py
@@ -420,7 +420,7 @@
     out_across = swap(sent_on, 0, 2)
     early = along_planes(early)
     early[1] = swap(early[0], 0, PLANE)
-    ready = token_of(token_of(early[2], cost=7 * 10**8), early[1], cost=24 * 10**8)
+    ready = token_of(token_of(early[2], cost=4 * 10**8), early[1], cost=35 * 10**8)
     early[3] = swap(after(early[2], ready), 0, PLANE)
     pieces = len(early)
 

time: 90.3 us -> 89.2 us (0.988)
  waiting for transfers between devices: 40 us -> 38.9 us
    ppermute x31, waiting for transfers between devices: 33.1 us -> 32 us  [swap(): return lax.ppermute(block, BOTH, route)]
  transfers between devices with their start and end apart: 33 -> 33, of which waited for: 21 -> 19; matrix products, arithmetic and copies ran while one was open for 0% -> 0% of each run, Pallas kernels for 8% -> 8%
where the time goes in v6:
time: 89.2 us; the launch traced here: 88.6 us
  waiting for transfers between devices  38.9 us (44%)
  starting transfers between devices  32.5 us (36%)
  Pallas kernels  11.5 us (13%)
  local copies, waits for them, and re-layouts  5.43 us (6%)
    ppermute x31, waiting for transfers between devices, swap(): return lax.ppermute(block, BOTH, route)  32 us
    ppermute x31, starting transfers between devices, swap(): return lax.ppermute(block, BOTH, route)  24.3 us
    pallas_call x16, Pallas kernels, call(): pl.pallas_call(kernel, out_shape=[jax.ShapeDtypeStruct(s, d) for s, d in...  11.5 us
    ppermute x2, starting transfers between devices, from_plane_behind(): lax.ppermute(block, 'ctx', [(i, i + PLANE) for i in range(wide - PLANE)])  8.19 us
    ppermute x2, waiting for transfers between devices, from_plane_behind(): lax.ppermute(block, 'ctx', [(i, i + PLANE) for i in range(wide - PLANE)])  6.9 us
    unnamed x12, local copies, waits for them, and re-layouts  5.43 us
  transfers between devices with their start and end apart: 33, of which 19 were waited for; matrix products, arithmetic and copies ran while one was open for 0% of the time, Pallas kernels for 8%

profile of v6, /device:TPU:14, one launch (start us, length us, event | category | flops | bytes accessed | tf_op | source)
XLA Modules:
  0.0 88.6 jit_solution(14119067093930896848)
XLA Ops:
  0.0 1.0 %copy-done.2 = bf16[1,128,2048]{2,1,0:T(8,128)(2,1)S(1)} copy-done((bf16[1,128,2048]{2,1,0:T(8,128)(2,1)S(1)}, bf16[1,128,2048]{2,1,0:T(8,128)(2,1)}, u32[]{:S(2)}) %copy-start.2) | copy-done | bytes 524312
  1.0 0.1 shard_map.56
  1.1 0.6 collective-permute-start
  1.7 0.5 collective-permute-start.1
  2.2 2.4 %collective-permute-start.2 = (bf16[128,512]{1,0:T(8,128)(2,1)S(1)}, bf16[128,512]{1,0:T(8,128)(2,1)S(1)}, u32[]{:S(2)}, u32[]{:S(2)}) collective-permute-start(bf16[128,512]{1,0:T(8,128)(2,1)S(1)} %get-tuple-element.57), channel_id=1, source_target_pairs={{0,18},{1,19},{2,16},{3,17},{4,22},{5,23},{6,20},{7,21},{8,26},{9,... | collective-permute-start | bytes 393224 | tf_op jit(solution)/shard_map/ppermute | solution.py:28
  4.7 2.2 %copy-done = bf16[1,1024,2048]{2,1,0:T(8,128)(2,1)S(1)} copy-done((bf16[1,1024,2048]{2,1,0:T(8,128)(2,1)S(1)}, bf16[1,1024,2048]{2,1,0:T(8,128)(2,1)}, u32[]{:S(2)}) %copy-start) | copy-done | bytes 4194328
  6.9 2.2 %copy-done.5 = bf16[1,2048,1024]{2,1,0:T(8,128)(2,1)S(1)} copy-done((bf16[1,2048,1024]{2,1,0:T(8,128)(2,1)S(1)}, bf16[1,2048,1024]{2,1,0:T(8,128)(2,1)}, u32[]{:S(2)}) %copy-start.5) | copy-done | bytes 4194328
  9.1 0.4 shard_map.57
  9.5 0.9 %collective-permute-done.2.across_both = bf16[128,512]{1,0:T(8,128)(2,1)S(1)} collective-permute-done((bf16[128,512]{1,0:T(8,128)(2,1)S(1)}, bf16[128,512]{1,0:T(8,128)(2,1)S(1)}, u32[]{:S(2)}, u32[]{:S(2)}) %collective-permute-start.2) | collective-permute-done | bytes 131104 | tf_op jit(solution)/shard_map/ppermute | solution.py:28
  10.4 0.1 shard_map.58
  10.5 0.1 collective-permute-start.3
  10.6 0.6 collective-permute-start.12
  11.2 0.9 %collective-permute-done.3.far_ref = bf16[2,256,256]{2,1,0:T(8,128)(2,1)S(1)} collective-permute-done((bf16[2,256,256]{2,1,0:T(8,128)(2,1)S(1)}, bf16[2,256,256]{2,1,0:T(8,128)(2,1)S(1)}, u32[]{:S(2)}, u32[]{:S(2)}) %collective-permute-start.3) | collective-permute-done | bytes 262176 | tf_op jit(solution)/shard_map/ppermute | solution.py:28
  12.2 2.7 %collective-permute-start.5 = (bf16[512,256]{1,0:T(8,128)(2,1)S(1)}, bf16[512,256]{1,0:T(8,128)(2,1)S(1)}, u32[]{:S(2)}, u32[]{:S(2)}) collective-permute-start(bf16[512,256]{1,0:T(8,128)(2,1)S(1)} %get-tuple-element.60.refs_0_), channel_id=1, source_target_pairs={{0,8},{1,9},{2,10},{3,11},{4,12},{5,13},{6,14},{7,15},{8,0},{9,1},... | collective-permute-start | bytes 786440 | tf_op jit(solution)/shard_map/ppermute | solution.py:28
  14.8 0.4 collective-permute-start.6
  15.3 0.2 shard_map.55.refs_0_
  15.4 0.6 collective-permute-start.4
  16.0 10.2 %collective-permute-done.5.refs_2_ = bf16[512,256]{1,0:T(8,128)(2,1)S(1)} collective-permute-done((bf16[512,256]{1,0:T(8,128)(2,1)S(1)}, bf16[512,256]{1,0:T(8,128)(2,1)S(1)}, u32[]{:S(2)}, u32[]{:S(2)}) %collective-permute-start.5) | collective-permute-done | bytes 262176 | tf_op jit(solution)/shard_map/ppermute | solution.py:28
  26.2 1.1 %collective-permute-done.6.refs_1_ = bf16[512,256]{1,0:T(8,128)(2,1)S(1)} collective-permute-done((bf16[512,256]{1,0:T(8,128)(2,1)S(1)}, bf16[512,256]{1,0:T(8,128)(2,1)S(1)}, u32[]{:S(2)}, u32[]{:S(2)}) %collective-permute-start.6) | collective-permute-done | bytes 262176 | tf_op jit(solution)/shard_map/ppermute | solution.py:28
  27.3 0.6 collective-permute-start.10
  27.8 1.8 %collective-permute-done.4.refs_1_ = bf16[128,2176]{1,0:T(8,128)(2,1)S(1)} collective-permute-done((bf16[128,2176]{1,0:T(8,128)(2,1)S(1)}, bf16[128,2176]{1,0:T(8,128)(2,1)S(1)}, u32[]{:S(2)}, u32[]{:S(2)}) %collective-permute-start.4) | collective-permute-done | bytes 557088 | tf_op jit(solution)/shard_map/ppermute | solution.py:28
  29.7 0.6 collective-permute-start.13
  30.3 1.3 %collective-permute-done.8.refs_3_ = bf16[128,2176]{1,0:T(8,128)(2,1)S(1)} collective-permute-done((bf16[128,2176]{1,0:T(8,128)(2,1)S(1)}, bf16[128,2176]{1,0:T(8,128)(2,1)S(1)}, u32[]{:S(2)}, u32[]{:S(2)}) %collective-permute-start.8) | collective-permute-done | bytes 557088 | tf_op jit(solution)/shard_map/ppermute | solution.py:28
  31.6 1.4 %shard_map.60 = (bf16[512,2048]{1,0:T(8,128)(2,1)S(1)}, bf16[512,128]{1,0:T(8,128)(2,1)S(1)}, bf16[512,128]{1,0:T(8,128)(2,1)S(1)}, bf16[16,256]{1,0:T(8,128)(2,1)S(1)}) custom-call(bf16[128,2176]{1,0:T(8,128)(2,1)S(1)} %shard_map.55.refs_0_, bf16[128,2176]{1,0:T(8,128)(2,1)S(1)} %collective-permute-done.4.refs_1_, ...), custom_call_target="tpu_custom_call" | custom-call | bytes 3276800 | tf_op jit(solution)/shard_map/pallas_call | solution.py:49
  33.0 0.7 collective-permute-start.9
  33.7 1.4 %collective-permute-start.15 = (bf16[320,1024]{1,0:T(8,128)(2,1)S(1)}, bf16[320,1024]{1,0:T(8,128)(2,1)S(1)}, u32[]{:S(2)}, u32[]{:S(2)}) collective-permute-start(bf16[320,1024]{1,0:T(8,128)(2,1)S(1)} %get-tuple-element.77), channel_id=1, source_target_pairs={{0,16},{1,17},{2,18},{3,19},{4,20},{5,21},{6,22},{7,23},{8,24},{9,... | collective-permute-start | bytes 1966088 | tf_op jit(solution)/shard_map/ppermute | solution.py:28
  35.1 0.9 collective-permute-done.10.refs_3_
  36.0 0.8 shard_map.61
  36.8 3.3 %collective-permute-start.11 = (bf16[400,256]{1,0:T(8,128)(2,1)S(1)}, bf16[400,256]{1,0:T(8,128)(2,1)S(1)}, u32[]{:S(2)}, u32[]{:S(2)}) collective-permute-start(bf16[400,256]{1,0:T(8,128)(2,1)S(1)} %get-tuple-element.70), channel_id=1, source_target_pairs={{0,4},{1,5},{2,6},{3,7},{4,8},{5,9},{6,10},{7,11},{8,12},{9,13},{1... | collective-permute-start | bytes 614408 | tf_op jit(solution)/shard_map/ppermute | solution.py:33
  40.1 0.6 collective-permute-start.23
  40.7 2.6 %collective-permute-start.24 = (bf16[512,256]{1,0:T(8,128)(2,1)S(1)}, bf16[512,256]{1,0:T(8,128)(2,1)S(1)}, u32[]{:S(2)}, u32[]{:S(2)}) collective-permute-start(bf16[512,256]{1,0:T(8,128)(2,1)S(1)} %get-tuple-element.83.refs_4_), channel_id=1, source_target_pairs={{0,4},{1,5},{2,6},{3,7},{4,0},{5,1},{6,2},{7,3},{8,12},{9,13},{10,... | collective-permute-start | bytes 786440 | tf_op jit(solution)/shard_map/ppermute | solution.py:28
  43.4 6.9 %collective-permute-done.11.refs_4_.past_ref = bf16[400,256]{1,0:T(8,128)(2,1)S(1)} collective-permute-done((bf16[400,256]{1,0:T(8,128)(2,1)S(1)}, bf16[400,256]{1,0:T(8,128)(2,1)S(1)}, u32[]{:S(2)}, u32[]{:S(2)}) %collective-permute-start.11) | collective-permute-done | bytes 204832 | tf_op jit(solution)/shard_map/ppermute | solution.py:33
  50.3 0.2 shard_map.62.bias_ref
  50.5 1.2 %shard_map.64.refs_4_ = bf16[512,128]{1,0:T(8,128)(2,1)S(1)} custom-call(bf16[512,128]{1,0:T(8,128)(2,1)S(1)} %get-tuple-element.65.mine_ref, bf16[512,128]{1,0:T(8,128)(2,1)S(1)} %collective-permute-done.9.got_ref, f32[4,128,512]{2,1,0:T(8,128)S(1)} %shard_map.62.bias_ref, bf16[512,256]{1,0:T(8,128)(2,1)S(1)} %get-tuple-element.75.kv_ref, ...), custom_call_target="tpu_custom_call" | custom-call | bytes 1777664 | tf_op jit(solution)/shard_map/pallas_call | solution.py:49
  51.7 0.6 collective-permute-start.20
  52.4 1.4 %collective-permute-start.18 = (bf16[512,128]{1,0:T(8,128)(2,1)S(1)}, bf16[512,128]{1,0:T(8,128)(2,1)S(1)}, u32[]{:S(2)}, u32[]{:S(2)}) collective-permute-start(bf16[512,128]{1,0:T(8,128)(2,1)S(1)} %shard_map.64.refs_4_), channel_id=1, source_target_pairs={{0,16},{1,17},{2,18},{3,19},{4,20},{5,21},{6,22},{7,23},{8,24},{9,... | collective-permute-start | bytes 393224 | tf_op jit(solution)/shard_map/ppermute | solution.py:28
  53.8 1.5 %collective-permute-start.16 = (bf16[512,128]{1,0:T(8,128)(2,1)S(1)}, bf16[512,128]{1,0:T(8,128)(2,1)S(1)}, u32[]{:S(2)}, u32[]{:S(2)}) collective-permute-start(bf16[512,128]{1,0:T(8,128)(2,1)S(1)} %shard_map.64.refs_4_), channel_id=1, source_target_pairs={{0,2},{1,3},{2,0},{3,1},{4,6},{5,7},{6,4},{7,5},{8,10},{9,11},{10,... | collective-permute-start | bytes 393224 | tf_op jit(solution)/shard_map/ppermute | solution.py:28
  55.3 2.4 %collective-permute-done.20.refs_10_ = bf16[512,128]{1,0:T(8,128)(2,1)S(1)} collective-permute-done((bf16[512,128]{1,0:T(8,128)(2,1)S(1)}, bf16[512,128]{1,0:T(8,128)(2,1)S(1)}, u32[]{:S(2)}, u32[]{:S(2)}) %collective-permute-start.20) | collective-permute-done | bytes 131104 | tf_op jit(solution)/shard_map/ppermute | solution.py:28
  57.7 0.7 collective-permute-start.25
  58.5 0.5 collective-permute-start.21
  59.0 0.1 collective-permute-done.16.refs_6_
  59.1 0.4 collective-permute-start.17
  59.5 0.3 collective-permute-done.14.refs_5_
  59.8 0.5 collective-permute-done.19.refs_9_
  60.3 0.2 collective-permute-done.17.refs_7_
  60.5 1.2 %shard_map.65.refs_0_ = bf16[512,512]{1,0:T(8,128)(2,1)S(1)} custom-call(bf16[128,2176]{1,0:T(8,128)(2,1)S(1)} %shard_map.55.refs_0_, bf16[128,2176]{1,0:T(8,128)(2,1)S(1)} %collective-permute-done.4.refs_1_, bf16[128,2176]{1,0:T(8,128)(2,1)S(1)} %collective-permute-done.7.refs_2_, bf16[128,2176]{1,0:T(8,128)(2,1)S(1)} %collective-permute-done.8.refs_3_, ...), custom_call_target="tpu_custom_call" | custom-call | bytes 9568256 | tf_op jit(solution)/shard_map/pallas_call | solution.py:49
  61.7 0.4 collective-permute-start.22
  62.1 1.2 %shard_map.66.refs_1_ = bf16[512,512]{1,0:T(8,128)(2,1)S(1)} custom-call(bf16[128,2176]{1,0:T(8,128)(2,1)S(1)} %shard_map.55.refs_0_, bf16[128,2176]{1,0:T(8,128)(2,1)S(1)} %collective-permute-done.4.refs_1_, bf16[128,2176]{1,0:T(8,128)(2,1)S(1)} %collective-permute-done.7.refs_2_, bf16[128,2176]{1,0:T(8,128)(2,1)S(1)} %collective-permute-done.8.refs_3_, ...), custom_call_target="tpu_custom_call" | custom-call | bytes 9568256 | tf_op jit(solution)/shard_map/pallas_call | solution.py:49
  63.3 0.8 collective-permute-done.25.refs_7_
  64.1 1.9 %collective-permute-done.26.refs_3_ = bf16[512,512]{1,0:T(8,128)(2,1)S(1)} collective-permute-done((bf16[512,512]{1,0:T(8,128)(2,1)S(1)}, bf16[512,512]{1,0:T(8,128)(2,1)S(1)}, u32[]{:S(2)}, u32[]{:S(2)}) %collective-permute-start.26) | collective-permute-done | bytes 524320 | tf_op jit(solution)/shard_map/ppermute | solution.py:28
  66.0 1.9 %shard_map.67 = (bf16[128,2048]{1,0:T(8,128)(2,1)S(1)}, bf16[512,128]{1,0:T(8,128)(2,1)S(1)}, bf16[512,128]{1,0:T(8,128)(2,1)S(1)}, bf16[512,256]{1,0:T(8,128)(2,1)S(1)}, bf16[384,256]{1,0:T(8,128)(2,1)S(1)}) custom-call(bf16[512,512]{1,0:T(8,128)(2,1)S(1)} %shard_map.65.refs_0_, bf16[512,512]{1,0:T(8,128)(2,1)S(1)} %shard_map.66.refs_1_, ...), custom_call_target="tpu_custom_call" | custom-call | bytes 4194304 | tf_op jit(solution)/shard_map/pallas_call | solution.py:49
  67.9 4.9 %collective-permute-start.28 = (bf16[384,256]{1,0:T(8,128)(2,1)S(1)}, bf16[384,256]{1,0:T(8,128)(2,1)S(1)}, u32[]{:S(2)}, u32[]{:S(2)}) collective-permute-start(bf16[384,256]{1,0:T(8,128)(2,1)S(1)} %get-tuple-element.89), channel_id=1, source_target_pairs={{0,4},{1,5},{2,6},{3,7},{4,8},{5,9},{6,10},{7,11},{8,12},{9,13},{1... | collective-permute-start | bytes 589832 | tf_op jit(solution)/shard_map/ppermute | solution.py:33
  72.8 0.7 collective-permute-start.27
  73.4 4.7 %collective-permute-done.27.got_ref = bf16[512,128]{1,0:T(8,128)(2,1)S(1)} collective-permute-done((bf16[512,128]{1,0:T(8,128)(2,1)S(1)}, bf16[512,128]{1,0:T(8,128)(2,1)S(1)}, u32[]{:S(2)}, u32[]{:S(2)}) %collective-permute-start.27) | collective-permute-done | bytes 131104 | tf_op jit(solution)/shard_map/ppermute | solution.py:28
  78.1 1.2 %shard_map.68 = (bf16[256,128]{1,0:T(8,128)(2,1)S(1)}, bf16[256,128]{1,0:T(8,128)(2,1)S(1)}) custom-call(bf16[512,128]{1,0:T(8,128)(2,1)S(1)} %get-tuple-element.86.mine_ref, bf16[512,128]{1,0:T(8,128)(2,1)S(1)} %collective-permute-done.27.got_ref, f32[4,128,512]{2,1,0:T(8,128)S(1)} %shard_map.62.bias_ref, bf16[512,256]{1,0:T(8,128)(2,1)S(1)} %get-tuple-element.88.kv_ref, ...), custom_call_target="tpu_custom_call" | custom-call | flops 134217728 | bytes 1769472 | tf_op jit(solution)/shard_map/pallas_call | solution.py:49
  79.3 0.1 collective-permute-start.29
  79.4 1.2 %collective-permute-done.29.got_ref = bf16[256,128]{1,0:T(8,128)(2,1)S(1)} collective-permute-done((bf16[256,128]{1,0:T(8,128)(2,1)S(1)}, bf16[256,128]{1,0:T(8,128)(2,1)S(1)}, u32[]{:S(2)}, u32[]{:S(2)}) %collective-permute-start.29) | collective-permute-done | bytes 65568 | tf_op jit(solution)/shard_map/ppermute | solution.py:28
  80.6 0.6 collective-permute-start.32
  81.2 1.5 %collective-permute-start.30 = (bf16[256,128]{1,0:T(8,128)(2,1)S(1)}, bf16[256,128]{1,0:T(8,128)(2,1)S(1)}, u32[]{:S(2)}, u32[]{:S(2)}) collective-permute-start(bf16[256,128]{1,0:T(8,128)(2,1)S(1)} %get-tuple-element.93), channel_id=1, source_target_pairs={{0,2},{1,3},{2,0},{3,1},{4,6},{5,7},{6,4},{7,5},{8,10},{9,11},{10,... | collective-permute-start | bytes 196616 | tf_op jit(solution)/shard_map/ppermute | solution.py:28
  82.8 1.4 %collective-permute-start.31 = (bf16[256,128]{1,0:T(8,128)(2,1)S(1)}, bf16[256,128]{1,0:T(8,128)(2,1)S(1)}, u32[]{:S(2)}, u32[]{:S(2)}) collective-permute-start(bf16[256,128]{1,0:T(8,128)(2,1)S(1)} %get-tuple-element.92.refs_0_), channel_id=1, source_target_pairs={{0,16},{1,17},{2,18},{3,19},{4,20},{5,21},{6,22},{7,23},{8,24},{9,... | collective-permute-start | bytes 196616 | tf_op jit(solution)/shard_map/ppermute | solution.py:28
  84.2 2.3 %collective-permute-done.32.refs_3_ = bf16[256,128]{1,0:T(8,128)(2,1)S(1)} collective-permute-done((bf16[256,128]{1,0:T(8,128)(2,1)S(1)}, bf16[256,128]{1,0:T(8,128)(2,1)S(1)}, u32[]{:S(2)}, u32[]{:S(2)}) %collective-permute-start.32) | collective-permute-done | bytes 65568 | tf_op jit(solution)/shard_map/ppermute | solution.py:28
  86.5 0.0 collective-permute-done.30.refs_1_
  86.5 0.5 collective-permute-done.31.refs_2_
  87.0 1.6 %shard_map.70 = bf16[128,2048]{1,0:T(8,128)(2,1)} custom-call(bf16[256,128]{1,0:T(8,128)(2,1)S(1)} %get-tuple-element.92.refs_0_, bf16[256,128]{1,0:T(8,128)(2,1)S(1)} %collective-permute-done.30.refs_1_, bf16[256,128]{1,0:T(8,128)(2,1)S(1)} %collective-permute-done.31.refs_2_, bf16[256,128]{1,0:T(8,128)(2,1)S(1)} %collective-permute-done.32.refs_3_, ...), custom_call_target="tpu_custom_call" | custom-call | flops 536870912 | bytes 4980736 | tf_op jit(solution)/shard_map/pallas_call | solution.py:49
  (30 shorter events, 0.2 us)
Async XLA Ops:
  0.0 1.0 %copy-start.2 = (bf16[1,128,2048]{2,1,0:T(8,128)(2,1)S(1)}, bf16[1,128,2048]{2,1,0:T(8,128)(2,1)}, u32[]{:S(2)}) copy-start(bf16[1,128,2048]{2,1,0:T(8,128)(2,1)} %param.8) | copy-start | bytes 1572868
  1.1 8.4 %collective-permute-start = (bf16[128,512]{1,0:T(8,128)(2,1)S(1)}, bf16[128,512]{1,0:T(8,128)(2,1)S(1)}, u32[]{:S(2)}, u32[]{:S(2)}) collective-permute-start(bf16[128,512]{1,0:T(8,128)(2,1)S(1)} %get-tuple-element.55), channel_id=1, source_target_pairs={{0,2},{1,3},{2,0},{3,1},{4,6},{5,7},{6,4},{7,5},{8,10},{9,11},{10,... | collective-permute-start | bytes 393224 | tf_op jit(solution)/shard_map/ppermute | solution.py:28
  1.7 7.8 %collective-permute-start.1 = (bf16[128,512]{1,0:T(8,128)(2,1)S(1)}, bf16[128,512]{1,0:T(8,128)(2,1)S(1)}, u32[]{:S(2)}, u32[]{:S(2)}) collective-permute-start(bf16[128,512]{1,0:T(8,128)(2,1)S(1)} %get-tuple-element.56), channel_id=1, source_target_pairs={{0,16},{1,17},{2,18},{3,19},{4,20},{5,21},{6,22},{7,23},{8,24},{9,... | collective-permute-start | bytes 393224 | tf_op jit(solution)/shard_map/ppermute | solution.py:28
  2.2 8.2 %collective-permute-start.2 = (bf16[128,512]{1,0:T(8,128)(2,1)S(1)}, bf16[128,512]{1,0:T(8,128)(2,1)S(1)}, u32[]{:S(2)}, u32[]{:S(2)}) collective-permute-start(bf16[128,512]{1,0:T(8,128)(2,1)S(1)} %get-tuple-element.57), channel_id=1, source_target_pairs={{0,18},{1,19},{2,16},{3,17},{4,22},{5,23},{6,20},{7,21},{8,26},{9,... | collective-permute-start | bytes 393224 | tf_op jit(solution)/shard_map/ppermute | solution.py:28
  4.7 2.2 %copy-start = (bf16[1,1024,2048]{2,1,0:T(8,128)(2,1)S(1)}, bf16[1,1024,2048]{2,1,0:T(8,128)(2,1)}, u32[]{:S(2)}) copy-start(bf16[1,1024,2048]{2,1,0:T(8,128)(2,1)} %param.9) | copy-start | bytes 12582916
  6.9 2.2 %copy-start.5 = (bf16[1,2048,1024]{2,1,0:T(8,128)(2,1)S(1)}, bf16[1,2048,1024]{2,1,0:T(8,128)(2,1)}, u32[]{:S(2)}) copy-start(bf16[1,2048,1024]{2,1,0:T(8,128)(2,1)} %param.7) | copy-start | bytes 12582916
  9.0 6.2 %copy-start.3 = (bf16[1,128,2048]{2,1,0:T(8,128)(2,1)S(1)}, bf16[1,128,2048]{2,1,0:T(8,128)(2,1)}, u32[]{:S(2)}) copy-start(bf16[1,128,2048]{2,1,0:T(8,128)(2,1)} %param.5) | copy-start | bytes 1572868
  9.0 6.2 %copy-start.4 = (s32[1,128]{1,0:T(1,128)S(1)}, s32[1,128]{1,0:T(1,128)}, u32[]{:S(2)}) copy-start(s32[1,128]{1,0:T(1,128)} %id_ref.1) | copy-start | bytes 1540
  10.5 1.6 %collective-permute-start.3 = (bf16[2,256,256]{2,1,0:T(8,128)(2,1)S(1)}, bf16[2,256,256]{2,1,0:T(8,128)(2,1)S(1)}, u32[]{:S(2)}, u32[]{:S(2)}) collective-permute-start(bf16[2,256,256]{2,1,0:T(8,128)(2,1)S(1)} %get-tuple-element.59), channel_id=1, source_target_pairs={{0,1},{1,0},{2,3},{3,2},{4,5},{5,4},{6,7},{7,6},{8,9},{9,8},{10,11... | collective-permute-start | bytes 786440 | tf_op jit(solution)/shard_map/ppermute | solution.py:28
  10.6 19.0 %collective-permute-start.12 = (bf16[352,1024]{1,0:T(8,128)(2,1)S(1)}, bf16[352,1024]{1,0:T(8,128)(2,1)S(1)}, u32[]{:S(2)}, u32[]{:S(2)}) collective-permute-start(bf16[352,1024]{1,0:T(8,128)(2,1)S(1)} %get-tuple-element.73), channel_id=1, source_target_pairs={{0,16},{1,17},{2,18},{3,19},{4,20},{5,21},{6,22},{7,23},{8,24},{9,... | collective-permute-start | bytes 2162696 | tf_op jit(solution)/shard_map/ppermute | solution.py:28
  12.2 14.0 %collective-permute-start.5 = (bf16[512,256]{1,0:T(8,128)(2,1)S(1)}, bf16[512,256]{1,0:T(8,128)(2,1)S(1)}, u32[]{:S(2)}, u32[]{:S(2)}) collective-permute-start(bf16[512,256]{1,0:T(8,128)(2,1)S(1)} %get-tuple-element.60.refs_0_), channel_id=1, source_target_pairs={{0,8},{1,9},{2,10},{3,11},{4,12},{5,13},{6,14},{7,15},{8,0},{9,1},... | collective-permute-start | bytes 786440 | tf_op jit(solution)/shard_map/ppermute | solution.py:28
  14.8 12.4 %collective-permute-start.6 = (bf16[512,256]{1,0:T(8,128)(2,1)S(1)}, bf16[512,256]{1,0:T(8,128)(2,1)S(1)}, u32[]{:S(2)}, u32[]{:S(2)}) collective-permute-start(bf16[512,256]{1,0:T(8,128)(2,1)S(1)} %get-tuple-element.60.refs_0_), channel_id=1, source_target_pairs={{0,4},{1,5},{2,6},{3,7},{4,0},{5,1},{6,2},{7,3},{8,12},{9,13},{10,... | collective-permute-start | bytes 786440 | tf_op jit(solution)/shard_map/ppermute | solution.py:28
  15.4 14.2 %collective-permute-start.4 = (bf16[128,2176]{1,0:T(8,128)(2,1)S(1)}, bf16[128,2176]{1,0:T(8,128)(2,1)S(1)}, u32[]{:S(2)}, u32[]{:S(2)}) collective-permute-start(bf16[128,2176]{1,0:T(8,128)(2,1)S(1)} %shard_map.55.refs_0_), channel_id=1, source_target_pairs={{0,2},{1,3},{2,0},{3,1},{4,6},{5,7},{6,4},{7,5},{8,10},{9,11},{10,... | collective-permute-start | bytes 1671176 | tf_op jit(solution)/shard_map/ppermute | solution.py:28
  27.3 3.0 %collective-permute-start.7 = (bf16[128,2176]{1,0:T(8,128)(2,1)S(1)}, bf16[128,2176]{1,0:T(8,128)(2,1)S(1)}, u32[]{:S(2)}, u32[]{:S(2)}) collective-permute-start(bf16[128,2176]{1,0:T(8,128)(2,1)S(1)} %shard_map.55.refs_0_), channel_id=1, source_target_pairs={{0,1},{1,0},{2,3},{3,2},{4,5},{5,4},{6,7},{7,6},{8,9},{9,8},{10,11... | collective-permute-start | bytes 1671176 | tf_op jit(solution)/shard_map/ppermute | solution.py:28
  27.3 8.7 %collective-permute-start.10 = (bf16[512,256]{1,0:T(8,128)(2,1)S(1)}, bf16[512,256]{1,0:T(8,128)(2,1)S(1)}, u32[]{:S(2)}, u32[]{:S(2)}) collective-permute-start(bf16[512,256]{1,0:T(8,128)(2,1)S(1)} %collective-permute-done.5.refs_2_), channel_id=1, source_target_pairs={{0,4},{1,5},{2,6},{3,7},{4,0},{5,1},{6,2},{7,3},{8,12},{9,13},{10,... | collective-permute-start | bytes 786440 | tf_op jit(solution)/shard_map/ppermute | solution.py:28
  29.6 2.0 %collective-permute-start.8 = (bf16[128,2176]{1,0:T(8,128)(2,1)S(1)}, bf16[128,2176]{1,0:T(8,128)(2,1)S(1)}, u32[]{:S(2)}, u32[]{:S(2)}) collective-permute-start(bf16[128,2176]{1,0:T(8,128)(2,1)S(1)} %collective-permute-done.4.refs_1_), channel_id=1, source_target_pairs={{0,1},{1,0},{2,3},{3,2},{4,5},{5,4},{6,7},{7,6},{8,9},{9,8},{10,11... | collective-permute-start | bytes 1671176 | tf_op jit(solution)/shard_map/ppermute | solution.py:28
  29.7 20.8 %collective-permute-start.13 = (bf16[352,1024]{1,0:T(8,128)(2,1)S(1)}, bf16[352,1024]{1,0:T(8,128)(2,1)S(1)}, u32[]{:S(2)}, u32[]{:S(2)}) collective-permute-start(bf16[352,1024]{1,0:T(8,128)(2,1)S(1)} %shard_map.63), channel_id=1, source_target_pairs={{0,2},{1,3},{2,0},{3,1},{4,6},{5,7},{6,4},{7,5},{8,10},{9,11},{10,... | collective-permute-start | bytes 2162696 | tf_op jit(solution)/shard_map/ppermute | solution.py:28
  33.0 7.7 %collective-permute-start.9 = (bf16[512,128]{1,0:T(8,128)(2,1)S(1)}, bf16[512,128]{1,0:T(8,128)(2,1)S(1)}, u32[]{:S(2)}, u32[]{:S(2)}) collective-permute-start(bf16[512,128]{1,0:T(8,128)(2,1)S(1)} %get-tuple-element.66), channel_id=1, source_target_pairs={{0,16},{1,17},{2,18},{3,19},{4,20},{5,21},{6,22},{7,23},{8,24},{9,... | collective-permute-start | bytes 393224 | tf_op jit(solution)/shard_map/ppermute | solution.py:28
  33.7 20.1 %collective-permute-start.15 = (bf16[320,1024]{1,0:T(8,128)(2,1)S(1)}, bf16[320,1024]{1,0:T(8,128)(2,1)S(1)}, u32[]{:S(2)}, u32[]{:S(2)}) collective-permute-start(bf16[320,1024]{1,0:T(8,128)(2,1)S(1)} %get-tuple-element.77), channel_id=1, source_target_pairs={{0,16},{1,17},{2,18},{3,19},{4,20},{5,21},{6,22},{7,23},{8,24},{9,... | collective-permute-start | bytes 1966088 | tf_op jit(solution)/shard_map/ppermute | solution.py:28
  36.8 23.8 %copy-start.1 = (bf16[1,1024,2048]{2,1,0:T(8,128)(2,1)S(1)}, bf16[1,1024,2048]{2,1,0:T(8,128)(2,1)}, u32[]{:S(2)}) copy-start(bf16[1,1024,2048]{2,1,0:T(8,128)(2,1)} %param.9) | copy-start | bytes 12582916
  36.8 13.5 %collective-permute-start.11 = (bf16[400,256]{1,0:T(8,128)(2,1)S(1)}, bf16[400,256]{1,0:T(8,128)(2,1)S(1)}, u32[]{:S(2)}, u32[]{:S(2)}) collective-permute-start(bf16[400,256]{1,0:T(8,128)(2,1)S(1)} %get-tuple-element.70), channel_id=1, source_target_pairs={{0,4},{1,5},{2,6},{3,7},{4,8},{5,9},{6,10},{7,11},{8,12},{9,13},{1... | collective-permute-start | bytes 614408 | tf_op jit(solution)/shard_map/ppermute | solution.py:33
  40.1 17.6 %collective-permute-start.23 = (bf16[512,256]{1,0:T(8,128)(2,1)S(1)}, bf16[512,256]{1,0:T(8,128)(2,1)S(1)}, u32[]{:S(2)}, u32[]{:S(2)}) collective-permute-start(bf16[512,256]{1,0:T(8,128)(2,1)S(1)} %get-tuple-element.83.refs_4_), channel_id=1, source_target_pairs={{0,8},{1,9},{2,10},{3,11},{4,12},{5,13},{6,14},{7,15},{8,0},{9,1},... | collective-permute-start | bytes 786440 | tf_op jit(solution)/shard_map/ppermute | solution.py:28
  40.7 17.0 %collective-permute-start.24 = (bf16[512,256]{1,0:T(8,128)(2,1)S(1)}, bf16[512,256]{1,0:T(8,128)(2,1)S(1)}, u32[]{:S(2)}, u32[]{:S(2)}) collective-permute-start(bf16[512,256]{1,0:T(8,128)(2,1)S(1)} %get-tuple-element.83.refs_4_), channel_id=1, source_target_pairs={{0,4},{1,5},{2,6},{3,7},{4,0},{5,1},{6,2},{7,3},{8,12},{9,13},{10,... | collective-permute-start | bytes 786440 | tf_op jit(solution)/shard_map/ppermute | solution.py:28
  51.7 6.0 %collective-permute-start.20 = (bf16[512,128]{1,0:T(8,128)(2,1)S(1)}, bf16[512,128]{1,0:T(8,128)(2,1)S(1)}, u32[]{:S(2)}, u32[]{:S(2)}) collective-permute-start(bf16[512,128]{1,0:T(8,128)(2,1)S(1)} %shard_map.64.refs_4_), channel_id=1, source_target_pairs={{0,18},{1,19},{2,16},{3,17},{4,22},{5,23},{6,20},{7,21},{8,26},{9,... | collective-permute-start | bytes 393224 | tf_op jit(solution)/shard_map/ppermute | solution.py:28
  52.4 6.6 %collective-permute-start.18 = (bf16[512,128]{1,0:T(8,128)(2,1)S(1)}, bf16[512,128]{1,0:T(8,128)(2,1)S(1)}, u32[]{:S(2)}, u32[]{:S(2)}) collective-permute-start(bf16[512,128]{1,0:T(8,128)(2,1)S(1)} %shard_map.64.refs_4_), channel_id=1, source_target_pairs={{0,16},{1,17},{2,18},{3,19},{4,20},{5,21},{6,22},{7,23},{8,24},{9,... | collective-permute-start | bytes 393224 | tf_op jit(solution)/shard_map/ppermute | solution.py:28
  53.8 5.3 %collective-permute-start.16 = (bf16[512,128]{1,0:T(8,128)(2,1)S(1)}, bf16[512,128]{1,0:T(8,128)(2,1)S(1)}, u32[]{:S(2)}, u32[]{:S(2)}) collective-permute-start(bf16[512,128]{1,0:T(8,128)(2,1)S(1)} %shard_map.64.refs_4_), channel_id=1, source_target_pairs={{0,2},{1,3},{2,0},{3,1},{4,6},{5,7},{6,4},{7,5},{8,10},{9,11},{10,... | collective-permute-start | bytes 393224 | tf_op jit(solution)/shard_map/ppermute | solution.py:28
  57.7 6.4 %collective-permute-start.25 = (bf16[512,256]{1,0:T(8,128)(2,1)S(1)}, bf16[512,256]{1,0:T(8,128)(2,1)S(1)}, u32[]{:S(2)}, u32[]{:S(2)}) collective-permute-start(bf16[512,256]{1,0:T(8,128)(2,1)S(1)} %collective-permute-done.23.refs_6_), channel_id=1, source_target_pairs={{0,4},{1,5},{2,6},{3,7},{4,0},{5,1},{6,2},{7,3},{8,12},{9,13},{10,... | collective-permute-start | bytes 786440 | tf_op jit(solution)/shard_map/ppermute | solution.py:28
  58.5 1.3 %collective-permute-start.14 = (bf16[512,128]{1,0:T(8,128)(2,1)S(1)}, bf16[512,128]{1,0:T(8,128)(2,1)S(1)}, u32[]{:S(2)}, u32[]{:S(2)}) collective-permute-start(bf16[512,128]{1,0:T(8,128)(2,1)S(1)} %shard_map.64.refs_4_), channel_id=1, source_target_pairs={{0,1},{1,0},{2,3},{3,2},{4,5},{5,4},{6,7},{7,6},{8,9},{9,8},{10,11... | collective-permute-start | bytes 393224 | tf_op jit(solution)/shard_map/ppermute | solution.py:28
  58.5 1.9 %collective-permute-start.21 = (bf16[512,128]{1,0:T(8,128)(2,1)S(1)}, bf16[512,128]{1,0:T(8,128)(2,1)S(1)}, u32[]{:S(2)}, u32[]{:S(2)}) collective-permute-start(bf16[512,128]{1,0:T(8,128)(2,1)S(1)} %collective-permute-done.20.refs_10_), channel_id=1, source_target_pairs={{0,1},{1,0},{2,3},{3,2},{4,5},{5,4},{6,7},{7,6},{8,9},{9,8},{10,11... | collective-permute-start | bytes 393224 | tf_op jit(solution)/shard_map/ppermute | solution.py:28
  59.0 1.3 %collective-permute-start.19 = (bf16[512,128]{1,0:T(8,128)(2,1)S(1)}, bf16[512,128]{1,0:T(8,128)(2,1)S(1)}, u32[]{:S(2)}, u32[]{:S(2)}) collective-permute-start(bf16[512,128]{1,0:T(8,128)(2,1)S(1)} %collective-permute-done.18.refs_8_), channel_id=1, source_target_pairs={{0,1},{1,0},{2,3},{3,2},{4,5},{5,4},{6,7},{7,6},{8,9},{9,8},{10,11... | collective-permute-start | bytes 393224 | tf_op jit(solution)/shard_map/ppermute | solution.py:28
  59.1 1.4 %collective-permute-start.17 = (bf16[512,128]{1,0:T(8,128)(2,1)S(1)}, bf16[512,128]{1,0:T(8,128)(2,1)S(1)}, u32[]{:S(2)}, u32[]{:S(2)}) collective-permute-start(bf16[512,128]{1,0:T(8,128)(2,1)S(1)} %collective-permute-done.16.refs_6_), channel_id=1, source_target_pairs={{0,1},{1,0},{2,3},{3,2},{4,5},{5,4},{6,7},{7,6},{8,9},{9,8},{10,11... | collective-permute-start | bytes 393224 | tf_op jit(solution)/shard_map/ppermute | solution.py:28
  61.7 2.4 %collective-permute-start.22 = (bf16[512,512]{1,0:T(8,128)(2,1)S(1)}, bf16[512,512]{1,0:T(8,128)(2,1)S(1)}, u32[]{:S(2)}, u32[]{:S(2)}) collective-permute-start(bf16[512,512]{1,0:T(8,128)(2,1)S(1)} %shard_map.65.refs_0_), channel_id=1, source_target_pairs={{0,1},{1,0},{2,3},{3,2},{4,5},{5,4},{6,7},{7,6},{8,9},{9,8},{10,11... | collective-permute-start | bytes 1572872 | tf_op jit(solution)/shard_map/ppermute | solution.py:28
  64.1 1.9 %collective-permute-start.26 = (bf16[512,512]{1,0:T(8,128)(2,1)S(1)}, bf16[512,512]{1,0:T(8,128)(2,1)S(1)}, u32[]{:S(2)}, u32[]{:S(2)}) collective-permute-start(bf16[512,512]{1,0:T(8,128)(2,1)S(1)} %shard_map.66.refs_1_), channel_id=1, source_target_pairs={{0,1},{1,0},{2,3},{3,2},{4,5},{5,4},{6,7},{7,6},{8,9},{9,8},{10,11... | collective-permute-start | bytes 1572872 | tf_op jit(solution)/shard_map/ppermute | solution.py:28
  67.9 10.2 %collective-permute-start.28 = (bf16[384,256]{1,0:T(8,128)(2,1)S(1)}, bf16[384,256]{1,0:T(8,128)(2,1)S(1)}, u32[]{:S(2)}, u32[]{:S(2)}) collective-permute-start(bf16[384,256]{1,0:T(8,128)(2,1)S(1)} %get-tuple-element.89), channel_id=1, source_target_pairs={{0,4},{1,5},{2,6},{3,7},{4,8},{5,9},{6,10},{7,11},{8,12},{9,13},{1... | collective-permute-start | bytes 589832 | tf_op jit(solution)/shard_map/ppermute | solution.py:33
  72.8 5.3 %collective-permute-start.27 = (bf16[512,128]{1,0:T(8,128)(2,1)S(1)}, bf16[512,128]{1,0:T(8,128)(2,1)S(1)}, u32[]{:S(2)}, u32[]{:S(2)}) collective-permute-start(bf16[512,128]{1,0:T(8,128)(2,1)S(1)} %get-tuple-element.87), channel_id=1, source_target_pairs={{0,16},{1,17},{2,18},{3,19},{4,20},{5,21},{6,22},{7,23},{8,24},{9,... | collective-permute-start | bytes 393224 | tf_op jit(solution)/shard_map/ppermute | solution.py:28
  79.3 1.3 %collective-permute-start.29 = (bf16[256,128]{1,0:T(8,128)(2,1)S(1)}, bf16[256,128]{1,0:T(8,128)(2,1)S(1)}, u32[]{:S(2)}, u32[]{:S(2)}) collective-permute-start(bf16[256,128]{1,0:T(8,128)(2,1)S(1)} %get-tuple-element.91), channel_id=1, source_target_pairs={{0,1},{1,0},{2,3},{3,2},{4,5},{5,4},{6,7},{7,6},{8,9},{9,8},{10,11... | collective-permute-start | bytes 196616 | tf_op jit(solution)/shard_map/ppermute | solution.py:28
  80.6 5.8 %collective-permute-start.32 = (bf16[256,128]{1,0:T(8,128)(2,1)S(1)}, bf16[256,128]{1,0:T(8,128)(2,1)S(1)}, u32[]{:S(2)}, u32[]{:S(2)}) collective-permute-start(bf16[256,128]{1,0:T(8,128)(2,1)S(1)} %get-tuple-element.93), channel_id=1, source_target_pairs={{0,18},{1,19},{2,16},{3,17},{4,22},{5,23},{6,20},{7,21},{8,26},{9,... | collective-permute-start | bytes 196616 | tf_op jit(solution)/shard_map/ppermute | solution.py:28
  81.2 5.3 %collective-permute-start.30 = (bf16[256,128]{1,0:T(8,128)(2,1)S(1)}, bf16[256,128]{1,0:T(8,128)(2,1)S(1)}, u32[]{:S(2)}, u32[]{:S(2)}) collective-permute-start(bf16[256,128]{1,0:T(8,128)(2,1)S(1)} %get-tuple-element.93), channel_id=1, source_target_pairs={{0,2},{1,3},{2,0},{3,1},{4,6},{5,7},{6,4},{7,5},{8,10},{9,11},{10,... | collective-permute-start | bytes 196616 | tf_op jit(solution)/shard_map/ppermute | solution.py:28
  82.8 4.3 %collective-permute-start.31 = (bf16[256,128]{1,0:T(8,128)(2,1)S(1)}, bf16[256,128]{1,0:T(8,128)(2,1)S(1)}, u32[]{:S(2)}, u32[]{:S(2)}) collective-permute-start(bf16[256,128]{1,0:T(8,128)(2,1)S(1)} %get-tuple-element.92.refs_0_), channel_id=1, source_target_pairs={{0,16},{1,17},{2,18},{3,19},{4,20},{5,21},{6,22},{7,23},{8,24},{9,... | collective-permute-start | bytes 196616 | tf_op jit(solution)/shard_map/ppermute | solution.py:28

commit v7 on v6

--- a/solution.py
+++ b/solution.py
@@ -43,7 +43,7 @@
     return jnp.dot(a, b, preferred_element_type=jnp.float32)
 
 
-def call(kernel, outs, scratch, flops, *operands, far={}):
+def call(kernel, outs, scratch, flops, *operands, far={}, vmem=VMEM_BYTES):
     moved = sum(o.size * o.dtype.itemsize for o in operands)
     place = lambda i: far.get(i, pltpu.VMEM)
     return pl.pallas_call(
@@ -53,7 +53,7 @@
         out_specs=[pl.BlockSpec(memory_space=pltpu.VMEM)] * len(outs),
         scratch_shapes=[pltpu.VMEM(*s) if isinstance(s, tuple) else s for s in scratch],
         cost_estimate=pl.CostEstimate(flops=flops, bytes_accessed=moved, transcendentals=0),
-        compiler_params=pltpu.CompilerParams(vmem_limit_bytes=VMEM_BYTES),
+        compiler_params=pltpu.CompilerParams(vmem_limit_bytes=vmem),
     )(*operands)
 
 
@@ -396,7 +396,7 @@
     sent_first, sent_second, query_mat = call(
         slice_kernel,
         [((FIRST * unit, half), bf16), ((2 * REST * unit, half), bf16), ((width, 2 * part), bf16)],
-        [pltpu.SemaphoreType.DMA((5,))], LONG, w_out[0], w_query[0], far={0: pltpu.HBM, 1: pltpu.HBM},
+        [pltpu.SemaphoreType.DMA((5,))], LONG, w_out[0], w_query[0], far={0: pltpu.HBM, 1: pltpu.HBM}, vmem=60 * 1024 * 1024,
     )
 
     kept, for_y, for_x, for_both = call(

time: 89.2 us -> 89.2 us (level)
  local copies, waits for them, and re-layouts: 5.43 us -> 1.06 us
  Pallas kernels: 11.5 us -> 14.2 us
  waiting for transfers between devices: 38.9 us -> 40.5 us
    unnamed x12, local copies, waits for them, and re-layouts: 5.43 us -> 1.06 us
    pallas_call x16, Pallas kernels: 11.5 us -> 14.2 us  [call(): pl.pallas_call(kernel, out_shape=[jax.ShapeDtypeStruct(s, d) for s, d in...]
    ppermute x31, waiting for transfers between devices: 32 us -> 33.6 us  [swap(): return lax.ppermute(block, BOTH, route)]
  transfers between devices with their start and end apart: 33 -> 33, of which waited for: 19 -> 20; matrix products, arithmetic and copies ran while one was open for 0% -> 0% of each run, Pallas kernels for 8% -> 11%
where the time goes in v7:
time: 89.2 us; the launch traced here: 88.6 us
  waiting for transfers between devices  40.5 us (45%)
  starting transfers between devices  32.6 us (37%)
  Pallas kernels  14.2 us (16%)
  local copies, waits for them, and re-layouts  1.06 us (1%)
    ppermute x31, waiting for transfers between devices, swap(): return lax.ppermute(block, BOTH, route)  33.6 us
    ppermute x31, starting transfers between devices, swap(): return lax.ppermute(block, BOTH, route)  24.4 us
    pallas_call x16, Pallas kernels, call(): pl.pallas_call(kernel, out_shape=[jax.ShapeDtypeStruct(s, d) for s, d in...  14.2 us
    ppermute x2, starting transfers between devices, from_plane_behind(): lax.ppermute(block, 'ctx', [(i, i + PLANE) for i in range(wide - PLANE)])  8.2 us
    ppermute x2, waiting for transfers between devices, from_plane_behind(): lax.ppermute(block, 'ctx', [(i, i + PLANE) for i in range(wide - PLANE)])  6.9 us
  transfers between devices with their start and end apart: 33, of which 20 were waited for; matrix products, arithmetic and copies ran while one was open for 0% of the time, Pallas kernels for 11%

profile of v7, /device:TPU:14, one launch (start us, length us, event | category | flops | bytes accessed | tf_op | source)
XLA Modules:
  0.0 88.6 jit_solution(3670150874536889107)
XLA Ops:
  0.0 1.0 %copy-done.2 = bf16[1,128,2048]{2,1,0:T(8,128)(2,1)S(1)} copy-done((bf16[1,128,2048]{2,1,0:T(8,128)(2,1)S(1)}, bf16[1,128,2048]{2,1,0:T(8,128)(2,1)}, u32[]{:S(2)}) %copy-start.2) | copy-done | bytes 524312
  1.0 0.1 shard_map.56
  1.1 0.6 collective-permute-start
  1.7 0.5 collective-permute-start.1
  2.2 2.4 %collective-permute-start.2 = (bf16[128,512]{1,0:T(8,128)(2,1)S(1)}, bf16[128,512]{1,0:T(8,128)(2,1)S(1)}, u32[]{:S(2)}, u32[]{:S(2)}) collective-permute-start(bf16[128,512]{1,0:T(8,128)(2,1)S(1)} %get-tuple-element.57), channel_id=1, source_target_pairs={{0,18},{1,19},{2,16},{3,17},{4,22},{5,23},{6,20},{7,21},{8,26},{9,... | collective-permute-start | bytes 393224 | tf_op jit(solution)/shard_map/ppermute | solution.py:28
  4.7 3.1 %shard_map.57 = (bf16[352,1024]{1,0:T(8,128)(2,1)}, bf16[320,1024]{1,0:T(8,128)(2,1)}, bf16[2048,256]{1,0:T(8,128)(2,1)}) custom-call(bf16[1024,2048]{1,0:T(8,128)(2,1)} %bitcast.5, bf16[2048,1024]{1,0:T(8,128)(2,1)} %bitcast.11), custom_call_target="tpu_custom_call" | custom-call | flops 99999997952 | bytes 8388608 | tf_op jit(solution)/shard_map/pallas_call | solution.py:49
  7.8 0.2 collective-permute-done.1.across_x
  8.0 2.4 %collective-permute-done.2.across_both = bf16[128,512]{1,0:T(8,128)(2,1)S(1)} collective-permute-done((bf16[128,512]{1,0:T(8,128)(2,1)S(1)}, bf16[128,512]{1,0:T(8,128)(2,1)S(1)}, u32[]{:S(2)}, u32[]{:S(2)}) %collective-permute-start.2) | collective-permute-done | bytes 131104 | tf_op jit(solution)/shard_map/ppermute | solution.py:28
  10.4 0.1 shard_map.58
  10.5 0.1 collective-permute-start.3
  10.6 0.6 collective-permute-start.12
  11.2 0.9 %collective-permute-done.3.far_ref = bf16[2,256,256]{2,1,0:T(8,128)(2,1)S(1)} collective-permute-done((bf16[2,256,256]{2,1,0:T(8,128)(2,1)S(1)}, bf16[2,256,256]{2,1,0:T(8,128)(2,1)S(1)}, u32[]{:S(2)}, u32[]{:S(2)}) %collective-permute-start.3) | collective-permute-done | bytes 262176 | tf_op jit(solution)/shard_map/ppermute | solution.py:28
  12.2 2.7 %collective-permute-start.5 = (bf16[512,256]{1,0:T(8,128)(2,1)S(1)}, bf16[512,256]{1,0:T(8,128)(2,1)S(1)}, u32[]{:S(2)}, u32[]{:S(2)}) collective-permute-start(bf16[512,256]{1,0:T(8,128)(2,1)S(1)} %get-tuple-element.60.refs_0_), channel_id=1, source_target_pairs={{0,8},{1,9},{2,10},{3,11},{4,12},{5,13},{6,14},{7,15},{8,0},{9,1},... | collective-permute-start | bytes 786440 | tf_op jit(solution)/shard_map/ppermute | solution.py:28
  14.8 0.4 collective-permute-start.6
  15.3 0.2 shard_map.55.refs_0_
  15.5 0.6 collective-permute-start.4
  16.0 10.1 %collective-permute-done.5.refs_2_ = bf16[512,256]{1,0:T(8,128)(2,1)S(1)} collective-permute-done((bf16[512,256]{1,0:T(8,128)(2,1)S(1)}, bf16[512,256]{1,0:T(8,128)(2,1)S(1)}, u32[]{:S(2)}, u32[]{:S(2)}) %collective-permute-start.5) | collective-permute-done | bytes 262176 | tf_op jit(solution)/shard_map/ppermute | solution.py:28
  26.2 1.1 %collective-permute-done.6.refs_1_ = bf16[512,256]{1,0:T(8,128)(2,1)S(1)} collective-permute-done((bf16[512,256]{1,0:T(8,128)(2,1)S(1)}, bf16[512,256]{1,0:T(8,128)(2,1)S(1)}, u32[]{:S(2)}, u32[]{:S(2)}) %collective-permute-start.6) | collective-permute-done | bytes 262176 | tf_op jit(solution)/shard_map/ppermute | solution.py:28
  27.3 0.6 collective-permute-start.10
  27.8 1.8 %collective-permute-done.4.refs_1_ = bf16[128,2176]{1,0:T(8,128)(2,1)S(1)} collective-permute-done((bf16[128,2176]{1,0:T(8,128)(2,1)S(1)}, bf16[128,2176]{1,0:T(8,128)(2,1)S(1)}, u32[]{:S(2)}, u32[]{:S(2)}) %collective-permute-start.4) | collective-permute-done | bytes 557088 | tf_op jit(solution)/shard_map/ppermute | solution.py:28
  29.7 0.6 collective-permute-start.13
  30.3 1.3 %collective-permute-done.8.refs_3_ = bf16[128,2176]{1,0:T(8,128)(2,1)S(1)} collective-permute-done((bf16[128,2176]{1,0:T(8,128)(2,1)S(1)}, bf16[128,2176]{1,0:T(8,128)(2,1)S(1)}, u32[]{:S(2)}, u32[]{:S(2)}) %collective-permute-start.8) | collective-permute-done | bytes 557088 | tf_op jit(solution)/shard_map/ppermute | solution.py:28
  31.6 1.4 %shard_map.60 = (bf16[512,2048]{1,0:T(8,128)(2,1)S(1)}, bf16[512,128]{1,0:T(8,128)(2,1)S(1)}, bf16[512,128]{1,0:T(8,128)(2,1)S(1)}, bf16[16,256]{1,0:T(8,128)(2,1)S(1)}) custom-call(bf16[128,2176]{1,0:T(8,128)(2,1)S(1)} %shard_map.55.refs_0_, bf16[128,2176]{1,0:T(8,128)(2,1)S(1)} %collective-permute-done.4.refs_1_, ...), custom_call_target="tpu_custom_call" | custom-call | bytes 3276800 | tf_op jit(solution)/shard_map/pallas_call | solution.py:49
  33.0 0.7 collective-permute-start.9
  33.7 1.4 %collective-permute-start.15 = (bf16[320,1024]{1,0:T(8,128)(2,1)S(1)}, bf16[320,1024]{1,0:T(8,128)(2,1)S(1)}, u32[]{:S(2)}, u32[]{:S(2)}) collective-permute-start(bf16[320,1024]{1,0:T(8,128)(2,1)S(1)} %copy-done.5), channel_id=1, source_target_pairs={{0,16},{1,17},{2,18},{3,19},{4,20},{5,21},{6,22},{7,23},{8,24},{9,... | collective-permute-start | bytes 1966088 | tf_op jit(solution)/shard_map/ppermute | solution.py:28
  35.1 0.9 collective-permute-done.10.refs_3_
  36.0 0.8 shard_map.61
  36.8 0.0 copy-start
  36.8 3.3 %collective-permute-start.11 = (bf16[400,256]{1,0:T(8,128)(2,1)S(1)}, bf16[400,256]{1,0:T(8,128)(2,1)S(1)}, u32[]{:S(2)}, u32[]{:S(2)}) collective-permute-start(bf16[400,256]{1,0:T(8,128)(2,1)S(1)} %get-tuple-element.70), channel_id=1, source_target_pairs={{0,4},{1,5},{2,6},{3,7},{4,8},{5,9},{6,10},{7,11},{8,12},{9,13},{1... | collective-permute-start | bytes 614408 | tf_op jit(solution)/shard_map/ppermute | solution.py:33
  40.1 0.6 collective-permute-start.23
  40.7 2.6 %collective-permute-start.24 = (bf16[512,256]{1,0:T(8,128)(2,1)S(1)}, bf16[512,256]{1,0:T(8,128)(2,1)S(1)}, u32[]{:S(2)}, u32[]{:S(2)}) collective-permute-start(bf16[512,256]{1,0:T(8,128)(2,1)S(1)} %get-tuple-element.83.refs_4_), channel_id=1, source_target_pairs={{0,4},{1,5},{2,6},{3,7},{4,0},{5,1},{6,2},{7,3},{8,12},{9,13},{10,... | collective-permute-start | bytes 786440 | tf_op jit(solution)/shard_map/ppermute | solution.py:28
  43.4 6.9 %collective-permute-done.11.refs_4_.past_ref = bf16[400,256]{1,0:T(8,128)(2,1)S(1)} collective-permute-done((bf16[400,256]{1,0:T(8,128)(2,1)S(1)}, bf16[400,256]{1,0:T(8,128)(2,1)S(1)}, u32[]{:S(2)}, u32[]{:S(2)}) %collective-permute-start.11) | collective-permute-done | bytes 204832 | tf_op jit(solution)/shard_map/ppermute | solution.py:33
  50.3 0.2 shard_map.62.bias_ref
  50.5 1.2 %shard_map.64.refs_4_ = bf16[512,128]{1,0:T(8,128)(2,1)S(1)} custom-call(bf16[512,128]{1,0:T(8,128)(2,1)S(1)} %get-tuple-element.65.mine_ref, bf16[512,128]{1,0:T(8,128)(2,1)S(1)} %collective-permute-done.9.got_ref, f32[4,128,512]{2,1,0:T(8,128)S(1)} %shard_map.62.bias_ref, bf16[512,256]{1,0:T(8,128)(2,1)S(1)} %get-tuple-element.75.kv_ref, ...), custom_call_target="tpu_custom_call" | custom-call | bytes 1777664 | tf_op jit(solution)/shard_map/pallas_call | solution.py:49
  51.7 0.6 collective-permute-start.20
  52.4 1.4 %collective-permute-start.18 = (bf16[512,128]{1,0:T(8,128)(2,1)S(1)}, bf16[512,128]{1,0:T(8,128)(2,1)S(1)}, u32[]{:S(2)}, u32[]{:S(2)}) collective-permute-start(bf16[512,128]{1,0:T(8,128)(2,1)S(1)} %shard_map.64.refs_4_), channel_id=1, source_target_pairs={{0,16},{1,17},{2,18},{3,19},{4,20},{5,21},{6,22},{7,23},{8,24},{9,... | collective-permute-start | bytes 393224 | tf_op jit(solution)/shard_map/ppermute | solution.py:28
  53.8 1.5 %collective-permute-start.16 = (bf16[512,128]{1,0:T(8,128)(2,1)S(1)}, bf16[512,128]{1,0:T(8,128)(2,1)S(1)}, u32[]{:S(2)}, u32[]{:S(2)}) collective-permute-start(bf16[512,128]{1,0:T(8,128)(2,1)S(1)} %shard_map.64.refs_4_), channel_id=1, source_target_pairs={{0,2},{1,3},{2,0},{3,1},{4,6},{5,7},{6,4},{7,5},{8,10},{9,11},{10,... | collective-permute-start | bytes 393224 | tf_op jit(solution)/shard_map/ppermute | solution.py:28
  55.3 2.4 %collective-permute-done.20.refs_10_ = bf16[512,128]{1,0:T(8,128)(2,1)S(1)} collective-permute-done((bf16[512,128]{1,0:T(8,128)(2,1)S(1)}, bf16[512,128]{1,0:T(8,128)(2,1)S(1)}, u32[]{:S(2)}, u32[]{:S(2)}) %collective-permute-start.20) | collective-permute-done | bytes 131104 | tf_op jit(solution)/shard_map/ppermute | solution.py:28
  57.7 0.8 collective-permute-start.25
  58.5 0.5 collective-permute-start.21
  59.0 0.1 collective-permute-done.16.refs_6_
  59.1 0.4 collective-permute-start.17
  59.5 0.3 collective-permute-done.14.refs_5_
  59.8 0.5 collective-permute-done.19.refs_9_
  60.4 0.2 collective-permute-done.17.refs_7_
  60.5 1.2 %shard_map.65.refs_0_ = bf16[512,512]{1,0:T(8,128)(2,1)S(1)} custom-call(bf16[128,2176]{1,0:T(8,128)(2,1)S(1)} %shard_map.55.refs_0_, bf16[128,2176]{1,0:T(8,128)(2,1)S(1)} %collective-permute-done.4.refs_1_, bf16[128,2176]{1,0:T(8,128)(2,1)S(1)} %collective-permute-done.7.refs_2_, bf16[128,2176]{1,0:T(8,128)(2,1)S(1)} %collective-permute-done.8.refs_3_, ...), custom_call_target="tpu_custom_call" | custom-call | bytes 9568256 | tf_op jit(solution)/shard_map/pallas_call | solution.py:49
  61.7 0.4 collective-permute-start.22
  62.1 1.2 %shard_map.66.refs_1_ = bf16[512,512]{1,0:T(8,128)(2,1)S(1)} custom-call(bf16[128,2176]{1,0:T(8,128)(2,1)S(1)} %shard_map.55.refs_0_, bf16[128,2176]{1,0:T(8,128)(2,1)S(1)} %collective-permute-done.4.refs_1_, bf16[128,2176]{1,0:T(8,128)(2,1)S(1)} %collective-permute-done.7.refs_2_, bf16[128,2176]{1,0:T(8,128)(2,1)S(1)} %collective-permute-done.8.refs_3_, ...), custom_call_target="tpu_custom_call" | custom-call | bytes 9568256 | tf_op jit(solution)/shard_map/pallas_call | solution.py:49
  63.3 0.8 collective-permute-done.25.refs_7_
  64.1 1.9 %collective-permute-done.26.refs_3_ = bf16[512,512]{1,0:T(8,128)(2,1)S(1)} collective-permute-done((bf16[512,512]{1,0:T(8,128)(2,1)S(1)}, bf16[512,512]{1,0:T(8,128)(2,1)S(1)}, u32[]{:S(2)}, u32[]{:S(2)}) %collective-permute-start.26) | collective-permute-done | bytes 524320 | tf_op jit(solution)/shard_map/ppermute | solution.py:28
  66.0 1.9 %shard_map.67 = (bf16[128,2048]{1,0:T(8,128)(2,1)S(1)}, bf16[512,128]{1,0:T(8,128)(2,1)S(1)}, bf16[512,128]{1,0:T(8,128)(2,1)S(1)}, bf16[512,256]{1,0:T(8,128)(2,1)S(1)}, bf16[384,256]{1,0:T(8,128)(2,1)S(1)}) custom-call(bf16[512,512]{1,0:T(8,128)(2,1)S(1)} %shard_map.65.refs_0_, bf16[512,512]{1,0:T(8,128)(2,1)S(1)} %shard_map.66.refs_1_, ...), custom_call_target="tpu_custom_call" | custom-call | bytes 4194304 | tf_op jit(solution)/shard_map/pallas_call | solution.py:49
  67.9 4.9 %collective-permute-start.28 = (bf16[384,256]{1,0:T(8,128)(2,1)S(1)}, bf16[384,256]{1,0:T(8,128)(2,1)S(1)}, u32[]{:S(2)}, u32[]{:S(2)}) collective-permute-start(bf16[384,256]{1,0:T(8,128)(2,1)S(1)} %get-tuple-element.89), channel_id=1, source_target_pairs={{0,4},{1,5},{2,6},{3,7},{4,8},{5,9},{6,10},{7,11},{8,12},{9,13},{1... | collective-permute-start | bytes 589832 | tf_op jit(solution)/shard_map/ppermute | solution.py:33
  72.8 0.7 collective-permute-start.27
  73.4 4.7 %collective-permute-done.27.got_ref = bf16[512,128]{1,0:T(8,128)(2,1)S(1)} collective-permute-done((bf16[512,128]{1,0:T(8,128)(2,1)S(1)}, bf16[512,128]{1,0:T(8,128)(2,1)S(1)}, u32[]{:S(2)}, u32[]{:S(2)}) %collective-permute-start.27) | collective-permute-done | bytes 131104 | tf_op jit(solution)/shard_map/ppermute | solution.py:28
  78.1 1.2 %shard_map.68 = (bf16[256,128]{1,0:T(8,128)(2,1)S(1)}, bf16[256,128]{1,0:T(8,128)(2,1)S(1)}) custom-call(bf16[512,128]{1,0:T(8,128)(2,1)S(1)} %get-tuple-element.86.mine_ref, bf16[512,128]{1,0:T(8,128)(2,1)S(1)} %collective-permute-done.27.got_ref, f32[4,128,512]{2,1,0:T(8,128)S(1)} %shard_map.62.bias_ref, bf16[512,256]{1,0:T(8,128)(2,1)S(1)} %get-tuple-element.88.kv_ref, ...), custom_call_target="tpu_custom_call" | custom-call | flops 134217728 | bytes 1769472 | tf_op jit(solution)/shard_map/pallas_call | solution.py:49
  79.3 0.1 collective-permute-start.29
  79.4 1.2 %collective-permute-done.29.got_ref = bf16[256,128]{1,0:T(8,128)(2,1)S(1)} collective-permute-done((bf16[256,128]{1,0:T(8,128)(2,1)S(1)}, bf16[256,128]{1,0:T(8,128)(2,1)S(1)}, u32[]{:S(2)}, u32[]{:S(2)}) %collective-permute-start.29) | collective-permute-done | bytes 65568 | tf_op jit(solution)/shard_map/ppermute | solution.py:28
  80.6 0.6 collective-permute-start.32
  81.2 1.5 %collective-permute-start.30 = (bf16[256,128]{1,0:T(8,128)(2,1)S(1)}, bf16[256,128]{1,0:T(8,128)(2,1)S(1)}, u32[]{:S(2)}, u32[]{:S(2)}) collective-permute-start(bf16[256,128]{1,0:T(8,128)(2,1)S(1)} %get-tuple-element.93), channel_id=1, source_target_pairs={{0,2},{1,3},{2,0},{3,1},{4,6},{5,7},{6,4},{7,5},{8,10},{9,11},{10,... | collective-permute-start | bytes 196616 | tf_op jit(solution)/shard_map/ppermute | solution.py:28
  82.8 1.4 %collective-permute-start.31 = (bf16[256,128]{1,0:T(8,128)(2,1)S(1)}, bf16[256,128]{1,0:T(8,128)(2,1)S(1)}, u32[]{:S(2)}, u32[]{:S(2)}) collective-permute-start(bf16[256,128]{1,0:T(8,128)(2,1)S(1)} %get-tuple-element.92.refs_0_), channel_id=1, source_target_pairs={{0,16},{1,17},{2,18},{3,19},{4,20},{5,21},{6,22},{7,23},{8,24},{9,... | collective-permute-start | bytes 196616 | tf_op jit(solution)/shard_map/ppermute | solution.py:28
  84.2 2.3 %collective-permute-done.32.refs_3_ = bf16[256,128]{1,0:T(8,128)(2,1)S(1)} collective-permute-done((bf16[256,128]{1,0:T(8,128)(2,1)S(1)}, bf16[256,128]{1,0:T(8,128)(2,1)S(1)}, u32[]{:S(2)}, u32[]{:S(2)}) %collective-permute-start.32) | collective-permute-done | bytes 65568 | tf_op jit(solution)/shard_map/ppermute | solution.py:28
  86.5 0.0 collective-permute-done.30.refs_1_
  86.5 0.5 collective-permute-done.31.refs_2_
  87.0 1.6 %shard_map.70 = bf16[128,2048]{1,0:T(8,128)(2,1)} custom-call(bf16[256,128]{1,0:T(8,128)(2,1)S(1)} %get-tuple-element.92.refs_0_, bf16[256,128]{1,0:T(8,128)(2,1)S(1)} %collective-permute-done.30.refs_1_, bf16[256,128]{1,0:T(8,128)(2,1)S(1)} %collective-permute-done.31.refs_2_, bf16[256,128]{1,0:T(8,128)(2,1)S(1)} %collective-permute-done.32.refs_3_, ...), custom_call_target="tpu_custom_call" | custom-call | flops 536870912 | bytes 4980736 | tf_op jit(solution)/shard_map/pallas_call | solution.py:49
  (30 shorter events, 0.2 us)
Async XLA Ops:
  0.0 1.0 %copy-start.2 = (bf16[1,128,2048]{2,1,0:T(8,128)(2,1)S(1)}, bf16[1,128,2048]{2,1,0:T(8,128)(2,1)}, u32[]{:S(2)}) copy-start(bf16[1,128,2048]{2,1,0:T(8,128)(2,1)} %param.8) | copy-start | bytes 1572868
  1.1 6.7 %collective-permute-start = (bf16[128,512]{1,0:T(8,128)(2,1)S(1)}, bf16[128,512]{1,0:T(8,128)(2,1)S(1)}, u32[]{:S(2)}, u32[]{:S(2)}) collective-permute-start(bf16[128,512]{1,0:T(8,128)(2,1)S(1)} %get-tuple-element.55), channel_id=1, source_target_pairs={{0,2},{1,3},{2,0},{3,1},{4,6},{5,7},{6,4},{7,5},{8,10},{9,11},{10,... | collective-permute-start | bytes 393224 | tf_op jit(solution)/shard_map/ppermute | solution.py:28
  1.7 6.4 %collective-permute-start.1 = (bf16[128,512]{1,0:T(8,128)(2,1)S(1)}, bf16[128,512]{1,0:T(8,128)(2,1)S(1)}, u32[]{:S(2)}, u32[]{:S(2)}) collective-permute-start(bf16[128,512]{1,0:T(8,128)(2,1)S(1)} %get-tuple-element.56), channel_id=1, source_target_pairs={{0,16},{1,17},{2,18},{3,19},{4,20},{5,21},{6,22},{7,23},{8,24},{9,... | collective-permute-start | bytes 393224 | tf_op jit(solution)/shard_map/ppermute | solution.py:28
  2.2 8.2 %collective-permute-start.2 = (bf16[128,512]{1,0:T(8,128)(2,1)S(1)}, bf16[128,512]{1,0:T(8,128)(2,1)S(1)}, u32[]{:S(2)}, u32[]{:S(2)}) collective-permute-start(bf16[128,512]{1,0:T(8,128)(2,1)S(1)} %get-tuple-element.57), channel_id=1, source_target_pairs={{0,18},{1,19},{2,16},{3,17},{4,22},{5,23},{6,20},{7,21},{8,26},{9,... | collective-permute-start | bytes 393224 | tf_op jit(solution)/shard_map/ppermute | solution.py:28
  4.7 10.6 %copy-start.3 = (bf16[1,128,2048]{2,1,0:T(8,128)(2,1)S(1)}, bf16[1,128,2048]{2,1,0:T(8,128)(2,1)}, u32[]{:S(2)}) copy-start(bf16[1,128,2048]{2,1,0:T(8,128)(2,1)} %param.5) | copy-start | bytes 1572868
  4.7 10.6 %copy-start.4 = (s32[1,128]{1,0:T(1,128)S(1)}, s32[1,128]{1,0:T(1,128)}, u32[]{:S(2)}) copy-start(s32[1,128]{1,0:T(1,128)} %id_ref.1) | copy-start | bytes 1540
  10.5 1.6 %collective-permute-start.3 = (bf16[2,256,256]{2,1,0:T(8,128)(2,1)S(1)}, bf16[2,256,256]{2,1,0:T(8,128)(2,1)S(1)}, u32[]{:S(2)}, u32[]{:S(2)}) collective-permute-start(bf16[2,256,256]{2,1,0:T(8,128)(2,1)S(1)} %get-tuple-element.59), channel_id=1, source_target_pairs={{0,1},{1,0},{2,3},{3,2},{4,5},{5,4},{6,7},{7,6},{8,9},{9,8},{10,11... | collective-permute-start | bytes 786440 | tf_op jit(solution)/shard_map/ppermute | solution.py:28
  10.6 19.0 %collective-permute-start.12 = (bf16[352,1024]{1,0:T(8,128)(2,1)}, bf16[352,1024]{1,0:T(8,128)(2,1)S(1)}, u32[]{:S(2)}, u32[]{:S(2)}) collective-permute-start(bf16[352,1024]{1,0:T(8,128)(2,1)} %get-tuple-element.73), channel_id=1, source_target_pairs={{0,16},{1,17},{2,18},{3,19},{4,20},{5,21},{6,22},{7,23},{8,24},{9,... | collective-permute-start | bytes 2162696 | tf_op jit(solution)/shard_map/ppermute | solution.py:28
  12.2 14.0 %collective-permute-start.5 = (bf16[512,256]{1,0:T(8,128)(2,1)S(1)}, bf16[512,256]{1,0:T(8,128)(2,1)S(1)}, u32[]{:S(2)}, u32[]{:S(2)}) collective-permute-start(bf16[512,256]{1,0:T(8,128)(2,1)S(1)} %get-tuple-element.60.refs_0_), channel_id=1, source_target_pairs={{0,8},{1,9},{2,10},{3,11},{4,12},{5,13},{6,14},{7,15},{8,0},{9,1},... | collective-permute-start | bytes 786440 | tf_op jit(solution)/shard_map/ppermute | solution.py:28
  14.8 12.4 %collective-permute-start.6 = (bf16[512,256]{1,0:T(8,128)(2,1)S(1)}, bf16[512,256]{1,0:T(8,128)(2,1)S(1)}, u32[]{:S(2)}, u32[]{:S(2)}) collective-permute-start(bf16[512,256]{1,0:T(8,128)(2,1)S(1)} %get-tuple-element.60.refs_0_), channel_id=1, source_target_pairs={{0,4},{1,5},{2,6},{3,7},{4,0},{5,1},{6,2},{7,3},{8,12},{9,13},{10,... | collective-permute-start | bytes 786440 | tf_op jit(solution)/shard_map/ppermute | solution.py:28
  15.4 16.2 %copy-start.1 = (bf16[2048,256]{1,0:T(8,128)(2,1)S(1)}, bf16[2048,256]{1,0:T(8,128)(2,1)}, u32[]{:S(2)}) copy-start(bf16[2048,256]{1,0:T(8,128)(2,1)} %get-tuple-element.64.refs_4_.refs_8_) | copy-start | bytes 3145732
  15.5 18.2 %copy-start.5 = (bf16[320,1024]{1,0:T(8,128)(2,1)S(1)}, bf16[320,1024]{1,0:T(8,128)(2,1)}, u32[]{:S(2)}) copy-start(bf16[320,1024]{1,0:T(8,128)(2,1)} %get-tuple-element.77) | copy-start | bytes 1966084
  15.5 14.2 %collective-permute-start.4 = (bf16[128,2176]{1,0:T(8,128)(2,1)S(1)}, bf16[128,2176]{1,0:T(8,128)(2,1)S(1)}, u32[]{:S(2)}, u32[]{:S(2)}) collective-permute-start(bf16[128,2176]{1,0:T(8,128)(2,1)S(1)} %shard_map.55.refs_0_), channel_id=1, source_target_pairs={{0,2},{1,3},{2,0},{3,1},{4,6},{5,7},{6,4},{7,5},{8,10},{9,11},{10,... | collective-permute-start | bytes 1671176 | tf_op jit(solution)/shard_map/ppermute | solution.py:28
  27.3 3.0 %collective-permute-start.7 = (bf16[128,2176]{1,0:T(8,128)(2,1)S(1)}, bf16[128,2176]{1,0:T(8,128)(2,1)S(1)}, u32[]{:S(2)}, u32[]{:S(2)}) collective-permute-start(bf16[128,2176]{1,0:T(8,128)(2,1)S(1)} %shard_map.55.refs_0_), channel_id=1, source_target_pairs={{0,1},{1,0},{2,3},{3,2},{4,5},{5,4},{6,7},{7,6},{8,9},{9,8},{10,11... | collective-permute-start | bytes 1671176 | tf_op jit(solution)/shard_map/ppermute | solution.py:28
  27.3 8.7 %collective-permute-start.10 = (bf16[512,256]{1,0:T(8,128)(2,1)S(1)}, bf16[512,256]{1,0:T(8,128)(2,1)S(1)}, u32[]{:S(2)}, u32[]{:S(2)}) collective-permute-start(bf16[512,256]{1,0:T(8,128)(2,1)S(1)} %collective-permute-done.5.refs_2_), channel_id=1, source_target_pairs={{0,4},{1,5},{2,6},{3,7},{4,0},{5,1},{6,2},{7,3},{8,12},{9,13},{10,... | collective-permute-start | bytes 786440 | tf_op jit(solution)/shard_map/ppermute | solution.py:28
  29.6 2.0 %collective-permute-start.8 = (bf16[128,2176]{1,0:T(8,128)(2,1)S(1)}, bf16[128,2176]{1,0:T(8,128)(2,1)S(1)}, u32[]{:S(2)}, u32[]{:S(2)}) collective-permute-start(bf16[128,2176]{1,0:T(8,128)(2,1)S(1)} %collective-permute-done.4.refs_1_), channel_id=1, source_target_pairs={{0,1},{1,0},{2,3},{3,2},{4,5},{5,4},{6,7},{7,6},{8,9},{9,8},{10,11... | collective-permute-start | bytes 1671176 | tf_op jit(solution)/shard_map/ppermute | solution.py:28
  29.7 20.8 %collective-permute-start.13 = (bf16[352,1024]{1,0:T(8,128)(2,1)S(1)}, bf16[352,1024]{1,0:T(8,128)(2,1)S(1)}, u32[]{:S(2)}, u32[]{:S(2)}) collective-permute-start(bf16[352,1024]{1,0:T(8,128)(2,1)S(1)} %shard_map.63), channel_id=1, source_target_pairs={{0,2},{1,3},{2,0},{3,1},{4,6},{5,7},{6,4},{7,5},{8,10},{9,11},{10,... | collective-permute-start | bytes 2162696 | tf_op jit(solution)/shard_map/ppermute | solution.py:28
  33.0 7.7 %collective-permute-start.9 = (bf16[512,128]{1,0:T(8,128)(2,1)S(1)}, bf16[512,128]{1,0:T(8,128)(2,1)S(1)}, u32[]{:S(2)}, u32[]{:S(2)}) collective-permute-start(bf16[512,128]{1,0:T(8,128)(2,1)S(1)} %get-tuple-element.66), channel_id=1, source_target_pairs={{0,16},{1,17},{2,18},{3,19},{4,20},{5,21},{6,22},{7,23},{8,24},{9,... | collective-permute-start | bytes 393224 | tf_op jit(solution)/shard_map/ppermute | solution.py:28
  33.7 20.1 %collective-permute-start.15 = (bf16[320,1024]{1,0:T(8,128)(2,1)S(1)}, bf16[320,1024]{1,0:T(8,128)(2,1)S(1)}, u32[]{:S(2)}, u32[]{:S(2)}) collective-permute-start(bf16[320,1024]{1,0:T(8,128)(2,1)S(1)} %copy-done.5), channel_id=1, source_target_pairs={{0,16},{1,17},{2,18},{3,19},{4,20},{5,21},{6,22},{7,23},{8,24},{9,... | collective-permute-start | bytes 1966088 | tf_op jit(solution)/shard_map/ppermute | solution.py:28
  36.8 23.8 %copy-start = (bf16[1,1024,2048]{2,1,0:T(8,128)(2,1)S(1)}, bf16[1,1024,2048]{2,1,0:T(8,128)(2,1)}, u32[]{:S(2)}) copy-start(bf16[1,1024,2048]{2,1,0:T(8,128)(2,1)} %param.9) | copy-start | bytes 12582916
  36.8 13.5 %collective-permute-start.11 = (bf16[400,256]{1,0:T(8,128)(2,1)S(1)}, bf16[400,256]{1,0:T(8,128)(2,1)S(1)}, u32[]{:S(2)}, u32[]{:S(2)}) collective-permute-start(bf16[400,256]{1,0:T(8,128)(2,1)S(1)} %get-tuple-element.70), channel_id=1, source_target_pairs={{0,4},{1,5},{2,6},{3,7},{4,8},{5,9},{6,10},{7,11},{8,12},{9,13},{1... | collective-permute-start | bytes 614408 | tf_op jit(solution)/shard_map/ppermute | solution.py:33
  40.1 17.6 %collective-permute-start.23 = (bf16[512,256]{1,0:T(8,128)(2,1)S(1)}, bf16[512,256]{1,0:T(8,128)(2,1)S(1)}, u32[]{:S(2)}, u32[]{:S(2)}) collective-permute-start(bf16[512,256]{1,0:T(8,128)(2,1)S(1)} %get-tuple-element.83.refs_4_), channel_id=1, source_target_pairs={{0,8},{1,9},{2,10},{3,11},{4,12},{5,13},{6,14},{7,15},{8,0},{9,1},... | collective-permute-start | bytes 786440 | tf_op jit(solution)/shard_map/ppermute | solution.py:28
  40.7 17.0 %collective-permute-start.24 = (bf16[512,256]{1,0:T(8,128)(2,1)S(1)}, bf16[512,256]{1,0:T(8,128)(2,1)S(1)}, u32[]{:S(2)}, u32[]{:S(2)}) collective-permute-start(bf16[512,256]{1,0:T(8,128)(2,1)S(1)} %get-tuple-element.83.refs_4_), channel_id=1, source_target_pairs={{0,4},{1,5},{2,6},{3,7},{4,0},{5,1},{6,2},{7,3},{8,12},{9,13},{10,... | collective-permute-start | bytes 786440 | tf_op jit(solution)/shard_map/ppermute | solution.py:28
  51.7 6.0 %collective-permute-start.20 = (bf16[512,128]{1,0:T(8,128)(2,1)S(1)}, bf16[512,128]{1,0:T(8,128)(2,1)S(1)}, u32[]{:S(2)}, u32[]{:S(2)}) collective-permute-start(bf16[512,128]{1,0:T(8,128)(2,1)S(1)} %shard_map.64.refs_4_), channel_id=1, source_target_pairs={{0,18},{1,19},{2,16},{3,17},{4,22},{5,23},{6,20},{7,21},{8,26},{9,... | collective-permute-start | bytes 393224 | tf_op jit(solution)/shard_map/ppermute | solution.py:28
  52.4 6.6 %collective-permute-start.18 = (bf16[512,128]{1,0:T(8,128)(2,1)S(1)}, bf16[512,128]{1,0:T(8,128)(2,1)S(1)}, u32[]{:S(2)}, u32[]{:S(2)}) collective-permute-start(bf16[512,128]{1,0:T(8,128)(2,1)S(1)} %shard_map.64.refs_4_), channel_id=1, source_target_pairs={{0,16},{1,17},{2,18},{3,19},{4,20},{5,21},{6,22},{7,23},{8,24},{9,... | collective-permute-start | bytes 393224 | tf_op jit(solution)/shard_map/ppermute | solution.py:28
  53.8 5.3 %collective-permute-start.16 = (bf16[512,128]{1,0:T(8,128)(2,1)S(1)}, bf16[512,128]{1,0:T(8,128)(2,1)S(1)}, u32[]{:S(2)}, u32[]{:S(2)}) collective-permute-start(bf16[512,128]{1,0:T(8,128)(2,1)S(1)} %shard_map.64.refs_4_), channel_id=1, source_target_pairs={{0,2},{1,3},{2,0},{3,1},{4,6},{5,7},{6,4},{7,5},{8,10},{9,11},{10,... | collective-permute-start | bytes 393224 | tf_op jit(solution)/shard_map/ppermute | solution.py:28
  57.7 6.4 %collective-permute-start.25 = (bf16[512,256]{1,0:T(8,128)(2,1)S(1)}, bf16[512,256]{1,0:T(8,128)(2,1)S(1)}, u32[]{:S(2)}, u32[]{:S(2)}) collective-permute-start(bf16[512,256]{1,0:T(8,128)(2,1)S(1)} %collective-permute-done.23.refs_6_), channel_id=1, source_target_pairs={{0,4},{1,5},{2,6},{3,7},{4,0},{5,1},{6,2},{7,3},{8,12},{9,13},{10,... | collective-permute-start | bytes 786440 | tf_op jit(solution)/shard_map/ppermute | solution.py:28
  58.5 1.3 %collective-permute-start.14 = (bf16[512,128]{1,0:T(8,128)(2,1)S(1)}, bf16[512,128]{1,0:T(8,128)(2,1)S(1)}, u32[]{:S(2)}, u32[]{:S(2)}) collective-permute-start(bf16[512,128]{1,0:T(8,128)(2,1)S(1)} %shard_map.64.refs_4_), channel_id=1, source_target_pairs={{0,1},{1,0},{2,3},{3,2},{4,5},{5,4},{6,7},{7,6},{8,9},{9,8},{10,11... | collective-permute-start | bytes 393224 | tf_op jit(solution)/shard_map/ppermute | solution.py:28
  58.5 1.9 %collective-permute-start.21 = (bf16[512,128]{1,0:T(8,128)(2,1)S(1)}, bf16[512,128]{1,0:T(8,128)(2,1)S(1)}, u32[]{:S(2)}, u32[]{:S(2)}) collective-permute-start(bf16[512,128]{1,0:T(8,128)(2,1)S(1)} %collective-permute-done.20.refs_10_), channel_id=1, source_target_pairs={{0,1},{1,0},{2,3},{3,2},{4,5},{5,4},{6,7},{7,6},{8,9},{9,8},{10,11... | collective-permute-start | bytes 393224 | tf_op jit(solution)/shard_map/ppermute | solution.py:28
  59.0 1.3 %collective-permute-start.19 = (bf16[512,128]{1,0:T(8,128)(2,1)S(1)}, bf16[512,128]{1,0:T(8,128)(2,1)S(1)}, u32[]{:S(2)}, u32[]{:S(2)}) collective-permute-start(bf16[512,128]{1,0:T(8,128)(2,1)S(1)} %collective-permute-done.18.refs_8_), channel_id=1, source_target_pairs={{0,1},{1,0},{2,3},{3,2},{4,5},{5,4},{6,7},{7,6},{8,9},{9,8},{10,11... | collective-permute-start | bytes 393224 | tf_op jit(solution)/shard_map/ppermute | solution.py:28
  59.1 1.5 %collective-permute-start.17 = (bf16[512,128]{1,0:T(8,128)(2,1)S(1)}, bf16[512,128]{1,0:T(8,128)(2,1)S(1)}, u32[]{:S(2)}, u32[]{:S(2)}) collective-permute-start(bf16[512,128]{1,0:T(8,128)(2,1)S(1)} %collective-permute-done.16.refs_6_), channel_id=1, source_target_pairs={{0,1},{1,0},{2,3},{3,2},{4,5},{5,4},{6,7},{7,6},{8,9},{9,8},{10,11... | collective-permute-start | bytes 393224 | tf_op jit(solution)/shard_map/ppermute | solution.py:28
  61.7 2.4 %collective-permute-start.22 = (bf16[512,512]{1,0:T(8,128)(2,1)S(1)}, bf16[512,512]{1,0:T(8,128)(2,1)S(1)}, u32[]{:S(2)}, u32[]{:S(2)}) collective-permute-start(bf16[512,512]{1,0:T(8,128)(2,1)S(1)} %shard_map.65.refs_0_), channel_id=1, source_target_pairs={{0,1},{1,0},{2,3},{3,2},{4,5},{5,4},{6,7},{7,6},{8,9},{9,8},{10,11... | collective-permute-start | bytes 1572872 | tf_op jit(solution)/shard_map/ppermute | solution.py:28
  64.1 1.9 %collective-permute-start.26 = (bf16[512,512]{1,0:T(8,128)(2,1)S(1)}, bf16[512,512]{1,0:T(8,128)(2,1)S(1)}, u32[]{:S(2)}, u32[]{:S(2)}) collective-permute-start(bf16[512,512]{1,0:T(8,128)(2,1)S(1)} %shard_map.66.refs_1_), channel_id=1, source_target_pairs={{0,1},{1,0},{2,3},{3,2},{4,5},{5,4},{6,7},{7,6},{8,9},{9,8},{10,11... | collective-permute-start | bytes 1572872 | tf_op jit(solution)/shard_map/ppermute | solution.py:28
  67.9 10.2 %collective-permute-start.28 = (bf16[384,256]{1,0:T(8,128)(2,1)S(1)}, bf16[384,256]{1,0:T(8,128)(2,1)S(1)}, u32[]{:S(2)}, u32[]{:S(2)}) collective-permute-start(bf16[384,256]{1,0:T(8,128)(2,1)S(1)} %get-tuple-element.89), channel_id=1, source_target_pairs={{0,4},{1,5},{2,6},{3,7},{4,8},{5,9},{6,10},{7,11},{8,12},{9,13},{1... | collective-permute-start | bytes 589832 | tf_op jit(solution)/shard_map/ppermute | solution.py:33
  72.8 5.3 %collective-permute-start.27 = (bf16[512,128]{1,0:T(8,128)(2,1)S(1)}, bf16[512,128]{1,0:T(8,128)(2,1)S(1)}, u32[]{:S(2)}, u32[]{:S(2)}) collective-permute-start(bf16[512,128]{1,0:T(8,128)(2,1)S(1)} %get-tuple-element.87), channel_id=1, source_target_pairs={{0,16},{1,17},{2,18},{3,19},{4,20},{5,21},{6,22},{7,23},{8,24},{9,... | collective-permute-start | bytes 393224 | tf_op jit(solution)/shard_map/ppermute | solution.py:28
  79.3 1.3 %collective-permute-start.29 = (bf16[256,128]{1,0:T(8,128)(2,1)S(1)}, bf16[256,128]{1,0:T(8,128)(2,1)S(1)}, u32[]{:S(2)}, u32[]{:S(2)}) collective-permute-start(bf16[256,128]{1,0:T(8,128)(2,1)S(1)} %get-tuple-element.91), channel_id=1, source_target_pairs={{0,1},{1,0},{2,3},{3,2},{4,5},{5,4},{6,7},{7,6},{8,9},{9,8},{10,11... | collective-permute-start | bytes 196616 | tf_op jit(solution)/shard_map/ppermute | solution.py:28
  80.6 5.8 %collective-permute-start.32 = (bf16[256,128]{1,0:T(8,128)(2,1)S(1)}, bf16[256,128]{1,0:T(8,128)(2,1)S(1)}, u32[]{:S(2)}, u32[]{:S(2)}) collective-permute-start(bf16[256,128]{1,0:T(8,128)(2,1)S(1)} %get-tuple-element.93), channel_id=1, source_target_pairs={{0,18},{1,19},{2,16},{3,17},{4,22},{5,23},{6,20},{7,21},{8,26},{9,... | collective-permute-start | bytes 196616 | tf_op jit(solution)/shard_map/ppermute | solution.py:28
  81.2 5.3 %collective-permute-start.30 = (bf16[256,128]{1,0:T(8,128)(2,1)S(1)}, bf16[256,128]{1,0:T(8,128)(2,1)S(1)}, u32[]{:S(2)}, u32[]{:S(2)}) collective-permute-start(bf16[256,128]{1,0:T(8,128)(2,1)S(1)} %get-tuple-element.93), channel_id=1, source_target_pairs={{0,2},{1,3},{2,0},{3,1},{4,6},{5,7},{6,4},{7,5},{8,10},{9,11},{10,... | collective-permute-start | bytes 196616 | tf_op jit(solution)/shard_map/ppermute | solution.py:28
  82.8 4.3 %collective-permute-start.31 = (bf16[256,128]{1,0:T(8,128)(2,1)S(1)}, bf16[256,128]{1,0:T(8,128)(2,1)S(1)}, u32[]{:S(2)}, u32[]{:S(2)}) collective-permute-start(bf16[256,128]{1,0:T(8,128)(2,1)S(1)} %get-tuple-element.92.refs_0_), channel_id=1, source_target_pairs={{0,16},{1,17},{2,18},{3,19},{4,20},{5,21},{6,22},{7,23},{8,24},{9,... | collective-permute-start | bytes 196616 | tf_op jit(solution)/shard_map/ppermute | solution.py:28
